TPU v7x, 128 devices: a whole 4x4x4 slice. The times are simulated.
128 devices in a mesh: role: 2 (over core), dp: 8 (over y, x_lo), tensor: 8 (over z, x_hi).
Axes of the slice: x: 4 (x_hi: 2, x_lo: 2; x = x_hi * 2 + x_lo), y: 4, z: 4, core: 2. Of those that a mesh axis runs over, the one named last changes fastest.
Arguments:
- teacher_in: bfloat16 [2, 2048, 16384], P(None, 'dp', ('role', 'tensor')), may hold values from -16 to 16
- teacher_weight: bfloat16 [16384, 8192], P(('role', 'tensor')), may hold values from -0.046875 to 0.046875
- student_in: bfloat16 [4096, 8192], P(('role', 'dp')), may hold values from -6 to 6
- student_weight: bfloat16 [8192, 4096], P(('role', 'dp'), 'tensor'), may hold values from -0.0625 to 0.0625
- projector: bfloat16 [4096, 8192], P('tensor', ('role', 'dp')), may hold values from -0.09375 to 0.09375
Outputs:
- grad_weight: float32 [8192, 4096], P(('role', 'dp'), 'tensor')
- loss: float32 [], replicated
All inputs are finite; a program needn't handle non-finite values.
Results may differ from a plain program's by a relative error of at most 0.015.
Values may be sent and summed in bfloat16 or wider, within the bound.
No kernel may reach another device: no remote copies, remote signals or barrier semaphores. Data moves between devices by JAX's collectives and lax.ppermute only.
A program may use at most 192 MiB of HBM per device.

v0:
```python
import jax
import jax.numpy as jnp
from jax import lax
from jax.sharding import PartitionSpec as P


def shards(teacher_in, teacher_weight, student_in, student_weight, projector):
    n_role = lax.axis_size("role")
    n_data = lax.axis_size("dp")
    n_model = lax.axis_size("tensor")
    halves, half_rows, feat_local = teacher_in.shape
    out_width = teacher_weight.shape[1]
    col_width = out_width // n_model
    weight_blocks = teacher_weight.reshape(feat_local, n_model, col_width)
    blocks = half_rows * lax.axis_size(("role", "tensor")) // half_rows
    owners = jnp.arange(blocks, dtype=jnp.int32)
    chosen_rows = jnp.take(teacher_in, owners // n_model, axis=0)
    chosen_cols = jnp.take(weight_blocks, owners % n_model, axis=1)
    term = jnp.einsum("bif,fbc->bic", chosen_rows, chosen_cols, preferred_element_type=jnp.float32)
    teacher_hidden = lax.psum_scatter(
        term.reshape(blocks * half_rows, col_width),
        ("role", "tensor"),
        scatter_dimension=0,
        tiled=True,
    )
    rows = student_in.shape[0]
    total_rows = rows * n_role * n_data
    columns = student_in
    pre = jnp.dot(
        columns,
        lax.all_gather(student_weight, ("role", "dp"), axis=0, tiled=True),
        preferred_element_type=jnp.float32,
    )
    hidden = jax.nn.silu(pre).astype(jnp.bfloat16)
    projector_full = lax.all_gather(projector, ("role", "dp"), axis=1, tiled=True)
    partial_value = jnp.dot(hidden, projector_full, preferred_element_type=jnp.float32)
    projection = lax.psum_scatter(
        partial_value.astype(jnp.bfloat16), "tensor", scatter_dimension=1, tiled=True
    ).astype(jnp.float32)
    difference = projection - teacher_hidden
    loss = lax.psum(jnp.sum(difference * difference), ("role", "dp", "tensor")) / (
        2.0 * total_rows * out_width
    )
    residual = difference.astype(jnp.bfloat16)
    residual_all = lax.all_gather(residual, "tensor", axis=1, tiled=True)
    back = lax.dot_general(
        residual_all, projector_full, (((1,), (1,)), ((), ())), preferred_element_type=jnp.float32
    )
    sigma = jax.nn.sigmoid(pre)
    delta = (back * sigma * (1.0 + pre * (1.0 - sigma))).astype(jnp.bfloat16)
    columns = student_in
    grad_weight = lax.psum_scatter(
        lax.dot_general(
            columns, delta, (((0,), (0,)), ((), ())), preferred_element_type=jnp.float32
        ),
        ("role", "dp"),
        scatter_dimension=0,
        tiled=True,
    )
    return (grad_weight / jnp.sqrt(jnp.float32(total_rows)), loss)


def solution(mesh):
    in_specs = (
        P(None, "dp", ("role", "tensor")),
        P(("role", "tensor"), None),
        P(("role", "dp"), None),
        P(("role", "dp"), "tensor"),
        P("tensor", ("role", "dp")),
    )
    out_specs = (P(("role", "dp"), "tensor"), P())
    return jax.shard_map(shards, mesh=mesh, in_specs=in_specs, out_specs=out_specs, check_vma=False)
```

profile of v0, /device:TPU:0, one launch (start us, length us, event | category | flops | bytes accessed | tf_op | source)
XLA Modules:
  0.0 830.2 jit_solution(16803095397064915489)
XLA Ops:
  7.2 0.0 copy-start
  7.2 0.0 all-gather.4.cloned.1.call-start
  7.2 0.7 all-gather.4.cloned.1.call-update
  7.9 0.0 all-gather.6.cloned.1.call-start
  8.0 0.7 all-gather.6.cloned.1.call-update
  8.7 0.0 reduce-scatter.4.cloned.1.call-start
  8.7 55.6 %all-gather.4.cloned.1.call-done = bf16[8192,512]{1,0:T(8,128)(2,1)} async-done(((bf16[512,512]{1,0:T(8,128)(2,1)}), bf16[8192,512]{1,0:T(8,128)(2,1)}) %all-gather.4.cloned.1.call-update) | async-done | bytes 8388624 | tf_op jit(solution)/shard_map/all_gather | solution.py:31
  64.3 7.0 fusion.23
  71.3 47.8 %all-gather.6.cloned.1.call-done = bf16[512,8192]{1,0:T(8,128)(2,1)} async-done(((bf16[512,512]{1,0:T(8,128)(2,1)}), bf16[512,8192]{1,0:T(8,128)(2,1)}) %all-gather.6.cloned.1.call-update) | async-done | bytes 8388624 | tf_op jit(solution)/shard_map/all_gather | solution.py:35
  119.1 7.8 convolution_convert_fusion
  126.9 0.0 reduce-scatter.4.cloned.1.call-update
  126.9 0.0 reduce-scatter.6.cloned.1.call-start
  127.0 11.7 %fusion.22 = (bf16[512,8192]{1,0:T(8,128)(2,1)}, bf16[512,8192]{1,0:T(8,128)(2,1)}) fusion(bf16[1024,8192]{1,0:T(8,128)(2,1)} %param.6), kind=kLoop, calls=%fused_computation.52 | loop fusion | bytes 33554432 | tf_op jit(solution)/shard_map/jit(_take)/gather | solution.py:18
  138.7 11.9 %copy.14 = bf16[512,8192]{0,1:T(8,128)(2,1)} copy(bf16[512,8192]{1,0:T(8,128)(2,1)} %get-tuple-element.8) | data formatting | bytes 16777216
  150.6 11.6 %copy.10 = bf16[512,8,1024]{2,0,1:T(8,128)(2,1)} copy(bf16[512,8,1024]{0,2,1:T(8,128)(2,1)} %bitcast.17) | data formatting | bytes 16777216 | tf_op jit(solution)/shard_map/jit(_take)/gather | solution.py:18
  162.3 12.0 %copy.15 = bf16[512,8192]{0,1:T(8,128)(2,1)} copy(bf16[512,8192]{1,0:T(8,128)(2,1)} %get-tuple-element.9) | data formatting | bytes 16777216
  174.3 11.5 %copy.12 = bf16[512,8,1024]{2,0,1:T(8,128)(2,1)} copy(bf16[512,8,1024]{0,2,1:T(8,128)(2,1)} %bitcast.18) | data formatting | bytes 16777216 | tf_op jit(solution)/shard_map/jit(_take)/gather | solution.py:18
  185.8 10.7 %gather_fusion.1 = bf16[16,512,1024]{2,1,0:T(8,128)(2,1)} fusion(bf16[512,8,1024]{2,0,1:T(8,128)(2,1)} %copy.10, s32[1024]{0:T(1024)S(1)} %pad_clamp_fusion), kind=kCustom, calls=%fused_computation.1 | custom fusion | bytes 33554496 | tf_op jit(solution)/shard_map/jit(_take)/gather | solution.py:18
  196.5 10.7 %gather_fusion.2 = bf16[16,512,1024]{2,1,0:T(8,128)(2,1)} fusion(bf16[512,8,1024]{2,0,1:T(8,128)(2,1)} %copy.12, s32[1024]{0:T(1024)S(1)} %pad_clamp_fusion), kind=kCustom, calls=%fused_computation.2 | custom fusion | bytes 33554496 | tf_op jit(solution)/shard_map/jit(_take)/gather | solution.py:18
  207.2 0.0 copy-done
  207.2 4.9 gather_fusion
  212.1 22.0 %fusion = f32[16,256,1024]{2,1,0:T(8,128)} fusion(bf16[512,16,1024]{2,0,1:T(8,128)(2,1)} %bitcast.21, bf16[512,16,1024]{2,0,1:T(8,128)(2,1)} %bitcast.20, pred[16]{0:T(512)(128)(4,1)S(1)} %get-tuple-element.12, bf16[16,256,1024]{2,1,0:T(8,128)(2,1)} %gather_fusion, pred[16]{0:T(512)(128)(4,1)S(1)} %get-tuple-element.13), kind=kOutput, calls=%fused_computation.4 | convolution fusion | flops 8678014976 | bytes 58720288 | tf_op jit(solution)/shard_map/bif,fbc->bic/dot_general | solution.py:19
  234.1 0.0 reduce-scatter.6.cloned.1.call-update
  234.1 0.0 all-gather.8.cloned.1.call-start
  234.1 0.0 reduce-scatter.4.cloned.1.call-done
  234.2 148.6 %reduce-scatter.6.cloned.1.call-done = f32[256,1024]{1,0:T(8,128)} async-done(((f32[4096,1024]{1,0:T(8,128)}), f32[256,1024]{1,0:T(8,128)}) %reduce-scatter.6.cloned.1.call-update) | async-done | bytes 1048592 | tf_op jit(solution)/shard_map/reduce_scatter | solution.py:20
  382.8 3.0 multiply_reduce_fusion
  385.8 0.0 all-gather.8.cloned.1.call-update
  385.8 0.2 reduce-scatter.8.cloned.1.call-start
  386.0 69.3 %all-gather.8.cloned.1.call-done = bf16[256,8192]{1,0:T(8,128)(2,1)} async-done(((bf16[256,1024]{1,0:T(8,128)(2,1)}), bf16[256,8192]{1,0:T(8,128)(2,1)}) %all-gather.8.cloned.1.call-update) | async-done | bytes 4194320 | tf_op jit(solution)/shard_map/all_gather | solution.py:45
  455.3 16.3 %convolution_bitcast_fusion = f32[8192,512]{0,1:T(8,128)} fusion(bf16[256,8192]{1,0:T(8,128)(2,1)} %param.7, bf16[256,8192]{1,0:T(8,128)(2,1)} %all-gather.8.cloned.1.call-done, bf16[512,8192]{1,0:T(8,128)(2,1)} %all-gather.6.cloned.1.call-done, f32[256,512]{1,0:T(8,128)S(1)} %fusion.23), kind=kOutput, calls=%fused_computation.9 | convolution fusion | flops 4296146944 | bytes 34078720 | tf_op jit(solution)/shard_map/dot_general | solution.py:53
  471.6 0.0 copy-start.1
  471.6 0.0 reduce-scatter.8.cloned.1.call-update
  471.6 67.1 %psum.7 = f32[]{:T(128)} all-reduce(f32[]{:T(128)} %get-tuple-element.10), channel_id=1, replica_groups=mesh['role'=2,'dp'=8,'tensor'=8] {'role','dp','tensor'}, use_global_device_ids=true, to_apply=%region_4.5 | all-reduce | flops 1 | bytes 8 | tf_op jit(solution)/shard_map/psum | solution.py:41
  539.4 280.2 %reduce-scatter.8.cloned.1.call-done = f32[512,512]{0,1:T(8,128)} async-done(((f32[8192,512]{0,1:T(8,128)}), f32[512,512]{0,1:T(8,128)}) %reduce-scatter.8.cloned.1.call-update) | async-done | bytes 1048592 | tf_op jit(solution)/shard_map/reduce_scatter | solution.py:52
  819.6 1.3 broadcast_multiply_fusion
  820.9 1.3 copy.13
  822.3 0.0 copy-done.1
  (5 shorter events, 0.0 us)
Async XLA Ops:
  7.2 200.0 %copy-start = (bf16[2,256,1024]{2,1,0:T(8,128)(2,1)S(1)}, bf16[2,256,1024]{2,1,0:T(8,128)(2,1)}, u32[]{:S(2)}) copy-start(bf16[2,256,1024]{2,1,0:T(8,128)(2,1)} %param.5) | copy-start | bytes 3145732
  7.2 57.1 %all-gather.4.cloned.1.call-start = ((), (), s32[]{:S(2)}) async-start(), calls=%async_computation.3 | async-start | bytes 8912896 | tf_op jit(solution)/shard_map/all_gather | solution.py:31
  7.9 111.2 %all-gather.6.cloned.1.call-start = ((), (), s32[]{:S(2)}) async-start(), calls=%async_computation.4 | async-start | bytes 8912896 | tf_op jit(solution)/shard_map/all_gather | solution.py:35
  8.7 225.5 %reduce-scatter.4.cloned.1.call-start = ((), (), s32[]{:S(2)}) async-start(), calls=%async_computation.5 | async-start | bytes 4718592 | tf_op jit(solution)/shard_map/reduce_scatter | solution.py:37
  126.9 255.9 %reduce-scatter.6.cloned.1.call-start = ((), (), s32[]{:S(2)}) async-start(), calls=%async_computation.6 | async-start | bytes 17825792 | tf_op jit(solution)/shard_map/reduce_scatter | solution.py:20
  234.1 221.2 %all-gather.8.cloned.1.call-start = ((), (), s32[]{:S(2)}) async-start(), calls=%async_computation.7 | async-start | bytes 4718592 | tf_op jit(solution)/shard_map/all_gather | solution.py:45
  385.8 433.8 %reduce-scatter.8.cloned.1.call-start = ((), (), s32[]{:S(2)}) async-start(), calls=%async_computation.8 | async-start | bytes 17825792 | tf_op jit(solution)/shard_map/reduce_scatter | solution.py:52
  471.6 350.7 %copy-start.1 = (bf16[2,256,1024]{2,1,0:T(8,128)(2,1)S(1)}, bf16[2,256,1024]{2,1,0:T(8,128)(2,1)}, u32[]{:S(2)}) copy-start(bf16[2,256,1024]{2,1,0:T(8,128)(2,1)} %param.5) | copy-start | bytes 3145732
Sparse Core Ops, SparseCore 0:
  9.7 54.5 all-gather.3
  66.0 53.0 all-gather.5
  127.0 85.6 reduce-scatter.3
  234.2 148.5 reduce-scatter.5
  385.9 69.3 all-gather.7
  471.7 347.8 reduce-scatter.7
where the time goes:
time: 833 us; the launch traced here: 830 us
  waiting for transfers between devices  603 us (72%)
  local copies, waits for them, and re-layouts  86.4 us (10%)
  blocking collectives  67.1 us (8%)
  matrix products  53 us (6%)
  between operations  15.9 us (2%)
    reduce_scatter x1, waiting for transfers between devices, shards(): lax.psum_scatter(lax.dot_general(columns, delta, (((0,), (0,)), ((), ()))...  280 us
    reduce_scatter x1, waiting for transfers between devices, shards(): lax.psum_scatter(term.reshape(blocks * half_rows, col_width), ('role', 't...  149 us
    all_gather x1, waiting for transfers between devices, shards(): residual_all = lax.all_gather(residual, 'tensor', axis=1, tiled=True)  69.3 us
    psum x1, blocking collectives, shards(): lax.psum(jnp.sum(difference * difference), ('role', 'dp', 'tensor'))  67.1 us
    gather x5, local copies, waits for them, and re-layouts, shards(): chosen_cols = jnp.take(weight_blocks, owners % n_model, axis=1)  56.2 us
    all_gather x1, waiting for transfers between devices, shards(): lax.all_gather(student_weight, ('role', 'dp'), axis=0, tiled=True)  55.6 us
    all_gather x1, waiting for transfers between devices, shards(): lax.all_gather(projector, ('role', 'dp'), axis=1, tiled=True)  47.8 us
    unnamed x7, local copies, waits for them, and re-layouts  25.2 us
  transfers between devices with their start and end apart: 6, of which 5 were waited for; matrix products, arithmetic and copies ran while one was open for 14% of the time, Pallas kernels for 0%

commit v1 on v0

v1 whole, which is shorter than its diff:
```python
import jax
import jax.numpy as jnp
from jax import lax
from jax.sharding import PartitionSpec as P

BF16 = jnp.bfloat16
F32 = jnp.float32
NOTE = 16
OFFSETS = ((0, 0), (0, 1), (1, 0), (-1, 0), (2, 0), (1, 1), (-1, 1), (2, 1))


def shift(value, axis, k, e):
    perm = [(i, ((i // 2 + k) % 4) * 2 + ((i % 2) ^ e)) for i in range(8)]
    return lax.ppermute(value, axis, perm)


def flip(value):
    return lax.ppermute(value, "role", [(0, 1), (1, 0)])


def sources(axis):
    me = lax.axis_index(axis)
    return [((((me >> 1) - k) & 3) << 1) | ((me & 1) ^ e) for k, e in OFFSETS]


def after(value, *others):
    return lax.optimization_barrier((value, *others))[0]


def gather_start(block, axis):
    return [shift(block, axis, 0, 1), shift(block, axis, 1, 0), shift(block, axis, -1, 0)]


def gather_middle(block, first, axis):
    other, before, nxt = first
    half = block.shape[0] // 2
    up = shift(jnp.concatenate([other, before[:half]], axis=0), axis, 1, 0)
    down = shift(jnp.concatenate([other, nxt[half:]], axis=0), axis, -1, 0)
    return [up, down]


def gather_end(block, first, middle, axis, by_pair):
    other, before, nxt = first
    up, down = middle
    rows = block.shape[0]
    half = rows // 2
    far = jnp.concatenate([up[rows:], down[rows:]], axis=0)
    if by_pair:
        other_far = shift(far, axis, 0, 1)
    else:
        other_far = jnp.concatenate(
            [shift(up[:half], axis, 1, 0), shift(down[half:rows], axis, -1, 0)], axis=0
        )
    return [block, other, before, nxt, far, up[:rows], down[:rows], other_far]


def place(blocks, at, dim):
    size = blocks[0].shape[dim]
    shape = list(blocks[0].shape)
    shape[dim] = 8 * size
    out = jnp.zeros(shape, blocks[0].dtype)
    for block, s in zip(blocks, at):
        out = lax.dynamic_update_slice_in_dim(out, block, s * size, axis=dim)
    return out


def ring_pair(by, k, axis):
    pair = jnp.concatenate([by[k, 0], by[k, 1]], axis=0).astype(BF16)
    return shift(pair, axis, -k, 0)


def ring_end(by, got, axis):
    rows = by[0, 0].shape[0]
    near, cross = by[0, 0].astype(F32), by[0, 1].astype(F32)
    for g in got:
        near = near + g[:rows].astype(F32)
        cross = cross + g[rows:].astype(F32)
    return near + shift(cross.astype(BF16), axis, 0, 1).astype(F32)


def scatter_ring_first(blocks, axis):
    by = dict(zip(OFFSETS, blocks))
    return ring_end(by, [ring_pair(by, k, axis) for k in (1, -1, 2)], axis)


def pack(scalar, width):
    terms = []
    for _ in range(3):
        term = lax.reduce_precision(scalar, 8, 7)
        terms.append(jnp.full((NOTE, width // 4), term).astype(BF16))
        scalar = scalar - term
    return jnp.concatenate(terms + [jnp.zeros((NOTE, width // 4), BF16)], axis=1)


def unpack(note):
    quarter = note.shape[-1] // 4
    return sum(note[..., 0, i * quarter].astype(F32) for i in range(3))


def scatter_pair_first(blocks, axis, scalar):
    by = dict(zip(OFFSETS, blocks))
    rows, width = blocks[0].shape
    ring = (1, -1, 2, 0)
    got = jnp.concatenate([by[k, 1] for k in ring] + [pack(scalar, width)], axis=0).astype(BF16)
    got = shift(got, axis, 0, 1)
    sums = {
        k: by[k, 0].astype(F32) + got[i * rows : (i + 1) * rows].astype(F32)
        for i, k in enumerate(ring)
    }
    scalar = scalar + unpack(got[4 * rows :])
    note = pack(scalar, width)
    total, scalars = sums[0], {0: scalar}
    for k in (1, -1, 2):
        got = shift(jnp.concatenate([sums[k].astype(BF16), note], axis=0), axis, -k, 0)
        total = total + got[:rows].astype(F32)
        scalars[k] = unpack(got[rows:])
    return total, (scalars[0] + scalars[2]) + (scalars[1] + scalars[-1])


def dot(a, b, dims=((1,), (0,))):
    return lax.dot_general(a, b, (dims, ((), ())), preferred_element_type=F32)


def shards(teacher_in, teacher_weight, student_in, student_weight, projector):
    role = lax.axis_index("role")
    n_tensor = lax.axis_size("tensor")
    own_rows = student_in.shape[0]
    rows = 2 * own_rows
    total_rows = rows * lax.axis_size("dp")
    out_width = teacher_weight.shape[1]
    half = out_width // 2
    feat, hid = student_weight.shape
    wide = feat * 8
    cols = projector.shape[1]
    feat_from = sources("dp")
    model_from = sources("tensor")

    swap = [(d * 8 + t, t * 8 + d) for d in range(8) for t in range(8)]

    teacher_rows = teacher_in.reshape(rows, teacher_in.shape[2])
    away = dot(teacher_rows, lax.dynamic_slice_in_dim(teacher_weight, (1 - role) * half, half, axis=1))
    away = flip(away.astype(BF16))
    teacher = dot(teacher_rows, lax.dynamic_slice_in_dim(teacher_weight, role * half, half, axis=1))
    teacher = teacher + away.astype(F32)
    teacher = [lax.dynamic_slice_in_dim(teacher, s * cols, cols, axis=1) for s in model_from]

    w_first = gather_start(student_weight, "dp")
    w_first = lax.optimization_barrier((*w_first, away))[:3]
    w_middle = gather_middle(student_weight, w_first, "dp")
    p_block = lax.ppermute(after(projector, w_first[0]), ("dp", "tensor"), swap)
    *w_middle, p_block = lax.optimization_barrier((*w_middle, p_block))
    weight = gather_end(student_weight, w_first, w_middle, "dp", False)
    weight = place(weight, feat_from, 0)

    p_first = gather_start(after(p_block, *w_middle), "dp")
    teacher = dict(zip(OFFSETS, teacher))
    t_got = [ring_pair(teacher, k, "tensor") for k in (1, -1, 2)]

    mine = lax.dynamic_slice_in_dim(student_in, role * wide, wide, axis=1)
    theirs = flip(lax.dynamic_slice_in_dim(student_in, (1 - role) * wide, wide, axis=1))
    student = jnp.concatenate([mine, theirs], axis=0)

    pre = dot(student, weight)
    pre = pre[:own_rows] + flip(pre[own_rows:])
    sigma = jax.nn.sigmoid(pre)
    hidden = (pre * sigma).astype(BF16)
    hidden, *p_first, t_got[0], t_got[1] = lax.optimization_barrier((hidden, *p_first, t_got[0], t_got[1]))

    p_middle = gather_middle(p_block, p_first, "dp")
    h_first = gather_start(hidden, "tensor")
    h_middle = gather_middle(hidden, h_first, "tensor")
    h_middle[0], *p_middle, t_got[2] = lax.optimization_barrier((h_middle[0], *p_middle, t_got[2]))
    projector = place(gather_end(p_block, p_first, p_middle, "dp", True), feat_from, 0)
    hidden = place(gather_end(hidden, h_first, h_middle, "tensor", True), model_from, 1)
    hidden_other = flip(hidden)
    teacher = ring_end(teacher, t_got, "tensor")

    teacher_own = lax.dynamic_slice_in_dim(teacher, role * own_rows, own_rows, axis=0)
    teacher_other = lax.dynamic_slice_in_dim(teacher, (1 - role) * own_rows, own_rows, axis=0)
    difference = dot(hidden, projector) - teacher_own
    difference_other = dot(hidden_other, projector) - teacher_other
    square = jnp.sum(difference * difference) + jnp.sum(difference_other * difference_other)
    square = square + flip(square)

    back_other = dot(difference_other.astype(BF16), projector, ((1,), (1,)))
    back = dot(difference.astype(BF16), projector, ((1,), (1,))) + flip(back_other.astype(BF16)).astype(F32)
    back = back.astype(BF16)
    note = pack(square, hid)
    back = jnp.concatenate(
        [x for i in range(n_tensor) for x in (back[:, i * hid : (i + 1) * hid], note)], axis=0
    )
    back = lax.all_to_all(back, "tensor", 0, 0, tiled=True)
    back = back.reshape(n_tensor, own_rows + NOTE, hid)
    square = jnp.sum(unpack(back[:, own_rows:]))
    back = jnp.sum(back[:, :own_rows].astype(F32), axis=0)

    delta = (back * sigma * (1.0 + pre * (1.0 - sigma))).astype(BF16)
    delta = jnp.concatenate([delta, flip(delta)], axis=0)

    grad = dot(student, delta, ((0,), (0,))).astype(BF16)
    blocks = [lax.dynamic_slice_in_dim(grad, s * feat, feat, axis=0) for s in feat_from]
    mid = feat // 2
    first, square = scatter_pair_first([b[:mid] for b in blocks], "dp", square)
    second = scatter_ring_first([b[mid:] for b in blocks], "dp")
    loss = square / (2.0 * total_rows * out_width)
    grad_weight = jnp.concatenate([first, second], axis=0)
    return (grad_weight / jnp.sqrt(jnp.float32(total_rows)), loss)


def solution(mesh):
    in_specs = (
        P(None, "dp", ("role", "tensor")),
        P(("role", "tensor"), None),
        P(("role", "dp"), None),
        P(("role", "dp"), "tensor"),
        P("tensor", ("role", "dp")),
    )
    out_specs = (P(("role", "dp"), "tensor"), P())
    return jax.shard_map(shards, mesh=mesh, in_specs=in_specs, out_specs=out_specs, check_vma=False)
```

time: 833 us -> 334 us (0.40)
  waiting for transfers between devices: 603 us -> 95.8 us
  starting transfers between devices: 0.42 us -> 83.2 us
  local copies, waits for them, and re-layouts: 86.4 us -> 29.3 us
  blocking collectives: 67.1 us -> 34.2 us
  other arithmetic: 4.32 us -> 17.6 us
  between operations: 15.9 us -> 26.9 us
    reduce_scatter x3 -> x0, waiting for transfers between devices: 429 us -> none  [the longest x1 280 us: shards(): lax.psum_scatter(lax.dot_general(columns, delta, (((0,), (0,)), ((), ()))...]
    all_gather x3 -> x0, waiting for transfers between devices: 173 us -> none  [the longest x1 69.3 us: shards(): residual_all = lax.all_gather(residual, 'tensor', axis=1, tiled=True)]
    ppermute x0 -> x39, waiting for transfers between devices: none -> 95.8 us  [the longest x31 95.4 us: shift(): return lax.ppermute(value, axis, perm)]
    ppermute x0 -> x39, starting transfers between devices: none -> 83.2 us  [the longest x31 79.9 us: shift(): return lax.ppermute(value, axis, perm)]
    psum x1 -> x0, blocking collectives: 67.1 us -> none  [shards(): lax.psum(jnp.sum(difference * difference), ('role', 'dp', 'tensor'))]
    gather x6 -> x0, local copies, waits for them, and re-layouts: 61.1 us -> none  [the longest x5 56.2 us: shards(): chosen_cols = jnp.take(weight_blocks, owners % n_model, axis=1)]
    all_to_all x0 -> x1, blocking collectives: none -> 34.2 us  [shards(): back = lax.all_to_all(back, 'tensor', 0, 0, tiled=True)]
    unnamed x7 -> x72, local copies, waits for them, and re-layouts: 25.2 us -> 4.52 us
  transfers between devices with their start and end apart: 6 -> 39, of which waited for: 5 -> 19; matrix products, arithmetic and copies ran while one was open for 14% -> 18% of each run, Pallas kernels for 0% -> 0%
where the time goes in v1:
time: 334 us; the launch traced here: 333 us
  waiting for transfers between devices  95.8 us (29%)
  starting transfers between devices  83.2 us (25%)
  matrix products  46 us (14%)
  blocking collectives  34.2 us (10%)
  local copies, waits for them, and re-layouts  29.3 us (9%)
  between operations  26.9 us (8%)
  other arithmetic  17.6 us (5%)
    ppermute x31, waiting for transfers between devices, shift(): return lax.ppermute(value, axis, perm)  95.4 us
    ppermute x31, starting transfers between devices, shift(): return lax.ppermute(value, axis, perm)  79.9 us
    dot_general x8, matrix products, dot(): return lax.dot_general(a, b, (dims, ((), ())), preferred_element_type=F32)  46 us
    all_to_all x1, blocking collectives, shards(): back = lax.all_to_all(back, 'tensor', 0, 0, tiled=True)  34.2 us
    dynamic_update_slice x20, local copies, waits for them, and re-layouts, place(): out = lax.dynamic_update_slice_in_dim(out, block, s * size, axis=dim)  9.16 us
  transfers between devices with their start and end apart: 39, of which 19 were waited for; matrix products, arithmetic and copies ran while one was open for 18% of the time, Pallas kernels for 0%

profile of v1, /device:TPU:0, one launch (start us, length us, event | category | flops | bytes accessed | tf_op | source)
XLA Modules:
  0.0 333.1 jit_solution(10813736985193863217)
XLA Ops:
  1.9 9.8 %fusion.9 = bf16[512,4096]{0,1:T(8,128)(2,1)} fusion(bf16[512,1024]{1,0:T(8,128)(2,1)S(1)} %bitcast.20, bf16[1024,8192]{1,0:T(8,128)(2,1)} %param.6, s32[]{:T(128)S(6)} %select_n.41), kind=kOutput, calls=%fused_computation.7 | convolution fusion | flops 4297064448 | bytes 13631492 | tf_op jit(solution)/shard_map/dot_general | solution.py:121
  11.6 1.6 collective-permute-start.1
  13.2 1.6 collective-permute-start.2
  14.8 1.6 collective-permute-start.3
  16.4 3.9 %constant_dynamic-slice_fusion.7 = (bf16[256,4096]{1,0:T(8,128)(2,1)S(1)}, bf16[256,4096]{1,0:T(8,128)(2,1)}) fusion(bf16[256,8192]{1,0:T(8,128)(2,1)} %param.7, s32[]{:T(128)S(6)} %select_n.40, s32[]{:T(128)S(6)} %select_n.41), kind=kLoop, calls=%fused_computation.116 | loop fusion | bytes 8388616 | tf_op jit(solution)/shard_map/dynamic_slice | solution.py:159
  20.6 1.6 constant_dynamic-update-slice_fusion.24
  22.2 4.1 %collective-permute-done.1 = bf16[512,512]{1,0:T(8,128)(2,1)} collective-permute-done((bf16[512,512]{1,0:T(8,128)(2,1)}, bf16[512,512]{1,0:T(8,128)(2,1)}, u32[]{:S(2)}, u32[]{:S(2)}) %collective-permute-start.1) | collective-permute-done | bytes 524320 | tf_op jit(solution)/shard_map/ppermute | solution.py:14
  26.3 2.6 collective-permute-done.2
  30.8 2.0 pad_maximum_fusion.6
  32.9 1.6 collective-permute-start.5
  34.4 1.7 collective-permute-start.6
  37.6 12.4 %bitcast_add_fusion = f32[512,4096]{0,1:T(8,128)S(1)} fusion(bf16[512,4096]{0,1:T(8,128)(2,1)} %collective-permute-done.4, bf16[512,1024]{1,0:T(8,128)(2,1)S(1)} %bitcast.21, bf16[1024,8192]{1,0:T(8,128)(2,1)} %param.6, s32[]{:T(128)S(6)} %select_n.40), kind=kOutput, calls=%fused_computation | convolution fusion | flops 4299161600 | bytes 22020100 | tf_op jit(solution)/shard_map/dot_general | solution.py:121
  50.6 4.9 %collective-permute-start.14 = (bf16[1024,512]{0,1:T(8,128)(2,1)S(1)}, bf16[1024,512]{0,1:T(8,128)(2,1)S(1)}, u32[]{:S(2)}, u32[]{:S(2)}) collective-permute-start(bf16[1024,512]{0,1:T(8,128)(2,1)S(1)} %pad_maximum_fusion.3), channel_id=1, source_target_pairs={{0,6},{1,7},{2,0},{3,1},{4,2},{5,3},{6,4},{7,5},{8,14},{9,15},{10,... | collective-permute-start | bytes 3145736 | tf_op jit(solution)/shard_map/ppermute | solution.py:14
  58.9 16.5 %collective-permute-start.15 = (bf16[1024,512]{0,1:T(8,128)(2,1)S(1)}, bf16[1024,512]{0,1:T(8,128)(2,1)S(1)}, u32[]{:S(2)}, u32[]{:S(2)}) collective-permute-start(bf16[1024,512]{0,1:T(8,128)(2,1)S(1)} %pad_maximum_fusion.4), channel_id=1, source_target_pairs={{0,2},{1,3},{2,4},{3,5},{4,6},{5,7},{6,0},{7,1},{8,10},{9,11},{10,... | collective-permute-start | bytes 3145736 | tf_op jit(solution)/shard_map/ppermute | solution.py:14
  76.2 6.3 %collective-permute-start.9 = (bf16[256,512]{1,0:T(8,128)(2,1)S(1)}, bf16[256,512]{1,0:T(8,128)(2,1)S(1)}, u32[]{:S(2)}, u32[]{:S(2)}) collective-permute-start(bf16[256,512]{1,0:T(8,128)(2,1)S(1)} %get-tuple-element.63), channel_id=1, source_target_pairs={{0,48},{8,56},{16,0},{24,8},{32,16},{40,24},{48,32},{56,40},{1,49}... | collective-permute-start | bytes 786440 | tf_op jit(solution)/shard_map/ppermute | solution.py:14
  82.6 4.3 %collective-permute-done.8 = bf16[256,512]{1,0:T(8,128)(2,1)S(1)} collective-permute-done((bf16[256,512]{1,0:T(8,128)(2,1)S(1)}, bf16[256,512]{1,0:T(8,128)(2,1)S(1)}, u32[]{:S(2)}, u32[]{:S(2)}) %collective-permute-start.8) | collective-permute-done | bytes 262176 | tf_op jit(solution)/shard_map/ppermute | solution.py:14
  87.0 4.0 %fusion.13 = f32[512,512]{1,0:T(8,128)S(1)} fusion(bf16[4096,512]{1,0:T(8,128)(2,1)S(1)} %maximum_dynamic-update-slice_fusion.1, bf16[256,4096]{1,0:T(8,128)(2,1)} %collective-permute-done, bf16[256,4096]{1,0:T(8,128)(2,1)S(1)} %get-tuple-element.56), kind=kOutput, calls=%fused_computation.13 | convolution fusion | flops 2155872256 | bytes 9437184 | tf_op jit(solution)/shard_map/dot_general | solution.py:121
  93.0 3.3 collective-permute-start.13
  98.9 1.5 collective-permute-done.15
  100.4 5.2 %collective-permute-done.11 = bf16[512,512]{1,0:T(8,128)(2,1)S(1)} collective-permute-done((bf16[512,512]{1,0:T(8,128)(2,1)}, bf16[512,512]{1,0:T(8,128)(2,1)S(1)}, u32[]{:S(2)}, u32[]{:S(2)}) %collective-permute-start.11) | collective-permute-done | bytes 524320 | tf_op jit(solution)/shard_map/ppermute | solution.py:14
  105.6 1.5 collective-permute-done.12
  108.0 2.5 collective-permute-start.16
  110.6 3.1 collective-permute-start.18
  116.5 13.4 %collective-permute-done.17 = bf16[256,512]{1,0:T(8,128)(2,1)S(1)} collective-permute-done((bf16[256,512]{1,0:T(8,128)(2,1)S(1)}, bf16[256,512]{1,0:T(8,128)(2,1)S(1)}, u32[]{:S(2)}, u32[]{:S(2)}) %collective-permute-start.17) | collective-permute-done | bytes 262176 | tf_op jit(solution)/shard_map/ppermute | solution.py:14
  129.9 12.3 %collective-permute-start.21 = (bf16[768,512]{1,0:T(8,128)(2,1)}, bf16[768,512]{1,0:T(8,128)(2,1)}, u32[]{:S(2)}, u32[]{:S(2)}) collective-permute-start(bf16[768,512]{1,0:T(8,128)(2,1)} %get-tuple-element.67), channel_id=1, source_target_pairs={{0,48},{8,56},{16,0},{24,8},{32,16},{40,24},{48,32},{56,40},{1,49}... | collective-permute-start | bytes 2359304 | tf_op jit(solution)/shard_map/ppermute | solution.py:14
  143.0 2.7 collective-permute-start.23
  146.8 4.2 %collective-permute-done.23 = bf16[384,512]{1,0:T(8,128)(2,1)S(1)} collective-permute-done((bf16[384,512]{1,0:T(8,128)(2,1)S(1)}, bf16[384,512]{1,0:T(8,128)(2,1)S(1)}, u32[]{:S(2)}, u32[]{:S(2)}) %collective-permute-start.23) | collective-permute-done | bytes 393248 | tf_op jit(solution)/shard_map/ppermute | solution.py:14
  152.2 7.8 %collective-permute-done.24 = bf16[256,512]{1,0:T(8,128)(2,1)S(1)} collective-permute-done((bf16[256,512]{1,0:T(8,128)(2,1)S(1)}, bf16[256,512]{1,0:T(8,128)(2,1)S(1)}, u32[]{:S(2)}, u32[]{:S(2)}) %collective-permute-start.24) | collective-permute-done | bytes 262176 | tf_op jit(solution)/shard_map/ppermute | solution.py:14
  160.5 1.8 constant_dynamic-update-slice_fusion.14
  164.7 1.7 add_convert_fusion
  166.5 3.8 %collective-permute-start.26 = (bf16[512,512]{0,1:T(8,128)(2,1)S(1)}, bf16[512,512]{0,1:T(8,128)(2,1)S(1)}, u32[]{:S(2)}, u32[]{:S(2)}) collective-permute-start(bf16[512,512]{0,1:T(8,128)(2,1)S(1)} %add_convert_fusion), channel_id=1, source_target_pairs={{0,1},{1,0},{2,3},{3,2},{4,5},{5,4},{6,7},{7,6},{8,9},{9,8},{10,11... | collective-permute-start | bytes 1572872 | tf_op jit(solution)/shard_map/ppermute | solution.py:14
  172.4 7.1 %collective-permute-done.25 = bf16[512,512]{1,0:T(8,128)(2,1)S(1)} collective-permute-done((bf16[512,512]{1,0:T(8,128)(2,1)S(1)}, bf16[512,512]{1,0:T(8,128)(2,1)S(1)}, u32[]{:S(2)}, u32[]{:S(2)}) %collective-permute-start.25) | collective-permute-done | bytes 524320 | tf_op jit(solution)/shard_map/ppermute | solution.py:14
  179.6 11.5 %collective-permute-done.26 = bf16[512,512]{0,1:T(8,128)(2,1)S(1)} collective-permute-done((bf16[512,512]{0,1:T(8,128)(2,1)S(1)}, bf16[512,512]{0,1:T(8,128)(2,1)S(1)}, u32[]{:S(2)}, u32[]{:S(2)}) %collective-permute-start.26) | collective-permute-done | bytes 524320 | tf_op jit(solution)/shard_map/ppermute | solution.py:14
  191.1 1.7 convert_add_fusion
  192.9 4.4 %multiply_reduce_fusion = (f32[]{:T(128)}, bf16[256,512]{0,1:T(8,128)(2,1)S(1)}) fusion(f32[512,512]{0,1:T(8,128)S(1)} %convert_add_fusion, s32[]{:T(128)S(6)} %select_n.105, bf16[256,4096]{1,0:T(8,128)(2,1)} %collective-permute-done.27, bf16[4096,512]{1,0:T(8,128)(2,1)S(1)} %constant_dynamic-update-slice_fusion.9), kind=kOutput, calls=%fused_computation.49 | convolution fusion | flops 1074266112 | bytes 7077896 | tf_op jit(solution)/shard_map/dot_general | solution.py:121
  198.7 5.3 %multiply_reduce_fusion.1 = (f32[]{:T(128)}, bf16[256,512]{0,1:T(8,128)(2,1)S(1)}) fusion(f32[512,512]{0,1:T(8,128)} %copy-done.15, s32[]{:T(128)S(6)} %select_n.104, bf16[256,4096]{1,0:T(8,128)(2,1)} %copy-done.8, bf16[4096,512]{1,0:T(8,128)(2,1)} %copy-done.2), kind=kOutput, calls=%fused_computation.50 | convolution fusion | flops 1074266112 | bytes 7077896 | tf_op jit(solution)/shard_map/dot_general | solution.py:121
  205.3 1.6 collective-permute-start.29
  212.3 4.2 %fusion.12 = bf16[256,4096]{1,0:T(8,128)(2,1)S(1)} fusion(bf16[4096,512]{1,0:T(8,128)(2,1)} %copy-done.2, bf16[256,4096]{1,0:T(8,128)(2,1)} %collective-permute-done.28, bf16[256,512]{0,1:T(8,128)(2,1)S(1)} %get-tuple-element.88), kind=kOutput, calls=%fused_computation.9 | convolution fusion | flops 1076887552 | bytes 8650752 | tf_op jit(solution)/shard_map/dot_general | solution.py:121
  216.9 34.2 %all_to_all.9 = bf16[8,272,512]{2,1,0:T(8,128)(2,1)S(1)} all-to-all(bf16[8,272,512]{2,1,0:T(8,128)(2,1)S(1)} %bitcast.22), channel_id=1, replica_groups=mesh['role'=2,'dp'=8,'tensor'=8] {'tensor'}, dimensions={0} | all-to-all | bytes 4456448 | tf_op jit(solution)/shard_map/all_to_all | solution.py:192
  259.4 4.6 %convolution_convert_fusion = bf16[4096,512]{1,0:T(8,128)(2,1)S(1)} fusion(bf16[256,4096]{1,0:T(8,128)(2,1)} %collective-permute-done, bf16[256,4096]{1,0:T(8,128)(2,1)} %copy-done.5, bf16[256,512]{1,0:T(8,128)(2,1)S(1)} %collective-permute-done.30, bf16[256,512]{1,0:T(8,128)(2,1)S(1)} %multiply_convert_fusion), kind=kOutput, calls=%fused_computation.6 | convolution fusion | flops 2159017984 | bytes 8912896 | tf_op jit(solution)/shard_map/dot_general | solution.py:121
  264.3 1.6 collective-permute-start.31
  266.7 2.0 collective-permute-start.35
  271.9 18.4 %collective-permute-done.31 = bf16[1040,512]{1,0:T(8,128)(2,1)S(1)} collective-permute-done((bf16[1040,512]{1,0:T(8,128)(2,1)S(1)}, bf16[1040,512]{1,0:T(8,128)(2,1)S(1)}, u32[]{:S(2)}, u32[]{:S(2)}) %collective-permute-start.31) | collective-permute-done | bytes 1064992 | tf_op jit(solution)/shard_map/ppermute | solution.py:14
  299.4 3.2 collective-permute-start.32
  303.5 6.1 %collective-permute-done.33 = bf16[272,512]{1,0:T(8,128)(2,1)S(1)} collective-permute-done((bf16[272,512]{1,0:T(8,128)(2,1)}, bf16[272,512]{1,0:T(8,128)(2,1)S(1)}, u32[]{:S(2)}, u32[]{:S(2)}) %collective-permute-start.33) | collective-permute-done | bytes 278560 | tf_op jit(solution)/shard_map/ppermute | solution.py:14
  309.6 5.0 %collective-permute-done.32 = bf16[272,512]{1,0:T(8,128)(2,1)S(1)} collective-permute-done((bf16[272,512]{1,0:T(8,128)(2,1)}, bf16[272,512]{1,0:T(8,128)(2,1)S(1)}, u32[]{:S(2)}, u32[]{:S(2)}) %collective-permute-start.32) | collective-permute-done | bytes 278560 | tf_op jit(solution)/shard_map/ppermute | solution.py:14
  316.1 1.8 convert_add_fusion.2
  317.9 2.1 collective-permute-start.38
  (198 shorter events, 46.2 us)
Async XLA Ops:
  11.6 17.3 %collective-permute-start.4 = (bf16[512,4096]{0,1:T(8,128)(2,1)}, bf16[512,4096]{0,1:T(8,128)(2,1)}, u32[]{:S(2)}, u32[]{:S(2)}) collective-permute-start(bf16[512,4096]{0,1:T(8,128)(2,1)} %fusion.9), channel_id=1, source_target_pairs={{0,64},{64,0},{1,65},{65,1},{2,66},{66,2},{3,67},{67,3},{4,68},{68... | collective-permute-start | bytes 12582920 | tf_op jit(solution)/shard_map/ppermute | solution.py:18
  11.6 14.7 %collective-permute-start.1 = (bf16[512,512]{1,0:T(8,128)(2,1)}, bf16[512,512]{1,0:T(8,128)(2,1)}, u32[]{:S(2)}, u32[]{:S(2)}) collective-permute-start(bf16[512,512]{1,0:T(8,128)(2,1)} %param.8), channel_id=1, source_target_pairs={{0,8},{8,0},{16,24},{24,16},{32,40},{40,32},{48,56},{56,48},{1,9},... | collective-permute-start | bytes 1572872 | tf_op jit(solution)/shard_map/ppermute | solution.py:14
  13.2 15.7 %collective-permute-start.2 = (bf16[512,512]{1,0:T(8,128)(2,1)}, bf16[512,512]{1,0:T(8,128)(2,1)}, u32[]{:S(2)}, u32[]{:S(2)}) collective-permute-start(bf16[512,512]{1,0:T(8,128)(2,1)} %param.8), channel_id=1, source_target_pairs={{0,16},{8,24},{16,32},{24,40},{32,48},{40,56},{48,0},{56,8},{1,17}... | collective-permute-start | bytes 1572872 | tf_op jit(solution)/shard_map/ppermute | solution.py:14
  14.8 14.1 %collective-permute-start.3 = (bf16[512,512]{1,0:T(8,128)(2,1)}, bf16[512,512]{1,0:T(8,128)(2,1)}, u32[]{:S(2)}, u32[]{:S(2)}) collective-permute-start(bf16[512,512]{1,0:T(8,128)(2,1)} %param.8), channel_id=1, source_target_pairs={{0,48},{8,56},{16,0},{24,8},{32,16},{40,24},{48,32},{56,40},{1,49}... | collective-permute-start | bytes 1572872 | tf_op jit(solution)/shard_map/ppermute | solution.py:14
  20.3 66.6 %copy-start.5 = (bf16[256,4096]{1,0:T(8,128)(2,1)}, bf16[256,4096]{1,0:T(8,128)(2,1)S(1)}, u32[]{:S(2)}) copy-start(bf16[256,4096]{1,0:T(8,128)(2,1)S(1)} %get-tuple-element.56) | copy-start | bytes 6291460
  20.3 66.6 %collective-permute-start = (bf16[256,4096]{1,0:T(8,128)(2,1)}, bf16[256,4096]{1,0:T(8,128)(2,1)}, u32[]{:S(2)}, u32[]{:S(2)}) collective-permute-start(bf16[256,4096]{1,0:T(8,128)(2,1)} %get-tuple-element.57), channel_id=1, source_target_pairs={{0,64},{64,0},{1,65},{65,1},{2,66},{66,2},{3,67},{67,3},{4,68},{68... | collective-permute-start | bytes 6291464 | tf_op jit(solution)/shard_map/ppermute | solution.py:18
  20.6 15.5 %copy-start.29 = (bf16[512,512]{1,0:T(8,128)(2,1)S(1)}, bf16[512,512]{1,0:T(8,128)(2,1)}, u32[]{:S(2)}) copy-start(bf16[512,512]{1,0:T(8,128)(2,1)} %param.9) | copy-start | bytes 1572868
  32.9 42.5 %collective-permute-start.5 = (bf16[768,512]{1,0:T(8,128)(2,1)}, bf16[768,512]{1,0:T(8,128)(2,1)S(1)}, u32[]{:S(2)}, u32[]{:S(2)}) collective-permute-start(bf16[768,512]{1,0:T(8,128)(2,1)} %get-tuple-element.70), channel_id=1, source_target_pairs={{0,16},{8,24},{16,32},{24,40},{32,48},{40,56},{48,0},{56,8},{1,17}... | collective-permute-start | bytes 2359304 | tf_op jit(solution)/shard_map/ppermute | solution.py:14
  34.4 40.9 %collective-permute-start.6 = (bf16[768,512]{1,0:T(8,128)(2,1)S(1)}, bf16[768,512]{1,0:T(8,128)(2,1)S(1)}, u32[]{:S(2)}, u32[]{:S(2)}) collective-permute-start(bf16[768,512]{1,0:T(8,128)(2,1)S(1)} %get-tuple-element.69), channel_id=1, source_target_pairs={{0,48},{8,56},{16,0},{24,8},{32,16},{40,24},{48,32},{56,40},{1,49}... | collective-permute-start | bytes 2359304 | tf_op jit(solution)/shard_map/ppermute | solution.py:14
  36.1 22.8 %collective-permute-start.7 = (bf16[512,512]{1,0:T(8,128)(2,1)S(1)}, bf16[512,512]{1,0:T(8,128)(2,1)}, u32[]{:S(2)}, u32[]{:S(2)}) collective-permute-start(bf16[512,512]{1,0:T(8,128)(2,1)S(1)} %copy-done.29), channel_id=1, source_target_pairs={{0,0},{1,8},{2,16},{3,24},{4,32},{5,40},{6,48},{7,56},{8,1},{9,9},... | collective-permute-start | bytes 1572872 | tf_op jit(solution)/shard_map/ppermute | solution.py:150
  50.6 47.0 %collective-permute-start.14 = (bf16[1024,512]{0,1:T(8,128)(2,1)S(1)}, bf16[1024,512]{0,1:T(8,128)(2,1)S(1)}, u32[]{:S(2)}, u32[]{:S(2)}) collective-permute-start(bf16[1024,512]{0,1:T(8,128)(2,1)S(1)} %pad_maximum_fusion.3), channel_id=1, source_target_pairs={{0,6},{1,7},{2,0},{3,1},{4,2},{5,3},{6,4},{7,5},{8,14},{9,15},{10,... | collective-permute-start | bytes 3145736 | tf_op jit(solution)/shard_map/ppermute | solution.py:14
  58.9 41.6 %collective-permute-start.15 = (bf16[1024,512]{0,1:T(8,128)(2,1)S(1)}, bf16[1024,512]{0,1:T(8,128)(2,1)S(1)}, u32[]{:S(2)}, u32[]{:S(2)}) collective-permute-start(bf16[1024,512]{0,1:T(8,128)(2,1)S(1)} %pad_maximum_fusion.4), channel_id=1, source_target_pairs={{0,2},{1,3},{2,4},{3,5},{4,6},{5,7},{6,0},{7,1},{8,10},{9,11},{10,... | collective-permute-start | bytes 3145736 | tf_op jit(solution)/shard_map/ppermute | solution.py:14
  75.4 11.5 %collective-permute-start.8 = (bf16[256,512]{1,0:T(8,128)(2,1)S(1)}, bf16[256,512]{1,0:T(8,128)(2,1)S(1)}, u32[]{:S(2)}, u32[]{:S(2)}) collective-permute-start(bf16[256,512]{1,0:T(8,128)(2,1)S(1)} %get-tuple-element.61), channel_id=1, source_target_pairs={{0,16},{8,24},{16,32},{24,40},{32,48},{40,56},{48,0},{56,8},{1,17}... | collective-permute-start | bytes 786440 | tf_op jit(solution)/shard_map/ppermute | solution.py:14
  76.2 10.7 %collective-permute-start.9 = (bf16[256,512]{1,0:T(8,128)(2,1)S(1)}, bf16[256,512]{1,0:T(8,128)(2,1)S(1)}, u32[]{:S(2)}, u32[]{:S(2)}) collective-permute-start(bf16[256,512]{1,0:T(8,128)(2,1)S(1)} %get-tuple-element.63), channel_id=1, source_target_pairs={{0,48},{8,56},{16,0},{24,8},{32,16},{40,24},{48,32},{56,40},{1,49}... | collective-permute-start | bytes 786440 | tf_op jit(solution)/shard_map/ppermute | solution.py:14
  91.0 2.0 collective-permute-start.10
  91.1 14.6 %collective-permute-start.11 = (bf16[512,512]{1,0:T(8,128)(2,1)}, bf16[512,512]{1,0:T(8,128)(2,1)S(1)}, u32[]{:S(2)}, u32[]{:S(2)}) collective-permute-start(bf16[512,512]{1,0:T(8,128)(2,1)} %collective-permute-done.7), channel_id=1, source_target_pairs={{0,8},{8,0},{16,24},{24,16},{32,40},{40,32},{48,56},{56,48},{1,9},... | collective-permute-start | bytes 1572872 | tf_op jit(solution)/shard_map/ppermute | solution.py:14
  91.2 16.0 %collective-permute-start.12 = (bf16[512,512]{1,0:T(8,128)(2,1)}, bf16[512,512]{1,0:T(8,128)(2,1)S(1)}, u32[]{:S(2)}, u32[]{:S(2)}) collective-permute-start(bf16[512,512]{1,0:T(8,128)(2,1)} %collective-permute-done.7), channel_id=1, source_target_pairs={{0,16},{8,24},{16,32},{24,40},{32,48},{40,56},{48,0},{56,8},{1,17}... | collective-permute-start | bytes 1572872 | tf_op jit(solution)/shard_map/ppermute | solution.py:14
  93.0 15.1 %collective-permute-start.13 = (bf16[512,512]{1,0:T(8,128)(2,1)}, bf16[512,512]{1,0:T(8,128)(2,1)S(1)}, u32[]{:S(2)}, u32[]{:S(2)}) collective-permute-start(bf16[512,512]{1,0:T(8,128)(2,1)} %collective-permute-done.7), channel_id=1, source_target_pairs={{0,48},{8,56},{16,0},{24,8},{32,16},{40,24},{48,32},{56,40},{1,49}... | collective-permute-start | bytes 1572872 | tf_op jit(solution)/shard_map/ppermute | solution.py:14
  97.6 32.3 %copy-start.18 = (bf16[1024,512]{0,1:T(8,128)(2,1)}, bf16[1024,512]{0,1:T(8,128)(2,1)S(1)}, u32[]{:S(2)}) copy-start(bf16[1024,512]{0,1:T(8,128)(2,1)S(1)} %collective-permute-done.14) | copy-start | bytes 3145732
  97.6 53.4 %collective-permute-start.22 = (bf16[1024,512]{0,1:T(8,128)(2,1)}, bf16[1024,512]{0,1:T(8,128)(2,1)}, u32[]{:S(2)}, u32[]{:S(2)}) collective-permute-start(bf16[1024,512]{0,1:T(8,128)(2,1)} %pad_maximum_fusion.5), channel_id=1, source_target_pairs={{0,4},{1,5},{2,6},{3,7},{4,0},{5,1},{6,2},{7,3},{8,12},{9,13},{10,... | collective-permute-start | bytes 3145736 | tf_op jit(solution)/shard_map/ppermute | solution.py:14
  100.4 29.5 %copy-start.20 = (bf16[1024,512]{0,1:T(8,128)(2,1)}, bf16[1024,512]{0,1:T(8,128)(2,1)S(1)}, u32[]{:S(2)}) copy-start(bf16[1024,512]{0,1:T(8,128)(2,1)S(1)} %collective-permute-done.15) | copy-start | bytes 3145732
  108.0 21.9 %collective-permute-start.17 = (bf16[256,512]{1,0:T(8,128)(2,1)S(1)}, bf16[256,512]{1,0:T(8,128)(2,1)S(1)}, u32[]{:S(2)}, u32[]{:S(2)}) collective-permute-start(bf16[256,512]{1,0:T(8,128)(2,1)S(1)} %multiply_convert_fusion.1), channel_id=1, source_target_pairs={{0,2},{1,3},{2,4},{3,5},{4,6},{5,7},{6,0},{7,1},{8,10},{9,11},{10,... | collective-permute-start | bytes 786440 | tf_op jit(solution)/shard_map/ppermute | solution.py:14
  108.0 34.2 %collective-permute-start.16 = (bf16[256,512]{1,0:T(8,128)(2,1)S(1)}, bf16[256,512]{1,0:T(8,128)(2,1)S(1)}, u32[]{:S(2)}, u32[]{:S(2)}) collective-permute-start(bf16[256,512]{1,0:T(8,128)(2,1)S(1)} %multiply_convert_fusion.1), channel_id=1, source_target_pairs={{0,1},{1,0},{2,3},{3,2},{4,5},{5,4},{6,7},{7,6},{8,9},{9,8},{10,11... | collective-permute-start | bytes 786440 | tf_op jit(solution)/shard_map/ppermute | solution.py:14
  110.6 31.6 %collective-permute-start.18 = (bf16[256,512]{1,0:T(8,128)(2,1)S(1)}, bf16[256,512]{1,0:T(8,128)(2,1)S(1)}, u32[]{:S(2)}, u32[]{:S(2)}) collective-permute-start(bf16[256,512]{1,0:T(8,128)(2,1)S(1)} %multiply_convert_fusion.1), channel_id=1, source_target_pairs={{0,6},{1,7},{2,0},{3,1},{4,2},{5,3},{6,4},{7,5},{8,14},{9,15},{10,... | collective-permute-start | bytes 786440 | tf_op jit(solution)/shard_map/ppermute | solution.py:14
  115.1 36.3 %collective-permute-start.20 = (bf16[768,512]{1,0:T(8,128)(2,1)}, bf16[768,512]{1,0:T(8,128)(2,1)}, u32[]{:S(2)}, u32[]{:S(2)}) collective-permute-start(bf16[768,512]{1,0:T(8,128)(2,1)} %get-tuple-element.68), channel_id=1, source_target_pairs={{0,16},{8,24},{16,32},{24,40},{32,48},{40,56},{48,0},{56,8},{1,17}... | collective-permute-start | bytes 2359304 | tf_op jit(solution)/shard_map/ppermute | solution.py:14
  129.9 12.5 %copy-start.22 = (bf16[256,512]{1,0:T(8,128)(2,1)}, bf16[256,512]{1,0:T(8,128)(2,1)S(1)}, u32[]{:S(2)}) copy-start(bf16[256,512]{1,0:T(8,128)(2,1)S(1)} %collective-permute-done.17) | copy-start | bytes 786436
  129.9 22.1 %collective-permute-start.21 = (bf16[768,512]{1,0:T(8,128)(2,1)}, bf16[768,512]{1,0:T(8,128)(2,1)}, u32[]{:S(2)}, u32[]{:S(2)}) collective-permute-start(bf16[768,512]{1,0:T(8,128)(2,1)} %get-tuple-element.67), channel_id=1, source_target_pairs={{0,48},{8,56},{16,0},{24,8},{32,16},{40,24},{48,32},{56,40},{1,49}... | collective-permute-start | bytes 2359304 | tf_op jit(solution)/shard_map/ppermute | solution.py:14
  142.3 9.1 %collective-permute-start.19 = (bf16[384,512]{1,0:T(8,128)(2,1)S(1)}, bf16[384,512]{1,0:T(8,128)(2,1)S(1)}, u32[]{:S(2)}, u32[]{:S(2)}) collective-permute-start(bf16[384,512]{1,0:T(8,128)(2,1)S(1)} %get-tuple-element.83), channel_id=1, source_target_pairs={{0,2},{1,3},{2,4},{3,5},{4,6},{5,7},{6,0},{7,1},{8,10},{9,11},{10,... | collective-permute-start | bytes 1179656 | tf_op jit(solution)/shard_map/ppermute | solution.py:14
  143.0 8.0 %collective-permute-start.23 = (bf16[384,512]{1,0:T(8,128)(2,1)S(1)}, bf16[384,512]{1,0:T(8,128)(2,1)S(1)}, u32[]{:S(2)}, u32[]{:S(2)}) collective-permute-start(bf16[384,512]{1,0:T(8,128)(2,1)S(1)} %get-tuple-element.82), channel_id=1, source_target_pairs={{0,6},{1,7},{2,0},{3,1},{4,2},{5,3},{6,4},{7,5},{8,14},{9,15},{10,... | collective-permute-start | bytes 1179656 | tf_op jit(solution)/shard_map/ppermute | solution.py:14
  152.1 8.0 %collective-permute-start.24 = (bf16[256,512]{1,0:T(8,128)(2,1)S(1)}, bf16[256,512]{1,0:T(8,128)(2,1)S(1)}, u32[]{:S(2)}, u32[]{:S(2)}) collective-permute-start(bf16[256,512]{1,0:T(8,128)(2,1)S(1)} %get-tuple-element.80), channel_id=1, source_target_pairs={{0,1},{1,0},{2,3},{3,2},{4,5},{5,4},{6,7},{7,6},{8,9},{9,8},{10,11... | collective-permute-start | bytes 786440 | tf_op jit(solution)/shard_map/ppermute | solution.py:14
  160.1 32.8 %collective-permute-start.27 = (bf16[256,4096]{1,0:T(8,128)(2,1)S(1)}, bf16[256,4096]{1,0:T(8,128)(2,1)}, u32[]{:S(2)}, u32[]{:S(2)}) collective-permute-start(bf16[256,4096]{1,0:T(8,128)(2,1)S(1)} %constant_dynamic-update-slice_fusion.15), channel_id=1, source_target_pairs={{0,64},{64,0},{1,65},{65,1},{2,66},{66,2},{3,67},{67,3},{4,68},{68... | collective-permute-start | bytes 6291464 | tf_op jit(solution)/shard_map/ppermute | solution.py:18
  164.6 14.9 %collective-permute-start.25 = (bf16[512,512]{1,0:T(8,128)(2,1)S(1)}, bf16[512,512]{1,0:T(8,128)(2,1)S(1)}, u32[]{:S(2)}, u32[]{:S(2)}) collective-permute-start(bf16[512,512]{1,0:T(8,128)(2,1)S(1)} %get-tuple-element.65), channel_id=1, source_target_pairs={{0,8},{8,0},{16,24},{24,16},{32,40},{40,32},{48,56},{56,48},{1,9},... | collective-permute-start | bytes 1572872 | tf_op jit(solution)/shard_map/ppermute | solution.py:14
  166.5 24.6 %collective-permute-start.26 = (bf16[512,512]{0,1:T(8,128)(2,1)S(1)}, bf16[512,512]{0,1:T(8,128)(2,1)S(1)}, u32[]{:S(2)}, u32[]{:S(2)}) collective-permute-start(bf16[512,512]{0,1:T(8,128)(2,1)S(1)} %add_convert_fusion), channel_id=1, source_target_pairs={{0,1},{1,0},{2,3},{3,2},{4,5},{5,4},{6,7},{7,6},{8,9},{9,8},{10,11... | collective-permute-start | bytes 1572872 | tf_op jit(solution)/shard_map/ppermute | solution.py:14
  179.6 17.7 %copy-start.2 = (bf16[4096,512]{1,0:T(8,128)(2,1)}, bf16[4096,512]{1,0:T(8,128)(2,1)S(1)}, u32[]{:S(2)}) copy-start(bf16[4096,512]{1,0:T(8,128)(2,1)S(1)} %constant_dynamic-update-slice_fusion.9) | copy-start | bytes 12582916
  198.6 13.7 %collective-permute-start.28 = (bf16[256,4096]{1,0:T(8,128)(2,1)S(1)}, bf16[256,4096]{1,0:T(8,128)(2,1)}, u32[]{:S(2)}, u32[]{:S(2)}) collective-permute-start(bf16[256,4096]{1,0:T(8,128)(2,1)S(1)} %convolution_convert_fusion.1), channel_id=1, source_target_pairs={{0,64},{64,0},{1,65},{65,1},{2,66},{66,2},{3,67},{67,3},{4,68},{68... | collective-permute-start | bytes 6291464 | tf_op jit(solution)/shard_map/ppermute | solution.py:18
  205.3 1.6 collective-permute-start.29
  252.4 7.0 %collective-permute-start.30 = (bf16[256,512]{1,0:T(8,128)(2,1)S(1)}, bf16[256,512]{1,0:T(8,128)(2,1)S(1)}, u32[]{:S(2)}, u32[]{:S(2)}) collective-permute-start(bf16[256,512]{1,0:T(8,128)(2,1)S(1)} %multiply_convert_fusion), channel_id=1, source_target_pairs={{0,64},{64,0},{1,65},{65,1},{2,66},{66,2},{3,67},{67,3},{4,68},{68... | collective-permute-start | bytes 786440 | tf_op jit(solution)/shard_map/ppermute | solution.py:18
  264.0 26.3 %copy-start.3 = (bf16[4096,512]{1,0:T(8,128)(2,1)}, bf16[4096,512]{1,0:T(8,128)(2,1)S(1)}, u32[]{:S(2)}) copy-start(bf16[4096,512]{1,0:T(8,128)(2,1)S(1)} %convolution_convert_fusion) | copy-start | bytes 12582916
  264.3 26.0 %collective-permute-start.31 = (bf16[1040,512]{1,0:T(8,128)(2,1)S(1)}, bf16[1040,512]{1,0:T(8,128)(2,1)S(1)}, u32[]{:S(2)}, u32[]{:S(2)}) collective-permute-start(bf16[1040,512]{1,0:T(8,128)(2,1)S(1)} %constant_dynamic-update-slice_fusion.8), channel_id=1, source_target_pairs={{0,8},{8,0},{16,24},{24,16},{32,40},{40,32},{48,56},{56,48},{1,9},... | collective-permute-start | bytes 3194888 | tf_op jit(solution)/shard_map/ppermute | solution.py:14
  266.7 36.0 %collective-permute-start.35 = (bf16[512,512]{1,0:T(8,128)(2,1)}, bf16[512,512]{1,0:T(8,128)(2,1)S(1)}, u32[]{:S(2)}, u32[]{:S(2)}) collective-permute-start(bf16[512,512]{1,0:T(8,128)(2,1)} %pad_maximum_fusion.11), channel_id=1, source_target_pairs={{0,48},{8,56},{16,0},{24,8},{32,16},{40,24},{48,32},{56,40},{1,49}... | collective-permute-start | bytes 1572872 | tf_op jit(solution)/shard_map/ppermute | solution.py:14
  269.6 33.9 %collective-permute-start.36 = (bf16[512,512]{1,0:T(8,128)(2,1)}, bf16[512,512]{1,0:T(8,128)(2,1)S(1)}, u32[]{:S(2)}, u32[]{:S(2)}) collective-permute-start(bf16[512,512]{1,0:T(8,128)(2,1)} %pad_maximum_fusion.12), channel_id=1, source_target_pairs={{0,16},{8,24},{16,32},{24,40},{32,48},{40,56},{48,0},{56,8},{1,17}... | collective-permute-start | bytes 1572872 | tf_op jit(solution)/shard_map/ppermute | solution.py:14
  270.4 33.1 %collective-permute-start.37 = (bf16[512,512]{1,0:T(8,128)(2,1)}, bf16[512,512]{1,0:T(8,128)(2,1)}, u32[]{:S(2)}, u32[]{:S(2)}) collective-permute-start(bf16[512,512]{1,0:T(8,128)(2,1)} %pad_maximum_fusion.13), channel_id=1, source_target_pairs={{0,32},{8,40},{16,48},{24,56},{32,0},{40,8},{48,16},{56,24},{1,33}... | collective-permute-start | bytes 1572872 | tf_op jit(solution)/shard_map/ppermute | solution.py:14
  299.4 10.1 %collective-permute-start.33 = (bf16[272,512]{1,0:T(8,128)(2,1)}, bf16[272,512]{1,0:T(8,128)(2,1)S(1)}, u32[]{:S(2)}, u32[]{:S(2)}) collective-permute-start(bf16[272,512]{1,0:T(8,128)(2,1)} %get-tuple-element.85), channel_id=1, source_target_pairs={{0,16},{8,24},{16,32},{24,40},{32,48},{40,56},{48,0},{56,8},{1,17}... | collective-permute-start | bytes 835592 | tf_op jit(solution)/shard_map/ppermute | solution.py:14
  299.4 15.1 %collective-permute-start.32 = (bf16[272,512]{1,0:T(8,128)(2,1)}, bf16[272,512]{1,0:T(8,128)(2,1)S(1)}, u32[]{:S(2)}, u32[]{:S(2)}) collective-permute-start(bf16[272,512]{1,0:T(8,128)(2,1)} %get-tuple-element.84), channel_id=1, source_target_pairs={{0,48},{8,56},{16,0},{24,8},{32,16},{40,24},{48,32},{56,40},{1,49}... | collective-permute-start | bytes 835592 | tf_op jit(solution)/shard_map/ppermute | solution.py:14
  302.7 13.5 %collective-permute-start.34 = (bf16[272,512]{1,0:T(8,128)(2,1)}, bf16[272,512]{1,0:T(8,128)(2,1)}, u32[]{:S(2)}, u32[]{:S(2)}) collective-permute-start(bf16[272,512]{1,0:T(8,128)(2,1)} %get-tuple-element.86), channel_id=1, source_target_pairs={{0,32},{8,40},{16,48},{24,56},{32,0},{40,8},{48,16},{56,24},{1,33}... | collective-permute-start | bytes 835592 | tf_op jit(solution)/shard_map/ppermute | solution.py:14
  303.5 11.1 %copy-start.26 = (bf16[512,512]{1,0:T(8,128)(2,1)}, bf16[512,512]{1,0:T(8,128)(2,1)S(1)}, u32[]{:S(2)}) copy-start(bf16[512,512]{1,0:T(8,128)(2,1)S(1)} %collective-permute-done.36) | copy-start | bytes 1572868
  316.1 15.9 %copy-start.1 = (bf16[2,256,1024]{2,1,0:T(8,128)(2,1)S(1)}, bf16[2,256,1024]{2,1,0:T(8,128)(2,1)}, u32[]{:S(2)}) copy-start(bf16[2,256,1024]{2,1,0:T(8,128)(2,1)} %param.5) | copy-start | bytes 3145732
  317.9 11.7 %collective-permute-start.38 = (bf16[256,512]{1,0:T(8,128)(2,1)S(1)}, bf16[256,512]{1,0:T(8,128)(2,1)S(1)}, u32[]{:S(2)}, u32[]{:S(2)}) collective-permute-start(bf16[256,512]{1,0:T(8,128)(2,1)S(1)} %get-tuple-element.48), channel_id=1, source_target_pairs={{0,8},{8,0},{16,24},{24,16},{32,40},{40,32},{48,56},{56,48},{1,9},... | collective-permute-start | bytes 786440 | tf_op jit(solution)/shard_map/ppermute | solution.py:14
  (21 other events, 63.8 us)

commit v2 on v1

v2 whole, which is shorter than its diff:
```python
import jax
import jax.numpy as jnp
from jax import lax
from jax.experimental import pallas as pl
from jax.experimental.pallas import tpu as pltpu
from jax.sharding import PartitionSpec as P

BF16 = jnp.bfloat16
F32 = jnp.float32
NOTE = 16
OFFSETS = ((0, 0), (0, 1), (1, 0), (-1, 0), (2, 0), (1, 1), (-1, 1), (2, 1))


def shift(value, axis, k, e):
    perm = [(i, ((i // 2 + k) % 4) * 2 + ((i % 2) ^ e)) for i in range(8)]
    return lax.ppermute(value, axis, perm)


def flip(value):
    return lax.ppermute(value, "role", [(0, 1), (1, 0)])


def sources(axis):
    me = lax.axis_index(axis)
    return [((((me >> 1) - k) & 3) << 1) | ((me & 1) ^ e) for k, e in OFFSETS]


def after(value, *others):
    return lax.optimization_barrier((value, *others))[0]


def gather_start(block, axis):
    return [shift(block, axis, 0, 1), shift(block, axis, 1, 0), shift(block, axis, -1, 0)]


def gather_middle(block, first, axis):
    other, before, nxt = first
    half = block.shape[0] // 2
    up = shift(jnp.concatenate([other, before[:half]], axis=0), axis, 1, 0)
    down = shift(jnp.concatenate([other, nxt[half:]], axis=0), axis, -1, 0)
    return [up, down]


def gather_end(block, first, middle, axis):
    other, before, nxt = first
    up, down = middle
    rows = block.shape[0]
    far = jnp.concatenate([up[rows:], down[rows:]], axis=0)
    other_far = shift(far, axis, 0, 1)
    return [block, other, before, nxt, far, up[:rows], down[:rows], other_far]


def place(blocks, at, dim):
    size = blocks[0].shape[dim]
    shape = list(blocks[0].shape)
    shape[dim] = 8 * size
    out = jnp.zeros(shape, blocks[0].dtype)
    for block, s in zip(blocks, at):
        out = lax.dynamic_update_slice_in_dim(out, block, s * size, axis=dim)
    return out


def ring_pair(by, k, axis):
    pair = jnp.concatenate([by[k, 0], by[k, 1]], axis=0).astype(BF16)
    return shift(pair, axis, -k, 0)


def ring_end(by, got, axis):
    rows = by[0, 0].shape[0]
    near, cross = by[0, 0].astype(F32), by[0, 1].astype(F32)
    for g in got:
        near = near + g[:rows].astype(F32)
        cross = cross + g[rows:].astype(F32)
    return near + shift(cross.astype(BF16), axis, 0, 1).astype(F32)


def dot(a, b, dims=((1,), (0,))):
    return lax.dot_general(a, b, (dims, ((), ())), preferred_element_type=F32)


def split_note(value, width):
    value = jnp.broadcast_to(value, (1, width)).astype(F32)
    row = lax.broadcasted_iota(jnp.int32, (NOTE, width), 0)
    high = lax.reduce_precision(value, 8, 7)
    middle = lax.reduce_precision(value - high, 8, 7)
    low = value - high - middle
    note = jnp.where(row == 0, high, jnp.where(row == 1, middle, jnp.where(row == 2, low, 0.0)))
    return note.astype(BF16)


def join_note(note):
    return jnp.sum(note.astype(F32), axis=0, keepdims=True)


def project_kernel(hidden, projector, teacher, out, low, high, square):
    step, block = pl.program_id(0), pl.program_id(1)
    n, width = out.shape[0] - NOTE, out.shape[1]

    @pl.when((step == 0) & (block == 0))
    def _():
        low[...] = jnp.zeros_like(low)
        high[...] = jnp.zeros_like(high)

    @pl.when(step == 0)
    def _():
        low[...] += jnp.dot(hidden[...], projector[0], preferred_element_type=F32)
        high[...] += jnp.dot(hidden[...], projector[1], preferred_element_type=F32)

    @pl.when((step == 1) & (block == 0))
    def _():
        low[...] -= teacher[:, :width]
        high[...] -= teacher[:, width:]
        square[...] = jnp.broadcast_to(
            jnp.sum(low[...] * low[...] + high[...] * high[...], keepdims=True), square.shape
        )

    @pl.when(step == 1)
    def _():
        dims = (((1,), (1,)), ((), ()))
        back = lax.dot_general(low[...].astype(BF16), projector[0], dims, preferred_element_type=F32)
        back += lax.dot_general(high[...].astype(BF16), projector[1], dims, preferred_element_type=F32)
        out[:n] = back.astype(BF16)
        value = square[:1]
        row = lax.broadcasted_iota(jnp.int32, (NOTE, width), 0)
        top = value.astype(BF16).astype(F32)
        middle = (value - top).astype(BF16).astype(F32)
        bottom = value - top - middle
        note = jnp.where(row == 0, top, jnp.where(row == 1, middle, jnp.where(row == 2, bottom, 0.0)))
        out[n:] = note.astype(BF16)


def project(hidden, projector, teacher):
    rows, total = hidden.shape
    blocks = projector.shape[1]
    width = projector.shape[3]
    size = total // blocks
    return pl.pallas_call(
        project_kernel,
        grid=(2, blocks),
        in_specs=[
            pl.BlockSpec((rows, size), lambda s, b: (0, b * (1 - s) + (blocks - 1) * s)),
            pl.BlockSpec((2, None, size, width), lambda s, b: (0, b * (1 - s) + (blocks - 1 - b) * s, 0, 0)),
            pl.BlockSpec((rows, 2 * width), lambda s, b: (0, 0)),
        ],
        out_specs=pl.BlockSpec((None, rows + NOTE, size), lambda s, b: ((blocks - 1 - b) * s + (blocks - 1) * (1 - s), 0, 0)),
        out_shape=jax.ShapeDtypeStruct((blocks, rows + NOTE, size), BF16),
        scratch_shapes=[
            pltpu.VMEM((rows, width), F32),
            pltpu.VMEM((rows, width), F32),
            pltpu.VMEM((8, width), F32),
        ],
        compiler_params=pltpu.CompilerParams(
            dimension_semantics=("arbitrary", "arbitrary"), vmem_limit_bytes=32 * 1024 * 1024
        ),
        cost_estimate=pl.CostEstimate(
            flops=8 * rows * total * width, bytes_accessed=8 * total * width, transcendentals=0
        ),
    )(hidden, projector, teacher)


def shards(teacher_in, teacher_weight, student_in, student_weight, projector):
    role = lax.axis_index("role")
    n_tensor = lax.axis_size("tensor")
    n_data = lax.axis_size("dp")
    own_rows = student_in.shape[0]
    total_rows = 2 * own_rows * n_data
    out_width = teacher_weight.shape[1]
    half = out_width // 2
    feat, hid = student_weight.shape
    wide = feat * n_data
    cols = projector.shape[1]
    model_from = sources("tensor")

    weight = lax.all_gather(student_weight, ("role", "dp"), axis=0, tiled=True)

    swap = [(d * 8 + t, t * 8 + d) for d in range(8) for t in range(8)]
    projector = lax.ppermute(projector, ("dp", "tensor"), swap)
    projector = lax.all_gather(projector, ("role", "dp"), axis=0, tiled=True)
    projector = projector.reshape(2, n_data, hid, cols)

    away = dot(lax.dynamic_index_in_dim(teacher_in, 1 - role, 0, False), teacher_weight)
    away = flip(away.astype(BF16))
    teacher = dot(lax.dynamic_index_in_dim(teacher_in, role, 0, False), teacher_weight)
    teacher = teacher + away.astype(F32)
    teacher = [
        jnp.concatenate(
            [lax.dynamic_slice_in_dim(teacher, h * half + s * cols, cols, axis=1) for h in (0, 1)],
            axis=1,
        )
        for s in model_from
    ]
    teacher = dict(zip(OFFSETS, teacher))
    t_got = [ring_pair(teacher, k, "tensor") for k in (1, -1, 2)]

    mine = lax.dynamic_slice_in_dim(student_in, role * wide, wide, axis=1)
    theirs = flip(lax.dynamic_slice_in_dim(student_in, (1 - role) * wide, wide, axis=1))

    weight, *t_near = lax.optimization_barrier((weight, teacher[0, 0], teacher[0, 1]))
    teacher[0, 0], teacher[0, 1] = t_near
    pre = dot(student_in, weight)
    sigma = jax.nn.sigmoid(pre)
    hidden = (pre * sigma).astype(BF16)
    hidden, *t_got[:2] = lax.optimization_barrier((hidden, *t_got[:2]))
    h_first = gather_start(hidden, "tensor")
    h_middle = gather_middle(hidden, h_first, "tensor")
    h_middle[0], t_got[2], theirs = lax.optimization_barrier((h_middle[0], t_got[2], theirs))
    hidden = place(gather_end(hidden, h_first, h_middle, "tensor"), model_from, 1)
    teacher = ring_end(teacher, t_got, "tensor")
    hidden, teacher = lax.optimization_barrier((hidden, teacher))
    student = jnp.concatenate([mine, theirs], axis=0)

    back = project(hidden, projector, teacher)
    back = lax.all_to_all(back, "tensor", 0, 0, tiled=True)
    back = jnp.sum(back.astype(F32), axis=0)
    square = join_note(back[own_rows:])
    back = back[:own_rows]

    delta = (back * sigma * (1.0 + pre * (1.0 - sigma))).astype(BF16)
    packed = flip(jnp.concatenate([delta, split_note(square, hid)], axis=0))
    delta = jnp.concatenate([delta, packed[:own_rows]], axis=0)
    square = square + join_note(packed[own_rows:])

    grad = dot(student, delta, ((0,), (0,))).astype(BF16).reshape(n_data, feat, hid)
    note = jnp.broadcast_to(split_note(square, hid)[None], (n_data, NOTE, hid))
    grad = jnp.concatenate([grad, note], axis=1)
    grad = lax.all_to_all(grad, "dp", 0, 0, tiled=True)
    grad = jnp.sum(grad.astype(F32), axis=0)
    loss = join_note(grad[feat:])[0, 0] / (2.0 * total_rows * out_width)
    return (grad[:feat] / jnp.sqrt(jnp.float32(total_rows)), loss)


def solution(mesh):
    in_specs = (
        P(None, "dp", ("role", "tensor")),
        P(("role", "tensor"), None),
        P(("role", "dp"), None),
        P(("role", "dp"), "tensor"),
        P("tensor", ("role", "dp")),
    )
    out_specs = (P(("role", "dp"), "tensor"), P())
    return jax.shard_map(shards, mesh=mesh, in_specs=in_specs, out_specs=out_specs, check_vma=False)
```

time: 334 us -> 294 us (0.88)
  starting transfers between devices: 83.2 us -> 54.6 us
  blocking collectives: 34.2 us -> 55.1 us
  local copies, waits for them, and re-layouts: 29.3 us -> 11.5 us
  Pallas kernels: 0 us -> 10.9 us
  matrix products: 46 us -> 35.1 us
  between operations: 26.9 us -> 16.2 us
  other arithmetic: 17.6 us -> 10.1 us
  waiting for transfers between devices: 95.8 us -> 99.9 us
    ppermute x31 -> x10, starting transfers between devices: 79.9 us -> 48.6 us  [shift(): return lax.ppermute(value, axis, perm)]
    ppermute x31 -> x10, waiting for transfers between devices: 95.4 us -> 67.3 us  [shift(): return lax.ppermute(value, axis, perm)]
    all_to_all x0 -> x1, waiting for transfers between devices: none -> 28.1 us  [shards(): back = lax.all_to_all(back, 'tensor', 0, 0, tiled=True)]
    all_to_all x1, blocking collectives: 34.2 us -> 55.1 us  [shards(): grad = lax.all_to_all(grad, 'dp', 0, 0, tiled=True)]
    pallas_call x0 -> x1, Pallas kernels: none -> 10.9 us  [project(): pl.pallas_call(project_kernel, grid=(2, blocks), in_specs=[pl.BlockSpec((...]
    dot_general x8 -> x4, matrix products: 46 us -> 35.1 us  [dot(): return lax.dot_general(a, b, (dims, ((), ())), preferred_element_type=F32)]
    dynamic_update_slice x20 -> x7, local copies, waits for them, and re-layouts: 9.16 us -> 1.14 us  [place(): out = lax.dynamic_update_slice_in_dim(out, block, s * size, axis=dim)]
    slice x7 -> x2, local copies, waits for them, and re-layouts: 4.49 us -> 0.53 us  [the longest x1 0.51 us: shards(): loss = join_note(grad[feat:])[0, 0] / (2.0 * total_rows * out_width)]
  transfers between devices with their start and end apart: 39 -> 17, of which waited for: 19 -> 9; matrix products, arithmetic and copies ran while one was open for 18% -> 15% of each run, Pallas kernels for 0% -> 0%
where the time goes in v2:
time: 294 us; the launch traced here: 293 us
  waiting for transfers between devices  99.9 us (34%)
  blocking collectives  55.1 us (19%)
  starting transfers between devices  54.6 us (19%)
  matrix products  35.1 us (12%)
  between operations  16.2 us (6%)
  local copies, waits for them, and re-layouts  11.5 us (4%)
  Pallas kernels  10.9 us (4%)
  other arithmetic  10.1 us (3%)
    ppermute x10, waiting for transfers between devices, shift(): return lax.ppermute(value, axis, perm)  67.3 us
    all_to_all x1, blocking collectives, shards(): grad = lax.all_to_all(grad, 'dp', 0, 0, tiled=True)  55.1 us
    ppermute x10, starting transfers between devices, shift(): return lax.ppermute(value, axis, perm)  48.6 us
    dot_general x4, matrix products, dot(): return lax.dot_general(a, b, (dims, ((), ())), preferred_element_type=F32)  35.1 us
    all_to_all x1, waiting for transfers between devices, shards(): back = lax.all_to_all(back, 'tensor', 0, 0, tiled=True)  28.1 us
    pallas_call x1, Pallas kernels, project(): pl.pallas_call(project_kernel, grid=(2, blocks), in_specs=[pl.BlockSpec((...  10.9 us
  transfers between devices with their start and end apart: 17, of which 9 were waited for; matrix products, arithmetic and copies ran while one was open for 15% of the time, Pallas kernels for 0%

profile of v2, /device:TPU:0, one launch (start us, length us, event | category | flops | bytes accessed | tf_op | source)
XLA Modules:
  0.0 293.4 jit_solution(18176412304289955274)
XLA Ops:
  7.2 0.7 all-gather.3.cloned.1.call-update
  8.0 1.7 collective-permute-start.12
  9.7 0.8 copy-done.9
  10.5 11.8 %convolution_convert_fusion = bf16[256,8192]{1,0:T(8,128)(2,1)} fusion(bf16[1024,8192]{1,0:T(8,128)(2,1)} %param.6, bf16[2,256,1024]{2,1,0:T(8,128)(2,1)S(1)} %copy-done, s32[]{:T(128)S(6)} %select_n.119), kind=kOutput, calls=%fused_computation | convolution fusion | flops 4297064448 | bytes 21495812 | tf_op jit(solution)/shard_map/dot_general | solution.py:78
  22.3 4.7 %constant_dynamic-slice_fusion.5 = (bf16[256,4096]{1,0:T(8,128)(2,1)}, bf16[256,4096]{1,0:T(8,128)(2,1)}) fusion(bf16[256,8192]{1,0:T(8,128)(2,1)} %param.7, s32[]{:T(128)S(6)} %select_n.117, s32[]{:T(128)S(6)} %select_n.136), kind=kLoop, calls=%fused_computation.67 | loop fusion | bytes 8388616 | tf_op jit(solution)/shard_map/dynamic_slice | solution.py:195
  27.0 0.5 collective-permute-start.7
  27.5 2.3 collective-permute-done
  29.8 11.4 %convert_add_fusion = f32[256,8192]{1,0:T(8,128)S(1)} fusion(bf16[256,8192]{1,0:T(8,128)(2,1)} %collective-permute-done, bf16[1024,8192]{1,0:T(8,128)(2,1)} %param.6, bf16[2,256,1024]{2,1,0:T(8,128)(2,1)S(1)} %copy-done, s32[]{:T(128)S(6)} %select_n.118), kind=kOutput, calls=%fused_computation.2 | convolution fusion | flops 4299161600 | bytes 29884420 | tf_op jit(solution)/shard_map/dot_general | solution.py:78
  41.2 0.4 dynamic-slice_convert_fusion.3
  41.7 1.1 maximum_maximum_fusion.2
  42.8 30.7 %collective-permute-start.6 = (bf16[512,1024]{1,0:T(8,128)(2,1)}, bf16[512,1024]{1,0:T(8,128)(2,1)}, u32[]{:S(2)}, u32[]{:S(2)}) collective-permute-start(bf16[512,1024]{1,0:T(8,128)(2,1)} %maximum_maximum_fusion.2), channel_id=1, source_target_pairs={{0,4},{1,5},{2,6},{3,7},{4,0},{5,1},{6,2},{7,3},{8,12},{9,13},{10,... | collective-permute-start | bytes 3145736 | tf_op jit(solution)/shard_map/ppermute | solution.py:16
  73.6 0.1 maximum_maximum_fusion.1
  73.7 3.8 %collective-permute-start.2 = (bf16[512,1024]{1,0:T(8,128)(2,1)S(1)}, bf16[512,1024]{1,0:T(8,128)(2,1)}, u32[]{:S(2)}, u32[]{:S(2)}) collective-permute-start(bf16[512,1024]{1,0:T(8,128)(2,1)S(1)} %maximum_maximum_fusion.1), channel_id=1, source_target_pairs={{0,2},{1,3},{2,4},{3,5},{4,6},{5,7},{6,0},{7,1},{8,10},{9,11},{10,... | collective-permute-start | bytes 3145736 | tf_op jit(solution)/shard_map/ppermute | solution.py:16
  77.5 0.1 maximum_maximum_fusion
  77.7 0.2 constant_dynamic-slice_fusion.2
  77.9 1.1 pad_maximum_fusion.1
  79.0 7.9 %multiply_convert_fusion = (bf16[256,512]{1,0:T(8,128)(2,1)}, f32[256,512]{1,0:T(8,128)}) fusion(bf16[256,8192]{1,0:T(8,128)(2,1)} %param.7, bf16[8192,512]{1,0:T(8,128)(2,1)} %all-gather.3.cloned.1.call-done), kind=kOutput, calls=%fused_computation.39 | convolution fusion | flops 2148139008 | bytes 13369344 | tf_op jit(solution)/shard_map/dot_general | solution.py:78
  86.9 32.9 %collective-permute-done.2 = bf16[512,1024]{1,0:T(8,128)(2,1)} collective-permute-done((bf16[512,1024]{1,0:T(8,128)(2,1)S(1)}, bf16[512,1024]{1,0:T(8,128)(2,1)}, u32[]{:S(2)}, u32[]{:S(2)}) %collective-permute-start.2) | collective-permute-done | bytes 1048608 | tf_op jit(solution)/shard_map/ppermute | solution.py:16
  119.8 3.4 %collective-permute-done.1 = bf16[512,1024]{1,0:T(8,128)(2,1)} collective-permute-done((bf16[512,1024]{1,0:T(8,128)(2,1)S(1)}, bf16[512,1024]{1,0:T(8,128)(2,1)}, u32[]{:S(2)}, u32[]{:S(2)}) %collective-permute-start.1) | collective-permute-done | bytes 1048608 | tf_op jit(solution)/shard_map/ppermute | solution.py:16
  123.2 0.2 collective-permute-start.4
  123.5 3.0 %collective-permute-start.8 = (bf16[256,512]{1,0:T(8,128)(2,1)}, bf16[256,512]{1,0:T(8,128)(2,1)S(1)}, u32[]{:S(2)}, u32[]{:S(2)}) collective-permute-start(bf16[256,512]{1,0:T(8,128)(2,1)} %get-tuple-element.14), channel_id=1, source_target_pairs={{0,6},{1,7},{2,0},{3,1},{4,2},{5,3},{6,4},{7,5},{8,14},{9,15},{10,... | collective-permute-start | bytes 786440 | tf_op jit(solution)/shard_map/ppermute | solution.py:16
  126.5 3.5 %collective-permute-start.3 = (bf16[256,512]{1,0:T(8,128)(2,1)}, bf16[256,512]{1,0:T(8,128)(2,1)S(1)}, u32[]{:S(2)}, u32[]{:S(2)}) collective-permute-start(bf16[256,512]{1,0:T(8,128)(2,1)} %get-tuple-element.14), channel_id=1, source_target_pairs={{0,1},{1,0},{2,3},{3,2},{4,5},{5,4},{6,7},{7,6},{8,9},{9,8},{10,11... | collective-permute-start | bytes 786440 | tf_op jit(solution)/shard_map/ppermute | solution.py:16
  130.0 2.6 collective-permute-done.4
  132.6 5.3 %collective-permute-done.3 = bf16[256,512]{1,0:T(8,128)(2,1)S(1)} collective-permute-done((bf16[256,512]{1,0:T(8,128)(2,1)}, bf16[256,512]{1,0:T(8,128)(2,1)S(1)}, u32[]{:S(2)}, u32[]{:S(2)}) %collective-permute-start.3) | collective-permute-done | bytes 262176 | tf_op jit(solution)/shard_map/ppermute | solution.py:16
  138.0 1.6 collective-permute-start.5
  139.6 0.2 broadcast_in_dim.55
  139.8 1.0 constant_dynamic-update-slice_fusion.5
  140.8 1.9 collective-permute-start.9
  142.9 7.1 %collective-permute-done.5 = bf16[384,512]{1,0:T(8,128)(2,1)S(1)} collective-permute-done((bf16[384,512]{1,0:T(8,128)(2,1)S(1)}, bf16[384,512]{1,0:T(8,128)(2,1)S(1)}, u32[]{:S(2)}, u32[]{:S(2)}) %collective-permute-start.5) | collective-permute-done | bytes 393248 | tf_op jit(solution)/shard_map/ppermute | solution.py:16
  150.0 1.7 add_convert_fusion
  151.7 0.1 collective-permute-start.11
  151.9 3.6 %collective-permute-start.10 = (bf16[256,512]{1,0:T(8,128)(2,1)S(1)}, bf16[256,512]{1,0:T(8,128)(2,1)S(1)}, u32[]{:S(2)}, u32[]{:S(2)}) collective-permute-start(bf16[256,512]{1,0:T(8,128)(2,1)S(1)} %get-tuple-element.42), channel_id=1, source_target_pairs={{0,1},{1,0},{2,3},{3,2},{4,5},{5,4},{6,7},{7,6},{8,9},{9,8},{10,11... | collective-permute-start | bytes 786440 | tf_op jit(solution)/shard_map/ppermute | solution.py:16
  155.5 16.0 %collective-permute-done.10 = bf16[256,512]{1,0:T(8,128)(2,1)S(1)} collective-permute-done((bf16[256,512]{1,0:T(8,128)(2,1)S(1)}, bf16[256,512]{1,0:T(8,128)(2,1)S(1)}, u32[]{:S(2)}, u32[]{:S(2)}) %collective-permute-start.10) | collective-permute-done | bytes 262176 | tf_op jit(solution)/shard_map/ppermute | solution.py:16
  171.6 1.8 convert_add_fusion.1.teacher
  173.4 3.4 %copy-done.2 = bf16[8192,512]{1,0:T(8,128)(2,1)S(1)} copy-done((bf16[8192,512]{1,0:T(8,128)(2,1)S(1)}, bf16[8192,512]{1,0:T(8,128)(2,1)}, u32[]{:S(2)}) %copy-start.2) | copy-done | bytes 8388632
  176.7 10.9 %shard_map.68 = bf16[8,272,512]{2,1,0:T(8,128)(2,1)} custom-call(bf16[256,4096]{1,0:T(8,128)(2,1)S(1)} %constant_dynamic-update-slice_fusion.hidden, bf16[2,8,512,512]{3,2,1,0:T(8,128)(2,1)S(1)} %bitcast.18, f32[256,1024]{1,0:T(8,128)S(1)} %convert_add_fusion.1.teacher), custom_call_target="tpu_custom_call" | custom-call | flops 4294967296 | bytes 16777216 | tf_op jit(solution)/shard_map/pallas_call | solution.py:137
  187.6 3.6 %all-to-all-start = ((bf16[8,272,512]{2,1,0:T(8,128)(2,1)}), bf16[8,272,512]{2,1,0:T(8,128)(2,1)S(1)}, u32[]{:S(2)}, u32[]{:S(2)}) async-start(bf16[8,272,512]{2,1,0:T(8,128)(2,1)} %shard_map.68), calls=%async_computation | async-start | bytes 4456448 | tf_op jit(solution)/shard_map/all_to_all | solution.py:213
  191.3 28.1 %all-to-all-done = bf16[8,272,512]{2,1,0:T(8,128)(2,1)S(1)} async-done(((bf16[8,272,512]{2,1,0:T(8,128)(2,1)}), bf16[8,272,512]{2,1,0:T(8,128)(2,1)S(1)}, u32[]{:S(2)}, u32[]{:S(2)}) %all-to-all-start) | async-done | bytes 2228256 | tf_op jit(solution)/shard_map/all_to_all | solution.py:213
  219.4 0.3 convert_reduce_fusion.1
  219.7 1.4 fusion.4
  221.2 0.1 collective-permute-start.13
  221.3 1.5 collective-permute-done.13
  222.9 4.0 %convolution_convert_fusion.1 = bf16[4096,512]{1,0:T(8,128)(2,1)S(1)} fusion(bf16[256,4096]{1,0:T(8,128)(2,1)} %collective-permute-done.7, bf16[256,4096]{1,0:T(8,128)(2,1)S(1)} %copy-done.4, bf16[256,512]{1,0:T(8,128)(2,1)S(1)} %slice.82, bf16[256,512]{1,0:T(8,128)(2,1)S(1)} %fusion.4), kind=kOutput, calls=%fused_computation.3 | convolution fusion | flops 2159017984 | bytes 8912896 | tf_op jit(solution)/shard_map/dot_general | solution.py:78
  227.0 0.4 pad_maximum_fusion
  227.4 55.1 %all_to_all.10 = bf16[8,528,512]{2,1,0:T(8,128)(2,1)S(1)} all-to-all(bf16[8,528,512]{2,1,0:T(8,128)(2,1)S(1)} %pad_maximum_fusion), channel_id=1, replica_groups=mesh['role'=2,'dp'=8,'tensor'=8] {'dp'}, dimensions={0} | all-to-all | bytes 8650752 | tf_op jit(solution)/shard_map/all_to_all | solution.py:226
  282.5 0.6 convert_reduce_fusion
  283.2 1.1 slice_multiply_fusion
  284.3 0.5 slice.86
  (55 shorter events, 0.8 us)
Async XLA Ops:
  7.2 3.3 %copy-start = (bf16[2,256,1024]{2,1,0:T(8,128)(2,1)S(1)}, bf16[2,256,1024]{2,1,0:T(8,128)(2,1)}, u32[]{:S(2)}) copy-start(bf16[2,256,1024]{2,1,0:T(8,128)(2,1)} %param.5) | copy-start | bytes 3145732
  7.2 71.8 %all-gather.3.cloned.1.call-start = ((), (), s32[]{:S(2)}) async-start(), calls=%async_computation.2 | async-start | bytes 8912896 | tf_op jit(solution)/shard_map/all_gather | solution.py:174
  7.9 165.4 %all-gather.5.cloned.1.call-start = ((), (), s32[]{:S(2)}) async-start(), calls=%async_computation.3 | async-start | bytes 8912896 | tf_op jit(solution)/shard_map/all_gather | solution.py:178
  8.0 1.7 collective-permute-start.12
  9.7 0.8 copy-start.9
  22.3 7.5 %collective-permute-start = (bf16[256,8192]{1,0:T(8,128)(2,1)}, bf16[256,8192]{1,0:T(8,128)(2,1)}, u32[]{:S(2)}, u32[]{:S(2)}) collective-permute-start(bf16[256,8192]{1,0:T(8,128)(2,1)} %convolution_convert_fusion), channel_id=1, source_target_pairs={{0,64},{64,0},{1,65},{65,1},{2,66},{66,2},{3,67},{67,3},{4,68},{68... | collective-permute-start | bytes 12582920 | tf_op jit(solution)/shard_map/ppermute | solution.py:20
  27.0 115.9 %collective-permute-start.7 = (bf16[256,4096]{1,0:T(8,128)(2,1)}, bf16[256,4096]{1,0:T(8,128)(2,1)}, u32[]{:S(2)}, u32[]{:S(2)}) collective-permute-start(bf16[256,4096]{1,0:T(8,128)(2,1)} %get-tuple-element.41), channel_id=1, source_target_pairs={{0,64},{64,0},{1,65},{65,1},{2,66},{66,2},{3,67},{67,3},{4,68},{68... | collective-permute-start | bytes 6291464 | tf_op jit(solution)/shard_map/ppermute | solution.py:20
  42.8 100.1 %collective-permute-start.6 = (bf16[512,1024]{1,0:T(8,128)(2,1)}, bf16[512,1024]{1,0:T(8,128)(2,1)}, u32[]{:S(2)}, u32[]{:S(2)}) collective-permute-start(bf16[512,1024]{1,0:T(8,128)(2,1)} %maximum_maximum_fusion.2), channel_id=1, source_target_pairs={{0,4},{1,5},{2,6},{3,7},{4,0},{5,1},{6,2},{7,3},{8,12},{9,13},{10,... | collective-permute-start | bytes 3145736 | tf_op jit(solution)/shard_map/ppermute | solution.py:16
  73.7 46.1 %collective-permute-start.2 = (bf16[512,1024]{1,0:T(8,128)(2,1)S(1)}, bf16[512,1024]{1,0:T(8,128)(2,1)}, u32[]{:S(2)}, u32[]{:S(2)}) collective-permute-start(bf16[512,1024]{1,0:T(8,128)(2,1)S(1)} %maximum_maximum_fusion.1), channel_id=1, source_target_pairs={{0,2},{1,3},{2,4},{3,5},{4,6},{5,7},{6,0},{7,1},{8,10},{9,11},{10,... | collective-permute-start | bytes 3145736 | tf_op jit(solution)/shard_map/ppermute | solution.py:16
  77.6 45.6 %collective-permute-start.1 = (bf16[512,1024]{1,0:T(8,128)(2,1)S(1)}, bf16[512,1024]{1,0:T(8,128)(2,1)}, u32[]{:S(2)}, u32[]{:S(2)}) collective-permute-start(bf16[512,1024]{1,0:T(8,128)(2,1)S(1)} %maximum_maximum_fusion), channel_id=1, source_target_pairs={{0,6},{1,7},{2,0},{3,1},{4,2},{5,3},{6,4},{7,5},{8,14},{9,15},{10,... | collective-permute-start | bytes 3145736 | tf_op jit(solution)/shard_map/ppermute | solution.py:16
  123.2 9.3 %collective-permute-start.4 = (bf16[256,512]{1,0:T(8,128)(2,1)}, bf16[256,512]{1,0:T(8,128)(2,1)S(1)}, u32[]{:S(2)}, u32[]{:S(2)}) collective-permute-start(bf16[256,512]{1,0:T(8,128)(2,1)} %get-tuple-element.14), channel_id=1, source_target_pairs={{0,2},{1,3},{2,4},{3,5},{4,6},{5,7},{6,0},{7,1},{8,10},{9,11},{10,... | collective-permute-start | bytes 786440 | tf_op jit(solution)/shard_map/ppermute | solution.py:16
  123.5 9.1 %collective-permute-start.8 = (bf16[256,512]{1,0:T(8,128)(2,1)}, bf16[256,512]{1,0:T(8,128)(2,1)S(1)}, u32[]{:S(2)}, u32[]{:S(2)}) collective-permute-start(bf16[256,512]{1,0:T(8,128)(2,1)} %get-tuple-element.14), channel_id=1, source_target_pairs={{0,6},{1,7},{2,0},{3,1},{4,2},{5,3},{6,4},{7,5},{8,14},{9,15},{10,... | collective-permute-start | bytes 786440 | tf_op jit(solution)/shard_map/ppermute | solution.py:16
  126.5 11.4 %collective-permute-start.3 = (bf16[256,512]{1,0:T(8,128)(2,1)}, bf16[256,512]{1,0:T(8,128)(2,1)S(1)}, u32[]{:S(2)}, u32[]{:S(2)}) collective-permute-start(bf16[256,512]{1,0:T(8,128)(2,1)} %get-tuple-element.14), channel_id=1, source_target_pairs={{0,1},{1,0},{2,3},{3,2},{4,5},{5,4},{6,7},{7,6},{8,9},{9,8},{10,11... | collective-permute-start | bytes 786440 | tf_op jit(solution)/shard_map/ppermute | solution.py:16
  132.6 5.4 %copy-start.5 = (bf16[256,512]{1,0:T(8,128)(2,1)}, bf16[256,512]{1,0:T(8,128)(2,1)S(1)}, u32[]{:S(2)}) copy-start(bf16[256,512]{1,0:T(8,128)(2,1)S(1)} %collective-permute-done.4) | copy-start | bytes 786436
  132.6 5.4 %copy-start.7 = (bf16[256,512]{1,0:T(8,128)(2,1)}, bf16[256,512]{1,0:T(8,128)(2,1)S(1)}, u32[]{:S(2)}) copy-start(bf16[256,512]{1,0:T(8,128)(2,1)S(1)} %collective-permute-done.8) | copy-start | bytes 786436
  138.0 12.0 %collective-permute-start.5 = (bf16[384,512]{1,0:T(8,128)(2,1)S(1)}, bf16[384,512]{1,0:T(8,128)(2,1)S(1)}, u32[]{:S(2)}, u32[]{:S(2)}) collective-permute-start(bf16[384,512]{1,0:T(8,128)(2,1)S(1)} %get-tuple-element.44), channel_id=1, source_target_pairs={{0,2},{1,3},{2,4},{3,5},{4,6},{5,7},{6,0},{7,1},{8,10},{9,11},{10,... | collective-permute-start | bytes 1179656 | tf_op jit(solution)/shard_map/ppermute | solution.py:16
  139.6 3.2 %copy-start.6 = (bf16[256,512]{1,0:T(8,128)(2,1)S(1)}, bf16[256,512]{1,0:T(8,128)(2,1)}, u32[]{:S(2)}) copy-start(bf16[256,512]{1,0:T(8,128)(2,1)} %copy-done.5) | copy-start | bytes 786436
  139.6 3.2 %copy-start.8 = (bf16[256,512]{1,0:T(8,128)(2,1)S(1)}, bf16[256,512]{1,0:T(8,128)(2,1)}, u32[]{:S(2)}) copy-start(bf16[256,512]{1,0:T(8,128)(2,1)} %copy-done.7) | copy-start | bytes 786436
  140.8 10.9 %collective-permute-start.9 = (bf16[384,512]{1,0:T(8,128)(2,1)S(1)}, bf16[384,512]{1,0:T(8,128)(2,1)S(1)}, u32[]{:S(2)}, u32[]{:S(2)}) collective-permute-start(bf16[384,512]{1,0:T(8,128)(2,1)S(1)} %get-tuple-element.45), channel_id=1, source_target_pairs={{0,6},{1,7},{2,0},{3,1},{4,2},{5,3},{6,4},{7,5},{8,14},{9,15},{10,... | collective-permute-start | bytes 1179656 | tf_op jit(solution)/shard_map/ppermute | solution.py:16
  151.7 19.9 %copy-start.3 = (f32[256,1024]{1,0:T(8,128)S(1)}, f32[256,1024]{1,0:T(8,128)}, u32[]{:S(2)}) copy-start(f32[256,1024]{1,0:T(8,128)} %get-tuple-element.17) | copy-start | bytes 3145732
  151.7 19.9 %collective-permute-start.11 = (bf16[256,1024]{1,0:T(8,128)(2,1)S(1)}, bf16[256,1024]{1,0:T(8,128)(2,1)S(1)}, u32[]{:S(2)}, u32[]{:S(2)}) collective-permute-start(bf16[256,1024]{1,0:T(8,128)(2,1)S(1)} %add_convert_fusion), channel_id=1, source_target_pairs={{0,1},{1,0},{2,3},{3,2},{4,5},{5,4},{6,7},{7,6},{8,9},{9,8},{10,11... | collective-permute-start | bytes 1572872 | tf_op jit(solution)/shard_map/ppermute | solution.py:16
  151.9 19.6 %collective-permute-start.10 = (bf16[256,512]{1,0:T(8,128)(2,1)S(1)}, bf16[256,512]{1,0:T(8,128)(2,1)S(1)}, u32[]{:S(2)}, u32[]{:S(2)}) collective-permute-start(bf16[256,512]{1,0:T(8,128)(2,1)S(1)} %get-tuple-element.42), channel_id=1, source_target_pairs={{0,1},{1,0},{2,3},{3,2},{4,5},{5,4},{6,7},{7,6},{8,9},{9,8},{10,11... | collective-permute-start | bytes 786440 | tf_op jit(solution)/shard_map/ppermute | solution.py:16
  173.4 3.4 %copy-start.2 = (bf16[8192,512]{1,0:T(8,128)(2,1)S(1)}, bf16[8192,512]{1,0:T(8,128)(2,1)}, u32[]{:S(2)}) copy-start(bf16[8192,512]{1,0:T(8,128)(2,1)} %all-gather.5.cloned.1.call-done) | copy-start | bytes 25165828
  187.6 31.7 %all-to-all-start = ((bf16[8,272,512]{2,1,0:T(8,128)(2,1)}), bf16[8,272,512]{2,1,0:T(8,128)(2,1)S(1)}, u32[]{:S(2)}, u32[]{:S(2)}) async-start(bf16[8,272,512]{2,1,0:T(8,128)(2,1)} %shard_map.68), calls=%async_computation | async-start | bytes 4456448 | tf_op jit(solution)/shard_map/all_to_all | solution.py:213
  219.4 3.6 %copy-start.4 = (bf16[256,4096]{1,0:T(8,128)(2,1)S(1)}, bf16[256,4096]{1,0:T(8,128)(2,1)}, u32[]{:S(2)}) copy-start(bf16[256,4096]{1,0:T(8,128)(2,1)} %get-tuple-element.40) | copy-start | bytes 6291460
  221.2 1.6 collective-permute-start.13
  282.5 2.9 copy-start.1
Sparse Core Ops, SparseCore 0:
  9.7 61.2 all-gather.2
  72.7 60.2 all-gather.4

commit v3 on v2

--- a/solution.py
+++ b/solution.py
@@ -48,16 +48,6 @@
     far = jnp.concatenate([up[rows:], down[rows:]], axis=0)
     other_far = shift(far, axis, 0, 1)
     return [block, other, before, nxt, far, up[:rows], down[:rows], other_far]
-
-
-def place(blocks, at, dim):
-    size = blocks[0].shape[dim]
-    shape = list(blocks[0].shape)
-    shape[dim] = 8 * size
-    out = jnp.zeros(shape, blocks[0].dtype)
-    for block, s in zip(blocks, at):
-        out = lax.dynamic_update_slice_in_dim(out, block, s * size, axis=dim)
-    return out
 
 
 def ring_pair(by, k, axis):
@@ -92,7 +82,7 @@
     return jnp.sum(note.astype(F32), axis=0, keepdims=True)
 
 
-def project_kernel(hidden, projector, teacher, out, low, high, square):
+def project_kernel(order, hidden, projector, teacher, out, low, high, square):
     step, block = pl.program_id(0), pl.program_id(1)
     n, width = out.shape[0] - NOTE, out.shape[1]
 
@@ -129,33 +119,68 @@
         out[n:] = note.astype(BF16)
 
 
-def project(hidden, projector, teacher):
-    rows, total = hidden.shape
-    blocks = projector.shape[1]
-    width = projector.shape[3]
-    size = total // blocks
+def project(order, hidden, projector, teacher):
+    _, blocks, size, width = projector.shape
+    rows = teacher.shape[0]
+    last = blocks - 1
     return pl.pallas_call(
         project_kernel,
-        grid=(2, blocks),
-        in_specs=[
-            pl.BlockSpec((rows, size), lambda s, b: (0, b * (1 - s) + (blocks - 1) * s)),
-            pl.BlockSpec((2, None, size, width), lambda s, b: (0, b * (1 - s) + (blocks - 1 - b) * s, 0, 0)),
-            pl.BlockSpec((rows, 2 * width), lambda s, b: (0, 0)),
-        ],
-        out_specs=pl.BlockSpec((None, rows + NOTE, size), lambda s, b: ((blocks - 1 - b) * s + (blocks - 1) * (1 - s), 0, 0)),
+        grid_spec=pltpu.PrefetchScalarGridSpec(
+            num_scalar_prefetch=1,
+            grid=(2, blocks),
+            in_specs=[
+                pl.BlockSpec((rows, size), lambda s, b, order: (b * (1 - s) + last * s, 0)),
+                pl.BlockSpec(
+                    (2, None, size, width), lambda s, b, order: (0, b * (1 - s) + (last - b) * s, 0, 0)
+                ),
+                pl.BlockSpec((rows, 2 * width), lambda s, b, order: (0, 0)),
+            ],
+            out_specs=pl.BlockSpec((None, rows + NOTE, size), lambda s, b, order: (order[last - b * s], 0, 0)),
+            scratch_shapes=[
+                pltpu.VMEM((rows, width), F32),
+                pltpu.VMEM((rows, width), F32),
+                pltpu.VMEM((8, width), F32),
+            ],
+        ),
         out_shape=jax.ShapeDtypeStruct((blocks, rows + NOTE, size), BF16),
-        scratch_shapes=[
-            pltpu.VMEM((rows, width), F32),
-            pltpu.VMEM((rows, width), F32),
-            pltpu.VMEM((8, width), F32),
-        ],
         compiler_params=pltpu.CompilerParams(
             dimension_semantics=("arbitrary", "arbitrary"), vmem_limit_bytes=32 * 1024 * 1024
         ),
         cost_estimate=pl.CostEstimate(
-            flops=8 * rows * total * width, bytes_accessed=8 * total * width, transcendentals=0
-        ),
-    )(hidden, projector, teacher)
+            flops=8 * rows * blocks * size * width, bytes_accessed=8 * blocks * size * width, transcendentals=0
+        ),
+    )(order, hidden, projector, teacher)
+
+
+def teach_kernel(role, own, other, weight, out, away):
+    out[...] = jnp.dot(own[...], weight[...], preferred_element_type=F32)
+    away[...] = jnp.dot(other[...], weight[...], preferred_element_type=F32).astype(BF16)
+
+
+def teach(role, teacher_in, weight, blocks, width):
+    _, rows, depth = teacher_in.shape
+    shape = (blocks, rows, 2 * width)
+    place = pl.BlockSpec((None, rows, width), lambda j, role: (j % blocks, 0, j // blocks))
+    return pl.pallas_call(
+        teach_kernel,
+        grid_spec=pltpu.PrefetchScalarGridSpec(
+            num_scalar_prefetch=1,
+            grid=(2 * blocks,),
+            in_specs=[
+                pl.BlockSpec((None, rows, depth), lambda j, role: (role[0], 0, 0)),
+                pl.BlockSpec((None, rows, depth), lambda j, role: (1 - role[0], 0, 0)),
+                pl.BlockSpec((depth, width), lambda j, role: (0, j)),
+            ],
+            out_specs=[place, place],
+        ),
+        out_shape=[jax.ShapeDtypeStruct(shape, F32), jax.ShapeDtypeStruct(shape, BF16)],
+        compiler_params=pltpu.CompilerParams(
+            dimension_semantics=("arbitrary",), vmem_limit_bytes=32 * 1024 * 1024
+        ),
+        cost_estimate=pl.CostEstimate(
+            flops=8 * rows * depth * blocks * width, bytes_accessed=4 * depth * blocks * width, transcendentals=0
+        ),
+    )(role, teacher_in, teacher_in, weight)
 
 
 def shards(teacher_in, teacher_weight, student_in, student_weight, projector):
@@ -165,7 +190,6 @@
     own_rows = student_in.shape[0]
     total_rows = 2 * own_rows * n_data
     out_width = teacher_weight.shape[1]
-    half = out_width // 2
     feat, hid = student_weight.shape
     wide = feat * n_data
     cols = projector.shape[1]
@@ -173,43 +197,48 @@
 
     weight = lax.all_gather(student_weight, ("role", "dp"), axis=0, tiled=True)
 
-    swap = [(d * 8 + t, t * 8 + d) for d in range(8) for t in range(8)]
+    swap = []
+    for d in range(8):
+        for t in range(8):
+            to = ((t // 2 - d // 2) % 4) * 2 + (t ^ d) % 2
+            swap.append((d * 8 + t, to * 8 + d))
     projector = lax.ppermute(projector, ("dp", "tensor"), swap)
-    projector = lax.all_gather(projector, ("role", "dp"), axis=0, tiled=True)
-    projector = projector.reshape(2, n_data, hid, cols)
-
-    away = dot(lax.dynamic_index_in_dim(teacher_in, 1 - role, 0, False), teacher_weight)
-    away = flip(away.astype(BF16))
-    teacher = dot(lax.dynamic_index_in_dim(teacher_in, role, 0, False), teacher_weight)
-    teacher = teacher + away.astype(F32)
+
+    own, away = teach(jnp.full((1,), role, jnp.int32), teacher_in, teacher_weight, n_tensor, cols)
+    away = flip(away)
     teacher = [
-        jnp.concatenate(
-            [lax.dynamic_slice_in_dim(teacher, h * half + s * cols, cols, axis=1) for h in (0, 1)],
-            axis=1,
-        )
+        lax.dynamic_index_in_dim(own, s, 0, False) + lax.dynamic_index_in_dim(away, s, 0, False).astype(F32)
         for s in model_from
     ]
     teacher = dict(zip(OFFSETS, teacher))
-    t_got = [ring_pair(teacher, k, "tensor") for k in (1, -1, 2)]
-
-    mine = lax.dynamic_slice_in_dim(student_in, role * wide, wide, axis=1)
-    theirs = flip(lax.dynamic_slice_in_dim(student_in, (1 - role) * wide, wide, axis=1))
-
-    weight, *t_near = lax.optimization_barrier((weight, teacher[0, 0], teacher[0, 1]))
-    teacher[0, 0], teacher[0, 1] = t_near
+    t_got = [ring_pair(teacher, k, "tensor") for k in (1, -1)]
+    projector = lax.all_gather(after(projector, *t_got), ("role", "dp"), axis=0, tiled=True)
+    projector = projector.reshape(2, n_data, hid, cols)
+    weight, teacher[2, 0], *t_got = lax.optimization_barrier((weight, teacher[2, 0], *t_got))
+    t_got.append(ring_pair(teacher, 2, "tensor"))
+
     pre = dot(student_in, weight)
     sigma = jax.nn.sigmoid(pre)
     hidden = (pre * sigma).astype(BF16)
-    hidden, *t_got[:2] = lax.optimization_barrier((hidden, *t_got[:2]))
     h_first = gather_start(hidden, "tensor")
     h_middle = gather_middle(hidden, h_first, "tensor")
-    h_middle[0], t_got[2], theirs = lax.optimization_barrier((h_middle[0], t_got[2], theirs))
-    hidden = place(gather_end(hidden, h_first, h_middle, "tensor"), model_from, 1)
+
+    h_middle = list(lax.optimization_barrier((*h_middle, t_got[2])))
+    t_got[2] = h_middle.pop()
+
+    student = after(student_in, *h_middle)
+    mine = lax.dynamic_slice_in_dim(student, role * wide, wide, axis=1)
+    theirs = flip(lax.dynamic_slice_in_dim(student, (1 - role) * wide, wide, axis=1))
+
+    hidden = dict(zip(OFFSETS, gather_end(hidden, h_first, h_middle, "tensor")))
+    hidden = jnp.concatenate([hidden[k, e] for k in (0, -1, 2, 1) for e in (0, 1)], axis=0)
     teacher = ring_end(teacher, t_got, "tensor")
-    hidden, teacher = lax.optimization_barrier((hidden, teacher))
+    hidden, teacher, mine, theirs = lax.optimization_barrier((hidden, teacher, mine, theirs))
     student = jnp.concatenate([mine, theirs], axis=0)
 
-    back = project(hidden, projector, teacher)
+    me = lax.axis_index("tensor")
+    order = [((((me >> 1) + b // 2) & 3) << 1) | ((me & 1) ^ (b % 2)) for b in range(n_tensor)]
+    back = project(jnp.stack(order).astype(jnp.int32), hidden, projector, teacher)
     back = lax.all_to_all(back, "tensor", 0, 0, tiled=True)
     back = jnp.sum(back.astype(F32), axis=0)
     square = join_note(back[own_rows:])

time: 294 us -> 295 us (level)
  starting transfers between devices: 54.6 us -> 24.3 us
  matrix products: 35.1 us -> 11.8 us
  Pallas kernels: 10.9 us -> 30 us
  blocking collectives: 55.1 us -> 66.5 us
  other arithmetic: 10.1 us -> 18.8 us
  local copies, waits for them, and re-layouts: 11.5 us -> 20 us
  waiting for transfers between devices: 99.9 us -> 106 us
    ppermute x10, starting transfers between devices: 48.6 us -> 17.4 us  [shift(): return lax.ppermute(value, axis, perm)]
    dot_general x4 -> x2, matrix products: 35.1 us -> 11.8 us  [dot(): return lax.dot_general(a, b, (dims, ((), ())), preferred_element_type=F32)]
    pallas_call x1 -> x2, Pallas kernels: 10.9 us -> 30 us  [the longest x1 18.9 us: teach(): pl.pallas_call(teach_kernel, grid_spec=pltpu.PrefetchScalarGridSpec(num_s...]
    all_to_all x1, blocking collectives: 55.1 us -> 66.5 us  [shards(): grad = lax.all_to_all(grad, 'dp', 0, 0, tiled=True)]
    unnamed x20 -> x33, local copies, waits for them, and re-layouts: 4.21 us -> 11.7 us
    add x0 -> x2, other arithmetic: none -> 5.83 us  [shards(): lax.dynamic_index_in_dim(own, s, 0, False)]
    ppermute x3, waiting for transfers between devices: 3.85 us -> 9.42 us  [flip(): return lax.ppermute(value, 'role', [(0, 1), (1, 0)])]
  transfers between devices with their start and end apart: 17 -> 17, of which waited for: 9 -> 11; matrix products, arithmetic and copies ran while one was open for 15% -> 11% of each run, Pallas kernels for 0% -> 6%
where the time goes in v3:
time: 295 us; the launch traced here: 294 us
  waiting for transfers between devices  106 us (36%)
  blocking collectives  66.5 us (23%)
  Pallas kernels  30 us (10%)
  starting transfers between devices  24.3 us (8%)
  local copies, waits for them, and re-layouts  20 us (7%)
  other arithmetic  18.8 us (6%)
  between operations  16.1 us (5%)
  matrix products  11.8 us (4%)
    ppermute x10, waiting for transfers between devices, shift(): return lax.ppermute(value, axis, perm)  66.6 us
    all_to_all x1, blocking collectives, shards(): grad = lax.all_to_all(grad, 'dp', 0, 0, tiled=True)  66.5 us
    all_to_all x1, waiting for transfers between devices, shards(): back = lax.all_to_all(back, 'tensor', 0, 0, tiled=True)  29.7 us
    pallas_call x1, Pallas kernels, teach(): pl.pallas_call(teach_kernel, grid_spec=pltpu.PrefetchScalarGridSpec(num_s...  18.9 us
    ppermute x10, starting transfers between devices, shift(): return lax.ppermute(value, axis, perm)  17.4 us
    dot_general x2, matrix products, dot(): return lax.dot_general(a, b, (dims, ((), ())), preferred_element_type=F32)  11.8 us
    unnamed x33, local copies, waits for them, and re-layouts  11.7 us
    pallas_call x1, Pallas kernels, project(): pl.pallas_call(project_kernel, grid_spec=pltpu.PrefetchScalarGridSpec(num...  11 us
  transfers between devices with their start and end apart: 17, of which 11 were waited for; matrix products, arithmetic and copies ran while one was open for 11% of the time, Pallas kernels for 6%

profile of v3, /device:TPU:0, one launch (start us, length us, event | category | flops | bytes accessed | tf_op | source)
XLA Modules:
  0.0 293.9 jit_solution(17349420805028349419)
XLA Ops:
  7.2 0.7 all-gather.3.cloned.1.call-update
  8.0 1.2 copy-done.2
  9.2 18.9 %shard_map.68 = (f32[8,256,1024]{2,1,0:T(8,128)S(1)}, bf16[8,256,1024]{2,1,0:T(8,128)(2,1)}) custom-call(s32[1]{0:T(128)} %bitcast.role, bf16[2,256,1024]{2,1,0:T(8,128)(2,1)S(1)} %copy-done.2, bf16[2,256,1024]{2,1,0:T(8,128)(2,1)S(1)} %copy-done.2, bf16[1024,8192]{1,0:T(8,128)(2,1)} %weight.1), custom_call_target="tpu_custom_call" | custom-call | flops 8589934592 | bytes 16777216 | tf_op jit(solution)/shard_map/pallas_call | solution.py:164
  28.1 3.3 %copy-done = f32[8,256,1024]{2,1,0:T(8,128)} copy-done((f32[8,256,1024]{2,1,0:T(8,128)}, f32[8,256,1024]{2,1,0:T(8,128)S(1)}, u32[]{:S(2)}) %copy-start) | copy-done | bytes 8388632
  31.4 7.9 %collective-permute-done = bf16[8,256,1024]{2,1,0:T(8,128)(2,1)} collective-permute-done((bf16[8,256,1024]{2,1,0:T(8,128)(2,1)}, bf16[8,256,1024]{2,1,0:T(8,128)(2,1)}, u32[]{:S(2)}, u32[]{:S(2)}) %collective-permute-start) | collective-permute-done | bytes 4194336 | tf_op jit(solution)/shard_map/ppermute | solution.py:20
  39.2 4.3 %fusion.13 = (bf16[256,1024]{1,0:T(8,128)(2,1)S(1)}, bf16[256,1024]{1,0:T(8,128)(2,1)S(1)}, bf16[256,1024]{1,0:T(8,128)(2,1)S(1)}, bf16[256,1024]{1,0:T(8,128)(2,1)S(1)}, bf16[256,1024]{1,0:T(8,128)(2,1)S(1)}) fusion(f32[8,256,1024]{2,1,0:T(8,128)} %copy-done, s32[]{:T(128)S(6)} %select_n.77, bf16[8,256,1024]{2,1,0:T(8,128)(2,1)} %collective-permute-done, ...), kind=kLoop, calls=%fused_computation.30 | loop fusion | flops 3932160 | bytes 10485780 | tf_op jit(solution)/shard_map/add | solution.py:210
  43.6 1.1 pad_maximum_fusion.1
  44.7 4.1 %collective-permute-start.1 = (bf16[512,1024]{1,0:T(8,128)(2,1)}, bf16[512,1024]{1,0:T(8,128)(2,1)S(1)}, u32[]{:S(2)}, u32[]{:S(2)}) collective-permute-start(bf16[512,1024]{1,0:T(8,128)(2,1)} %pad_maximum_fusion.1), channel_id=1, source_target_pairs={{0,6},{1,7},{2,0},{3,1},{4,2},{5,3},{6,4},{7,5},{8,14},{9,15},{10,... | collective-permute-start | bytes 3145736 | tf_op jit(solution)/shard_map/ppermute | solution.py:16
  48.8 1.0 pad_maximum_fusion.2
  49.8 0.7 collective-permute-start.12
  50.5 21.2 %collective-permute-done.1 = bf16[512,1024]{1,0:T(8,128)(2,1)S(1)} collective-permute-done((bf16[512,1024]{1,0:T(8,128)(2,1)}, bf16[512,1024]{1,0:T(8,128)(2,1)S(1)}, u32[]{:S(2)}, u32[]{:S(2)}) %collective-permute-start.1) | collective-permute-done | bytes 1048608 | tf_op jit(solution)/shard_map/ppermute | solution.py:16
  71.8 4.3 %collective-permute-done.2 = bf16[512,1024]{1,0:T(8,128)(2,1)S(1)} collective-permute-done((bf16[512,1024]{1,0:T(8,128)(2,1)}, bf16[512,1024]{1,0:T(8,128)(2,1)S(1)}, u32[]{:S(2)}, u32[]{:S(2)}) %collective-permute-start.2) | collective-permute-done | bytes 1048608 | tf_op jit(solution)/shard_map/ppermute | solution.py:16
  76.1 1.0 copy-done.5
  77.1 1.5 add_bitcast_fusion
  78.6 1.0 pad_maximum_fusion.3
  79.7 2.6 collective-permute-start.8
  82.3 7.8 %constant_dynamic-update-slice_fusion.6 = (bf16[2048,512]{1,0:T(8,128)(2,1)S(1)}, bf16[256,512]{1,0:T(8,128)(2,1)S(1)}, f32[256,512]{1,0:T(8,128)}) fusion(bf16[256,8192]{1,0:T(8,128)(2,1)} %param.7, bf16[8192,512]{1,0:T(8,128)(2,1)} %all-gather.3.cloned.1.call-done), kind=kOutput, calls=%fused_computation.56 | convolution fusion | flops 2148139008 | bytes 13631488 | tf_op jit(solution)/shard_map/dot_general | solution.py:68
  90.1 2.0 collective-permute-start.5
  92.1 1.9 collective-permute-start.3
  94.0 14.3 %collective-permute-done.4 = bf16[256,512]{1,0:T(8,128)(2,1)S(1)} collective-permute-done((bf16[256,512]{1,0:T(8,128)(2,1)S(1)}, bf16[256,512]{1,0:T(8,128)(2,1)S(1)}, u32[]{:S(2)}, u32[]{:S(2)}) %collective-permute-start.4) | collective-permute-done | bytes 262176 | tf_op jit(solution)/shard_map/ppermute | solution.py:16
  108.3 2.9 collective-permute-done.5
  111.2 0.7 copy-done.7
  111.9 1.0 pad_maximum_fusion.4
  112.9 1.8 collective-permute-start.6
  114.7 1.4 collective-permute-start.7
  116.1 9.3 %collective-permute-done.6 = bf16[384,512]{1,0:T(8,128)(2,1)} collective-permute-done((bf16[384,512]{1,0:T(8,128)(2,1)}, bf16[384,512]{1,0:T(8,128)(2,1)}, u32[]{:S(2)}, u32[]{:S(2)}) %collective-permute-start.6) | collective-permute-done | bytes 393248 | tf_op jit(solution)/shard_map/ppermute | solution.py:16
  125.5 4.8 %constant_dynamic-slice_fusion = (bf16[256,4096]{1,0:T(8,128)(2,1)}, bf16[256,4096]{1,0:T(8,128)(2,1)}) fusion(bf16[256,8192]{1,0:T(8,128)(2,1)} %param.7, s32[]{:T(128)S(6)} %select_n.81, s32[]{:T(128)S(6)} %select_n.80), kind=kLoop, calls=%fused_computation.57 | loop fusion | bytes 8388616 | tf_op jit(solution)/shard_map/dynamic_slice | solution.py:231
  130.5 1.1 slice_dynamic-update-slice_fusion.1
  131.5 0.9 fusion.20
  132.5 0.9 fusion.21
  133.4 0.7 pad_maximum_fusion.7
  134.1 3.4 %collective-permute-start.9 = (bf16[256,512]{1,0:T(8,128)(2,1)}, bf16[256,512]{1,0:T(8,128)(2,1)}, u32[]{:S(2)}, u32[]{:S(2)}) collective-permute-start(bf16[256,512]{1,0:T(8,128)(2,1)} %pad_maximum_fusion.7), channel_id=1, source_target_pairs={{0,1},{1,0},{2,3},{3,2},{4,5},{5,4},{6,7},{7,6},{8,9},{9,8},{10,11... | collective-permute-start | bytes 786440 | tf_op jit(solution)/shard_map/ppermute | solution.py:16
  137.5 2.8 fusion.5
  140.5 5.4 %collective-permute-done.9 = bf16[256,512]{1,0:T(8,128)(2,1)} collective-permute-done((bf16[256,512]{1,0:T(8,128)(2,1)}, bf16[256,512]{1,0:T(8,128)(2,1)}, u32[]{:S(2)}, u32[]{:S(2)}) %collective-permute-start.9) | collective-permute-done | bytes 262176 | tf_op jit(solution)/shard_map/ppermute | solution.py:16
  145.9 1.0 constant_dynamic-update-slice_fusion.1
  146.9 1.0 slice_dynamic-update-slice_fusion.hidden
  147.9 9.1 %collective-permute-done.10 = bf16[256,1024]{1,0:T(8,128)(2,1)} collective-permute-done((bf16[256,1024]{1,0:T(8,128)(2,1)}, bf16[256,1024]{1,0:T(8,128)(2,1)}, u32[]{:S(2)}, u32[]{:S(2)}) %collective-permute-start.10) | collective-permute-done | bytes 524320 | tf_op jit(solution)/shard_map/ppermute | solution.py:16
  157.0 2.5 fusion.8.teacher
  159.5 3.4 %copy-done.1 = bf16[8192,512]{1,0:T(8,128)(2,1)S(1)} copy-done((bf16[8192,512]{1,0:T(8,128)(2,1)S(1)}, bf16[8192,512]{1,0:T(8,128)(2,1)}, u32[]{:S(2)}) %copy-start.1) | copy-done | bytes 8388632
  162.9 11.0 %shard_map.69 = bf16[8,272,512]{2,1,0:T(8,128)(2,1)} custom-call(s32[8]{0:T(128)S(1)} %stack.35.order, bf16[2048,512]{1,0:T(8,128)(2,1)S(1)} %slice_dynamic-update-slice_fusion.hidden, bf16[2,8,512,512]{3,2,1,0:T(8,128)(2,1)S(1)} %bitcast.45, f32[256,1024]{1,0:T(8,128)S(1)} %fusion.8.teacher), custom_call_target="tpu_custom_call" | custom-call | flops 4294967296 | bytes 16777216 | tf_op jit(solution)/shard_map/pallas_call | solution.py:126
  173.9 5.9 %all-to-all-start = ((bf16[8,272,512]{2,1,0:T(8,128)(2,1)}), bf16[8,272,512]{2,1,0:T(8,128)(2,1)S(1)}, u32[]{:S(2)}, u32[]{:S(2)}) async-start(bf16[8,272,512]{2,1,0:T(8,128)(2,1)} %shard_map.69), calls=%async_computation | async-start | bytes 4456448 | tf_op jit(solution)/shard_map/all_to_all | solution.py:242
  179.8 29.7 %all-to-all-done = bf16[8,272,512]{2,1,0:T(8,128)(2,1)S(1)} async-done(((bf16[8,272,512]{2,1,0:T(8,128)(2,1)}), bf16[8,272,512]{2,1,0:T(8,128)(2,1)S(1)}, u32[]{:S(2)}, u32[]{:S(2)}) %all-to-all-start) | async-done | bytes 2228256 | tf_op jit(solution)/shard_map/all_to_all | solution.py:242
  210.5 1.5 collective-permute-done.13
  212.1 4.0 %convolution_convert_fusion = bf16[4096,512]{1,0:T(8,128)(2,1)S(1)} fusion(bf16[256,4096]{1,0:T(8,128)(2,1)} %collective-permute-done.11, bf16[256,4096]{1,0:T(8,128)(2,1)S(1)} %copy-done.3, bf16[256,512]{1,0:T(8,128)(2,1)S(1)} %slice.80, bf16[256,512]{1,0:T(8,128)(2,1)S(1)} %fusion.15), kind=kOutput, calls=%fused_computation.1 | convolution fusion | flops 2159017984 | bytes 8912896 | tf_op jit(solution)/shard_map/dot_general | solution.py:68
  216.6 66.5 %all_to_all.10 = bf16[8,528,512]{2,1,0:T(8,128)(2,1)S(1)} all-to-all(bf16[8,528,512]{2,1,0:T(8,128)(2,1)S(1)} %pad_maximum_fusion), channel_id=1, replica_groups=mesh['role'=2,'dp'=8,'tensor'=8] {'dp'}, dimensions={0} | all-to-all | bytes 8650752 | tf_op jit(solution)/shard_map/all_to_all | solution.py:255
  283.0 0.6 convert_reduce_fusion
  283.6 1.1 slice_multiply_fusion
  284.7 0.5 slice.84
  (60 shorter events, 2.1 us)
Async XLA Ops:
  7.2 71.5 %all-gather.3.cloned.1.call-start = ((), (), s32[]{:S(2)}) async-start(), calls=%async_computation.2 | async-start | bytes 8912896 | tf_op jit(solution)/shard_map/all_gather | solution.py:198
  7.9 151.6 %all-gather.5.cloned.1.call-start = ((), (), s32[]{:S(2)}) async-start(), calls=%async_computation.3 | async-start | bytes 8912896 | tf_op jit(solution)/shard_map/all_gather | solution.py:215
  7.9 1.2 copy-start.2
  28.1 3.3 %copy-start = (f32[8,256,1024]{2,1,0:T(8,128)}, f32[8,256,1024]{2,1,0:T(8,128)S(1)}, u32[]{:S(2)}) copy-start(f32[8,256,1024]{2,1,0:T(8,128)S(1)} %get-tuple-element.17) | copy-start | bytes 25165828
  31.4 7.9 %collective-permute-start = (bf16[8,256,1024]{2,1,0:T(8,128)(2,1)}, bf16[8,256,1024]{2,1,0:T(8,128)(2,1)}, u32[]{:S(2)}, u32[]{:S(2)}) collective-permute-start(bf16[8,256,1024]{2,1,0:T(8,128)(2,1)} %get-tuple-element.18), channel_id=1, source_target_pairs={{0,64},{64,0},{1,65},{65,1},{2,66},{66,2},{3,67},{67,3},{4,68},{68... | collective-permute-start | bytes 12582920 | tf_op jit(solution)/shard_map/ppermute | solution.py:20
  43.6 6.2 %copy-start.13 = (bf16[512,512]{1,0:T(8,128)(2,1)S(1)}, bf16[512,512]{1,0:T(8,128)(2,1)}, u32[]{:S(2)}) copy-start(bf16[512,512]{1,0:T(8,128)(2,1)} %param.9) | copy-start | bytes 1572868
  44.7 27.1 %collective-permute-start.1 = (bf16[512,1024]{1,0:T(8,128)(2,1)}, bf16[512,1024]{1,0:T(8,128)(2,1)S(1)}, u32[]{:S(2)}, u32[]{:S(2)}) collective-permute-start(bf16[512,1024]{1,0:T(8,128)(2,1)} %pad_maximum_fusion.1), channel_id=1, source_target_pairs={{0,6},{1,7},{2,0},{3,1},{4,2},{5,3},{6,4},{7,5},{8,14},{9,15},{10,... | collective-permute-start | bytes 3145736 | tf_op jit(solution)/shard_map/ppermute | solution.py:16
  49.8 26.3 %collective-permute-start.2 = (bf16[512,1024]{1,0:T(8,128)(2,1)}, bf16[512,1024]{1,0:T(8,128)(2,1)S(1)}, u32[]{:S(2)}, u32[]{:S(2)}) collective-permute-start(bf16[512,1024]{1,0:T(8,128)(2,1)} %pad_maximum_fusion.2), channel_id=1, source_target_pairs={{0,2},{1,3},{2,4},{3,5},{4,6},{5,7},{6,0},{7,1},{8,10},{9,11},{10,... | collective-permute-start | bytes 3145736 | tf_op jit(solution)/shard_map/ppermute | solution.py:16
  49.8 0.7 collective-permute-start.12
  50.5 25.6 %copy-start.11 = (bf16[512,512]{1,0:T(8,128)(2,1)}, bf16[512,512]{1,0:T(8,128)(2,1)S(1)}, u32[]{:S(2)}) copy-start(bf16[512,512]{1,0:T(8,128)(2,1)S(1)} %collective-permute-done.12) | copy-start | bytes 1572868
  71.8 65.7 %copy-start.4 = (bf16[512,1024]{1,0:T(8,128)(2,1)}, bf16[512,1024]{1,0:T(8,128)(2,1)S(1)}, u32[]{:S(2)}) copy-start(bf16[512,1024]{1,0:T(8,128)(2,1)S(1)} %collective-permute-done.1) | copy-start | bytes 3145732
  76.1 1.0 copy-start.5
  79.7 45.9 %collective-permute-start.8 = (bf16[512,1024]{1,0:T(8,128)(2,1)}, bf16[512,1024]{1,0:T(8,128)(2,1)}, u32[]{:S(2)}, u32[]{:S(2)}) collective-permute-start(bf16[512,1024]{1,0:T(8,128)(2,1)} %pad_maximum_fusion.3), channel_id=1, source_target_pairs={{0,4},{1,5},{2,6},{3,7},{4,0},{5,1},{6,2},{7,3},{8,12},{9,13},{10,... | collective-permute-start | bytes 3145736 | tf_op jit(solution)/shard_map/ppermute | solution.py:16
  90.1 18.2 %collective-permute-start.4 = (bf16[256,512]{1,0:T(8,128)(2,1)S(1)}, bf16[256,512]{1,0:T(8,128)(2,1)S(1)}, u32[]{:S(2)}, u32[]{:S(2)}) collective-permute-start(bf16[256,512]{1,0:T(8,128)(2,1)S(1)} %get-tuple-element.33), channel_id=1, source_target_pairs={{0,6},{1,7},{2,0},{3,1},{4,2},{5,3},{6,4},{7,5},{8,14},{9,15},{10,... | collective-permute-start | bytes 786440 | tf_op jit(solution)/shard_map/ppermute | solution.py:16
  90.1 21.1 %collective-permute-start.5 = (bf16[256,512]{1,0:T(8,128)(2,1)S(1)}, bf16[256,512]{1,0:T(8,128)(2,1)S(1)}, u32[]{:S(2)}, u32[]{:S(2)}) collective-permute-start(bf16[256,512]{1,0:T(8,128)(2,1)S(1)} %get-tuple-element.33), channel_id=1, source_target_pairs={{0,2},{1,3},{2,4},{3,5},{4,6},{5,7},{6,0},{7,1},{8,10},{9,11},{10,... | collective-permute-start | bytes 786440 | tf_op jit(solution)/shard_map/ppermute | solution.py:16
  92.1 19.8 %collective-permute-start.3 = (bf16[256,512]{1,0:T(8,128)(2,1)S(1)}, bf16[256,512]{1,0:T(8,128)(2,1)S(1)}, u32[]{:S(2)}, u32[]{:S(2)}) collective-permute-start(bf16[256,512]{1,0:T(8,128)(2,1)S(1)} %get-tuple-element.33), channel_id=1, source_target_pairs={{0,1},{1,0},{2,3},{3,2},{4,5},{5,4},{6,7},{7,6},{8,9},{9,8},{10,11... | collective-permute-start | bytes 786440 | tf_op jit(solution)/shard_map/ppermute | solution.py:16
  108.3 3.6 %copy-start.9 = (bf16[256,512]{1,0:T(8,128)(2,1)}, bf16[256,512]{1,0:T(8,128)(2,1)S(1)}, u32[]{:S(2)}) copy-start(bf16[256,512]{1,0:T(8,128)(2,1)S(1)} %collective-permute-done.4) | copy-start | bytes 786436
  111.2 0.7 copy-start.7
  112.9 12.6 %collective-permute-start.6 = (bf16[384,512]{1,0:T(8,128)(2,1)}, bf16[384,512]{1,0:T(8,128)(2,1)}, u32[]{:S(2)}, u32[]{:S(2)}) collective-permute-start(bf16[384,512]{1,0:T(8,128)(2,1)} %get-tuple-element.46), channel_id=1, source_target_pairs={{0,2},{1,3},{2,4},{3,5},{4,6},{5,7},{6,0},{7,1},{8,10},{9,11},{10,... | collective-permute-start | bytes 1179656 | tf_op jit(solution)/shard_map/ppermute | solution.py:16
  114.7 10.9 %collective-permute-start.7 = (bf16[384,512]{1,0:T(8,128)(2,1)}, bf16[384,512]{1,0:T(8,128)(2,1)}, u32[]{:S(2)}, u32[]{:S(2)}) collective-permute-start(bf16[384,512]{1,0:T(8,128)(2,1)} %get-tuple-element.45), channel_id=1, source_target_pairs={{0,6},{1,7},{2,0},{3,1},{4,2},{5,3},{6,4},{7,5},{8,14},{9,15},{10,... | collective-permute-start | bytes 1179656 | tf_op jit(solution)/shard_map/ppermute | solution.py:16
  116.1 14.3 %copy-start.10 = (bf16[256,512]{1,0:T(8,128)(2,1)S(1)}, bf16[256,512]{1,0:T(8,128)(2,1)}, u32[]{:S(2)}) copy-start(bf16[256,512]{1,0:T(8,128)(2,1)} %copy-done.9) | copy-start | bytes 786436
  130.4 7.1 %copy-start.6 = (bf16[512,1024]{1,0:T(8,128)(2,1)S(1)}, bf16[512,1024]{1,0:T(8,128)(2,1)}, u32[]{:S(2)}) copy-start(bf16[512,1024]{1,0:T(8,128)(2,1)} %copy-done.5) | copy-start | bytes 3145732
  130.4 29.1 %collective-permute-start.11 = (bf16[256,4096]{1,0:T(8,128)(2,1)}, bf16[256,4096]{1,0:T(8,128)(2,1)}, u32[]{:S(2)}, u32[]{:S(2)}) collective-permute-start(bf16[256,4096]{1,0:T(8,128)(2,1)} %get-tuple-element.39), channel_id=1, source_target_pairs={{0,64},{64,0},{1,65},{65,1},{2,66},{66,2},{3,67},{67,3},{4,68},{68... | collective-permute-start | bytes 6291464 | tf_op jit(solution)/shard_map/ppermute | solution.py:20
  134.1 12.8 %copy-start.8 = (bf16[256,512]{1,0:T(8,128)(2,1)S(1)}, bf16[256,512]{1,0:T(8,128)(2,1)}, u32[]{:S(2)}) copy-start(bf16[256,512]{1,0:T(8,128)(2,1)} %copy-done.7) | copy-start | bytes 786436
  134.1 11.8 %collective-permute-start.9 = (bf16[256,512]{1,0:T(8,128)(2,1)}, bf16[256,512]{1,0:T(8,128)(2,1)}, u32[]{:S(2)}, u32[]{:S(2)}) collective-permute-start(bf16[256,512]{1,0:T(8,128)(2,1)} %pad_maximum_fusion.7), channel_id=1, source_target_pairs={{0,1},{1,0},{2,3},{3,2},{4,5},{5,4},{6,7},{7,6},{8,9},{9,8},{10,11... | collective-permute-start | bytes 786440 | tf_op jit(solution)/shard_map/ppermute | solution.py:16
  140.2 16.8 %collective-permute-start.10 = (bf16[256,1024]{1,0:T(8,128)(2,1)}, bf16[256,1024]{1,0:T(8,128)(2,1)}, u32[]{:S(2)}, u32[]{:S(2)}) collective-permute-start(bf16[256,1024]{1,0:T(8,128)(2,1)} %fusion.5), channel_id=1, source_target_pairs={{0,1},{1,0},{2,3},{3,2},{4,5},{5,4},{6,7},{7,6},{8,9},{9,8},{10,11... | collective-permute-start | bytes 1572872 | tf_op jit(solution)/shard_map/ppermute | solution.py:16
  159.5 3.4 %copy-start.1 = (bf16[8192,512]{1,0:T(8,128)(2,1)S(1)}, bf16[8192,512]{1,0:T(8,128)(2,1)}, u32[]{:S(2)}) copy-start(bf16[8192,512]{1,0:T(8,128)(2,1)} %all-gather.5.cloned.1.call-done) | copy-start | bytes 25165828
  173.9 35.6 %all-to-all-start = ((bf16[8,272,512]{2,1,0:T(8,128)(2,1)}), bf16[8,272,512]{2,1,0:T(8,128)(2,1)S(1)}, u32[]{:S(2)}, u32[]{:S(2)}) async-start(bf16[8,272,512]{2,1,0:T(8,128)(2,1)} %shard_map.69), calls=%async_computation | async-start | bytes 4456448 | tf_op jit(solution)/shard_map/all_to_all | solution.py:242
  179.8 30.1 %copy-start.12 = (f32[256,512]{1,0:T(8,128)S(1)}, f32[256,512]{1,0:T(8,128)}, u32[]{:S(2)}) copy-start(f32[256,512]{1,0:T(8,128)} %get-tuple-element.53) | copy-start | bytes 1572868
  209.5 2.6 copy-start.3
  210.2 1.8 collective-permute-start.13
Sparse Core Ops, SparseCore 0:
  9.7 65.6 all-gather.2
  77.1 63.9 all-gather.4

commit v4 on v3

--- a/solution.py
+++ b/solution.py
@@ -48,6 +48,16 @@
     far = jnp.concatenate([up[rows:], down[rows:]], axis=0)
     other_far = shift(far, axis, 0, 1)
     return [block, other, before, nxt, far, up[:rows], down[:rows], other_far]
+
+
+def place(blocks, at, dim):
+    size = blocks[0].shape[dim]
+    shape = list(blocks[0].shape)
+    shape[dim] = 8 * size
+    out = jnp.zeros(shape, blocks[0].dtype)
+    for block, s in zip(blocks, at):
+        out = lax.dynamic_update_slice_in_dim(out, block, s * size, axis=dim)
+    return out
 
 
 def ring_pair(by, k, axis):
@@ -82,33 +92,38 @@
     return jnp.sum(note.astype(F32), axis=0, keepdims=True)
 
 
-def project_kernel(order, hidden, projector, teacher, out, low, high, square):
+def project_kernel(order, hidden, whole, own, other, teacher, out, total, square):
     step, block = pl.program_id(0), pl.program_id(1)
     n, width = out.shape[0] - NOTE, out.shape[1]
+    part = width // 2
+    parts = (whole.at[0], whole.at[1], own, other)
 
     @pl.when((step == 0) & (block == 0))
     def _():
-        low[...] = jnp.zeros_like(low)
-        high[...] = jnp.zeros_like(high)
+        first = order[order.shape[0] - 1] == 0
+        late_low, late_high = teacher[:, part:width], teacher[:, width + part :]
+        total[0] = -teacher[:, :part]
+        total[1] = -teacher[:, width : width + part]
+        total[2] = -jnp.where(first, late_low, late_high)
+        total[3] = -jnp.where(first, late_high, late_low)
 
     @pl.when(step == 0)
     def _():
-        low[...] += jnp.dot(hidden[...], projector[0], preferred_element_type=F32)
-        high[...] += jnp.dot(hidden[...], projector[1], preferred_element_type=F32)
+        for i, p in enumerate(parts):
+            total[i] += jnp.dot(hidden[...], p[...], preferred_element_type=F32)
 
     @pl.when((step == 1) & (block == 0))
     def _():
-        low[...] -= teacher[:, :width]
-        high[...] -= teacher[:, width:]
-        square[...] = jnp.broadcast_to(
-            jnp.sum(low[...] * low[...] + high[...] * high[...], keepdims=True), square.shape
+        squares = jnp.sum(total[...] * total[...], axis=0)
+        square[...] = jnp.broadcast_to(jnp.sum(squares, keepdims=True), square.shape)
+
+    @pl.when(step == 1)
+    def _():
+        dims = (((1,), (1,)), ((), ()))
+        back = sum(
+            lax.dot_general(total[i].astype(BF16), p[...], dims, preferred_element_type=F32)
+            for i, p in enumerate(parts)
         )
-
-    @pl.when(step == 1)
-    def _():
-        dims = (((1,), (1,)), ((), ()))
-        back = lax.dot_general(low[...].astype(BF16), projector[0], dims, preferred_element_type=F32)
-        back += lax.dot_general(high[...].astype(BF16), projector[1], dims, preferred_element_type=F32)
         out[:n] = back.astype(BF16)
         value = square[:1]
         row = lax.broadcasted_iota(jnp.int32, (NOTE, width), 0)
@@ -119,10 +134,14 @@
         out[n:] = note.astype(BF16)
 
 
-def project(order, hidden, projector, teacher):
-    _, blocks, size, width = projector.shape
+def project(order, hidden, whole, own, other, teacher):
+    blocks, size, part = own.shape
     rows = teacher.shape[0]
     last = blocks - 1
+
+    def at(s, b):
+        return b * (1 - s) + (last - b) * s
+
     return pl.pallas_call(
         project_kernel,
         grid_spec=pltpu.PrefetchScalarGridSpec(
@@ -130,31 +149,30 @@
             grid=(2, blocks),
             in_specs=[
                 pl.BlockSpec((rows, size), lambda s, b, order: (b * (1 - s) + last * s, 0)),
-                pl.BlockSpec(
-                    (2, None, size, width), lambda s, b, order: (0, b * (1 - s) + (last - b) * s, 0, 0)
-                ),
-                pl.BlockSpec((rows, 2 * width), lambda s, b, order: (0, 0)),
+                pl.BlockSpec((2, None, size, part), lambda s, b, order: (0, at(s, b), 0, 0)),
+                pl.BlockSpec((None, size, part), lambda s, b, order: (at(s, b), 0, 0)),
+                pl.BlockSpec((None, size, part), lambda s, b, order: (at(s, b), 0, 0)),
+                pl.BlockSpec((rows, 4 * part), lambda s, b, order: (0, 0)),
             ],
             out_specs=pl.BlockSpec((None, rows + NOTE, size), lambda s, b, order: (order[last - b * s], 0, 0)),
-            scratch_shapes=[
-                pltpu.VMEM((rows, width), F32),
-                pltpu.VMEM((rows, width), F32),
-                pltpu.VMEM((8, width), F32),
-            ],
+            scratch_shapes=[pltpu.VMEM((4, rows, part), F32), pltpu.VMEM((8, size), F32)],
         ),
         out_shape=jax.ShapeDtypeStruct((blocks, rows + NOTE, size), BF16),
         compiler_params=pltpu.CompilerParams(
             dimension_semantics=("arbitrary", "arbitrary"), vmem_limit_bytes=32 * 1024 * 1024
         ),
         cost_estimate=pl.CostEstimate(
-            flops=8 * rows * blocks * size * width, bytes_accessed=8 * blocks * size * width, transcendentals=0
-        ),
-    )(order, hidden, projector, teacher)
-
-
-def teach_kernel(role, own, other, weight, out, away):
-    out[...] = jnp.dot(own[...], weight[...], preferred_element_type=F32)
-    away[...] = jnp.dot(other[...], weight[...], preferred_element_type=F32).astype(BF16)
+            flops=16 * rows * blocks * size * part, bytes_accessed=16 * blocks * size * part, transcendentals=0
+        ),
+    )(order, hidden, whole, own, other, teacher)
+
+
+def teach_kernel(role, tokens, weight, out, away):
+    product = jnp.dot(tokens[...], weight[...], preferred_element_type=F32)
+    rows = out.shape[0]
+    first = role[0] == 0
+    out[...] = jnp.where(first, product[:rows], product[rows:])
+    away[...] = jnp.where(first, product[rows:], product[:rows]).astype(BF16)
 
 
 def teach(role, teacher_in, weight, blocks, width):
@@ -167,8 +185,7 @@
             num_scalar_prefetch=1,
             grid=(2 * blocks,),
             in_specs=[
-                pl.BlockSpec((None, rows, depth), lambda j, role: (role[0], 0, 0)),
-                pl.BlockSpec((None, rows, depth), lambda j, role: (1 - role[0], 0, 0)),
+                pl.BlockSpec((2 * rows, depth), lambda j, role: (0, 0)),
                 pl.BlockSpec((depth, width), lambda j, role: (0, j)),
             ],
             out_specs=[place, place],
@@ -180,7 +197,7 @@
         cost_estimate=pl.CostEstimate(
             flops=8 * rows * depth * blocks * width, bytes_accessed=4 * depth * blocks * width, transcendentals=0
         ),
-    )(role, teacher_in, teacher_in, weight)
+    )(role, teacher_in.reshape(2 * rows, depth), weight)
 
 
 def shards(teacher_in, teacher_weight, student_in, student_weight, projector):
@@ -205,40 +222,48 @@
     projector = lax.ppermute(projector, ("dp", "tensor"), swap)
 
     own, away = teach(jnp.full((1,), role, jnp.int32), teacher_in, teacher_weight, n_tensor, cols)
-    away = flip(away)
+    away, projector = lax.optimization_barrier((flip(away), projector))
     teacher = [
         lax.dynamic_index_in_dim(own, s, 0, False) + lax.dynamic_index_in_dim(away, s, 0, False).astype(F32)
         for s in model_from
     ]
     teacher = dict(zip(OFFSETS, teacher))
     t_got = [ring_pair(teacher, k, "tensor") for k in (1, -1)]
-    projector = lax.all_gather(after(projector, *t_got), ("role", "dp"), axis=0, tiled=True)
-    projector = projector.reshape(2, n_data, hid, cols)
+
+    part = cols // 2
+    p_ring, p_whole = lax.optimization_barrier((projector[:, part:], projector[:, :part]))
+    p_first = gather_start(p_ring, "dp")
+    p_whole = lax.all_gather(p_whole, ("role", "dp"), axis=0, tiled=True)
+    p_whole = p_whole.reshape(2, n_data, hid, part)
+
+    mine = lax.dynamic_slice_in_dim(student_in, role * wide, wide, axis=1)
+    theirs = lax.dynamic_slice_in_dim(student_in, (1 - role) * wide, wide, axis=1)
+    mine, theirs, *p_first = lax.optimization_barrier((mine, theirs, *p_first))
+    theirs = flip(theirs)
+
     weight, teacher[2, 0], *t_got = lax.optimization_barrier((weight, teacher[2, 0], *t_got))
-    t_got.append(ring_pair(teacher, 2, "tensor"))
-
+    p_middle = gather_middle(p_ring, p_first, "dp")
     pre = dot(student_in, weight)
     sigma = jax.nn.sigmoid(pre)
     hidden = (pre * sigma).astype(BF16)
+    hidden, *p_middle = lax.optimization_barrier((hidden, *p_middle))
     h_first = gather_start(hidden, "tensor")
+    t_got.append(ring_pair(teacher, 2, "tensor"))
     h_middle = gather_middle(hidden, h_first, "tensor")
-
-    h_middle = list(lax.optimization_barrier((*h_middle, t_got[2])))
-    t_got[2] = h_middle.pop()
-
-    student = after(student_in, *h_middle)
-    mine = lax.dynamic_slice_in_dim(student, role * wide, wide, axis=1)
-    theirs = flip(lax.dynamic_slice_in_dim(student, (1 - role) * wide, wide, axis=1))
+    p_own = place(gather_end(p_ring, p_first, p_middle, "dp"), sources("dp"), 0)
+    p_other = flip(p_own)
 
     hidden = dict(zip(OFFSETS, gather_end(hidden, h_first, h_middle, "tensor")))
     hidden = jnp.concatenate([hidden[k, e] for k in (0, -1, 2, 1) for e in (0, 1)], axis=0)
     teacher = ring_end(teacher, t_got, "tensor")
-    hidden, teacher, mine, theirs = lax.optimization_barrier((hidden, teacher, mine, theirs))
+    hidden, teacher, p_own, p_other, theirs = lax.optimization_barrier((hidden, teacher, p_own, p_other, theirs))
     student = jnp.concatenate([mine, theirs], axis=0)
 
     me = lax.axis_index("tensor")
     order = [((((me >> 1) + b // 2) & 3) << 1) | ((me & 1) ^ (b % 2)) for b in range(n_tensor)]
-    back = project(jnp.stack(order).astype(jnp.int32), hidden, projector, teacher)
+    order = jnp.stack(order + [role]).astype(jnp.int32)
+    p_own, p_other = p_own.reshape(n_data, hid, part), p_other.reshape(n_data, hid, part)
+    back = project(order, hidden, p_whole, p_own, p_other, teacher)
     back = lax.all_to_all(back, "tensor", 0, 0, tiled=True)
     back = jnp.sum(back.astype(F32), axis=0)
     square = join_note(back[own_rows:])

time: 295 us -> 302 us (1.024)
  starting transfers between devices: 24.3 us -> 54.3 us
  waiting for transfers between devices: 106 us -> 87.8 us
  blocking collectives: 66.5 us -> 54.3 us
  local copies, waits for them, and re-layouts: 20 us -> 26.8 us
    ppermute x10 -> x16, starting transfers between devices: 17.4 us -> 49.8 us  [shift(): return lax.ppermute(value, axis, perm)]
    ppermute x10 -> x16, waiting for transfers between devices: 66.6 us -> 51.9 us  [shift(): return lax.ppermute(value, axis, perm)]
    all_to_all x1, blocking collectives: 66.5 us -> 54.3 us  [shards(): grad = lax.all_to_all(grad, 'dp', 0, 0, tiled=True)]
    dynamic_update_slice x0 -> x7, local copies, waits for them, and re-layouts: none -> 4.91 us  [place(): out = lax.dynamic_update_slice_in_dim(out, block, s * size, axis=dim)]
    pallas_call x1, Pallas kernels: 11 us -> 14.3 us  [project(): pl.pallas_call(project_kernel, grid_spec=pltpu.PrefetchScalarGridSpec(num...]
    ppermute x3 -> x4, waiting for transfers between devices: 9.42 us -> 8.24 us  [flip(): return lax.ppermute(value, 'role', [(0, 1), (1, 0)])]
    unnamed x33 -> x20, local copies, waits for them, and re-layouts: 11.7 us -> 12 us
  transfers between devices with their start and end apart: 17 -> 24, of which waited for: 11 -> 10; matrix products, arithmetic and copies ran while one was open for 11% -> 14% of each run, Pallas kernels for 6% -> 6%
where the time goes in v4:
time: 302 us; the launch traced here: 301 us
  waiting for transfers between devices  87.8 us (29%)
  starting transfers between devices  54.3 us (18%)
  blocking collectives  54.3 us (18%)
  Pallas kernels  31.9 us (11%)
  local copies, waits for them, and re-layouts  26.8 us (9%)
  other arithmetic  17.4 us (6%)
  between operations  16.2 us (5%)
  matrix products  11.9 us (4%)
    all_to_all x1, blocking collectives, shards(): grad = lax.all_to_all(grad, 'dp', 0, 0, tiled=True)  54.3 us
    ppermute x16, waiting for transfers between devices, shift(): return lax.ppermute(value, axis, perm)  51.9 us
    ppermute x16, starting transfers between devices, shift(): return lax.ppermute(value, axis, perm)  49.8 us
    all_to_all x1, waiting for transfers between devices, shards(): back = lax.all_to_all(back, 'tensor', 0, 0, tiled=True)  26.9 us
    pallas_call x1, Pallas kernels, teach(): pl.pallas_call(teach_kernel, grid_spec=pltpu.PrefetchScalarGridSpec(num_s...  17.6 us
    pallas_call x1, Pallas kernels, project(): pl.pallas_call(project_kernel, grid_spec=pltpu.PrefetchScalarGridSpec(num...  14.3 us
    unnamed x20, local copies, waits for them, and re-layouts  12 us
    dot_general x2, matrix products, dot(): return lax.dot_general(a, b, (dims, ((), ())), preferred_element_type=F32)  11.9 us
  transfers between devices with their start and end apart: 24, of which 10 were waited for; matrix products, arithmetic and copies ran while one was open for 14% of the time, Pallas kernels for 6%

profile of v4, /device:TPU:0, one launch (start us, length us, event | category | flops | bytes accessed | tf_op | source)
XLA Modules:
  0.0 300.6 jit_solution(6610346489786174324)
XLA Ops:
  8.0 1.2 copy-done.2
  9.2 17.6 %shard_map.68 = (f32[8,256,1024]{2,1,0:T(8,128)S(1)}, bf16[8,256,1024]{2,1,0:T(8,128)(2,1)S(1)}) custom-call(s32[1]{0:T(128)} %bitcast.role, bf16[512,1024]{1,0:T(8,128)(2,1)S(1)} %bitcast.50, bf16[1024,8192]{1,0:T(8,128)(2,1)} %weight.1), custom_call_target="tpu_custom_call" | custom-call | flops 8589934592 | bytes 16777216 | tf_op jit(solution)/shard_map/pallas_call | solution.py:182
  26.8 3.3 %copy-done = f32[8,256,1024]{2,1,0:T(8,128)} copy-done((f32[8,256,1024]{2,1,0:T(8,128)}, f32[8,256,1024]{2,1,0:T(8,128)S(1)}, u32[]{:S(2)}) %copy-start) | copy-done | bytes 8388632
  30.8 6.7 %collective-permute-done = bf16[8,256,1024]{2,1,0:T(8,128)(2,1)} collective-permute-done((bf16[8,256,1024]{2,1,0:T(8,128)(2,1)S(1)}, bf16[8,256,1024]{2,1,0:T(8,128)(2,1)}, u32[]{:S(2)}, u32[]{:S(2)}) %collective-permute-start) | collective-permute-done | bytes 4194336 | tf_op jit(solution)/shard_map/ppermute | solution.py:20
  38.4 19.1 %collective-permute-start.2 = (bf16[512,256]{1,0:T(8,128)(2,1)}, bf16[512,256]{1,0:T(8,128)(2,1)S(1)}, u32[]{:S(2)}, u32[]{:S(2)}) collective-permute-start(bf16[512,256]{1,0:T(8,128)(2,1)} %get-tuple-element.27), channel_id=1, source_target_pairs={{0,8},{8,0},{16,24},{24,16},{32,40},{40,32},{48,56},{56,48},{1,9},... | collective-permute-start | bytes 786440 | tf_op jit(solution)/shard_map/ppermute | solution.py:16
  57.5 4.2 %collective-permute-start.3 = (bf16[512,256]{1,0:T(8,128)(2,1)}, bf16[512,256]{1,0:T(8,128)(2,1)}, u32[]{:S(2)}, u32[]{:S(2)}) collective-permute-start(bf16[512,256]{1,0:T(8,128)(2,1)} %get-tuple-element.27), channel_id=1, source_target_pairs={{0,16},{8,24},{16,32},{24,40},{32,48},{40,56},{48,0},{56,8},{1,17}... | collective-permute-start | bytes 786440 | tf_op jit(solution)/shard_map/ppermute | solution.py:16
  61.7 5.5 %collective-permute-start.4 = (bf16[512,256]{1,0:T(8,128)(2,1)}, bf16[512,256]{1,0:T(8,128)(2,1)}, u32[]{:S(2)}, u32[]{:S(2)}) collective-permute-start(bf16[512,256]{1,0:T(8,128)(2,1)} %get-tuple-element.27), channel_id=1, source_target_pairs={{0,48},{8,56},{16,0},{24,8},{32,16},{40,24},{48,32},{56,40},{1,49}... | collective-permute-start | bytes 786440 | tf_op jit(solution)/shard_map/ppermute | solution.py:16
  67.2 4.3 %fusion.13 = (bf16[256,1024]{1,0:T(8,128)(2,1)S(1)}, bf16[256,1024]{1,0:T(8,128)(2,1)S(1)}, bf16[256,1024]{1,0:T(8,128)(2,1)S(1)}, bf16[256,1024]{1,0:T(8,128)(2,1)S(1)}, bf16[256,1024]{1,0:T(8,128)(2,1)S(1)}) fusion(f32[8,256,1024]{2,1,0:T(8,128)} %copy-done, s32[]{:T(128)S(6)} %select_n.104, bf16[8,256,1024]{2,1,0:T(8,128)(2,1)} %collective-permute-done, ...), kind=kLoop, calls=%fused_computation.30 | loop fusion | flops 3932160 | bytes 10485780 | tf_op jit(solution)/shard_map/add | solution.py:227
  71.6 1.1 pad_maximum_fusion.1
  73.5 1.0 pad_maximum_fusion.2
  74.6 1.1 collective-permute-start.6
  75.7 2.5 constant_dynamic-slice_fusion
  78.4 1.0 constant_dynamic-update-slice_fusion.10
  79.4 1.5 add_bitcast_fusion
  80.9 0.9 slice.84
  81.8 0.9 slice.83
  82.7 0.9 pad_maximum_fusion.4
  83.7 0.9 collective-permute-start.7
  84.6 2.3 collective-permute-start.8
  86.9 1.0 constant_dynamic-update-slice_fusion.8
  87.9 1.0 constant_dynamic-update-slice_fusion.7
  88.9 8.2 %collective-permute-done.5 = bf16[512,1024]{1,0:T(8,128)(2,1)} collective-permute-done((bf16[512,1024]{1,0:T(8,128)(2,1)}, bf16[512,1024]{1,0:T(8,128)(2,1)}, u32[]{:S(2)}, u32[]{:S(2)}) %collective-permute-start.5) | collective-permute-done | bytes 1048608 | tf_op jit(solution)/shard_map/ppermute | solution.py:16
  97.1 3.1 %collective-permute-done.6 = bf16[512,1024]{1,0:T(8,128)(2,1)} collective-permute-done((bf16[512,1024]{1,0:T(8,128)(2,1)}, bf16[512,1024]{1,0:T(8,128)(2,1)}, u32[]{:S(2)}, u32[]{:S(2)}) %collective-permute-start.6) | collective-permute-done | bytes 1048608 | tf_op jit(solution)/shard_map/ppermute | solution.py:16
  100.2 7.9 %multiply_convert_fusion = (bf16[256,512]{1,0:T(8,128)(2,1)S(1)}, f32[256,512]{1,0:T(8,128)}) fusion(bf16[256,8192]{1,0:T(8,128)(2,1)} %param.7, bf16[8192,512]{1,0:T(8,128)(2,1)} %all-gather.3.cloned.1.call-done), kind=kOutput, calls=%fused_computation.37 | convolution fusion | flops 2148139008 | bytes 13369344 | tf_op jit(solution)/shard_map/dot_general | solution.py:78
  108.1 6.4 %collective-permute-start.9 = (bf16[256,512]{1,0:T(8,128)(2,1)S(1)}, bf16[256,512]{1,0:T(8,128)(2,1)S(1)}, u32[]{:S(2)}, u32[]{:S(2)}) collective-permute-start(bf16[256,512]{1,0:T(8,128)(2,1)S(1)} %get-tuple-element.35), channel_id=1, source_target_pairs={{0,1},{1,0},{2,3},{3,2},{4,5},{5,4},{6,7},{7,6},{8,9},{9,8},{10,11... | collective-permute-start | bytes 786440 | tf_op jit(solution)/shard_map/ppermute | solution.py:16
  114.6 3.2 %collective-permute-start.10 = (bf16[256,512]{1,0:T(8,128)(2,1)S(1)}, bf16[256,512]{1,0:T(8,128)(2,1)S(1)}, u32[]{:S(2)}, u32[]{:S(2)}) collective-permute-start(bf16[256,512]{1,0:T(8,128)(2,1)S(1)} %get-tuple-element.35), channel_id=1, source_target_pairs={{0,6},{1,7},{2,0},{3,1},{4,2},{5,3},{6,4},{7,5},{8,14},{9,15},{10,... | collective-permute-start | bytes 786440 | tf_op jit(solution)/shard_map/ppermute | solution.py:16
  118.0 0.9 slice.98
  118.9 0.9 slice.97
  120.6 1.0 slice_dynamic-update-slice_fusion.3
  121.6 25.0 %collective-permute-done.12 = bf16[256,512]{1,0:T(8,128)(2,1)S(1)} collective-permute-done((bf16[256,512]{1,0:T(8,128)(2,1)S(1)}, bf16[256,512]{1,0:T(8,128)(2,1)S(1)}, u32[]{:S(2)}, u32[]{:S(2)}) %collective-permute-start.12) | collective-permute-done | bytes 262176 | tf_op jit(solution)/shard_map/ppermute | solution.py:16
  146.7 1.3 collective-permute-start.11
  148.0 1.0 slice_dynamic-update-slice_fusion.2
  149.8 3.1 %collective-permute-done.17 = bf16[512,256]{1,0:T(8,128)(2,1)S(1)} collective-permute-done((bf16[512,256]{1,0:T(8,128)(2,1)S(1)}, bf16[512,256]{1,0:T(8,128)(2,1)S(1)}, u32[]{:S(2)}, u32[]{:S(2)}) %collective-permute-start.17) | collective-permute-done | bytes 262176 | tf_op jit(solution)/shard_map/ppermute | solution.py:16
  155.2 2.8 collective-permute-done.13
  160.5 2.3 fusion.5
  162.8 3.4 %collective-permute-start.16 = (bf16[256,1024]{1,0:T(8,128)(2,1)S(1)}, bf16[256,1024]{1,0:T(8,128)(2,1)}, u32[]{:S(2)}, u32[]{:S(2)}) collective-permute-start(bf16[256,1024]{1,0:T(8,128)(2,1)S(1)} %fusion.5), channel_id=1, source_target_pairs={{0,1},{1,0},{2,3},{3,2},{4,5},{5,4},{6,7},{7,6},{8,9},{9,8},{10,11... | collective-permute-start | bytes 1572872 | tf_op jit(solution)/shard_map/ppermute | solution.py:16
  166.2 4.9 %collective-permute-done.14 = bf16[256,512]{1,0:T(8,128)(2,1)} collective-permute-done((bf16[256,512]{1,0:T(8,128)(2,1)}, bf16[256,512]{1,0:T(8,128)(2,1)}, u32[]{:S(2)}, u32[]{:S(2)}) %collective-permute-start.14) | collective-permute-done | bytes 262176 | tf_op jit(solution)/shard_map/ppermute | solution.py:16
  171.2 1.7 constant_dynamic-update-slice_fusion.1
  174.3 4.8 %collective-permute-done.16 = bf16[256,1024]{1,0:T(8,128)(2,1)} collective-permute-done((bf16[256,1024]{1,0:T(8,128)(2,1)S(1)}, bf16[256,1024]{1,0:T(8,128)(2,1)}, u32[]{:S(2)}, u32[]{:S(2)}) %collective-permute-start.16) | collective-permute-done | bytes 524320 | tf_op jit(solution)/shard_map/ppermute | solution.py:16
  179.0 2.5 fusion.8.teacher
  181.6 2.2 copy-done.1
  183.7 14.3 %shard_map.69 = bf16[8,272,512]{2,1,0:T(8,128)(2,1)} custom-call(s32[9]{0:T(128)S(1)} %stack.36.order, bf16[2048,512]{1,0:T(8,128)(2,1)} %slice_dynamic-update-slice_fusion.hidden, bf16[2,8,512,256]{3,2,1,0:T(8,128)(2,1)S(1)} %bitcast.49, bf16[8,512,256]{2,1,0:T(8,128)(2,1)S(1)} %bitcast.48, bf16[8,512,256]{2,1,0:T(8,128)(2,1)} %bitcast.21.other, ...), custom_call_target="tpu_custom_call" | custom-call | flops 4294967296 | bytes 16777216 | tf_op jit(solution)/shard_map/pallas_call | solution.py:145
  198.1 3.6 %all-to-all-start = ((bf16[8,272,512]{2,1,0:T(8,128)(2,1)}), bf16[8,272,512]{2,1,0:T(8,128)(2,1)S(1)}, u32[]{:S(2)}, u32[]{:S(2)}) async-start(bf16[8,272,512]{2,1,0:T(8,128)(2,1)} %shard_map.69), calls=%async_computation | async-start | bytes 4456448 | tf_op jit(solution)/shard_map/all_to_all | solution.py:267
  201.7 26.9 %all-to-all-done = bf16[8,272,512]{2,1,0:T(8,128)(2,1)S(1)} async-done(((bf16[8,272,512]{2,1,0:T(8,128)(2,1)}), bf16[8,272,512]{2,1,0:T(8,128)(2,1)S(1)}, u32[]{:S(2)}, u32[]{:S(2)}) %all-to-all-start) | async-done | bytes 2228256 | tf_op jit(solution)/shard_map/all_to_all | solution.py:267
  229.4 1.5 collective-permute-done.20
  231.1 4.0 %convolution_convert_fusion = bf16[4096,512]{1,0:T(8,128)(2,1)S(1)} fusion(bf16[256,4096]{1,0:T(8,128)(2,1)} %collective-permute-done.19, bf16[256,4096]{1,0:T(8,128)(2,1)S(1)} %copy-done.4, bf16[256,512]{1,0:T(8,128)(2,1)S(1)} %slice.118, bf16[256,512]{1,0:T(8,128)(2,1)S(1)} %fusion.15), kind=kOutput, calls=%fused_computation.1 | convolution fusion | flops 2159017984 | bytes 8912896 | tf_op jit(solution)/shard_map/dot_general | solution.py:78
  235.5 54.3 %all_to_all.10 = bf16[8,528,512]{2,1,0:T(8,128)(2,1)S(1)} all-to-all(bf16[8,528,512]{2,1,0:T(8,128)(2,1)S(1)} %pad_maximum_fusion), channel_id=1, replica_groups=mesh['role'=2,'dp'=8,'tensor'=8] {'dp'}, dimensions={0} | all-to-all | bytes 8650752 | tf_op jit(solution)/shard_map/all_to_all | solution.py:280
  290.4 1.1 slice_multiply_fusion
  (76 shorter events, 14.0 us)
Async XLA Ops:
  7.2 93.0 %all-gather.3.cloned.1.call-start = ((), (), s32[]{:S(2)}) async-start(), calls=%async_computation.2 | async-start | bytes 8912896 | tf_op jit(solution)/shard_map/all_gather | solution.py:215
  7.9 173.7 %all-gather.5.cloned.1.call-start = ((), (), s32[]{:S(2)}) async-start(), calls=%async_computation.3 | async-start | bytes 4456448 | tf_op jit(solution)/shard_map/all_gather | solution.py:236
  7.9 1.2 copy-start.2
  9.2 20.9 %copy-start.6 = (bf16[512,512]{1,0:T(8,128)(2,1)S(1)}, bf16[512,512]{1,0:T(8,128)(2,1)}, u32[]{:S(2)}) copy-start(bf16[512,512]{1,0:T(8,128)(2,1)} %param.9) | copy-start | bytes 1572868
  26.8 3.3 %copy-start = (f32[8,256,1024]{2,1,0:T(8,128)}, f32[8,256,1024]{2,1,0:T(8,128)S(1)}, u32[]{:S(2)}) copy-start(f32[8,256,1024]{2,1,0:T(8,128)S(1)} %get-tuple-element.29) | copy-start | bytes 25165828
  30.1 7.4 %collective-permute-start = (bf16[8,256,1024]{2,1,0:T(8,128)(2,1)S(1)}, bf16[8,256,1024]{2,1,0:T(8,128)(2,1)}, u32[]{:S(2)}, u32[]{:S(2)}) collective-permute-start(bf16[8,256,1024]{2,1,0:T(8,128)(2,1)S(1)} %get-tuple-element.25), channel_id=1, source_target_pairs={{0,64},{64,0},{1,65},{65,1},{2,66},{66,2},{3,67},{67,3},{4,68},{68... | collective-permute-start | bytes 12582920 | tf_op jit(solution)/shard_map/ppermute | solution.py:20
  30.1 0.7 collective-permute-start.1
  38.4 42.5 %collective-permute-start.2 = (bf16[512,256]{1,0:T(8,128)(2,1)}, bf16[512,256]{1,0:T(8,128)(2,1)S(1)}, u32[]{:S(2)}, u32[]{:S(2)}) collective-permute-start(bf16[512,256]{1,0:T(8,128)(2,1)} %get-tuple-element.27), channel_id=1, source_target_pairs={{0,8},{8,0},{16,24},{24,16},{32,40},{40,32},{48,56},{56,48},{1,9},... | collective-permute-start | bytes 786440 | tf_op jit(solution)/shard_map/ppermute | solution.py:16
  57.5 23.3 %collective-permute-start.3 = (bf16[512,256]{1,0:T(8,128)(2,1)}, bf16[512,256]{1,0:T(8,128)(2,1)}, u32[]{:S(2)}, u32[]{:S(2)}) collective-permute-start(bf16[512,256]{1,0:T(8,128)(2,1)} %get-tuple-element.27), channel_id=1, source_target_pairs={{0,16},{8,24},{16,32},{24,40},{32,48},{40,56},{48,0},{56,8},{1,17}... | collective-permute-start | bytes 786440 | tf_op jit(solution)/shard_map/ppermute | solution.py:16
  61.7 19.2 %collective-permute-start.4 = (bf16[512,256]{1,0:T(8,128)(2,1)}, bf16[512,256]{1,0:T(8,128)(2,1)}, u32[]{:S(2)}, u32[]{:S(2)}) collective-permute-start(bf16[512,256]{1,0:T(8,128)(2,1)} %get-tuple-element.27), channel_id=1, source_target_pairs={{0,48},{8,56},{16,0},{24,8},{32,16},{40,24},{48,32},{56,40},{1,49}... | collective-permute-start | bytes 786440 | tf_op jit(solution)/shard_map/ppermute | solution.py:16
  71.6 4.1 %copy-start.3 = (bf16[256,8192]{1,0:T(8,128)(2,1)S(1)}, bf16[256,8192]{1,0:T(8,128)(2,1)}, u32[]{:S(2)}) copy-start(bf16[256,8192]{1,0:T(8,128)(2,1)} %param.7) | copy-start | bytes 12582916
  72.6 24.5 %collective-permute-start.5 = (bf16[512,1024]{1,0:T(8,128)(2,1)}, bf16[512,1024]{1,0:T(8,128)(2,1)}, u32[]{:S(2)}, u32[]{:S(2)}) collective-permute-start(bf16[512,1024]{1,0:T(8,128)(2,1)} %pad_maximum_fusion.1), channel_id=1, source_target_pairs={{0,6},{1,7},{2,0},{3,1},{4,2},{5,3},{6,4},{7,5},{8,14},{9,15},{10,... | collective-permute-start | bytes 3145736 | tf_op jit(solution)/shard_map/ppermute | solution.py:16
  74.6 25.6 %collective-permute-start.6 = (bf16[512,1024]{1,0:T(8,128)(2,1)}, bf16[512,1024]{1,0:T(8,128)(2,1)}, u32[]{:S(2)}, u32[]{:S(2)}) collective-permute-start(bf16[512,1024]{1,0:T(8,128)(2,1)} %pad_maximum_fusion.2), channel_id=1, source_target_pairs={{0,2},{1,3},{2,4},{3,5},{4,6},{5,7},{6,0},{7,1},{8,10},{9,11},{10,... | collective-permute-start | bytes 3145736 | tf_op jit(solution)/shard_map/ppermute | solution.py:16
  83.7 24.5 %collective-permute-start.7 = (bf16[768,256]{1,0:T(8,128)(2,1)}, bf16[768,256]{1,0:T(8,128)(2,1)}, u32[]{:S(2)}, u32[]{:S(2)}) collective-permute-start(bf16[768,256]{1,0:T(8,128)(2,1)} %get-tuple-element.66), channel_id=1, source_target_pairs={{0,16},{8,24},{16,32},{24,40},{32,48},{40,56},{48,0},{56,8},{1,17}... | collective-permute-start | bytes 1179656 | tf_op jit(solution)/shard_map/ppermute | solution.py:16
  84.6 23.5 %collective-permute-start.8 = (bf16[768,256]{1,0:T(8,128)(2,1)}, bf16[768,256]{1,0:T(8,128)(2,1)}, u32[]{:S(2)}, u32[]{:S(2)}) collective-permute-start(bf16[768,256]{1,0:T(8,128)(2,1)} %get-tuple-element.65), channel_id=1, source_target_pairs={{0,48},{8,56},{16,0},{24,8},{32,16},{40,24},{48,32},{56,40},{1,49}... | collective-permute-start | bytes 1179656 | tf_op jit(solution)/shard_map/ppermute | solution.py:16
  86.9 94.6 %collective-permute-start.19 = (bf16[256,4096]{1,0:T(8,128)(2,1)}, bf16[256,4096]{1,0:T(8,128)(2,1)}, u32[]{:S(2)}, u32[]{:S(2)}) collective-permute-start(bf16[256,4096]{1,0:T(8,128)(2,1)} %get-tuple-element.41), channel_id=1, source_target_pairs={{0,64},{64,0},{1,65},{65,1},{2,66},{66,2},{3,67},{67,3},{4,68},{68... | collective-permute-start | bytes 6291464 | tf_op jit(solution)/shard_map/ppermute | solution.py:20
  108.1 38.4 %collective-permute-start.9 = (bf16[256,512]{1,0:T(8,128)(2,1)S(1)}, bf16[256,512]{1,0:T(8,128)(2,1)S(1)}, u32[]{:S(2)}, u32[]{:S(2)}) collective-permute-start(bf16[256,512]{1,0:T(8,128)(2,1)S(1)} %get-tuple-element.35), channel_id=1, source_target_pairs={{0,1},{1,0},{2,3},{3,2},{4,5},{5,4},{6,7},{7,6},{8,9},{9,8},{10,11... | collective-permute-start | bytes 786440 | tf_op jit(solution)/shard_map/ppermute | solution.py:16
  114.6 32.0 %collective-permute-start.12 = (bf16[256,512]{1,0:T(8,128)(2,1)S(1)}, bf16[256,512]{1,0:T(8,128)(2,1)S(1)}, u32[]{:S(2)}, u32[]{:S(2)}) collective-permute-start(bf16[256,512]{1,0:T(8,128)(2,1)S(1)} %get-tuple-element.35), channel_id=1, source_target_pairs={{0,2},{1,3},{2,4},{3,5},{4,6},{5,7},{6,0},{7,1},{8,10},{9,11},{10,... | collective-permute-start | bytes 786440 | tf_op jit(solution)/shard_map/ppermute | solution.py:16
  114.6 32.0 %collective-permute-start.10 = (bf16[256,512]{1,0:T(8,128)(2,1)S(1)}, bf16[256,512]{1,0:T(8,128)(2,1)S(1)}, u32[]{:S(2)}, u32[]{:S(2)}) collective-permute-start(bf16[256,512]{1,0:T(8,128)(2,1)S(1)} %get-tuple-element.35), channel_id=1, source_target_pairs={{0,6},{1,7},{2,0},{3,1},{4,2},{5,3},{6,4},{7,5},{8,14},{9,15},{10,... | collective-permute-start | bytes 786440 | tf_op jit(solution)/shard_map/ppermute | solution.py:16
  117.9 42.6 %collective-permute-start.15 = (bf16[512,1024]{1,0:T(8,128)(2,1)S(1)}, bf16[512,1024]{1,0:T(8,128)(2,1)}, u32[]{:S(2)}, u32[]{:S(2)}) collective-permute-start(bf16[512,1024]{1,0:T(8,128)(2,1)S(1)} %pad_maximum_fusion.3), channel_id=1, source_target_pairs={{0,4},{1,5},{2,6},{3,7},{4,0},{5,1},{6,2},{7,3},{8,12},{9,13},{10,... | collective-permute-start | bytes 3145736 | tf_op jit(solution)/shard_map/ppermute | solution.py:16
  146.5 6.4 %collective-permute-start.17 = (bf16[512,256]{1,0:T(8,128)(2,1)S(1)}, bf16[512,256]{1,0:T(8,128)(2,1)S(1)}, u32[]{:S(2)}, u32[]{:S(2)}) collective-permute-start(bf16[512,256]{1,0:T(8,128)(2,1)S(1)} %get-tuple-element.61), channel_id=1, source_target_pairs={{0,8},{8,0},{16,24},{24,16},{32,40},{40,32},{48,56},{56,48},{1,9},... | collective-permute-start | bytes 786440 | tf_op jit(solution)/shard_map/ppermute | solution.py:16
  146.7 7.8 %collective-permute-start.11 = (bf16[384,512]{1,0:T(8,128)(2,1)S(1)}, bf16[384,512]{1,0:T(8,128)(2,1)S(1)}, u32[]{:S(2)}, u32[]{:S(2)}) collective-permute-start(bf16[384,512]{1,0:T(8,128)(2,1)S(1)} %get-tuple-element.64), channel_id=1, source_target_pairs={{0,6},{1,7},{2,0},{3,1},{4,2},{5,3},{6,4},{7,5},{8,14},{9,15},{10,... | collective-permute-start | bytes 1179656 | tf_op jit(solution)/shard_map/ppermute | solution.py:16
  149.0 9.1 %collective-permute-start.13 = (bf16[384,512]{1,0:T(8,128)(2,1)S(1)}, bf16[384,512]{1,0:T(8,128)(2,1)S(1)}, u32[]{:S(2)}, u32[]{:S(2)}) collective-permute-start(bf16[384,512]{1,0:T(8,128)(2,1)S(1)} %get-tuple-element.63), channel_id=1, source_target_pairs={{0,2},{1,3},{2,4},{3,5},{4,6},{5,7},{6,0},{7,1},{8,10},{9,11},{10,... | collective-permute-start | bytes 1179656 | tf_op jit(solution)/shard_map/ppermute | solution.py:16
  152.9 28.6 %collective-permute-start.18 = (bf16[4096,256]{1,0:T(8,128)(2,1)S(1)}, bf16[4096,256]{1,0:T(8,128)(2,1)}, u32[]{:S(2)}, u32[]{:S(2)}) collective-permute-start(bf16[4096,256]{1,0:T(8,128)(2,1)S(1)} %constant_dynamic-update-slice_fusion.11), channel_id=1, source_target_pairs={{0,64},{64,0},{1,65},{65,1},{2,66},{66,2},{3,67},{67,3},{4,68},{68... | collective-permute-start | bytes 6291464 | tf_op jit(solution)/shard_map/ppermute | solution.py:20
  160.1 11.1 %collective-permute-start.14 = (bf16[256,512]{1,0:T(8,128)(2,1)}, bf16[256,512]{1,0:T(8,128)(2,1)}, u32[]{:S(2)}, u32[]{:S(2)}) collective-permute-start(bf16[256,512]{1,0:T(8,128)(2,1)} %pad_maximum_fusion.9), channel_id=1, source_target_pairs={{0,1},{1,0},{2,3},{3,2},{4,5},{5,4},{6,7},{7,6},{8,9},{9,8},{10,11... | collective-permute-start | bytes 786440 | tf_op jit(solution)/shard_map/ppermute | solution.py:16
  162.8 16.3 %collective-permute-start.16 = (bf16[256,1024]{1,0:T(8,128)(2,1)S(1)}, bf16[256,1024]{1,0:T(8,128)(2,1)}, u32[]{:S(2)}, u32[]{:S(2)}) collective-permute-start(bf16[256,1024]{1,0:T(8,128)(2,1)S(1)} %fusion.5), channel_id=1, source_target_pairs={{0,1},{1,0},{2,3},{3,2},{4,5},{5,4},{6,7},{7,6},{8,9},{9,8},{10,11... | collective-permute-start | bytes 1572872 | tf_op jit(solution)/shard_map/ppermute | solution.py:16
  181.6 2.2 copy-start.1
  198.1 30.6 %all-to-all-start = ((bf16[8,272,512]{2,1,0:T(8,128)(2,1)}), bf16[8,272,512]{2,1,0:T(8,128)(2,1)S(1)}, u32[]{:S(2)}, u32[]{:S(2)}) async-start(bf16[8,272,512]{2,1,0:T(8,128)(2,1)} %shard_map.69), calls=%async_computation | async-start | bytes 4456448 | tf_op jit(solution)/shard_map/all_to_all | solution.py:267
  201.7 27.3 %copy-start.5 = (f32[256,512]{1,0:T(8,128)S(1)}, f32[256,512]{1,0:T(8,128)}, u32[]{:S(2)}) copy-start(f32[256,512]{1,0:T(8,128)} %get-tuple-element.74) | copy-start | bytes 1572868
  228.6 2.5 copy-start.4
  229.3 1.6 collective-permute-start.20
Sparse Core Ops, SparseCore 0:
  9.7 71.3 all-gather.2
  82.9 41.1 all-gather.4

commit v5 on v4

v5 whole, which is shorter than its diff:
```python
import jax
import jax.numpy as jnp
from jax import lax
from jax.experimental import pallas as pl
from jax.experimental.pallas import tpu as pltpu
from jax.sharding import PartitionSpec as P

BF16 = jnp.bfloat16
F32 = jnp.float32
NOTE = 16
OFFSETS = ((0, 0), (0, 1), (1, 0), (-1, 0), (2, 0), (1, 1), (-1, 1), (2, 1))


def shift(value, axis, k, e):
    perm = [(i, ((i // 2 + k) % 4) * 2 + ((i % 2) ^ e)) for i in range(8)]
    return lax.ppermute(value, axis, perm)


def flip(value):
    return lax.ppermute(value, "role", [(0, 1), (1, 0)])


def sources(axis):
    me = lax.axis_index(axis)
    return [((((me >> 1) - k) & 3) << 1) | ((me & 1) ^ e) for k, e in OFFSETS]


def after(value, *others):
    return lax.optimization_barrier((value, *others))[0]


def gather_start(block, axis):
    return [shift(block, axis, 0, 1), shift(block, axis, 1, 0), shift(block, axis, -1, 0)]


def gather_middle(block, first, axis):
    other, before, nxt = first
    half = block.shape[0] // 2
    up = shift(jnp.concatenate([other, before[:half]], axis=0), axis, 1, 0)
    down = shift(jnp.concatenate([other, nxt[half:]], axis=0), axis, -1, 0)
    return [up, down]


def gather_end(block, first, middle, axis):
    other, before, nxt = first
    up, down = middle
    rows = block.shape[0]
    far = jnp.concatenate([up[rows:], down[rows:]], axis=0)
    other_far = shift(far, axis, 0, 1)
    return [block, other, before, nxt, far, up[:rows], down[:rows], other_far]


def place(blocks, at, dim):
    size = blocks[0].shape[dim]
    shape = list(blocks[0].shape)
    shape[dim] = 8 * size
    out = jnp.zeros(shape, blocks[0].dtype)
    for block, s in zip(blocks, at):
        out = lax.dynamic_update_slice_in_dim(out, block, s * size, axis=dim)
    return out


def dot(a, b, dims=((1,), (0,))):
    return lax.dot_general(a, b, (dims, ((), ())), preferred_element_type=F32)


def split_note(value, width):
    value = jnp.broadcast_to(value, (1, width)).astype(F32)
    row = lax.broadcasted_iota(jnp.int32, (NOTE, width), 0)
    high = lax.reduce_precision(value, 8, 7)
    middle = lax.reduce_precision(value - high, 8, 7)
    low = value - high - middle
    note = jnp.where(row == 0, high, jnp.where(row == 1, middle, jnp.where(row == 2, low, 0.0)))
    return note.astype(BF16)


def join_note(note):
    return jnp.sum(note.astype(F32), axis=0, keepdims=True)


def project_kernel(order, hidden, own, other, teacher, out, total, kept, square):
    step, block = pl.program_id(0), pl.program_id(1)
    n, width = out.shape[0] - NOTE, out.shape[1]
    size = own.shape[0]

    @pl.when((step == 0) & (block == 0))
    def _():
        first = order[order.shape[0] - 1] == 0
        low, high = teacher[:, :width], teacher[:, width:]
        total[0] = -jnp.where(first, low, high)
        total[1] = -jnp.where(first, high, low)

    @pl.when(step == 0)
    def _():
        kept[0, block] = own[...]
        kept[1, block] = other[...]
        total[0] += jnp.dot(hidden[...], own[...], preferred_element_type=F32)
        total[1] += jnp.dot(hidden[...], other[...], preferred_element_type=F32)

    @pl.when((step == 1) & (block == 0))
    def _():
        squares = total[0] * total[0] + total[1] * total[1]
        square[...] = jnp.broadcast_to(jnp.sum(squares, keepdims=True), square.shape)

    @pl.when(step == 1)
    def _():
        dims = (((1,), (1,)), ((), ()))
        back = lax.dot_general(total[0].astype(BF16), kept[0, block], dims, preferred_element_type=F32)
        back += lax.dot_general(total[1].astype(BF16), kept[1, block], dims, preferred_element_type=F32)
        out[:n] = back.astype(BF16)
        value = square[:1]
        row = lax.broadcasted_iota(jnp.int32, (NOTE, width), 0)
        top = value.astype(BF16).astype(F32)
        middle = (value - top).astype(BF16).astype(F32)
        bottom = value - top - middle
        note = jnp.where(row == 0, top, jnp.where(row == 1, middle, jnp.where(row == 2, bottom, 0.0)))
        out[n:] = note.astype(BF16)


def project(order, hidden, own, other, teacher):
    blocks, size, width = own.shape
    rows = teacher.shape[0]
    last = blocks - 1
    p_spec = pl.BlockSpec(
        (None, size, width), lambda s, b, order: (order[blocks + b * (1 - s) + last * s], 0, 0)
    )
    return pl.pallas_call(
        project_kernel,
        grid_spec=pltpu.PrefetchScalarGridSpec(
            num_scalar_prefetch=1,
            grid=(2, blocks),
            in_specs=[
                pl.BlockSpec((None, rows, size), lambda s, b, order: (order[b * (1 - s) + last * s], 0, 0)),
                p_spec,
                p_spec,
                pl.BlockSpec((rows, 2 * width), lambda s, b, order: (0, 0)),
            ],
            out_specs=pl.BlockSpec((None, rows + NOTE, size), lambda s, b, order: (order[2 * blocks + b * s], 0, 0)),
            scratch_shapes=[
                pltpu.VMEM((2, rows, width), F32),
                pltpu.VMEM((2, blocks, size, width), BF16),
                pltpu.VMEM((8, size), F32),
            ],
        ),
        out_shape=jax.ShapeDtypeStruct((blocks, rows + NOTE, size), BF16),
        compiler_params=pltpu.CompilerParams(
            dimension_semantics=("arbitrary", "arbitrary"), vmem_limit_bytes=32 * 1024 * 1024
        ),
        cost_estimate=pl.CostEstimate(
            flops=8 * rows * blocks * size * width, bytes_accessed=4 * blocks * size * width, transcendentals=0
        ),
    )(order, hidden, own, other, teacher)


def teach_kernel(role, tokens, weight, out, away):
    product = jnp.dot(tokens[...], weight[...], preferred_element_type=F32)
    count, rows, width = out.shape
    first = role[0] == 0
    for i in range(count):
        low, high = product[:rows, i * width : (i + 1) * width], product[rows:, i * width : (i + 1) * width]
        out[i] = jnp.where(first, low, high)
        away[i] = jnp.where(first, high, low).astype(BF16)


def teach(role, teacher_in, weight, blocks, width):
    _, rows, depth = teacher_in.shape
    shape = (blocks, rows, 2 * width)
    count = 4
    steps = blocks // count
    place = pl.BlockSpec((count, rows, width), lambda j, role: (j % steps, 0, j // steps))
    return pl.pallas_call(
        teach_kernel,
        grid_spec=pltpu.PrefetchScalarGridSpec(
            num_scalar_prefetch=1,
            grid=(2 * steps,),
            in_specs=[
                pl.BlockSpec((2 * rows, depth), lambda j, role: (0, 0)),
                pl.BlockSpec((depth, count * width), lambda j, role: (0, j)),
            ],
            out_specs=[place, place],
        ),
        out_shape=[jax.ShapeDtypeStruct(shape, F32), jax.ShapeDtypeStruct(shape, BF16)],
        compiler_params=pltpu.CompilerParams(
            dimension_semantics=("arbitrary",), vmem_limit_bytes=40 * 1024 * 1024
        ),
        cost_estimate=pl.CostEstimate(
            flops=8 * rows * depth * blocks * width, bytes_accessed=4 * depth * blocks * width, transcendentals=0
        ),
    )(role, teacher_in.reshape(2 * rows, depth), weight)


def shards(teacher_in, teacher_weight, student_in, student_weight, projector):
    role = lax.axis_index("role")
    n_tensor = lax.axis_size("tensor")
    n_data = lax.axis_size("dp")
    own_rows = student_in.shape[0]
    total_rows = 2 * own_rows * n_data
    out_width = teacher_weight.shape[1]
    feat, hid = student_weight.shape
    wide = feat * n_data
    cols = projector.shape[1]

    xh = lax.axis_index("tensor") & 1

    w_first = gather_start(student_weight, "dp")

    swap = []
    for d in range(8):
        for t in range(8):
            to = ((t // 2 - d // 2) % 4) * 2 + (t ^ d) % 2
            swap.append((d * 8 + t, to * 8 + d))
    projector = lax.ppermute(projector, ("dp", "tensor"), swap)

    own, away = teach(jnp.full((1,), role, jnp.int32), teacher_in, teacher_weight, n_tensor, cols)
    away, projector, *w_first = lax.optimization_barrier((away, projector, *w_first))
    away = flip(away)

    w_middle = gather_middle(student_weight, w_first, "dp")
    p_other = shift(projector, "dp", 0, 1)

    mine = lax.dynamic_slice_in_dim(student_in, role * wide, wide, axis=1)
    theirs = flip(lax.dynamic_slice_in_dim(student_in, (1 - role) * wide, wide, axis=1))

    zt = lax.axis_index("tensor") >> 1
    teacher = {}
    for k in (0, 1, -1, 2):
        at = ((zt - k) & 3) * 2
        pair = lax.dynamic_slice_in_dim(own, at, 2, axis=0) + lax.dynamic_slice_in_dim(away, at, 2, axis=0).astype(F32)
        teacher[k] = pair if k == 0 else pair.astype(BF16)
    teacher[1], teacher[-1], theirs, p_other, *w_middle = lax.optimization_barrier(
        (teacher[1], teacher[-1], theirs, p_other, *w_middle)
    )
    for k in (1, -1):
        teacher[k] = shift(teacher[k], "tensor", -k, 0)

    weight = gather_end(student_weight, w_first, w_middle, "dp")
    p_first = [shift(projector, "dp", 1, 0), shift(projector, "dp", -1, 0)]
    weight[-1], *p_first = lax.optimization_barrier((weight[-1], *p_first))
    p_first = [p_other, *p_first]

    weight = place(weight, sources("dp"), 0)
    student = jnp.concatenate([mine, theirs], axis=0)
    pre = dot(student, weight)
    pre = pre[:own_rows] + flip(pre[own_rows:])
    sigma = jax.nn.sigmoid(pre)
    hidden = (pre * sigma).astype(BF16)

    p_middle = gather_middle(projector, p_first, "dp")
    hidden, teacher[1], teacher[-1], teacher[2] = lax.optimization_barrier(
        (hidden, teacher[1], teacher[-1], teacher[2])
    )
    h_other = shift(hidden, "tensor", 0, 1)
    teacher[2] = shift(teacher[2], "tensor", 2, 0)
    h_other, *p_middle = lax.optimization_barrier((h_other, *p_middle))
    h_pair = jnp.concatenate([hidden, h_other], axis=0)
    h_before, h_after = shift(h_pair, "tensor", 1, 0), shift(h_pair, "tensor", -1, 0)
    p_own = gather_end(projector, p_first, p_middle, "dp")
    h_before, h_after, teacher[2], p_own[-1] = lax.optimization_barrier((h_before, h_after, teacher[2], p_own[-1]))
    h_far = jnp.concatenate(
        [shift(h_before[:own_rows], "tensor", 1, 0), shift(h_after[own_rows:], "tensor", -1, 0)], axis=0
    )
    p_own = place(p_own, sources("dp"), 0)
    p_flip = flip(p_own)
    hidden = jnp.concatenate([h_pair, h_after, h_far, h_before], axis=0).reshape(n_tensor, own_rows, hid)
    p_own, p_flip = p_own.reshape(n_data, hid, cols), p_flip.reshape(n_data, hid, cols)

    teacher = teacher[0] + sum(teacher[k].astype(F32) for k in (1, -1, 2))
    cross = lax.dynamic_index_in_dim(teacher, 1 - xh, 0, False).astype(BF16)
    teacher = lax.dynamic_index_in_dim(teacher, xh, 0, False) + shift(cross, "tensor", 0, 1).astype(F32)

    order = (
        list(range(n_tensor))
        + list(range(n_data))
        + [(((zt + b // 2) & 3) * 2) + ((b % 2) ^ xh) for b in range(n_tensor)]
        + [role]
    )
    order = jnp.stack([jnp.asarray(x, jnp.int32) for x in order])
    back = project(order, hidden, p_own, p_flip, teacher)
    back = lax.all_to_all(back, "tensor", 0, 0, tiled=True)
    back = jnp.sum(back.astype(F32), axis=0)
    square = join_note(back[own_rows:])
    back = back[:own_rows]

    delta = (back * sigma * (1.0 + pre * (1.0 - sigma))).astype(BF16)
    packed = flip(jnp.concatenate([delta, split_note(square, hid)], axis=0))
    delta = jnp.concatenate([delta, packed[:own_rows]], axis=0)
    square = square + join_note(packed[own_rows:])

    grad = dot(student, delta, ((0,), (0,))).astype(BF16).reshape(n_data, feat, hid)
    note = jnp.broadcast_to(split_note(square, hid)[None], (n_data, NOTE, hid))
    grad = jnp.concatenate([grad, note], axis=1)
    grad = lax.all_to_all(grad, "dp", 0, 0, tiled=True)
    grad = jnp.sum(grad.astype(F32), axis=0)
    loss = join_note(grad[feat:])[0, 0] / (2.0 * total_rows * out_width)
    return (grad[:feat] / jnp.sqrt(jnp.float32(total_rows)), loss)


def solution(mesh):
    in_specs = (
        P(None, "dp", ("role", "tensor")),
        P(("role", "tensor"), None),
        P(("role", "dp"), None),
        P(("role", "dp"), "tensor"),
        P("tensor", ("role", "dp")),
    )
    out_specs = (P(("role", "dp"), "tensor"), P())
    return jax.shard_map(shards, mesh=mesh, in_specs=in_specs, out_specs=out_specs, check_vma=False)
```

time: 302 us -> 279 us (0.924)
  local copies, waits for them, and re-layouts: 26.8 us -> 46.1 us
  between operations: 16.2 us -> 2.8 us
  waiting for transfers between devices: 87.8 us -> 76.2 us
  starting transfers between devices: 54.3 us -> 43.4 us
  Pallas kernels: 31.9 us -> 27.3 us
    ppermute x16 -> x21, starting transfers between devices: 49.8 us -> 31.4 us  [shift(): return lax.ppermute(value, axis, perm)]
    dynamic_update_slice x7 -> x14, local copies, waits for them, and re-layouts: 4.91 us -> 19.8 us  [place(): out = lax.dynamic_update_slice_in_dim(out, block, s * size, axis=dim)]
    ppermute x16 -> x21, waiting for transfers between devices: 51.9 us -> 45.2 us  [shift(): return lax.ppermute(value, axis, perm)]
    ppermute x4 -> x5, waiting for transfers between devices: 8.24 us -> 1.56 us  [flip(): return lax.ppermute(value, 'role', [(0, 1), (1, 0)])]
    ppermute x1, starting transfers between devices: 0.68 us -> 5.36 us  [shards(): projector = lax.ppermute(projector, ('dp', 'tensor'), swap)]
    another operation x1 -> x3, local copies, waits for them, and re-layouts: 0.08 us -> 4.75 us  [shards(): order = jnp.stack(order + [role]).astype(jnp.int32)]
    pallas_call x1, Pallas kernels: 17.6 us -> 13.3 us  [teach(): pl.pallas_call(teach_kernel, grid_spec=pltpu.PrefetchScalarGridSpec(num_s...]
    add x3 -> x2, other arithmetic: 8.29 us -> 5.31 us  [the longest x1 3.74 us: shards(): teacher = teacher[0] + sum((teacher[k].astype(F32) for k in (1, -1, 2)))]
  transfers between devices with their start and end apart: 24 -> 28, of which waited for: 10 -> 10; matrix products, arithmetic and copies ran while one was open for 14% -> 20% of each run, Pallas kernels for 6% -> 5%
where the time goes in v5:
time: 279 us; the launch traced here: 278 us
  waiting for transfers between devices  76.2 us (27%)
  blocking collectives  54 us (19%)
  local copies, waits for them, and re-layouts  46.1 us (17%)
  starting transfers between devices  43.4 us (16%)
  Pallas kernels  27.3 us (10%)
  other arithmetic  18.6 us (7%)
  matrix products  9.17 us (3%)
  between operations  2.8 us (1%)
    all_to_all x1, blocking collectives, shards(): grad = lax.all_to_all(grad, 'dp', 0, 0, tiled=True)  54 us
    ppermute x21, waiting for transfers between devices, shift(): return lax.ppermute(value, axis, perm)  45.2 us
    ppermute x21, starting transfers between devices, shift(): return lax.ppermute(value, axis, perm)  31.4 us
    all_to_all x1, waiting for transfers between devices, shards(): back = lax.all_to_all(back, 'tensor', 0, 0, tiled=True)  29.4 us
    dynamic_update_slice x14, local copies, waits for them, and re-layouts, place(): out = lax.dynamic_update_slice_in_dim(out, block, s * size, axis=dim)  19.8 us
    pallas_call x1, Pallas kernels, project(): pl.pallas_call(project_kernel, grid_spec=pltpu.PrefetchScalarGridSpec(num...  14.1 us
    pallas_call x1, Pallas kernels, teach(): pl.pallas_call(teach_kernel, grid_spec=pltpu.PrefetchScalarGridSpec(num_s...  13.3 us
    unnamed x36, local copies, waits for them, and re-layouts  9.65 us
  transfers between devices with their start and end apart: 28, of which 10 were waited for; matrix products, arithmetic and copies ran while one was open for 20% of the time, Pallas kernels for 5%

profile of v5, /device:TPU:0, one launch (start us, length us, event | category | flops | bytes accessed | tf_op | source)
XLA Modules:
  0.0 277.7 jit_solution(16228603621718228297)
XLA Ops:
  0.6 1.7 collective-permute-start.1
  2.3 1.6 collective-permute-start.2
  3.9 1.7 collective-permute-start.3
  5.5 5.4 %collective-permute-start = (bf16[512,512]{1,0:T(8,128)(2,1)}, bf16[512,512]{1,0:T(8,128)(2,1)}, u32[]{:S(2)}, u32[]{:S(2)}) collective-permute-start(bf16[512,512]{1,0:T(8,128)(2,1)} %param.9), channel_id=1, source_target_pairs={{0,0},{1,8},{2,16},{3,24},{4,32},{5,40},{6,48},{7,56},{8,9},{9,1},... | collective-permute-start | bytes 1572872 | tf_op jit(solution)/shard_map/ppermute | solution.py:212
  10.9 1.2 copy-done.2
  12.1 13.3 %shard_map.68 = (f32[8,256,1024]{2,1,0:T(8,128)S(1)}, bf16[8,256,1024]{2,1,0:T(8,128)(2,1)}) custom-call(s32[1]{0:T(128)} %bitcast.role, bf16[512,1024]{1,0:T(8,128)(2,1)S(1)} %bitcast.22, bf16[1024,8192]{1,0:T(8,128)(2,1)} %weight.1), custom_call_target="tpu_custom_call" | custom-call | flops 8589934592 | bytes 16777216 | tf_op jit(solution)/shard_map/pallas_call | solution.py:171
  25.4 3.3 %copy-done = f32[8,256,1024]{2,1,0:T(8,128)} copy-done((f32[8,256,1024]{2,1,0:T(8,128)}, f32[8,256,1024]{2,1,0:T(8,128)S(1)}, u32[]{:S(2)}) %copy-start) | copy-done | bytes 8388632
  29.5 4.0 %constant_dynamic-slice_fusion.1 = (bf16[256,4096]{1,0:T(8,128)(2,1)S(1)}, bf16[256,4096]{1,0:T(8,128)(2,1)}) fusion(bf16[256,8192]{1,0:T(8,128)(2,1)} %param.7, s32[]{:T(128)S(6)} %select_n.93, s32[]{:T(128)S(6)} %select_n.96), kind=kLoop, calls=%fused_computation.60 | loop fusion | bytes 8388616 | tf_op jit(solution)/shard_map/dynamic_slice | solution.py:221
  33.5 1.4 pad_maximum_fusion.4
  34.9 1.5 collective-permute-start.7
  36.4 4.8 %collective-permute-start.8 = (bf16[768,512]{1,0:T(8,128)(2,1)}, bf16[768,512]{1,0:T(8,128)(2,1)}, u32[]{:S(2)}, u32[]{:S(2)}) collective-permute-start(bf16[768,512]{1,0:T(8,128)(2,1)} %get-tuple-element.67), channel_id=1, source_target_pairs={{0,48},{8,56},{16,0},{24,8},{32,16},{40,24},{48,32},{56,40},{1,49}... | collective-permute-start | bytes 2359304 | tf_op jit(solution)/shard_map/ppermute | solution.py:16
  41.2 2.4 broadcast.80.clone
  43.6 2.6 constant_dynamic-update-slice_fusion.19
  47.9 1.9 constant_dynamic-update-slice_fusion.16
  49.8 4.5 %add_convert_fusion = (bf16[2,256,1024]{2,1,0:T(8,128)(2,1)}, bf16[2,256,1024]{2,1,0:T(8,128)(2,1)}, bf16[2,256,1024]{2,1,0:T(8,128)(2,1)}) fusion(f32[8,256,1024]{2,1,0:T(8,128)S(1)} %copy-done.1, s32[]{:T(128)S(6)} %select_n.105, bf16[8,256,1024]{2,1,0:T(8,128)(2,1)} %collective-permute-done.4, s32[]{:T(128)S(6)} %select_n.95, s32[]{:T(128)S(6)} %select_n.94), kind=kLoop, calls=%fused_computation.7 | loop fusion | flops 4718592 | bytes 12582924 | tf_op jit(solution)/shard_map/convert_element_type | solution.py:229
  54.3 6.1 %collective-permute-done.6 = bf16[512,512]{1,0:T(8,128)(2,1)} collective-permute-done((bf16[512,512]{1,0:T(8,128)(2,1)}, bf16[512,512]{1,0:T(8,128)(2,1)}, u32[]{:S(2)}, u32[]{:S(2)}) %collective-permute-start.6) | collective-permute-done | bytes 524320 | tf_op jit(solution)/shard_map/ppermute | solution.py:16
  60.4 1.8 collective-permute-start.11
  66.2 1.3 collective-permute-start.14
  67.6 1.9 slice_dynamic-update-slice_fusion.3
  69.4 1.9 slice_dynamic-update-slice_fusion.2
  71.3 2.4 collective-permute-done.11
  73.7 4.3 %collective-permute-done.9 = bf16[512,512]{1,0:T(8,128)(2,1)} collective-permute-done((bf16[512,512]{1,0:T(8,128)(2,1)}, bf16[512,512]{1,0:T(8,128)(2,1)}, u32[]{:S(2)}, u32[]{:S(2)}) %collective-permute-start.9) | collective-permute-done | bytes 524320 | tf_op jit(solution)/shard_map/ppermute | solution.py:16
  78.0 1.9 constant_dynamic-update-slice_fusion.14
  79.9 5.2 %fusion = f32[512,512]{1,0:T(8,128)S(1)} fusion(bf16[4096,512]{1,0:T(8,128)(2,1)} %constant_dynamic-update-slice_fusion.14, bf16[256,4096]{1,0:T(8,128)(2,1)} %collective-permute-done.5, bf16[256,4096]{1,0:T(8,128)(2,1)S(1)} %get-tuple-element.59), kind=kOutput, calls=%fused_computation.5 | convolution fusion | flops 2155872256 | bytes 9437184 | tf_op jit(solution)/shard_map/dot_general | solution.py:64
  85.3 1.2 pad_maximum_fusion.6
  87.1 2.6 collective-permute-start.17
  89.7 2.2 broadcast.80.clone.1
  92.0 1.9 constant_dynamic-update-slice_fusion.13
  93.9 1.9 constant_dynamic-update-slice_fusion.12
  96.5 2.2 collective-permute-start.20
  100.4 7.3 %collective-permute-done.16 = bf16[768,512]{1,0:T(8,128)(2,1)S(1)} collective-permute-done((bf16[768,512]{1,0:T(8,128)(2,1)S(1)}, bf16[768,512]{1,0:T(8,128)(2,1)S(1)}, u32[]{:S(2)}, u32[]{:S(2)}) %collective-permute-start.16) | collective-permute-done | bytes 786464 | tf_op jit(solution)/shard_map/ppermute | solution.py:16
  107.8 3.2 %collective-permute-start.19 = (bf16[512,512]{1,0:T(8,128)(2,1)S(1)}, bf16[512,512]{1,0:T(8,128)(2,1)}, u32[]{:S(2)}, u32[]{:S(2)}) collective-permute-start(bf16[512,512]{1,0:T(8,128)(2,1)S(1)} %get-tuple-element.69), channel_id=1, source_target_pairs={{0,6},{1,7},{2,0},{3,1},{4,2},{5,3},{6,4},{7,5},{8,14},{9,15},{10,... | collective-permute-start | bytes 1572872 | tf_op jit(solution)/shard_map/ppermute | solution.py:16
  114.3 19.7 %collective-permute-done.18 = bf16[512,512]{1,0:T(8,128)(2,1)} collective-permute-done((bf16[512,512]{1,0:T(8,128)(2,1)S(1)}, bf16[512,512]{1,0:T(8,128)(2,1)}, u32[]{:S(2)}, u32[]{:S(2)}) %collective-permute-start.18) | collective-permute-done | bytes 524320 | tf_op jit(solution)/shard_map/ppermute | solution.py:16
  136.0 1.7 slice.81
  138.2 3.7 %add_add_fusion = f32[2,256,1024]{2,1,0:T(8,128)S(1)} fusion(bf16[2,256,1024]{2,1,0:T(8,128)(2,1)} %copy-done.15, bf16[2,256,1024]{2,1,0:T(8,128)(2,1)} %copy-done.14, bf16[2,256,1024]{2,1,0:T(8,128)(2,1)} %copy-done.13, f32[8,256,1024]{2,1,0:T(8,128)} %copy-done, s32[]{:T(128)S(6)} %select_n.106, bf16[8,256,1024]{2,1,0:T(8,128)(2,1)} %collective-permute-done.4), kind=kLoop, calls=%fused_computation.6 | loop fusion | flops 4194304 | bytes 8388612 | tf_op jit(solution)/shard_map/add | solution.py:267
  142.0 1.3 copy-done.3
  144.2 2.5 collective-permute-start.25
  146.7 1.7 slice.82
  148.3 3.2 %collective-permute-start.23 = (bf16[256,512]{1,0:T(8,128)(2,1)}, bf16[256,512]{1,0:T(8,128)(2,1)}, u32[]{:S(2)}, u32[]{:S(2)}) collective-permute-start(bf16[256,512]{1,0:T(8,128)(2,1)} %slice.82), channel_id=1, source_target_pairs={{0,6},{1,7},{2,0},{3,1},{4,2},{5,3},{6,4},{7,5},{8,14},{9,15},{10,... | collective-permute-start | bytes 786440 | tf_op jit(solution)/shard_map/ppermute | solution.py:16
  152.8 4.8 %collective-permute-done.23 = bf16[256,512]{1,0:T(8,128)(2,1)} collective-permute-done((bf16[256,512]{1,0:T(8,128)(2,1)}, bf16[256,512]{1,0:T(8,128)(2,1)}, u32[]{:S(2)}, u32[]{:S(2)}) %collective-permute-start.23) | collective-permute-done | bytes 262176 | tf_op jit(solution)/shard_map/ppermute | solution.py:16
  160.1 1.6 bitcast_add_fusion.teacher
  161.7 14.1 %shard_map.69 = bf16[8,272,512]{2,1,0:T(8,128)(2,1)} custom-call(s32[25]{0:T(128)S(1)} %stack.36.order, bf16[8,256,512]{2,1,0:T(8,128)(2,1)S(1)} %bitcast.21, bf16[8,512,512]{2,1,0:T(8,128)(2,1)} %bitcast.11.own, bf16[8,512,512]{2,1,0:T(8,128)(2,1)} %bitcast.12.other, f32[256,1024]{1,0:T(8,128)S(1)} %bitcast_add_fusion.teacher), custom_call_target="tpu_custom_call" | custom-call | flops 4294967296 | bytes 8388608 | tf_op jit(solution)/shard_map/pallas_call | solution.py:127
  175.7 6.4 %all-to-all-start = ((bf16[8,272,512]{2,1,0:T(8,128)(2,1)}), bf16[8,272,512]{2,1,0:T(8,128)(2,1)S(1)}, u32[]{:S(2)}, u32[]{:S(2)}) async-start(bf16[8,272,512]{2,1,0:T(8,128)(2,1)} %shard_map.69), calls=%async_computation | async-start | bytes 4456448 | tf_op jit(solution)/shard_map/all_to_all | solution.py:279
  182.2 29.4 %all-to-all-done = bf16[8,272,512]{2,1,0:T(8,128)(2,1)S(1)} async-done(((bf16[8,272,512]{2,1,0:T(8,128)(2,1)}), bf16[8,272,512]{2,1,0:T(8,128)(2,1)S(1)}, u32[]{:S(2)}, u32[]{:S(2)}) %all-to-all-start) | async-done | bytes 2228256 | tf_op jit(solution)/shard_map/all_to_all | solution.py:279
  212.0 1.5 fusion.3
  213.6 1.5 collective-permute-done.26
  215.2 4.0 %convolution_convert_fusion = bf16[4096,512]{1,0:T(8,128)(2,1)S(1)} fusion(bf16[256,4096]{1,0:T(8,128)(2,1)} %collective-permute-done.5, bf16[256,4096]{1,0:T(8,128)(2,1)S(1)} %copy-done.5, bf16[256,512]{1,0:T(8,128)(2,1)S(1)} %slice.96, bf16[256,512]{1,0:T(8,128)(2,1)S(1)} %fusion.3), kind=kOutput, calls=%fused_computation.1 | convolution fusion | flops 2159017984 | bytes 8912896 | tf_op jit(solution)/shard_map/dot_general | solution.py:64
  219.7 54.0 %all_to_all.10 = bf16[8,528,512]{2,1,0:T(8,128)(2,1)S(1)} all-to-all(bf16[8,528,512]{2,1,0:T(8,128)(2,1)S(1)} %pad_maximum_fusion), channel_id=1, replica_groups=mesh['role'=2,'dp'=8,'tensor'=8] {'dp'}, dimensions={0} | all-to-all | bytes 8650752 | tf_op jit(solution)/shard_map/all_to_all | solution.py:292
  (110 shorter events, 23.6 us)
Async XLA Ops:
  0.6 28.1 %collective-permute-start.1 = (bf16[512,512]{1,0:T(8,128)(2,1)}, bf16[512,512]{1,0:T(8,128)(2,1)S(1)}, u32[]{:S(2)}, u32[]{:S(2)}) collective-permute-start(bf16[512,512]{1,0:T(8,128)(2,1)} %param.8), channel_id=1, source_target_pairs={{0,8},{8,0},{16,24},{24,16},{32,40},{40,32},{48,56},{56,48},{1,9},... | collective-permute-start | bytes 1572872 | tf_op jit(solution)/shard_map/ppermute | solution.py:16
  2.3 26.4 %collective-permute-start.2 = (bf16[512,512]{1,0:T(8,128)(2,1)}, bf16[512,512]{1,0:T(8,128)(2,1)S(1)}, u32[]{:S(2)}, u32[]{:S(2)}) collective-permute-start(bf16[512,512]{1,0:T(8,128)(2,1)} %param.8), channel_id=1, source_target_pairs={{0,16},{8,24},{16,32},{24,40},{32,48},{40,56},{48,0},{56,8},{1,17}... | collective-permute-start | bytes 1572872 | tf_op jit(solution)/shard_map/ppermute | solution.py:16
  3.9 24.8 %collective-permute-start.3 = (bf16[512,512]{1,0:T(8,128)(2,1)}, bf16[512,512]{1,0:T(8,128)(2,1)S(1)}, u32[]{:S(2)}, u32[]{:S(2)}) collective-permute-start(bf16[512,512]{1,0:T(8,128)(2,1)} %param.8), channel_id=1, source_target_pairs={{0,48},{8,56},{16,0},{24,8},{32,16},{40,24},{48,32},{56,40},{1,49}... | collective-permute-start | bytes 1572872 | tf_op jit(solution)/shard_map/ppermute | solution.py:16
  5.5 23.2 %collective-permute-start = (bf16[512,512]{1,0:T(8,128)(2,1)}, bf16[512,512]{1,0:T(8,128)(2,1)}, u32[]{:S(2)}, u32[]{:S(2)}) collective-permute-start(bf16[512,512]{1,0:T(8,128)(2,1)} %param.9), channel_id=1, source_target_pairs={{0,0},{1,8},{2,16},{3,24},{4,32},{5,40},{6,48},{7,56},{8,9},{9,1},... | collective-permute-start | bytes 1572872 | tf_op jit(solution)/shard_map/ppermute | solution.py:212
  10.9 1.2 copy-start.2
  25.4 3.3 %copy-start = (f32[8,256,1024]{2,1,0:T(8,128)}, f32[8,256,1024]{2,1,0:T(8,128)S(1)}, u32[]{:S(2)}) copy-start(f32[8,256,1024]{2,1,0:T(8,128)S(1)} %get-tuple-element.29) | copy-start | bytes 25165828
  28.7 0.8 copy-start.7
  28.7 21.1 %collective-permute-start.4 = (bf16[8,256,1024]{2,1,0:T(8,128)(2,1)}, bf16[8,256,1024]{2,1,0:T(8,128)(2,1)}, u32[]{:S(2)}, u32[]{:S(2)}) collective-permute-start(bf16[8,256,1024]{2,1,0:T(8,128)(2,1)} %get-tuple-element.31), channel_id=1, source_target_pairs={{0,64},{64,0},{1,65},{65,1},{2,66},{66,2},{3,67},{67,3},{4,68},{68... | collective-permute-start | bytes 12582920 | tf_op jit(solution)/shard_map/ppermute | solution.py:20
  29.5 4.0 %slice-start = ((bf16[512,512]{1,0:T(8,128)(2,1)}), bf16[256,512]{1,0:T(8,128)(2,1)S(1)}, s32[]{:S(2)}) async-start(bf16[512,512]{1,0:T(8,128)(2,1)} %copy-done.7), calls=%async_computation.2 | async-start | bytes 524288 | tf_op jit(solution)/shard_map/slice | solution.py:40
  33.5 46.4 %copy-start.4 = (bf16[256,4096]{1,0:T(8,128)(2,1)}, bf16[256,4096]{1,0:T(8,128)(2,1)S(1)}, u32[]{:S(2)}) copy-start(bf16[256,4096]{1,0:T(8,128)(2,1)S(1)} %get-tuple-element.59) | copy-start | bytes 6291460
  33.5 28.7 %collective-permute-start.5 = (bf16[256,4096]{1,0:T(8,128)(2,1)}, bf16[256,4096]{1,0:T(8,128)(2,1)}, u32[]{:S(2)}, u32[]{:S(2)}) collective-permute-start(bf16[256,4096]{1,0:T(8,128)(2,1)} %get-tuple-element.60), channel_id=1, source_target_pairs={{0,64},{64,0},{1,65},{65,1},{2,66},{66,2},{3,67},{67,3},{4,68},{68... | collective-permute-start | bytes 6291464 | tf_op jit(solution)/shard_map/ppermute | solution.py:20
  34.9 27.3 %collective-permute-start.7 = (bf16[768,512]{1,0:T(8,128)(2,1)}, bf16[768,512]{1,0:T(8,128)(2,1)}, u32[]{:S(2)}, u32[]{:S(2)}) collective-permute-start(bf16[768,512]{1,0:T(8,128)(2,1)} %get-tuple-element.68), channel_id=1, source_target_pairs={{0,16},{8,24},{16,32},{24,40},{32,48},{40,56},{48,0},{56,8},{1,17}... | collective-permute-start | bytes 2359304 | tf_op jit(solution)/shard_map/ppermute | solution.py:16
  36.4 25.8 %collective-permute-start.8 = (bf16[768,512]{1,0:T(8,128)(2,1)}, bf16[768,512]{1,0:T(8,128)(2,1)}, u32[]{:S(2)}, u32[]{:S(2)}) collective-permute-start(bf16[768,512]{1,0:T(8,128)(2,1)} %get-tuple-element.67), channel_id=1, source_target_pairs={{0,48},{8,56},{16,0},{24,8},{32,16},{40,24},{48,32},{56,40},{1,49}... | collective-permute-start | bytes 2359304 | tf_op jit(solution)/shard_map/ppermute | solution.py:16
  41.2 8.6 %copy-start.1 = (f32[8,256,1024]{2,1,0:T(8,128)S(1)}, f32[8,256,1024]{2,1,0:T(8,128)}, u32[]{:S(2)}) copy-start(f32[8,256,1024]{2,1,0:T(8,128)} %copy-done) | copy-start | bytes 25165828
  46.2 14.2 %collective-permute-start.6 = (bf16[512,512]{1,0:T(8,128)(2,1)}, bf16[512,512]{1,0:T(8,128)(2,1)}, u32[]{:S(2)}, u32[]{:S(2)}) collective-permute-start(bf16[512,512]{1,0:T(8,128)(2,1)} %collective-permute-done), channel_id=1, source_target_pairs={{0,8},{8,0},{16,24},{24,16},{32,40},{40,32},{48,56},{56,48},{1,9},... | collective-permute-start | bytes 1572872 | tf_op jit(solution)/shard_map/ppermute | solution.py:16
  49.8 21.5 %collective-permute-start.10 = (bf16[512,512]{1,0:T(8,128)(2,1)}, bf16[512,512]{1,0:T(8,128)(2,1)S(1)}, u32[]{:S(2)}, u32[]{:S(2)}) collective-permute-start(bf16[512,512]{1,0:T(8,128)(2,1)} %collective-permute-done), channel_id=1, source_target_pairs={{0,16},{8,24},{16,32},{24,40},{32,48},{40,56},{48,0},{56,8},{1,17}... | collective-permute-start | bytes 1572872 | tf_op jit(solution)/shard_map/ppermute | solution.py:16
  60.4 13.3 %collective-permute-start.11 = (bf16[512,512]{1,0:T(8,128)(2,1)}, bf16[512,512]{1,0:T(8,128)(2,1)S(1)}, u32[]{:S(2)}, u32[]{:S(2)}) collective-permute-start(bf16[512,512]{1,0:T(8,128)(2,1)} %collective-permute-done), channel_id=1, source_target_pairs={{0,48},{8,56},{16,0},{24,8},{32,16},{40,24},{48,32},{56,40},{1,49}... | collective-permute-start | bytes 1572872 | tf_op jit(solution)/shard_map/ppermute | solution.py:16
  65.2 12.8 %collective-permute-start.9 = (bf16[512,512]{1,0:T(8,128)(2,1)}, bf16[512,512]{1,0:T(8,128)(2,1)}, u32[]{:S(2)}, u32[]{:S(2)}) collective-permute-start(bf16[512,512]{1,0:T(8,128)(2,1)} %get-tuple-element.65), channel_id=1, source_target_pairs={{0,8},{8,0},{16,24},{24,16},{32,40},{40,32},{48,56},{56,48},{1,9},... | collective-permute-start | bytes 1572872 | tf_op jit(solution)/shard_map/ppermute | solution.py:16
  65.5 30.4 %collective-permute-start.13 = (bf16[2,256,1024]{2,1,0:T(8,128)(2,1)}, bf16[2,256,1024]{2,1,0:T(8,128)(2,1)S(1)}, u32[]{:S(2)}, u32[]{:S(2)}) collective-permute-start(bf16[2,256,1024]{2,1,0:T(8,128)(2,1)} %get-tuple-element.40), channel_id=1, source_target_pairs={{0,6},{1,7},{2,0},{3,1},{4,2},{5,3},{6,4},{7,5},{8,14},{9,15},{10,... | collective-permute-start | bytes 3145736 | tf_op jit(solution)/shard_map/ppermute | solution.py:16
  66.2 29.8 %collective-permute-start.14 = (bf16[2,256,1024]{2,1,0:T(8,128)(2,1)}, bf16[2,256,1024]{2,1,0:T(8,128)(2,1)S(1)}, u32[]{:S(2)}, u32[]{:S(2)}) collective-permute-start(bf16[2,256,1024]{2,1,0:T(8,128)(2,1)} %get-tuple-element.41), channel_id=1, source_target_pairs={{0,2},{1,3},{2,4},{3,5},{4,6},{5,7},{6,0},{7,1},{8,10},{9,11},{10,... | collective-permute-start | bytes 3145736 | tf_op jit(solution)/shard_map/ppermute | solution.py:16
  71.3 8.5 %copy-start.8 = (bf16[512,512]{1,0:T(8,128)(2,1)}, bf16[512,512]{1,0:T(8,128)(2,1)S(1)}, u32[]{:S(2)}) copy-start(bf16[512,512]{1,0:T(8,128)(2,1)S(1)} %collective-permute-done.10) | copy-start | bytes 1572868
  73.7 6.1 %copy-start.10 = (bf16[512,512]{1,0:T(8,128)(2,1)}, bf16[512,512]{1,0:T(8,128)(2,1)S(1)}, u32[]{:S(2)}) copy-start(bf16[512,512]{1,0:T(8,128)(2,1)S(1)} %collective-permute-done.11) | copy-start | bytes 1572868
  79.9 5.4 %slice-start.1 = ((bf16[512,512]{1,0:T(8,128)(2,1)}), bf16[256,512]{1,0:T(8,128)(2,1)S(1)}, s32[]{:S(2)}) async-start(bf16[512,512]{1,0:T(8,128)(2,1)} %copy-done.8), calls=%async_computation.3 | async-start | bytes 524288 | tf_op jit(solution)/shard_map/slice | solution.py:39
  79.9 5.4 %slice-start.2 = ((bf16[512,512]{1,0:T(8,128)(2,1)}), bf16[256,512]{1,0:T(8,128)(2,1)S(1)}, s32[]{:S(2)}) async-start(bf16[512,512]{1,0:T(8,128)(2,1)} %copy-done.10), calls=%async_computation.4 | async-start | bytes 524288 | tf_op jit(solution)/shard_map/slice | solution.py:40
  85.1 10.6 %collective-permute-start.12 = (f32[256,512]{1,0:T(8,128)S(1)}, f32[256,512]{1,0:T(8,128)S(1)}, u32[]{:S(2)}, u32[]{:S(2)}) collective-permute-start(f32[256,512]{1,0:T(8,128)S(1)} %slice.93), channel_id=1, source_target_pairs={{0,64},{64,0},{1,65},{65,1},{2,66},{66,2},{3,67},{67,3},{4,68},{68... | collective-permute-start | bytes 1572872 | tf_op jit(solution)/shard_map/ppermute | solution.py:20
  86.4 10.0 %copy-start.12 = (bf16[2,256,1024]{2,1,0:T(8,128)(2,1)S(1)}, bf16[2,256,1024]{2,1,0:T(8,128)(2,1)}, u32[]{:S(2)}) copy-start(bf16[2,256,1024]{2,1,0:T(8,128)(2,1)} %get-tuple-element.47) | copy-start | bytes 3145732
  86.4 12.2 %copy-start.9 = (bf16[512,512]{1,0:T(8,128)(2,1)S(1)}, bf16[512,512]{1,0:T(8,128)(2,1)}, u32[]{:S(2)}) copy-start(bf16[512,512]{1,0:T(8,128)(2,1)} %copy-done.8) | copy-start | bytes 1572868
  86.4 21.2 %collective-permute-start.16 = (bf16[768,512]{1,0:T(8,128)(2,1)S(1)}, bf16[768,512]{1,0:T(8,128)(2,1)S(1)}, u32[]{:S(2)}, u32[]{:S(2)}) collective-permute-start(bf16[768,512]{1,0:T(8,128)(2,1)S(1)} %get-tuple-element.64), channel_id=1, source_target_pairs={{0,16},{8,24},{16,32},{24,40},{32,48},{40,56},{48,0},{56,8},{1,17}... | collective-permute-start | bytes 2359304 | tf_op jit(solution)/shard_map/ppermute | solution.py:16
  87.1 12.4 %copy-start.11 = (bf16[512,512]{1,0:T(8,128)(2,1)S(1)}, bf16[512,512]{1,0:T(8,128)(2,1)}, u32[]{:S(2)}) copy-start(bf16[512,512]{1,0:T(8,128)(2,1)} %copy-done.10) | copy-start | bytes 1572868
  87.1 20.5 %collective-permute-start.17 = (bf16[768,512]{1,0:T(8,128)(2,1)S(1)}, bf16[768,512]{1,0:T(8,128)(2,1)S(1)}, u32[]{:S(2)}, u32[]{:S(2)}) collective-permute-start(bf16[768,512]{1,0:T(8,128)(2,1)S(1)} %get-tuple-element.63), channel_id=1, source_target_pairs={{0,48},{8,56},{16,0},{24,8},{32,16},{40,24},{48,32},{56,40},{1,49}... | collective-permute-start | bytes 2359304 | tf_op jit(solution)/shard_map/ppermute | solution.py:16
  95.8 11.9 %copy-start.6 = (f32[256,512]{1,0:T(8,128)}, f32[256,512]{1,0:T(8,128)S(1)}, u32[]{:S(2)}) copy-start(f32[256,512]{1,0:T(8,128)S(1)} %collective-permute-done.12) | copy-start | bytes 1572868
  96.0 18.3 %copy-start.13 = (bf16[2,256,1024]{2,1,0:T(8,128)(2,1)}, bf16[2,256,1024]{2,1,0:T(8,128)(2,1)S(1)}, u32[]{:S(2)}) copy-start(bf16[2,256,1024]{2,1,0:T(8,128)(2,1)S(1)} %collective-permute-done.13) | copy-start | bytes 3145732
  96.0 18.3 %copy-start.14 = (bf16[2,256,1024]{2,1,0:T(8,128)(2,1)}, bf16[2,256,1024]{2,1,0:T(8,128)(2,1)S(1)}, u32[]{:S(2)}) copy-start(bf16[2,256,1024]{2,1,0:T(8,128)(2,1)S(1)} %collective-permute-done.14) | copy-start | bytes 3145732
  96.0 11.6 %collective-permute-start.15 = (bf16[256,512]{1,0:T(8,128)(2,1)S(1)}, bf16[256,512]{1,0:T(8,128)(2,1)S(1)}, u32[]{:S(2)}, u32[]{:S(2)}) collective-permute-start(bf16[256,512]{1,0:T(8,128)(2,1)S(1)} %multiply_convert_fusion), channel_id=1, source_target_pairs={{0,1},{1,0},{2,3},{3,2},{4,5},{5,4},{6,7},{7,6},{8,9},{9,8},{10,11... | collective-permute-start | bytes 786440 | tf_op jit(solution)/shard_map/ppermute | solution.py:16
  96.5 37.7 %collective-permute-start.20 = (bf16[2,256,1024]{2,1,0:T(8,128)(2,1)S(1)}, bf16[2,256,1024]{2,1,0:T(8,128)(2,1)S(1)}, u32[]{:S(2)}, u32[]{:S(2)}) collective-permute-start(bf16[2,256,1024]{2,1,0:T(8,128)(2,1)S(1)} %copy-done.12), channel_id=1, source_target_pairs={{0,4},{1,5},{2,6},{3,7},{4,0},{5,1},{6,2},{7,3},{8,12},{9,13},{10,... | collective-permute-start | bytes 3145736 | tf_op jit(solution)/shard_map/ppermute | solution.py:16
  107.7 26.3 %collective-permute-start.18 = (bf16[512,512]{1,0:T(8,128)(2,1)S(1)}, bf16[512,512]{1,0:T(8,128)(2,1)}, u32[]{:S(2)}, u32[]{:S(2)}) collective-permute-start(bf16[512,512]{1,0:T(8,128)(2,1)S(1)} %get-tuple-element.69), channel_id=1, source_target_pairs={{0,2},{1,3},{2,4},{3,5},{4,6},{5,7},{6,0},{7,1},{8,10},{9,11},{10,... | collective-permute-start | bytes 1572872 | tf_op jit(solution)/shard_map/ppermute | solution.py:16
  107.8 26.4 %collective-permute-start.19 = (bf16[512,512]{1,0:T(8,128)(2,1)S(1)}, bf16[512,512]{1,0:T(8,128)(2,1)}, u32[]{:S(2)}, u32[]{:S(2)}) collective-permute-start(bf16[512,512]{1,0:T(8,128)(2,1)S(1)} %get-tuple-element.69), channel_id=1, source_target_pairs={{0,6},{1,7},{2,0},{3,1},{4,2},{5,3},{6,4},{7,5},{8,14},{9,15},{10,... | collective-permute-start | bytes 1572872 | tf_op jit(solution)/shard_map/ppermute | solution.py:16
  111.9 22.2 %collective-permute-start.21 = (bf16[512,512]{1,0:T(8,128)(2,1)S(1)}, bf16[512,512]{1,0:T(8,128)(2,1)S(1)}, u32[]{:S(2)}, u32[]{:S(2)}) collective-permute-start(bf16[512,512]{1,0:T(8,128)(2,1)S(1)} %get-tuple-element.62), channel_id=1, source_target_pairs={{0,8},{8,0},{16,24},{24,16},{32,40},{40,32},{48,56},{56,48},{1,9},... | collective-permute-start | bytes 1572872 | tf_op jit(solution)/shard_map/ppermute | solution.py:16
  134.2 1.0 copy-start.15
  136.0 25.6 %collective-permute-start.24 = (bf16[4096,512]{1,0:T(8,128)(2,1)}, bf16[4096,512]{1,0:T(8,128)(2,1)}, u32[]{:S(2)}, u32[]{:S(2)}) collective-permute-start(bf16[4096,512]{1,0:T(8,128)(2,1)} %constant_dynamic-update-slice_fusion.8), channel_id=1, source_target_pairs={{0,64},{64,0},{1,65},{65,1},{2,66},{66,2},{3,67},{67,3},{4,68},{68... | collective-permute-start | bytes 12582920 | tf_op jit(solution)/shard_map/ppermute | solution.py:20
  137.7 15.1 %collective-permute-start.22 = (bf16[256,512]{1,0:T(8,128)(2,1)}, bf16[256,512]{1,0:T(8,128)(2,1)S(1)}, u32[]{:S(2)}, u32[]{:S(2)}) collective-permute-start(bf16[256,512]{1,0:T(8,128)(2,1)} %slice.81), channel_id=1, source_target_pairs={{0,2},{1,3},{2,4},{3,5},{4,6},{5,7},{6,0},{7,1},{8,10},{9,11},{10,... | collective-permute-start | bytes 786440 | tf_op jit(solution)/shard_map/ppermute | solution.py:16
  142.0 1.3 copy-start.3
  144.2 15.9 %collective-permute-start.25 = (bf16[256,1024]{1,0:T(8,128)(2,1)}, bf16[256,1024]{1,0:T(8,128)(2,1)}, u32[]{:S(2)}, u32[]{:S(2)}) collective-permute-start(bf16[256,1024]{1,0:T(8,128)(2,1)} %fusion.1), channel_id=1, source_target_pairs={{0,1},{1,0},{2,3},{3,2},{4,5},{5,4},{6,7},{7,6},{8,9},{9,8},{10,11... | collective-permute-start | bytes 1572872 | tf_op jit(solution)/shard_map/ppermute | solution.py:16
  148.3 9.2 %collective-permute-start.23 = (bf16[256,512]{1,0:T(8,128)(2,1)}, bf16[256,512]{1,0:T(8,128)(2,1)}, u32[]{:S(2)}, u32[]{:S(2)}) collective-permute-start(bf16[256,512]{1,0:T(8,128)(2,1)} %slice.82), channel_id=1, source_target_pairs={{0,6},{1,7},{2,0},{3,1},{4,2},{5,3},{6,4},{7,5},{8,14},{9,15},{10,... | collective-permute-start | bytes 786440 | tf_op jit(solution)/shard_map/ppermute | solution.py:16
  175.7 35.9 %all-to-all-start = ((bf16[8,272,512]{2,1,0:T(8,128)(2,1)}), bf16[8,272,512]{2,1,0:T(8,128)(2,1)S(1)}, u32[]{:S(2)}, u32[]{:S(2)}) async-start(bf16[8,272,512]{2,1,0:T(8,128)(2,1)} %shard_map.69), calls=%async_computation | async-start | bytes 4456448 | tf_op jit(solution)/shard_map/all_to_all | solution.py:279
  211.6 3.6 %copy-start.5 = (bf16[256,4096]{1,0:T(8,128)(2,1)S(1)}, bf16[256,4096]{1,0:T(8,128)(2,1)}, u32[]{:S(2)}) copy-start(bf16[256,4096]{1,0:T(8,128)(2,1)} %copy-done.4) | copy-start | bytes 6291460
  213.5 1.6 collective-permute-start.26

commit v6 on v5

--- a/solution.py
+++ b/solution.py
@@ -39,25 +39,6 @@
     up = shift(jnp.concatenate([other, before[:half]], axis=0), axis, 1, 0)
     down = shift(jnp.concatenate([other, nxt[half:]], axis=0), axis, -1, 0)
     return [up, down]
-
-
-def gather_end(block, first, middle, axis):
-    other, before, nxt = first
-    up, down = middle
-    rows = block.shape[0]
-    far = jnp.concatenate([up[rows:], down[rows:]], axis=0)
-    other_far = shift(far, axis, 0, 1)
-    return [block, other, before, nxt, far, up[:rows], down[:rows], other_far]
-
-
-def place(blocks, at, dim):
-    size = blocks[0].shape[dim]
-    shape = list(blocks[0].shape)
-    shape[dim] = 8 * size
-    out = jnp.zeros(shape, blocks[0].dtype)
-    for block, s in zip(blocks, at):
-        out = lax.dynamic_update_slice_in_dim(out, block, s * size, axis=dim)
-    return out
 
 
 def dot(a, b, dims=((1,), (0,))):
@@ -78,78 +59,97 @@
     return jnp.sum(note.astype(F32), axis=0, keepdims=True)
 
 
-def project_kernel(order, hidden, own, other, teacher, out, total, kept, square):
-    step, block = pl.program_id(0), pl.program_id(1)
-    n, width = out.shape[0] - NOTE, out.shape[1]
-    size = own.shape[0]
-
-    @pl.when((step == 0) & (block == 0))
-    def _():
-        first = order[order.shape[0] - 1] == 0
-        low, high = teacher[:, :width], teacher[:, width:]
-        total[0] = -jnp.where(first, low, high)
-        total[1] = -jnp.where(first, high, low)
-
-    @pl.when(step == 0)
-    def _():
-        kept[0, block] = own[...]
-        kept[1, block] = other[...]
-        total[0] += jnp.dot(hidden[...], own[...], preferred_element_type=F32)
-        total[1] += jnp.dot(hidden[...], other[...], preferred_element_type=F32)
-
-    @pl.when((step == 1) & (block == 0))
-    def _():
-        squares = total[0] * total[0] + total[1] * total[1]
-        square[...] = jnp.broadcast_to(jnp.sum(squares, keepdims=True), square.shape)
-
-    @pl.when(step == 1)
-    def _():
+def project_kernel(order, *refs):
+    h_refs, own_refs, other_refs = refs[:6], refs[6:13], refs[13:15]
+    teacher, out, h_kept, p_kept, total, residual, h_sem, p_sem = refs[15:]
+    n, width = out.shape[1] - NOTE, out.shape[2]
+    size = p_kept.shape[2]
+    half = size // 2
+    lengths = [size] * 4 + [size + half] * 2 + [size]
+    starts = [0, size, 2 * size, 3 * size, 0, size + half, 2 * (size + half)]
+    other_refs = [
+        other_refs[i // 4].at[pl.ds(at, length)] for i, (at, length) in enumerate(zip(starts, lengths))
+    ]
+    h_copies = []
+    for i, (ref, at, count) in enumerate(zip(h_refs, (0, 1, 2, 4, 5, 6), (1, 1, 2, 1, 1, 2))):
+        h_copies.append(pltpu.make_async_copy(ref, h_kept.at[pl.ds(at, count)], h_sem.at[i]))
+    for copy in h_copies:
+        copy.start()
+
+    low, high = pl.ds(0, half), pl.ds(half, half)
+
+    def pieces(parts):
+        block, other, before, nxt, up, down, far = parts
+        for whole in (block, other, before, nxt):
+            yield whole.at[low], whole.at[high]
+        yield up.at[pl.ds(size, half)], down.at[pl.ds(size, half)]
+        for whole in (up, down, far):
+            yield whole.at[low], whole.at[high]
+
+    for j, sources_ in enumerate(zip(pieces(own_refs), pieces(other_refs))):
+        for side, halves in enumerate(sources_):
+            for part, source in enumerate(halves):
+                target = p_kept.at[side, j, pl.ds(part * half, half)]
+                pltpu.make_async_copy(source, target, p_sem.at[side, j, part]).start()
+
+    first = order[16] == 0
+    t_low, t_high = teacher[:, :width], teacher[:, width:]
+    total[0] = -jnp.where(first, t_low, t_high)
+    total[1] = -jnp.where(first, t_high, t_low)
+    for copy in h_copies:
+        copy.wait()
+
+    @pl.loop(0, 8)
+    def _(j):
+        h = h_kept[order[j]]
+        for side in range(2):
+            for part in range(2):
+                target = p_kept.at[side, j, pl.ds(part * half, half)]
+                pltpu.make_async_copy(target, target, p_sem.at[side, j, part]).wait()
+            total[side] += jnp.dot(h, p_kept[side, j], preferred_element_type=F32)
+
+    squares = total[0] * total[0] + total[1] * total[1]
+    value = jnp.broadcast_to(jnp.sum(squares, keepdims=True), (1, width))
+    residual[...] = total[...].astype(BF16)
+    row = lax.broadcasted_iota(jnp.int32, (NOTE, width), 0)
+    top = value.astype(BF16).astype(F32)
+    middle = (value - top).astype(BF16).astype(F32)
+    bottom = value - top - middle
+    note = jnp.where(row == 0, top, jnp.where(row == 1, middle, jnp.where(row == 2, bottom, 0.0)))
+    note = note.astype(BF16)
+
+    @pl.loop(0, 8)
+    def _(j):
         dims = (((1,), (1,)), ((), ()))
-        back = lax.dot_general(total[0].astype(BF16), kept[0, block], dims, preferred_element_type=F32)
-        back += lax.dot_general(total[1].astype(BF16), kept[1, block], dims, preferred_element_type=F32)
-        out[:n] = back.astype(BF16)
-        value = square[:1]
-        row = lax.broadcasted_iota(jnp.int32, (NOTE, width), 0)
-        top = value.astype(BF16).astype(F32)
-        middle = (value - top).astype(BF16).astype(F32)
-        bottom = value - top - middle
-        note = jnp.where(row == 0, top, jnp.where(row == 1, middle, jnp.where(row == 2, bottom, 0.0)))
-        out[n:] = note.astype(BF16)
+        back = lax.dot_general(residual[0], p_kept[0, j], dims, preferred_element_type=F32)
+        back += lax.dot_general(residual[1], p_kept[1, j], dims, preferred_element_type=F32)
+        out[order[8 + j], :n] = back.astype(BF16)
+        out[order[8 + j], n:] = note
 
 
 def project(order, hidden, own, other, teacher):
-    blocks, size, width = own.shape
+    size, width = own[0].shape
     rows = teacher.shape[0]
-    last = blocks - 1
-    p_spec = pl.BlockSpec(
-        (None, size, width), lambda s, b, order: (order[blocks + b * (1 - s) + last * s], 0, 0)
-    )
+    anywhere = pl.BlockSpec(memory_space=pl.ANY)
+    inside = pl.BlockSpec(memory_space=pltpu.VMEM)
     return pl.pallas_call(
         project_kernel,
-        grid_spec=pltpu.PrefetchScalarGridSpec(
-            num_scalar_prefetch=1,
-            grid=(2, blocks),
-            in_specs=[
-                pl.BlockSpec((None, rows, size), lambda s, b, order: (order[b * (1 - s) + last * s], 0, 0)),
-                p_spec,
-                p_spec,
-                pl.BlockSpec((rows, 2 * width), lambda s, b, order: (0, 0)),
-            ],
-            out_specs=pl.BlockSpec((None, rows + NOTE, size), lambda s, b, order: (order[2 * blocks + b * s], 0, 0)),
-            scratch_shapes=[
-                pltpu.VMEM((2, rows, width), F32),
-                pltpu.VMEM((2, blocks, size, width), BF16),
-                pltpu.VMEM((8, size), F32),
-            ],
+        in_specs=[pl.BlockSpec(memory_space=pltpu.SMEM)] + [anywhere] * 15 + [inside],
+        out_specs=inside,
+        scratch_shapes=[
+            pltpu.VMEM((8, rows, size), BF16),
+            pltpu.VMEM((2, 8, size, width), BF16),
+            pltpu.VMEM((2, rows, width), F32),
+            pltpu.VMEM((2, rows, width), BF16),
+            pltpu.SemaphoreType.DMA((6,)),
+            pltpu.SemaphoreType.DMA((2, 8, 2)),
+        ],
+        out_shape=jax.ShapeDtypeStruct((8, rows + NOTE, size), BF16),
+        compiler_params=pltpu.CompilerParams(vmem_limit_bytes=32 * 1024 * 1024),
+        cost_estimate=pl.CostEstimate(
+            flops=64 * rows * size * width, bytes_accessed=32 * size * width, transcendentals=0
         ),
-        out_shape=jax.ShapeDtypeStruct((blocks, rows + NOTE, size), BF16),
-        compiler_params=pltpu.CompilerParams(
-            dimension_semantics=("arbitrary", "arbitrary"), vmem_limit_bytes=32 * 1024 * 1024
-        ),
-        cost_estimate=pl.CostEstimate(
-            flops=8 * rows * blocks * size * width, bytes_accessed=4 * blocks * size * width, transcendentals=0
-        ),
-    )(order, hidden, own, other, teacher)
+    )(order, *hidden, *own, *other, teacher)
 
 
 def teach_kernel(role, tokens, weight, out, away):
@@ -227,20 +227,31 @@
         at = ((zt - k) & 3) * 2
         pair = lax.dynamic_slice_in_dim(own, at, 2, axis=0) + lax.dynamic_slice_in_dim(away, at, 2, axis=0).astype(F32)
         teacher[k] = pair if k == 0 else pair.astype(BF16)
-    teacher[1], teacher[-1], theirs, p_other, *w_middle = lax.optimization_barrier(
-        (teacher[1], teacher[-1], theirs, p_other, *w_middle)
+    teacher[0], teacher[1], teacher[-1], teacher[2] = lax.optimization_barrier(
+        (teacher[0], teacher[1], teacher[-1], teacher[2])
+    )
+
+    projector, p_other, theirs, teacher[1], teacher[-1], *w_middle = lax.optimization_barrier(
+        (projector, p_other, theirs, teacher[1], teacher[-1], *w_middle)
     )
     for k in (1, -1):
         teacher[k] = shift(teacher[k], "tensor", -k, 0)
-
-    weight = gather_end(student_weight, w_first, w_middle, "dp")
+    student = jnp.concatenate([mine, theirs], axis=0)
+    up, down = w_middle
+    w_far = shift(jnp.concatenate([up[feat:], down[feat:]], axis=0), "dp", 0, 1)
     p_first = [shift(projector, "dp", 1, 0), shift(projector, "dp", -1, 0)]
-    weight[-1], *p_first = lax.optimization_barrier((weight[-1], *p_first))
+    w_far, *p_first = lax.optimization_barrier((w_far, *p_first))
     p_first = [p_other, *p_first]
 
-    weight = place(weight, sources("dp"), 0)
-    student = jnp.concatenate([mine, theirs], axis=0)
-    pre = dot(student, weight)
+    part = feat // 2
+    at = sources("dp")
+    pre = 0.0
+    for j, block in enumerate((student_weight, *w_first, None, up[:feat], down[:feat], w_far)):
+        columns = lax.dynamic_slice_in_dim(student, at[j] * feat, feat, axis=1)
+        if block is None:
+            pre = pre + dot(columns[:, :part], up[feat:]) + dot(columns[:, part:], down[feat:])
+        else:
+            pre = pre + dot(columns, block)
     pre = pre[:own_rows] + flip(pre[own_rows:])
     sigma = jax.nn.sigmoid(pre)
     hidden = (pre * sigma).astype(BF16)
@@ -251,31 +262,33 @@
     )
     h_other = shift(hidden, "tensor", 0, 1)
     teacher[2] = shift(teacher[2], "tensor", 2, 0)
-    h_other, *p_middle = lax.optimization_barrier((h_other, *p_middle))
+    near = lax.optimization_barrier(teacher[0] + teacher[1].astype(F32) + teacher[-1].astype(F32))
+    p_flip = flip(jnp.concatenate([projector, *p_first], axis=0))
+    h_other, up, down, p_flip = lax.optimization_barrier((h_other, *p_middle, p_flip))
     h_pair = jnp.concatenate([hidden, h_other], axis=0)
     h_before, h_after = shift(h_pair, "tensor", 1, 0), shift(h_pair, "tensor", -1, 0)
-    p_own = gather_end(projector, p_first, p_middle, "dp")
-    h_before, h_after, teacher[2], p_own[-1] = lax.optimization_barrier((h_before, h_after, teacher[2], p_own[-1]))
-    h_far = jnp.concatenate(
-        [shift(h_before[:own_rows], "tensor", 1, 0), shift(h_after[own_rows:], "tensor", -1, 0)], axis=0
-    )
-    p_own = place(p_own, sources("dp"), 0)
-    p_flip = flip(p_own)
-    hidden = jnp.concatenate([h_pair, h_after, h_far, h_before], axis=0).reshape(n_tensor, own_rows, hid)
-    p_own, p_flip = p_own.reshape(n_data, hid, cols), p_flip.reshape(n_data, hid, cols)
-
-    teacher = teacher[0] + sum(teacher[k].astype(F32) for k in (1, -1, 2))
-    cross = lax.dynamic_index_in_dim(teacher, 1 - xh, 0, False).astype(BF16)
-    teacher = lax.dynamic_index_in_dim(teacher, xh, 0, False) + shift(cross, "tensor", 0, 1).astype(F32)
-
+    p_far = shift(jnp.concatenate([up[feat:], down[feat:]], axis=0), "dp", 0, 1)
+    h_before, h_after, teacher[2], p_far = lax.optimization_barrier((h_before, h_after, teacher[2], p_far))
+    far_0 = shift(h_before[:own_rows], "tensor", 1, 0)
+    far_1 = shift(h_after[own_rows:], "tensor", -1, 0)
+    p_own = [projector, *p_first, up, down, p_far]
+    p_flip = [p_flip, flip(jnp.concatenate([up, down, p_far], axis=0))]
+
+    near = near + teacher[2].astype(F32)
+    cross = lax.dynamic_index_in_dim(near, 1 - xh, 0, False).astype(BF16)
+    teacher = lax.dynamic_index_in_dim(near, xh, 0, False) + shift(cross, "tensor", 0, 1).astype(F32)
+
+    def ring_blocks(x):
+        return x.reshape(-1, own_rows, hid)
+
+    pieces = [ring_blocks(x) for x in (hidden, h_other, h_after, far_0, far_1, h_before)]
     order = (
-        list(range(n_tensor))
-        + list(range(n_data))
-        + [(((zt + b // 2) & 3) * 2) + ((b % 2) ^ xh) for b in range(n_tensor)]
+        at
+        + [((((zt + (d >> 1)) & 3) << 1) | ((d & 1) ^ xh)) for d in at]
         + [role]
     )
     order = jnp.stack([jnp.asarray(x, jnp.int32) for x in order])
-    back = project(order, hidden, p_own, p_flip, teacher)
+    back = project(order, pieces, p_own, p_flip, teacher)
     back = lax.all_to_all(back, "tensor", 0, 0, tiled=True)
     back = jnp.sum(back.astype(F32), axis=0)
     square = join_note(back[own_rows:])

time: 279 us -> 270 us (0.968)
  local copies, waits for them, and re-layouts: 46.1 us -> 18.6 us
  waiting for transfers between devices: 76.2 us -> 88.7 us
  matrix products: 9.17 us -> 14.4 us
    dynamic_update_slice x14 -> x0, local copies, waits for them, and re-layouts: 19.8 us -> none  [place(): out = lax.dynamic_update_slice_in_dim(out, block, s * size, axis=dim)]
    ppermute x21, waiting for transfers between devices: 45.2 us -> 56.1 us  [shift(): return lax.ppermute(value, axis, perm)]
    ppermute x21, starting transfers between devices: 31.4 us -> 36.6 us  [shift(): return lax.ppermute(value, axis, perm)]
    dot_general x2 -> x10, matrix products: 9.17 us -> 14.4 us  [dot(): return lax.dot_general(a, b, (dims, ((), ())), preferred_element_type=F32)]
    another operation x2 -> x0, local copies, waits for them, and re-layouts: 4.65 us -> none
    ppermute x1, starting transfers between devices: 5.36 us -> 1.69 us  [shards(): projector = lax.ppermute(projector, ('dp', 'tensor'), swap)]
    convert_element_type x1, other arithmetic: 4.47 us -> 7.73 us  [shards(): teacher[k] = pair if k == 0 else pair.astype(BF16)]
    slice x6 -> x7, local copies, waits for them, and re-layouts: 5.34 us -> 2.48 us  [the longest x1 1.1 us: shards(): far_0 = shift(h_before[:own_rows], 'tensor', 1, 0)]
  transfers between devices with their start and end apart: 28 -> 29, of which waited for: 10 -> 13; matrix products, arithmetic and copies ran while one was open for 20% -> 13% of each run, Pallas kernels for 5% -> 5%
where the time goes in v6:
time: 270 us; the launch traced here: 269 us
  waiting for transfers between devices  88.7 us (33%)
  blocking collectives  54 us (20%)
  starting transfers between devices  44.1 us (16%)
  Pallas kernels  25.7 us (10%)
  other arithmetic  20.9 us (8%)
  local copies, waits for them, and re-layouts  18.6 us (7%)
  matrix products  14.4 us (5%)
  between operations  3.06 us (1%)
    ppermute x21, waiting for transfers between devices, shift(): return lax.ppermute(value, axis, perm)  56.1 us
    all_to_all x1, blocking collectives, shards(): grad = lax.all_to_all(grad, 'dp', 0, 0, tiled=True)  54 us
    ppermute x21, starting transfers between devices, shift(): return lax.ppermute(value, axis, perm)  36.6 us
    all_to_all x1, waiting for transfers between devices, shards(): back = lax.all_to_all(back, 'tensor', 0, 0, tiled=True)  29.7 us
    dot_general x10, matrix products, dot(): return lax.dot_general(a, b, (dims, ((), ())), preferred_element_type=F32)  14.4 us
    pallas_call x1, Pallas kernels, teach(): pl.pallas_call(teach_kernel, grid_spec=pltpu.PrefetchScalarGridSpec(num_s...  13.3 us
    pallas_call x1, Pallas kernels, project(): pl.pallas_call(project_kernel, in_specs=[pl.BlockSpec(memory_space=pltpu....  12.4 us
    unnamed x59, local copies, waits for them, and re-layouts  9.34 us
  transfers between devices with their start and end apart: 29, of which 13 were waited for; matrix products, arithmetic and copies ran while one was open for 13% of the time, Pallas kernels for 5%

profile of v6, /device:TPU:0, one launch (start us, length us, event | category | flops | bytes accessed | tf_op | source)
XLA Modules:
  0.0 269.3 jit_solution(4728116518504544772)
XLA Ops:
  0.6 1.7 collective-permute-start.1
  2.3 1.6 collective-permute-start.2
  3.9 1.7 collective-permute-start.3
  5.5 1.7 collective-permute-start
  7.2 1.2 copy-done.11
  8.4 13.3 %shard_map.68 = (f32[8,256,1024]{2,1,0:T(8,128)S(1)}, bf16[8,256,1024]{2,1,0:T(8,128)(2,1)}) custom-call(s32[1]{0:T(128)} %bitcast.role, bf16[512,1024]{1,0:T(8,128)(2,1)S(1)} %bitcast.39, bf16[1024,8192]{1,0:T(8,128)(2,1)} %weight.1), custom_call_target="tpu_custom_call" | custom-call | flops 8589934592 | bytes 16777216 | tf_op jit(solution)/shard_map/pallas_call | solution.py:171
  21.7 3.3 %copy-done = f32[8,256,1024]{2,1,0:T(8,128)} copy-done((f32[8,256,1024]{2,1,0:T(8,128)}, f32[8,256,1024]{2,1,0:T(8,128)S(1)}, u32[]{:S(2)}) %copy-start) | copy-done | bytes 8388632
  25.2 5.1 %constant_dynamic-slice_fusion = (bf16[256,4096]{1,0:T(8,128)(2,1)}, bf16[256,4096]{1,0:T(8,128)(2,1)}) fusion(bf16[256,8192]{1,0:T(8,128)(2,1)} %param.7, s32[]{:T(128)S(6)} %select_n.86, s32[]{:T(128)S(6)} %select_n.85), kind=kLoop, calls=%fused_computation.85 | loop fusion | bytes 8388616 | tf_op jit(solution)/shard_map/dynamic_slice | solution.py:222
  30.4 1.3 pad_maximum_fusion.5
  31.7 5.0 %collective-permute-start.7 = (bf16[768,512]{1,0:T(8,128)(2,1)}, bf16[768,512]{1,0:T(8,128)(2,1)S(1)}, u32[]{:S(2)}, u32[]{:S(2)}) collective-permute-start(bf16[768,512]{1,0:T(8,128)(2,1)} %get-tuple-element.77), channel_id=1, source_target_pairs={{0,16},{8,24},{16,32},{24,40},{32,48},{40,56},{48,0},{56,8},{1,17}... | collective-permute-start | bytes 2359304 | tf_op jit(solution)/shard_map/ppermute | solution.py:16
  36.7 4.8 %collective-permute-start.8 = (bf16[768,512]{1,0:T(8,128)(2,1)}, bf16[768,512]{1,0:T(8,128)(2,1)S(1)}, u32[]{:S(2)}, u32[]{:S(2)}) collective-permute-start(bf16[768,512]{1,0:T(8,128)(2,1)} %get-tuple-element.76), channel_id=1, source_target_pairs={{0,48},{8,56},{16,0},{24,8},{32,16},{40,24},{48,32},{56,40},{1,49}... | collective-permute-start | bytes 2359304 | tf_op jit(solution)/shard_map/ppermute | solution.py:16
  41.5 7.7 %add_convert_fusion = (bf16[2,256,1024]{2,1,0:T(8,128)(2,1)S(1)}, bf16[2,256,1024]{2,1,0:T(8,128)(2,1)S(1)}, bf16[2,256,1024]{2,1,0:T(8,128)(2,1)S(1)}, f32[2,256,1024]{2,1,0:T(8,128)}) fusion(f32[8,256,1024]{2,1,0:T(8,128)} %copy-done, s32[]{:T(128)S(6)} %select_n.90, bf16[8,256,1024]{2,1,0:T(8,128)(2,1)} %collective-permute-done.6, s32[]{:T(128)S(6)} %select_n.89, ...), kind=kLoop, calls=%fused_computation.25 | loop fusion | flops 5767168 | bytes 17825808 | tf_op jit(solution)/shard_map/convert_element_type | solution.py:229
  49.2 6.3 %collective-permute-done.4.refs_7_ = bf16[512,512]{1,0:T(8,128)(2,1)S(1)} collective-permute-done((bf16[512,512]{1,0:T(8,128)(2,1)S(1)}, bf16[512,512]{1,0:T(8,128)(2,1)S(1)}, u32[]{:S(2)}, u32[]{:S(2)}) %collective-permute-start.4) | collective-permute-done | bytes 524320 | tf_op jit(solution)/shard_map/ppermute | solution.py:16
  55.5 4.4 %collective-permute-done.7 = bf16[768,512]{1,0:T(8,128)(2,1)S(1)} collective-permute-done((bf16[768,512]{1,0:T(8,128)(2,1)}, bf16[768,512]{1,0:T(8,128)(2,1)S(1)}, u32[]{:S(2)}, u32[]{:S(2)}) %collective-permute-start.7) | collective-permute-done | bytes 786464 | tf_op jit(solution)/shard_map/ppermute | solution.py:16
  60.7 1.1 collective-permute-start.10
  61.9 2.1 collective-permute-start.11
  66.2 1.4 fusion.26
  69.7 1.4 convolution_add_fusion.4
  71.1 1.4 fusion.24
  72.6 1.4 fusion.2
  74.1 5.3 %collective-permute-done.9 = bf16[512,512]{1,0:T(8,128)(2,1)S(1)} collective-permute-done((bf16[512,512]{1,0:T(8,128)(2,1)S(1)}, bf16[512,512]{1,0:T(8,128)(2,1)S(1)}, u32[]{:S(2)}, u32[]{:S(2)}) %collective-permute-start.9) | collective-permute-done | bytes 524320 | tf_op jit(solution)/shard_map/ppermute | solution.py:16
  79.6 1.4 convolution_add_fusion.2
  81.0 1.4 convolution_add_fusion.1
  82.4 1.4 convolution_add_fusion
  84.8 1.3 collective-permute-done.12
  86.1 1.9 collective-permute-start.17
  88.3 3.8 %collective-permute-done.13 = bf16[2,256,1024]{2,1,0:T(8,128)(2,1)S(1)} collective-permute-done((bf16[2,256,1024]{2,1,0:T(8,128)(2,1)S(1)}, bf16[2,256,1024]{2,1,0:T(8,128)(2,1)S(1)}, u32[]{:S(2)}, u32[]{:S(2)}) %collective-permute-start.13) | collective-permute-done | bytes 1048608 | tf_op jit(solution)/shard_map/ppermute | solution.py:16
  92.1 1.3 collective-permute-done.14
  94.2 3.0 %collective-permute-start.15 = (bf16[256,512]{1,0:T(8,128)(2,1)S(1)}, bf16[256,512]{1,0:T(8,128)(2,1)S(1)}, u32[]{:S(2)}, u32[]{:S(2)}) collective-permute-start(bf16[256,512]{1,0:T(8,128)(2,1)S(1)} %multiply_convert_fusion), channel_id=1, source_target_pairs={{0,1},{1,0},{2,3},{3,2},{4,5},{5,4},{6,7},{7,6},{8,9},{9,8},{10,11... | collective-permute-start | bytes 786440 | tf_op jit(solution)/shard_map/ppermute | solution.py:16
  97.2 8.3 %collective-permute-done.16.refs_10_ = bf16[768,512]{1,0:T(8,128)(2,1)S(1)} collective-permute-done((bf16[768,512]{1,0:T(8,128)(2,1)S(1)}, bf16[768,512]{1,0:T(8,128)(2,1)S(1)}, u32[]{:S(2)}, u32[]{:S(2)}) %collective-permute-start.16) | collective-permute-done | bytes 786464 | tf_op jit(solution)/shard_map/ppermute | solution.py:16
  106.6 3.2 %collective-permute-start.20 = (bf16[512,512]{1,0:T(8,128)(2,1)S(1)}, bf16[512,512]{1,0:T(8,128)(2,1)}, u32[]{:S(2)}, u32[]{:S(2)}) collective-permute-start(bf16[512,512]{1,0:T(8,128)(2,1)S(1)} %constant_dynamic-update-slice_fusion), channel_id=1, source_target_pairs={{0,6},{1,7},{2,0},{3,1},{4,2},{5,3},{6,4},{7,5},{8,14},{9,15},{10,... | collective-permute-start | bytes 1572872 | tf_op jit(solution)/shard_map/ppermute | solution.py:16
  109.8 11.3 %collective-permute-done.21 = bf16[2,256,1024]{2,1,0:T(8,128)(2,1)S(1)} collective-permute-done((bf16[2,256,1024]{2,1,0:T(8,128)(2,1)S(1)}, bf16[2,256,1024]{2,1,0:T(8,128)(2,1)S(1)}, u32[]{:S(2)}, u32[]{:S(2)}) %collective-permute-start.21) | collective-permute-done | bytes 1048608 | tf_op jit(solution)/shard_map/ppermute | solution.py:16
  121.1 7.7 %collective-permute-done.19 = bf16[512,512]{1,0:T(8,128)(2,1)S(1)} collective-permute-done((bf16[512,512]{1,0:T(8,128)(2,1)S(1)}, bf16[512,512]{1,0:T(8,128)(2,1)S(1)}, u32[]{:S(2)}, u32[]{:S(2)}) %collective-permute-start.19) | collective-permute-done | bytes 524320 | tf_op jit(solution)/shard_map/ppermute | solution.py:16
  129.6 1.5 pad_maximum_fusion.4
  131.2 2.7 %convert_add_fusion.1 = f32[2,256,1024]{2,1,0:T(8,128)S(1)} fusion(bf16[2,256,1024]{2,1,0:T(8,128)(2,1)} %copy-done.27, f32[2,256,1024]{2,1,0:T(8,128)} %get-tuple-element.64, bf16[2,256,1024]{2,1,0:T(8,128)(2,1)} %copy-done.26), kind=kLoop, calls=%fused_computation.24 | loop fusion | flops 2097152 | bytes 6291456 | tf_op jit(solution)/shard_map/add | solution.py:265
  134.5 1.4 copy-done.15
  136.7 3.8 %collective-permute-start.26 = (bf16[256,1024]{1,0:T(8,128)(2,1)}, bf16[256,1024]{1,0:T(8,128)(2,1)}, u32[]{:S(2)}, u32[]{:S(2)}) collective-permute-start(bf16[256,1024]{1,0:T(8,128)(2,1)} %fusion.16), channel_id=1, source_target_pairs={{0,1},{1,0},{2,3},{3,2},{4,5},{5,4},{6,7},{7,6},{8,9},{9,8},{10,11... | collective-permute-start | bytes 1572872 | tf_op jit(solution)/shard_map/ppermute | solution.py:16
  142.8 3.3 %collective-permute-start.24 = (bf16[256,512]{1,0:T(8,128)(2,1)S(1)}, bf16[256,512]{1,0:T(8,128)(2,1)S(1)}, u32[]{:S(2)}, u32[]{:S(2)}) collective-permute-start(bf16[256,512]{1,0:T(8,128)(2,1)S(1)} %slice.86), channel_id=1, source_target_pairs={{0,6},{1,7},{2,0},{3,1},{4,2},{5,3},{6,4},{7,5},{8,14},{9,15},{10,... | collective-permute-start | bytes 786440 | tf_op jit(solution)/shard_map/ppermute | solution.py:16
  146.0 7.3 %collective-permute-done.26 = bf16[256,1024]{1,0:T(8,128)(2,1)} collective-permute-done((bf16[256,1024]{1,0:T(8,128)(2,1)}, bf16[256,1024]{1,0:T(8,128)(2,1)}, u32[]{:S(2)}, u32[]{:S(2)}) %collective-permute-start.26) | collective-permute-done | bytes 524320 | tf_op jit(solution)/shard_map/ppermute | solution.py:16
  153.4 1.6 bitcast_add_fusion.refs_15_
  155.0 1.6 copy-done.10
  156.6 12.4 %shard_map.69 = bf16[8,272,512]{2,1,0:T(8,128)(2,1)} custom-call(s32[17]{0:T(128)S(1)} %stack.68.order, bf16[1,256,512]{2,1,0:T(8,128)(2,1)S(1)} %bitcast.36, bf16[1,256,512]{2,1,0:T(8,128)(2,1)S(1)} %bitcast.37, bf16[2,256,512]{2,1,0:T(8,128)(2,1)} %bitcast.20.refs_2_, bf16[1,256,512]{2,1,0:T(8,128)(2,1)S(1)} %bitcast.40, ...), custom_call_target="tpu_custom_call" | custom-call | flops 4294967296 | bytes 8388608 | tf_op jit(solution)/shard_map/pallas_call | solution.py:135
  169.0 4.6 %all-to-all-start = ((bf16[8,272,512]{2,1,0:T(8,128)(2,1)}), bf16[8,272,512]{2,1,0:T(8,128)(2,1)S(1)}, u32[]{:S(2)}, u32[]{:S(2)}) async-start(bf16[8,272,512]{2,1,0:T(8,128)(2,1)} %shard_map.69), calls=%async_computation | async-start | bytes 4456448 | tf_op jit(solution)/shard_map/all_to_all | solution.py:292
  173.6 29.7 %all-to-all-done = bf16[8,272,512]{2,1,0:T(8,128)(2,1)S(1)} async-done(((bf16[8,272,512]{2,1,0:T(8,128)(2,1)}), bf16[8,272,512]{2,1,0:T(8,128)(2,1)S(1)}, u32[]{:S(2)}, u32[]{:S(2)}) %all-to-all-start) | async-done | bytes 2228256 | tf_op jit(solution)/shard_map/all_to_all | solution.py:292
  203.7 1.4 fusion.18
  205.3 1.5 collective-permute-done.27
  206.8 4.0 %convolution_convert_fusion = bf16[4096,512]{1,0:T(8,128)(2,1)S(1)} fusion(bf16[256,4096]{1,0:T(8,128)(2,1)} %collective-permute-done.5, bf16[256,4096]{1,0:T(8,128)(2,1)S(1)} %copy-done.13, bf16[256,512]{1,0:T(8,128)(2,1)S(1)} %slice.100, bf16[256,512]{1,0:T(8,128)(2,1)S(1)} %fusion.18), kind=kOutput, calls=%fused_computation.18 | convolution fusion | flops 2159017984 | bytes 8912896 | tf_op jit(solution)/shard_map/dot_general | solution.py:45
  211.3 54.0 %all_to_all.10 = bf16[8,528,512]{2,1,0:T(8,128)(2,1)S(1)} all-to-all(bf16[8,528,512]{2,1,0:T(8,128)(2,1)S(1)} %pad_maximum_fusion.1), channel_id=1, replica_groups=mesh['role'=2,'dp'=8,'tensor'=8] {'dp'}, dimensions={0} | all-to-all | bytes 8650752 | tf_op jit(solution)/shard_map/all_to_all | solution.py:305
  (128 shorter events, 16.4 us)
Async XLA Ops:
  0.6 24.4 %collective-permute-start.1 = (bf16[512,512]{1,0:T(8,128)(2,1)}, bf16[512,512]{1,0:T(8,128)(2,1)S(1)}, u32[]{:S(2)}, u32[]{:S(2)}) collective-permute-start(bf16[512,512]{1,0:T(8,128)(2,1)} %param.8), channel_id=1, source_target_pairs={{0,8},{8,0},{16,24},{24,16},{32,40},{40,32},{48,56},{56,48},{1,9},... | collective-permute-start | bytes 1572872 | tf_op jit(solution)/shard_map/ppermute | solution.py:16
  2.3 22.8 %collective-permute-start.2 = (bf16[512,512]{1,0:T(8,128)(2,1)}, bf16[512,512]{1,0:T(8,128)(2,1)S(1)}, u32[]{:S(2)}, u32[]{:S(2)}) collective-permute-start(bf16[512,512]{1,0:T(8,128)(2,1)} %param.8), channel_id=1, source_target_pairs={{0,16},{8,24},{16,32},{24,40},{32,48},{40,56},{48,0},{56,8},{1,17}... | collective-permute-start | bytes 1572872 | tf_op jit(solution)/shard_map/ppermute | solution.py:16
  3.9 21.2 %collective-permute-start.3 = (bf16[512,512]{1,0:T(8,128)(2,1)}, bf16[512,512]{1,0:T(8,128)(2,1)S(1)}, u32[]{:S(2)}, u32[]{:S(2)}) collective-permute-start(bf16[512,512]{1,0:T(8,128)(2,1)} %param.8), channel_id=1, source_target_pairs={{0,48},{8,56},{16,0},{24,8},{32,16},{40,24},{48,32},{56,40},{1,49}... | collective-permute-start | bytes 1572872 | tf_op jit(solution)/shard_map/ppermute | solution.py:16
  5.5 19.5 %collective-permute-start = (bf16[512,512]{1,0:T(8,128)(2,1)}, bf16[512,512]{1,0:T(8,128)(2,1)S(1)}, u32[]{:S(2)}, u32[]{:S(2)}) collective-permute-start(bf16[512,512]{1,0:T(8,128)(2,1)} %param.9), channel_id=1, source_target_pairs={{0,0},{1,8},{2,16},{3,24},{4,32},{5,40},{6,48},{7,56},{8,9},{9,1},... | collective-permute-start | bytes 1572872 | tf_op jit(solution)/shard_map/ppermute | solution.py:212
  21.7 3.3 %copy-start = (f32[8,256,1024]{2,1,0:T(8,128)}, f32[8,256,1024]{2,1,0:T(8,128)S(1)}, u32[]{:S(2)}) copy-start(f32[8,256,1024]{2,1,0:T(8,128)S(1)} %get-tuple-element.37) | copy-start | bytes 25165828
  25.0 54.3 %copy-start.1 = (bf16[512,512]{1,0:T(8,128)(2,1)}, bf16[512,512]{1,0:T(8,128)(2,1)S(1)}, u32[]{:S(2)}) copy-start(bf16[512,512]{1,0:T(8,128)(2,1)S(1)} %collective-permute-done.refs_6_) | copy-start | bytes 1572868
  25.1 5.3 %copy-start.20 = (bf16[512,512]{1,0:T(8,128)(2,1)}, bf16[512,512]{1,0:T(8,128)(2,1)S(1)}, u32[]{:S(2)}) copy-start(bf16[512,512]{1,0:T(8,128)(2,1)S(1)} %collective-permute-done.2) | copy-start | bytes 1572868
  25.1 5.3 %copy-start.22 = (bf16[512,512]{1,0:T(8,128)(2,1)}, bf16[512,512]{1,0:T(8,128)(2,1)S(1)}, u32[]{:S(2)}) copy-start(bf16[512,512]{1,0:T(8,128)(2,1)S(1)} %collective-permute-done.3) | copy-start | bytes 1572868
  25.1 16.4 %collective-permute-start.6 = (bf16[8,256,1024]{2,1,0:T(8,128)(2,1)}, bf16[8,256,1024]{2,1,0:T(8,128)(2,1)}, u32[]{:S(2)}, u32[]{:S(2)}) collective-permute-start(bf16[8,256,1024]{2,1,0:T(8,128)(2,1)} %get-tuple-element.38), channel_id=1, source_target_pairs={{0,64},{64,0},{1,65},{65,1},{2,66},{66,2},{3,67},{67,3},{4,68},{68... | collective-permute-start | bytes 12582920 | tf_op jit(solution)/shard_map/ppermute | solution.py:20
  30.3 30.4 %collective-permute-start.5 = (bf16[256,4096]{1,0:T(8,128)(2,1)}, bf16[256,4096]{1,0:T(8,128)(2,1)}, u32[]{:S(2)}, u32[]{:S(2)}) collective-permute-start(bf16[256,4096]{1,0:T(8,128)(2,1)} %get-tuple-element.72), channel_id=1, source_target_pairs={{0,64},{64,0},{1,65},{65,1},{2,66},{66,2},{3,67},{67,3},{4,68},{68... | collective-permute-start | bytes 6291464 | tf_op jit(solution)/shard_map/ppermute | solution.py:20
  31.7 28.1 %collective-permute-start.7 = (bf16[768,512]{1,0:T(8,128)(2,1)}, bf16[768,512]{1,0:T(8,128)(2,1)S(1)}, u32[]{:S(2)}, u32[]{:S(2)}) collective-permute-start(bf16[768,512]{1,0:T(8,128)(2,1)} %get-tuple-element.77), channel_id=1, source_target_pairs={{0,16},{8,24},{16,32},{24,40},{32,48},{40,56},{48,0},{56,8},{1,17}... | collective-permute-start | bytes 2359304 | tf_op jit(solution)/shard_map/ppermute | solution.py:16
  36.7 23.1 %collective-permute-start.8 = (bf16[768,512]{1,0:T(8,128)(2,1)}, bf16[768,512]{1,0:T(8,128)(2,1)S(1)}, u32[]{:S(2)}, u32[]{:S(2)}) collective-permute-start(bf16[768,512]{1,0:T(8,128)(2,1)} %get-tuple-element.76), channel_id=1, source_target_pairs={{0,48},{8,56},{16,0},{24,8},{32,16},{40,24},{48,32},{56,40},{1,49}... | collective-permute-start | bytes 2359304 | tf_op jit(solution)/shard_map/ppermute | solution.py:16
  41.5 14.0 %collective-permute-start.4 = (bf16[512,512]{1,0:T(8,128)(2,1)S(1)}, bf16[512,512]{1,0:T(8,128)(2,1)S(1)}, u32[]{:S(2)}, u32[]{:S(2)}) collective-permute-start(bf16[512,512]{1,0:T(8,128)(2,1)S(1)} %collective-permute-done.refs_6_), channel_id=1, source_target_pairs={{0,8},{8,0},{16,24},{24,16},{32,40},{40,32},{48,56},{56,48},{1,9},... | collective-permute-start | bytes 1572872 | tf_op jit(solution)/shard_map/ppermute | solution.py:16
  41.5 22.5 %copy-start.12 = (bf16[256,4096]{1,0:T(8,128)(2,1)S(1)}, bf16[256,4096]{1,0:T(8,128)(2,1)}, u32[]{:S(2)}) copy-start(bf16[256,4096]{1,0:T(8,128)(2,1)} %get-tuple-element.73) | copy-start | bytes 6291460
  60.7 18.6 %collective-permute-start.10 = (bf16[512,512]{1,0:T(8,128)(2,1)S(1)}, bf16[512,512]{1,0:T(8,128)(2,1)S(1)}, u32[]{:S(2)}, u32[]{:S(2)}) collective-permute-start(bf16[512,512]{1,0:T(8,128)(2,1)S(1)} %collective-permute-done.refs_6_), channel_id=1, source_target_pairs={{0,16},{8,24},{16,32},{24,40},{32,48},{40,56},{48,0},{56,8},{1,17}... | collective-permute-start | bytes 1572872 | tf_op jit(solution)/shard_map/ppermute | solution.py:16
  61.9 17.5 %collective-permute-start.11 = (bf16[512,512]{1,0:T(8,128)(2,1)S(1)}, bf16[512,512]{1,0:T(8,128)(2,1)S(1)}, u32[]{:S(2)}, u32[]{:S(2)}) collective-permute-start(bf16[512,512]{1,0:T(8,128)(2,1)S(1)} %collective-permute-done.refs_6_), channel_id=1, source_target_pairs={{0,48},{8,56},{16,0},{24,8},{32,16},{40,24},{48,32},{56,40},{1,49}... | collective-permute-start | bytes 1572872 | tf_op jit(solution)/shard_map/ppermute | solution.py:16
  66.1 13.2 %collective-permute-start.9 = (bf16[512,512]{1,0:T(8,128)(2,1)S(1)}, bf16[512,512]{1,0:T(8,128)(2,1)S(1)}, u32[]{:S(2)}, u32[]{:S(2)}) collective-permute-start(bf16[512,512]{1,0:T(8,128)(2,1)S(1)} %pad_maximum_fusion.9), channel_id=1, source_target_pairs={{0,8},{8,0},{16,24},{24,16},{32,40},{40,32},{48,56},{56,48},{1,9},... | collective-permute-start | bytes 1572872 | tf_op jit(solution)/shard_map/ppermute | solution.py:16
  67.6 3.5 %copy-start.23 = (bf16[512,512]{1,0:T(8,128)(2,1)S(1)}, bf16[512,512]{1,0:T(8,128)(2,1)}, u32[]{:S(2)}) copy-start(bf16[512,512]{1,0:T(8,128)(2,1)} %copy-done.22) | copy-start | bytes 1572868
  67.6 24.5 %collective-permute-start.13 = (bf16[2,256,1024]{2,1,0:T(8,128)(2,1)S(1)}, bf16[2,256,1024]{2,1,0:T(8,128)(2,1)S(1)}, u32[]{:S(2)}, u32[]{:S(2)}) collective-permute-start(bf16[2,256,1024]{2,1,0:T(8,128)(2,1)S(1)} %get-tuple-element.49), channel_id=1, source_target_pairs={{0,6},{1,7},{2,0},{3,1},{4,2},{5,3},{6,4},{7,5},{8,14},{9,15},{10,... | collective-permute-start | bytes 3145736 | tf_op jit(solution)/shard_map/ppermute | solution.py:16
  68.6 24.8 %collective-permute-start.14 = (bf16[2,256,1024]{2,1,0:T(8,128)(2,1)S(1)}, bf16[2,256,1024]{2,1,0:T(8,128)(2,1)S(1)}, u32[]{:S(2)}, u32[]{:S(2)}) collective-permute-start(bf16[2,256,1024]{2,1,0:T(8,128)(2,1)S(1)} %get-tuple-element.50), channel_id=1, source_target_pairs={{0,2},{1,3},{2,4},{3,5},{4,6},{5,7},{6,0},{7,1},{8,10},{9,11},{10,... | collective-permute-start | bytes 3145736 | tf_op jit(solution)/shard_map/ppermute | solution.py:16
  79.5 26.5 %collective-permute-start.18 = (bf16[2048,512]{1,0:T(8,128)(2,1)S(1)}, bf16[2048,512]{1,0:T(8,128)(2,1)S(1)}, u32[]{:S(2)}, u32[]{:S(2)}) collective-permute-start(bf16[2048,512]{1,0:T(8,128)(2,1)S(1)} %pad_maximum_fusion.3), channel_id=1, source_target_pairs={{0,64},{64,0},{1,65},{65,1},{2,66},{66,2},{3,67},{67,3},{4,68},{68... | collective-permute-start | bytes 6291464 | tf_op jit(solution)/shard_map/ppermute | solution.py:20
  83.8 4.3 %copy-start.14 = (f32[512,512]{1,0:T(8,128)}, f32[512,512]{1,0:T(8,128)S(1)}, u32[]{:S(2)}) copy-start(f32[512,512]{1,0:T(8,128)S(1)} %convolution_add_fusion) | copy-start | bytes 3145732
  83.8 2.3 collective-permute-start.12
  84.8 20.7 %collective-permute-start.16 = (bf16[768,512]{1,0:T(8,128)(2,1)S(1)}, bf16[768,512]{1,0:T(8,128)(2,1)S(1)}, u32[]{:S(2)}, u32[]{:S(2)}) collective-permute-start(bf16[768,512]{1,0:T(8,128)(2,1)S(1)} %get-tuple-element.75), channel_id=1, source_target_pairs={{0,16},{8,24},{16,32},{24,40},{32,48},{40,56},{48,0},{56,8},{1,17}... | collective-permute-start | bytes 2359304 | tf_op jit(solution)/shard_map/ppermute | solution.py:16
  86.1 20.3 %copy-start.16 = (f32[256,512]{1,0:T(8,128)}, f32[256,512]{1,0:T(8,128)S(1)}, u32[]{:S(2)}) copy-start(f32[256,512]{1,0:T(8,128)S(1)} %collective-permute-done.12) | copy-start | bytes 1572868
  86.1 19.8 %collective-permute-start.17 = (bf16[768,512]{1,0:T(8,128)(2,1)S(1)}, bf16[768,512]{1,0:T(8,128)(2,1)S(1)}, u32[]{:S(2)}, u32[]{:S(2)}) collective-permute-start(bf16[768,512]{1,0:T(8,128)(2,1)S(1)} %get-tuple-element.74), channel_id=1, source_target_pairs={{0,48},{8,56},{16,0},{24,8},{32,16},{40,24},{48,32},{56,40},{1,49}... | collective-permute-start | bytes 2359304 | tf_op jit(solution)/shard_map/ppermute | solution.py:16
  92.1 39.0 %copy-start.26 = (bf16[2,256,1024]{2,1,0:T(8,128)(2,1)}, bf16[2,256,1024]{2,1,0:T(8,128)(2,1)S(1)}, u32[]{:S(2)}) copy-start(bf16[2,256,1024]{2,1,0:T(8,128)(2,1)S(1)} %collective-permute-done.13) | copy-start | bytes 3145732
  93.4 37.7 %copy-start.27 = (bf16[2,256,1024]{2,1,0:T(8,128)(2,1)}, bf16[2,256,1024]{2,1,0:T(8,128)(2,1)S(1)}, u32[]{:S(2)}) copy-start(bf16[2,256,1024]{2,1,0:T(8,128)(2,1)S(1)} %collective-permute-done.14) | copy-start | bytes 3145732
  93.4 27.6 %collective-permute-start.21 = (bf16[2,256,1024]{2,1,0:T(8,128)(2,1)S(1)}, bf16[2,256,1024]{2,1,0:T(8,128)(2,1)S(1)}, u32[]{:S(2)}, u32[]{:S(2)}) collective-permute-start(bf16[2,256,1024]{2,1,0:T(8,128)(2,1)S(1)} %get-tuple-element.57), channel_id=1, source_target_pairs={{0,4},{1,5},{2,6},{3,7},{4,0},{5,1},{6,2},{7,3},{8,12},{9,13},{10,... | collective-permute-start | bytes 3145736 | tf_op jit(solution)/shard_map/ppermute | solution.py:16
  94.2 11.8 %collective-permute-start.15 = (bf16[256,512]{1,0:T(8,128)(2,1)S(1)}, bf16[256,512]{1,0:T(8,128)(2,1)S(1)}, u32[]{:S(2)}, u32[]{:S(2)}) collective-permute-start(bf16[256,512]{1,0:T(8,128)(2,1)S(1)} %multiply_convert_fusion), channel_id=1, source_target_pairs={{0,1},{1,0},{2,3},{3,2},{4,5},{5,4},{6,7},{7,6},{8,9},{9,8},{10,11... | collective-permute-start | bytes 786440 | tf_op jit(solution)/shard_map/ppermute | solution.py:16
  106.0 15.1 %copy-start.5 = (bf16[256,512]{1,0:T(8,128)(2,1)}, bf16[256,512]{1,0:T(8,128)(2,1)S(1)}, u32[]{:S(2)}) copy-start(bf16[256,512]{1,0:T(8,128)(2,1)S(1)} %collective-permute-done.15) | copy-start | bytes 786436
  106.0 22.8 %copy-start.9 = (bf16[2048,512]{1,0:T(8,128)(2,1)}, bf16[2048,512]{1,0:T(8,128)(2,1)S(1)}, u32[]{:S(2)}) copy-start(bf16[2048,512]{1,0:T(8,128)(2,1)S(1)} %collective-permute-done.18.refs_13_) | copy-start | bytes 6291460
  106.1 15.0 %collective-permute-start.22 = (bf16[512,512]{1,0:T(8,128)(2,1)S(1)}, bf16[512,512]{1,0:T(8,128)(2,1)S(1)}, u32[]{:S(2)}, u32[]{:S(2)}) collective-permute-start(bf16[512,512]{1,0:T(8,128)(2,1)S(1)} %pad_maximum_fusion.10), channel_id=1, source_target_pairs={{0,8},{8,0},{16,24},{24,16},{32,40},{40,32},{48,56},{56,48},{1,9},... | collective-permute-start | bytes 1572872 | tf_op jit(solution)/shard_map/ppermute | solution.py:16
  106.5 22.3 %collective-permute-start.19 = (bf16[512,512]{1,0:T(8,128)(2,1)S(1)}, bf16[512,512]{1,0:T(8,128)(2,1)S(1)}, u32[]{:S(2)}, u32[]{:S(2)}) collective-permute-start(bf16[512,512]{1,0:T(8,128)(2,1)S(1)} %constant_dynamic-update-slice_fusion), channel_id=1, source_target_pairs={{0,2},{1,3},{2,4},{3,5},{4,6},{5,7},{6,0},{7,1},{8,10},{9,11},{10,... | collective-permute-start | bytes 1572872 | tf_op jit(solution)/shard_map/ppermute | solution.py:16
  106.6 23.1 %collective-permute-start.20 = (bf16[512,512]{1,0:T(8,128)(2,1)S(1)}, bf16[512,512]{1,0:T(8,128)(2,1)}, u32[]{:S(2)}, u32[]{:S(2)}) collective-permute-start(bf16[512,512]{1,0:T(8,128)(2,1)S(1)} %constant_dynamic-update-slice_fusion), channel_id=1, source_target_pairs={{0,6},{1,7},{2,0},{3,1},{4,2},{5,3},{6,4},{7,5},{8,14},{9,15},{10,... | collective-permute-start | bytes 1572872 | tf_op jit(solution)/shard_map/ppermute | solution.py:16
  121.0 8.6 %copy-start.24 = (bf16[2,256,1024]{2,1,0:T(8,128)(2,1)}, bf16[2,256,1024]{2,1,0:T(8,128)(2,1)S(1)}, u32[]{:S(2)}) copy-start(bf16[2,256,1024]{2,1,0:T(8,128)(2,1)S(1)} %collective-permute-done.21) | copy-start | bytes 3145732
  121.1 10.1 %copy-start.3 = (bf16[512,512]{1,0:T(8,128)(2,1)}, bf16[512,512]{1,0:T(8,128)(2,1)S(1)}, u32[]{:S(2)}) copy-start(bf16[512,512]{1,0:T(8,128)(2,1)S(1)} %collective-permute-done.22.refs_12_) | copy-start | bytes 1572868
  131.1 23.8 %collective-permute-start.25 = (bf16[2048,512]{1,0:T(8,128)(2,1)}, bf16[2048,512]{1,0:T(8,128)(2,1)}, u32[]{:S(2)}, u32[]{:S(2)}) collective-permute-start(bf16[2048,512]{1,0:T(8,128)(2,1)} %pad_maximum_fusion.4), channel_id=1, source_target_pairs={{0,64},{64,0},{1,65},{65,1},{2,66},{66,2},{3,67},{67,3},{4,68},{68... | collective-permute-start | bytes 6291464 | tf_op jit(solution)/shard_map/ppermute | solution.py:20
  136.7 16.7 %collective-permute-start.26 = (bf16[256,1024]{1,0:T(8,128)(2,1)}, bf16[256,1024]{1,0:T(8,128)(2,1)}, u32[]{:S(2)}, u32[]{:S(2)}) collective-permute-start(bf16[256,1024]{1,0:T(8,128)(2,1)} %fusion.16), channel_id=1, source_target_pairs={{0,1},{1,0},{2,3},{3,2},{4,5},{5,4},{6,7},{7,6},{8,9},{9,8},{10,11... | collective-permute-start | bytes 1572872 | tf_op jit(solution)/shard_map/ppermute | solution.py:16
  140.6 14.4 %copy-start.2 = (bf16[512,512]{1,0:T(8,128)(2,1)S(1)}, bf16[512,512]{1,0:T(8,128)(2,1)}, u32[]{:S(2)}) copy-start(bf16[512,512]{1,0:T(8,128)(2,1)} %copy-done.1) | copy-start | bytes 1572868
  140.6 14.4 %copy-start.4 = (bf16[512,512]{1,0:T(8,128)(2,1)S(1)}, bf16[512,512]{1,0:T(8,128)(2,1)}, u32[]{:S(2)}) copy-start(bf16[512,512]{1,0:T(8,128)(2,1)} %copy-done.3) | copy-start | bytes 1572868
  140.6 14.4 %copy-start.6 = (bf16[256,512]{1,0:T(8,128)(2,1)S(1)}, bf16[256,512]{1,0:T(8,128)(2,1)}, u32[]{:S(2)}) copy-start(bf16[256,512]{1,0:T(8,128)(2,1)} %copy-done.5) | copy-start | bytes 786436
  140.6 14.4 %copy-start.8 = (bf16[512,512]{1,0:T(8,128)(2,1)S(1)}, bf16[512,512]{1,0:T(8,128)(2,1)}, u32[]{:S(2)}) copy-start(bf16[512,512]{1,0:T(8,128)(2,1)} %copy-done.7) | copy-start | bytes 1572868
  141.7 13.2 %collective-permute-start.23 = (bf16[256,512]{1,0:T(8,128)(2,1)S(1)}, bf16[256,512]{1,0:T(8,128)(2,1)S(1)}, u32[]{:S(2)}, u32[]{:S(2)}) collective-permute-start(bf16[256,512]{1,0:T(8,128)(2,1)S(1)} %slice.85), channel_id=1, source_target_pairs={{0,2},{1,3},{2,4},{3,5},{4,6},{5,7},{6,0},{7,1},{8,10},{9,11},{10,... | collective-permute-start | bytes 786440 | tf_op jit(solution)/shard_map/ppermute | solution.py:16
  142.8 12.2 %collective-permute-start.24 = (bf16[256,512]{1,0:T(8,128)(2,1)S(1)}, bf16[256,512]{1,0:T(8,128)(2,1)S(1)}, u32[]{:S(2)}, u32[]{:S(2)}) collective-permute-start(bf16[256,512]{1,0:T(8,128)(2,1)S(1)} %slice.86), channel_id=1, source_target_pairs={{0,6},{1,7},{2,0},{3,1},{4,2},{5,3},{6,4},{7,5},{8,14},{9,15},{10,... | collective-permute-start | bytes 786440 | tf_op jit(solution)/shard_map/ppermute | solution.py:16
  169.0 34.3 %all-to-all-start = ((bf16[8,272,512]{2,1,0:T(8,128)(2,1)}), bf16[8,272,512]{2,1,0:T(8,128)(2,1)S(1)}, u32[]{:S(2)}, u32[]{:S(2)}) async-start(bf16[8,272,512]{2,1,0:T(8,128)(2,1)} %shard_map.69), calls=%async_computation | async-start | bytes 4456448 | tf_op jit(solution)/shard_map/all_to_all | solution.py:292
  173.5 30.2 %copy-start.17 = (f32[256,512]{1,0:T(8,128)S(1)}, f32[256,512]{1,0:T(8,128)}, u32[]{:S(2)}) copy-start(f32[256,512]{1,0:T(8,128)} %copy-done.16) | copy-start | bytes 1572868
  205.2 1.6 collective-permute-start.27
  (11 other events, 16.9 us)

commit v7 on v6

--- a/solution.py
+++ b/solution.py
@@ -33,12 +33,15 @@
     return [shift(block, axis, 0, 1), shift(block, axis, 1, 0), shift(block, axis, -1, 0)]
 
 
-def gather_middle(block, first, axis):
+def ring_operands(block, first):
     other, before, nxt = first
     half = block.shape[0] // 2
-    up = shift(jnp.concatenate([other, before[:half]], axis=0), axis, 1, 0)
-    down = shift(jnp.concatenate([other, nxt[half:]], axis=0), axis, -1, 0)
-    return [up, down]
+    return jnp.concatenate([other, before[:half]], axis=0), jnp.concatenate([other, nxt[half:]], axis=0)
+
+
+def gather_middle(block, first, axis):
+    up, down = ring_operands(block, first)
+    return [shift(up, axis, 1, 0), shift(down, axis, -1, 0)]
 
 
 def dot(a, b, dims=((1,), (0,))):
@@ -75,7 +78,6 @@
         h_copies.append(pltpu.make_async_copy(ref, h_kept.at[pl.ds(at, count)], h_sem.at[i]))
     for copy in h_copies:
         copy.start()
-
     low, high = pl.ds(0, half), pl.ds(half, half)
 
     def pieces(parts):
@@ -158,7 +160,7 @@
     first = role[0] == 0
     for i in range(count):
         low, high = product[:rows, i * width : (i + 1) * width], product[rows:, i * width : (i + 1) * width]
-        out[i] = jnp.where(first, low, high)
+        out[i] = jnp.where(first, low, high).astype(BF16)
         away[i] = jnp.where(first, high, low).astype(BF16)
 
 
@@ -179,7 +181,7 @@
             ],
             out_specs=[place, place],
         ),
-        out_shape=[jax.ShapeDtypeStruct(shape, F32), jax.ShapeDtypeStruct(shape, BF16)],
+        out_shape=[jax.ShapeDtypeStruct(shape, BF16)] * 2,
         compiler_params=pltpu.CompilerParams(
             dimension_semantics=("arbitrary",), vmem_limit_bytes=40 * 1024 * 1024
         ),
@@ -215,30 +217,33 @@
     away, projector, *w_first = lax.optimization_barrier((away, projector, *w_first))
     away = flip(away)
 
-    w_middle = gather_middle(student_weight, w_first, "dp")
+    up, down = ring_operands(student_weight, w_first)
+    w_middle = [shift(up, "dp", 1, 0), shift(down, "dp", -1, 0)]
     p_other = shift(projector, "dp", 0, 1)
-
-    mine = lax.dynamic_slice_in_dim(student_in, role * wide, wide, axis=1)
-    theirs = flip(lax.dynamic_slice_in_dim(student_in, (1 - role) * wide, wide, axis=1))
 
     zt = lax.axis_index("tensor") >> 1
     teacher = {}
     for k in (0, 1, -1, 2):
         at = ((zt - k) & 3) * 2
-        pair = lax.dynamic_slice_in_dim(own, at, 2, axis=0) + lax.dynamic_slice_in_dim(away, at, 2, axis=0).astype(F32)
-        teacher[k] = pair if k == 0 else pair.astype(BF16)
-    teacher[0], teacher[1], teacher[-1], teacher[2] = lax.optimization_barrier(
-        (teacher[0], teacher[1], teacher[-1], teacher[2])
-    )
-
-    projector, p_other, theirs, teacher[1], teacher[-1], *w_middle = lax.optimization_barrier(
-        (projector, p_other, theirs, teacher[1], teacher[-1], *w_middle)
-    )
+        pair = lax.dynamic_slice_in_dim(own, at, 2, axis=0).astype(F32) + lax.dynamic_slice_in_dim(away, at, 2, axis=0).astype(F32)
+        teacher[k] = pair.astype(BF16) if k == 2 else pair
+    teacher = dict(zip(teacher, lax.optimization_barrier(tuple(teacher.values()))))
+    over = [shift(teacher[2][0], "tensor", -1, 0), shift(teacher[2][1], "tensor", 1, 0)]
+
+    student_in = after(student_in, teacher[2])
+    mine = lax.dynamic_slice_in_dim(student_in, role * wide, wide, axis=1)
+    theirs = flip(lax.dynamic_slice_in_dim(student_in, (1 - role) * wide, wide, axis=1))
+
+    projector, p_other, theirs, *over = lax.optimization_barrier((projector, p_other, theirs, *over, *w_middle))[:5]
+    teacher[1] = jnp.stack([teacher[1][0] + over[0].astype(F32), teacher[1][1]]).astype(BF16)
+    teacher[-1] = jnp.stack([teacher[-1][0], teacher[-1][1] + over[1].astype(F32)]).astype(BF16)
+    teacher[1], teacher[-1], student_weight = lax.optimization_barrier((teacher[1], teacher[-1], student_weight))
     for k in (1, -1):
         teacher[k] = shift(teacher[k], "tensor", -k, 0)
+    up, down = w_middle
+    w_far, mine, theirs = lax.optimization_barrier((jnp.concatenate([up[feat:], down[feat:]], axis=0), mine, theirs))
+    w_far = shift(w_far, "dp", 0, 1)
     student = jnp.concatenate([mine, theirs], axis=0)
-    up, down = w_middle
-    w_far = shift(jnp.concatenate([up[feat:], down[feat:]], axis=0), "dp", 0, 1)
     p_first = [shift(projector, "dp", 1, 0), shift(projector, "dp", -1, 0)]
     w_far, *p_first = lax.optimization_barrier((w_far, *p_first))
     p_first = [p_other, *p_first]
@@ -257,38 +262,28 @@
     hidden = (pre * sigma).astype(BF16)
 
     p_middle = gather_middle(projector, p_first, "dp")
-    hidden, teacher[1], teacher[-1], teacher[2] = lax.optimization_barrier(
-        (hidden, teacher[1], teacher[-1], teacher[2])
-    )
+    hidden, teacher[1], teacher[-1] = lax.optimization_barrier((hidden, teacher[1], teacher[-1]))
     h_other = shift(hidden, "tensor", 0, 1)
-    teacher[2] = shift(teacher[2], "tensor", 2, 0)
-    near = lax.optimization_barrier(teacher[0] + teacher[1].astype(F32) + teacher[-1].astype(F32))
+    near = teacher[0] + teacher[1].astype(F32) + teacher[-1].astype(F32)
+    cross = lax.dynamic_index_in_dim(near, 1 - xh, 0, False).astype(BF16)
+    cross = shift(cross, "tensor", 0, 1)
     p_flip = flip(jnp.concatenate([projector, *p_first], axis=0))
     h_other, up, down, p_flip = lax.optimization_barrier((h_other, *p_middle, p_flip))
     h_pair = jnp.concatenate([hidden, h_other], axis=0)
     h_before, h_after = shift(h_pair, "tensor", 1, 0), shift(h_pair, "tensor", -1, 0)
     p_far = shift(jnp.concatenate([up[feat:], down[feat:]], axis=0), "dp", 0, 1)
-    h_before, h_after, teacher[2], p_far = lax.optimization_barrier((h_before, h_after, teacher[2], p_far))
+    h_before, h_after, p_far, cross = lax.optimization_barrier((h_before, h_after, p_far, cross))
     far_0 = shift(h_before[:own_rows], "tensor", 1, 0)
     far_1 = shift(h_after[own_rows:], "tensor", -1, 0)
     p_own = [projector, *p_first, up, down, p_far]
     p_flip = [p_flip, flip(jnp.concatenate([up, down, p_far], axis=0))]
-
-    near = near + teacher[2].astype(F32)
-    cross = lax.dynamic_index_in_dim(near, 1 - xh, 0, False).astype(BF16)
-    teacher = lax.dynamic_index_in_dim(near, xh, 0, False) + shift(cross, "tensor", 0, 1).astype(F32)
-
-    def ring_blocks(x):
-        return x.reshape(-1, own_rows, hid)
-
-    pieces = [ring_blocks(x) for x in (hidden, h_other, h_after, far_0, far_1, h_before)]
-    order = (
-        at
-        + [((((zt + (d >> 1)) & 3) << 1) | ((d & 1) ^ xh)) for d in at]
-        + [role]
-    )
+    teacher = lax.dynamic_index_in_dim(near, xh, 0, False) + cross.astype(F32)
+    hidden = [x.reshape(-1, own_rows, hid) for x in (hidden, h_other, h_after, far_0, far_1, h_before)]
+
+    blocks = [((((zt + (d >> 1)) & 3) << 1) | ((d & 1) ^ xh)) for d in at]
+    order = sources("dp") + blocks + [role]
     order = jnp.stack([jnp.asarray(x, jnp.int32) for x in order])
-    back = project(order, pieces, p_own, p_flip, teacher)
+    back = project(order, hidden, p_own, p_flip, teacher)
     back = lax.all_to_all(back, "tensor", 0, 0, tiled=True)
     back = jnp.sum(back.astype(F32), axis=0)
     square = join_note(back[own_rows:])

time: 270 us -> 281 us (1.041)
  waiting for transfers between devices: 88.7 us -> 96.8 us
  other arithmetic: 20.9 us -> 25.2 us
  matrix products: 14.4 us -> 10.7 us
    ppermute x6, waiting for transfers between devices: 2.84 us -> 11.3 us  [flip(): return lax.ppermute(value, 'role', [(0, 1), (1, 0)])]
    another operation x0 -> x3, other arithmetic: none -> 4.05 us  [the longest x2 2.98 us: shards(): jnp.stack([teacher[1][0] + over[0].astype(F32), teacher[1][1]]).astype(BF16)]
    dot_general x10, matrix products: 14.4 us -> 10.7 us  [dot(): return lax.dot_general(a, b, (dims, ((), ())), preferred_element_type=F32)]
    all_to_all x1, starting transfers between devices: 4.58 us -> 7.45 us  [shards(): back = lax.all_to_all(back, 'tensor', 0, 0, tiled=True)]
    ppermute x21 -> x22, starting transfers between devices: 36.6 us -> 34.4 us  [shift(): return lax.ppermute(value, axis, perm)]
    unnamed x59 -> x56, local copies, waits for them, and re-layouts: 9.34 us -> 8.06 us
    ppermute x21 -> x22, waiting for transfers between devices: 56.1 us -> 56 us  [shift(): return lax.ppermute(value, axis, perm)]
  transfers between devices with their start and end apart: 29 -> 30, of which waited for: 13 -> 15; matrix products, arithmetic and copies ran while one was open for 13% -> 11% of each run, Pallas kernels for 5% -> 5%
where the time goes in v7:
time: 281 us; the launch traced here: 280 us
  waiting for transfers between devices  96.8 us (34%)
  blocking collectives  54 us (19%)
  starting transfers between devices  44.5 us (16%)
  Pallas kernels  25.7 us (9%)
  other arithmetic  25.2 us (9%)
  local copies, waits for them, and re-layouts  20.3 us (7%)
  matrix products  10.7 us (4%)
  between operations  3 us (1%)
    ppermute x22, waiting for transfers between devices, shift(): return lax.ppermute(value, axis, perm)  56 us
    all_to_all x1, blocking collectives, shards(): grad = lax.all_to_all(grad, 'dp', 0, 0, tiled=True)  54 us
    ppermute x22, starting transfers between devices, shift(): return lax.ppermute(value, axis, perm)  34.4 us
    all_to_all x1, waiting for transfers between devices, shards(): back = lax.all_to_all(back, 'tensor', 0, 0, tiled=True)  29.4 us
    pallas_call x1, Pallas kernels, teach(): pl.pallas_call(teach_kernel, grid_spec=pltpu.PrefetchScalarGridSpec(num_s...  13.2 us
    pallas_call x1, Pallas kernels, project(): pl.pallas_call(project_kernel, in_specs=[pl.BlockSpec(memory_space=pltpu....  12.5 us
    ppermute x6, waiting for transfers between devices, flip(): return lax.ppermute(value, 'role', [(0, 1), (1, 0)])  11.3 us
    dot_general x10, matrix products, dot(): return lax.dot_general(a, b, (dims, ((), ())), preferred_element_type=F32)  10.7 us
  transfers between devices with their start and end apart: 30, of which 15 were waited for; matrix products, arithmetic and copies ran while one was open for 11% of the time, Pallas kernels for 5%

profile of v7, /device:TPU:0, one launch (start us, length us, event | category | flops | bytes accessed | tf_op | source)
XLA Modules:
  0.0 280.2 jit_solution(15143788914019572969)
XLA Ops:
  0.6 1.7 collective-permute-start.1
  2.3 1.6 collective-permute-start.2
  3.9 1.7 collective-permute-start.3
  5.5 1.7 collective-permute-start
  7.2 1.2 copy-done.7
  8.4 13.2 %shard_map.68 = (bf16[8,256,1024]{2,1,0:T(8,128)(2,1)S(1)}, bf16[8,256,1024]{2,1,0:T(8,128)(2,1)}) custom-call(s32[1]{0:T(128)} %bitcast.role, bf16[512,1024]{1,0:T(8,128)(2,1)S(1)} %bitcast.59, bf16[1024,8192]{1,0:T(8,128)(2,1)} %weight.1), custom_call_target="tpu_custom_call" | custom-call | flops 8589934592 | bytes 16777216 | tf_op jit(solution)/shard_map/pallas_call | solution.py:173
  21.6 2.0 copy-done
  23.8 7.5 %collective-permute-done.6 = bf16[8,256,1024]{2,1,0:T(8,128)(2,1)} collective-permute-done((bf16[8,256,1024]{2,1,0:T(8,128)(2,1)}, bf16[8,256,1024]{2,1,0:T(8,128)(2,1)}, u32[]{:S(2)}, u32[]{:S(2)}) %collective-permute-start.6) | collective-permute-done | bytes 4194336 | tf_op jit(solution)/shard_map/ppermute | solution.py:20
  31.3 7.7 %add_convert_fusion = (bf16[2,256,1024]{2,1,0:T(8,128)(2,1)S(1)}, f32[2,256,1024]{2,1,0:T(8,128)S(1)}, f32[2,256,1024]{2,1,0:T(8,128)}, f32[2,256,1024]{2,1,0:T(8,128)}) fusion(bf16[8,256,1024]{2,1,0:T(8,128)(2,1)} %collective-permute-done.6, s32[]{:T(128)S(6)} %select_n.88, bf16[8,256,1024]{2,1,0:T(8,128)(2,1)} %copy-done, s32[]{:T(128)S(6)} %select_n.87, ...), kind=kLoop, calls=%fused_computation.7 | loop fusion | flops 6815744 | bytes 15728656 | tf_op jit(solution)/shard_map/convert_element_type | solution.py:229
  39.0 2.3 constant_dynamic-slice_fusion
  42.4 6.4 %collective-permute-start.4 = (bf16[768,512]{1,0:T(8,128)(2,1)S(1)}, bf16[768,512]{1,0:T(8,128)(2,1)}, u32[]{:S(2)}, u32[]{:S(2)}) collective-permute-start(bf16[768,512]{1,0:T(8,128)(2,1)S(1)} %get-tuple-element.86), channel_id=1, source_target_pairs={{0,16},{8,24},{16,32},{24,40},{32,48},{40,56},{48,0},{56,8},{1,17}... | collective-permute-start | bytes 2359304 | tf_op jit(solution)/shard_map/ppermute | solution.py:16
  48.9 4.8 %collective-permute-start.5 = (bf16[768,512]{1,0:T(8,128)(2,1)}, bf16[768,512]{1,0:T(8,128)(2,1)}, u32[]{:S(2)}, u32[]{:S(2)}) collective-permute-start(bf16[768,512]{1,0:T(8,128)(2,1)} %get-tuple-element.87), channel_id=1, source_target_pairs={{0,48},{8,56},{16,0},{24,8},{32,16},{40,24},{48,32},{56,40},{1,49}... | collective-permute-start | bytes 2359304 | tf_op jit(solution)/shard_map/ppermute | solution.py:16
  54.7 17.1 %collective-permute-done.4 = bf16[768,512]{1,0:T(8,128)(2,1)} collective-permute-done((bf16[768,512]{1,0:T(8,128)(2,1)S(1)}, bf16[768,512]{1,0:T(8,128)(2,1)}, u32[]{:S(2)}, u32[]{:S(2)}) %collective-permute-start.4) | collective-permute-done | bytes 786464 | tf_op jit(solution)/shard_map/ppermute | solution.py:16
  72.4 1.1 slice.120
  74.7 1.3 slice.168
  76.0 9.8 %collective-permute-done.9 = bf16[256,1024]{1,0:T(8,128)(2,1)} collective-permute-done((bf16[256,1024]{1,0:T(8,128)(2,1)}, bf16[256,1024]{1,0:T(8,128)(2,1)}, u32[]{:S(2)}, u32[]{:S(2)}) %collective-permute-start.9) | collective-permute-done | bytes 524320 | tf_op jit(solution)/shard_map/ppermute | solution.py:16
  85.8 3.2 %collective-permute-start.13 = (bf16[512,512]{1,0:T(8,128)(2,1)S(1)}, bf16[512,512]{1,0:T(8,128)(2,1)S(1)}, u32[]{:S(2)}, u32[]{:S(2)}) collective-permute-start(bf16[512,512]{1,0:T(8,128)(2,1)S(1)} %collective-permute-done.refs_6_), channel_id=1, source_target_pairs={{0,48},{8,56},{16,0},{24,8},{32,16},{40,24},{48,32},{56,40},{1,49}... | collective-permute-start | bytes 1572872 | tf_op jit(solution)/shard_map/ppermute | solution.py:16
  89.0 1.9 fusion.9
  93.3 2.0 collective-permute-start.15
  95.4 1.8 constant_dynamic-update-slice_fusion
  98.1 1.5 fusion.32
  99.7 1.5 fusion.15
  101.2 1.5 fusion.13
  102.7 1.3 fusion.30
  104.4 1.1 collective-permute-done.11
  105.5 1.5 pad_maximum_fusion.1
  109.8 2.3 collective-permute-done.14
  113.8 1.4 multiply_convert_fusion
  115.2 2.0 collective-permute-done.15
  117.1 2.3 collective-permute-done.16
  119.5 3.6 %collective-permute-start.17 = (bf16[256,512]{1,0:T(8,128)(2,1)S(1)}, bf16[256,512]{1,0:T(8,128)(2,1)S(1)}, u32[]{:S(2)}, u32[]{:S(2)}) collective-permute-start(bf16[256,512]{1,0:T(8,128)(2,1)S(1)} %multiply_convert_fusion), channel_id=1, source_target_pairs={{0,1},{1,0},{2,3},{3,2},{4,5},{5,4},{6,7},{7,6},{8,9},{9,8},{10,11... | collective-permute-start | bytes 786440 | tf_op jit(solution)/shard_map/ppermute | solution.py:16
  123.1 2.2 convert_add_fusion
  125.5 5.0 %collective-permute-done.18.refs_10_ = bf16[768,512]{1,0:T(8,128)(2,1)S(1)} collective-permute-done((bf16[768,512]{1,0:T(8,128)(2,1)S(1)}, bf16[768,512]{1,0:T(8,128)(2,1)S(1)}, u32[]{:S(2)}, u32[]{:S(2)}) %collective-permute-start.18) | collective-permute-done | bytes 786464 | tf_op jit(solution)/shard_map/ppermute | solution.py:16
  130.4 2.0 collective-permute-done.19.refs_11_
  133.6 3.2 %collective-permute-start.22 = (bf16[512,512]{1,0:T(8,128)(2,1)S(1)}, bf16[512,512]{1,0:T(8,128)(2,1)}, u32[]{:S(2)}, u32[]{:S(2)}) collective-permute-start(bf16[512,512]{1,0:T(8,128)(2,1)S(1)} %constant_dynamic-update-slice_fusion.2), channel_id=1, source_target_pairs={{0,6},{1,7},{2,0},{3,1},{4,2},{5,3},{6,4},{7,5},{8,14},{9,15},{10,... | collective-permute-start | bytes 1572872 | tf_op jit(solution)/shard_map/ppermute | solution.py:16
  136.8 4.5 %collective-permute-done.24 = bf16[256,1024]{1,0:T(8,128)(2,1)S(1)} collective-permute-done((bf16[256,1024]{1,0:T(8,128)(2,1)S(1)}, bf16[256,1024]{1,0:T(8,128)(2,1)S(1)}, u32[]{:S(2)}, u32[]{:S(2)}) %collective-permute-start.24) | collective-permute-done | bytes 524320 | tf_op jit(solution)/shard_map/ppermute | solution.py:16
  141.4 7.7 %collective-permute-done.23.refs_12_ = bf16[512,512]{1,0:T(8,128)(2,1)S(1)} collective-permute-done((bf16[512,512]{1,0:T(8,128)(2,1)S(1)}, bf16[512,512]{1,0:T(8,128)(2,1)S(1)}, u32[]{:S(2)}, u32[]{:S(2)}) %collective-permute-start.23) | collective-permute-done | bytes 524320 | tf_op jit(solution)/shard_map/ppermute | solution.py:16
  149.1 1.5 pad_maximum_fusion.2
  153.6 3.3 %collective-permute-start.26 = (bf16[256,512]{1,0:T(8,128)(2,1)S(1)}, bf16[256,512]{1,0:T(8,128)(2,1)S(1)}, u32[]{:S(2)}, u32[]{:S(2)}) collective-permute-start(bf16[256,512]{1,0:T(8,128)(2,1)S(1)} %slice.112), channel_id=1, source_target_pairs={{0,6},{1,7},{2,0},{3,1},{4,2},{5,3},{6,4},{7,5},{8,14},{9,15},{10,... | collective-permute-start | bytes 786440 | tf_op jit(solution)/shard_map/ppermute | solution.py:16
  156.9 1.6 bitcast_add_fusion.refs_15_
  158.4 4.1 %collective-permute-done.25 = bf16[256,512]{1,0:T(8,128)(2,1)S(1)} collective-permute-done((bf16[256,512]{1,0:T(8,128)(2,1)S(1)}, bf16[256,512]{1,0:T(8,128)(2,1)S(1)}, u32[]{:S(2)}, u32[]{:S(2)}) %collective-permute-start.25) | collective-permute-done | bytes 262176 | tf_op jit(solution)/shard_map/ppermute | solution.py:16
  165.8 12.5 %shard_map.69 = bf16[8,272,512]{2,1,0:T(8,128)(2,1)} custom-call(s32[17]{0:T(128)S(1)} %stack.84.order, bf16[1,256,512]{2,1,0:T(8,128)(2,1)S(1)} %bitcast.57, bf16[1,256,512]{2,1,0:T(8,128)(2,1)S(1)} %bitcast.58, bf16[2,256,512]{2,1,0:T(8,128)(2,1)} %bitcast.27.refs_2_, bf16[1,256,512]{2,1,0:T(8,128)(2,1)S(1)} %bitcast.60, ...), custom_call_target="tpu_custom_call" | custom-call | flops 4294967296 | bytes 8388608 | tf_op jit(solution)/shard_map/pallas_call | solution.py:137
  178.4 7.4 %all-to-all-start = ((bf16[8,272,512]{2,1,0:T(8,128)(2,1)}), bf16[8,272,512]{2,1,0:T(8,128)(2,1)S(1)}, u32[]{:S(2)}, u32[]{:S(2)}) async-start(bf16[8,272,512]{2,1,0:T(8,128)(2,1)} %shard_map.69), calls=%async_computation | async-start | bytes 4456448 | tf_op jit(solution)/shard_map/all_to_all | solution.py:287
  185.9 29.4 %all-to-all-done = bf16[8,272,512]{2,1,0:T(8,128)(2,1)S(1)} async-done(((bf16[8,272,512]{2,1,0:T(8,128)(2,1)}), bf16[8,272,512]{2,1,0:T(8,128)(2,1)S(1)}, u32[]{:S(2)}, u32[]{:S(2)}) %all-to-all-start) | async-done | bytes 2228256 | tf_op jit(solution)/shard_map/all_to_all | solution.py:287
  215.8 1.5 fusion.12
  217.6 1.5 collective-permute-done.28
  219.2 2.5 convolution_convert_fusion
  222.2 54.0 %all_to_all.10 = bf16[8,528,512]{2,1,0:T(8,128)(2,1)S(1)} all-to-all(bf16[8,528,512]{2,1,0:T(8,128)(2,1)S(1)} %pad_maximum_fusion), channel_id=1, replica_groups=mesh['role'=2,'dp'=8,'tensor'=8] {'dp'}, dimensions={0} | all-to-all | bytes 8650752 | tf_op jit(solution)/shard_map/all_to_all | solution.py:300
  (133 shorter events, 23.2 us)
Async XLA Ops:
  0.6 23.0 %collective-permute-start.1 = (bf16[512,512]{1,0:T(8,128)(2,1)}, bf16[512,512]{1,0:T(8,128)(2,1)S(1)}, u32[]{:S(2)}, u32[]{:S(2)}) collective-permute-start(bf16[512,512]{1,0:T(8,128)(2,1)} %param.8), channel_id=1, source_target_pairs={{0,8},{8,0},{16,24},{24,16},{32,40},{40,32},{48,56},{56,48},{1,9},... | collective-permute-start | bytes 1572872 | tf_op jit(solution)/shard_map/ppermute | solution.py:16
  2.3 21.3 %collective-permute-start.2 = (bf16[512,512]{1,0:T(8,128)(2,1)}, bf16[512,512]{1,0:T(8,128)(2,1)S(1)}, u32[]{:S(2)}, u32[]{:S(2)}) collective-permute-start(bf16[512,512]{1,0:T(8,128)(2,1)} %param.8), channel_id=1, source_target_pairs={{0,16},{8,24},{16,32},{24,40},{32,48},{40,56},{48,0},{56,8},{1,17}... | collective-permute-start | bytes 1572872 | tf_op jit(solution)/shard_map/ppermute | solution.py:16
  3.9 19.8 %collective-permute-start.3 = (bf16[512,512]{1,0:T(8,128)(2,1)}, bf16[512,512]{1,0:T(8,128)(2,1)S(1)}, u32[]{:S(2)}, u32[]{:S(2)}) collective-permute-start(bf16[512,512]{1,0:T(8,128)(2,1)} %param.8), channel_id=1, source_target_pairs={{0,48},{8,56},{16,0},{24,8},{32,16},{40,24},{48,32},{56,40},{1,49}... | collective-permute-start | bytes 1572872 | tf_op jit(solution)/shard_map/ppermute | solution.py:16
  5.5 18.1 %collective-permute-start = (bf16[512,512]{1,0:T(8,128)(2,1)}, bf16[512,512]{1,0:T(8,128)(2,1)S(1)}, u32[]{:S(2)}, u32[]{:S(2)}) collective-permute-start(bf16[512,512]{1,0:T(8,128)(2,1)} %param.9), channel_id=1, source_target_pairs={{0,0},{1,8},{2,16},{3,24},{4,32},{5,40},{6,48},{7,56},{8,9},{9,1},... | collective-permute-start | bytes 1572872 | tf_op jit(solution)/shard_map/ppermute | solution.py:214
  23.6 81.9 %copy-start.1 = (bf16[512,512]{1,0:T(8,128)(2,1)}, bf16[512,512]{1,0:T(8,128)(2,1)S(1)}, u32[]{:S(2)}) copy-start(bf16[512,512]{1,0:T(8,128)(2,1)S(1)} %collective-permute-done.refs_6_) | copy-start | bytes 1572868
  23.6 17.8 %copy-start.19 = (bf16[512,512]{1,0:T(8,128)(2,1)}, bf16[512,512]{1,0:T(8,128)(2,1)S(1)}, u32[]{:S(2)}) copy-start(bf16[512,512]{1,0:T(8,128)(2,1)S(1)} %collective-permute-done.1) | copy-start | bytes 1572868
  23.6 7.6 %copy-start.21 = (bf16[512,512]{1,0:T(8,128)(2,1)}, bf16[512,512]{1,0:T(8,128)(2,1)S(1)}, u32[]{:S(2)}) copy-start(bf16[512,512]{1,0:T(8,128)(2,1)S(1)} %collective-permute-done.2) | copy-start | bytes 1572868
  23.7 7.6 %copy-start.23 = (bf16[512,512]{1,0:T(8,128)(2,1)}, bf16[512,512]{1,0:T(8,128)(2,1)S(1)}, u32[]{:S(2)}) copy-start(bf16[512,512]{1,0:T(8,128)(2,1)S(1)} %collective-permute-done.3) | copy-start | bytes 1572868
  23.7 7.6 %collective-permute-start.6 = (bf16[8,256,1024]{2,1,0:T(8,128)(2,1)}, bf16[8,256,1024]{2,1,0:T(8,128)(2,1)}, u32[]{:S(2)}, u32[]{:S(2)}) collective-permute-start(bf16[8,256,1024]{2,1,0:T(8,128)(2,1)} %get-tuple-element.44), channel_id=1, source_target_pairs={{0,64},{64,0},{1,65},{65,1},{2,66},{66,2},{3,67},{67,3},{4,68},{68... | collective-permute-start | bytes 12582920 | tf_op jit(solution)/shard_map/ppermute | solution.py:20
  31.3 7.7 %copy-start.17 = (bf16[256,8192]{1,0:T(8,128)(2,1)S(1)}, bf16[256,8192]{1,0:T(8,128)(2,1)}, u32[]{:S(2)}) copy-start(bf16[256,8192]{1,0:T(8,128)(2,1)} %param.7) | copy-start | bytes 12582916
  39.0 35.6 %copy-start.15 = (f32[2,256,1024]{2,1,0:T(8,128)}, f32[2,256,1024]{2,1,0:T(8,128)S(1)}, u32[]{:S(2)}) copy-start(f32[2,256,1024]{2,1,0:T(8,128)S(1)} %get-tuple-element.53) | copy-start | bytes 6291460
  41.3 44.5 %collective-permute-start.8 = (bf16[256,4096]{1,0:T(8,128)(2,1)}, bf16[256,4096]{1,0:T(8,128)(2,1)}, u32[]{:S(2)}, u32[]{:S(2)}) collective-permute-start(bf16[256,4096]{1,0:T(8,128)(2,1)} %get-tuple-element.80), channel_id=1, source_target_pairs={{0,64},{64,0},{1,65},{65,1},{2,66},{66,2},{3,67},{67,3},{4,68},{68... | collective-permute-start | bytes 6291464 | tf_op jit(solution)/shard_map/ppermute | solution.py:20
  42.4 29.4 %collective-permute-start.4 = (bf16[768,512]{1,0:T(8,128)(2,1)S(1)}, bf16[768,512]{1,0:T(8,128)(2,1)}, u32[]{:S(2)}, u32[]{:S(2)}) collective-permute-start(bf16[768,512]{1,0:T(8,128)(2,1)S(1)} %get-tuple-element.86), channel_id=1, source_target_pairs={{0,16},{8,24},{16,32},{24,40},{32,48},{40,56},{48,0},{56,8},{1,17}... | collective-permute-start | bytes 2359304 | tf_op jit(solution)/shard_map/ppermute | solution.py:16
  48.9 24.7 %collective-permute-start.5 = (bf16[768,512]{1,0:T(8,128)(2,1)}, bf16[768,512]{1,0:T(8,128)(2,1)}, u32[]{:S(2)}, u32[]{:S(2)}) collective-permute-start(bf16[768,512]{1,0:T(8,128)(2,1)} %get-tuple-element.87), channel_id=1, source_target_pairs={{0,48},{8,56},{16,0},{24,8},{32,16},{40,24},{48,32},{56,40},{1,49}... | collective-permute-start | bytes 2359304 | tf_op jit(solution)/shard_map/ppermute | solution.py:16
  53.7 22.3 %collective-permute-start.7 = (bf16[512,512]{1,0:T(8,128)(2,1)S(1)}, bf16[512,512]{1,0:T(8,128)(2,1)S(1)}, u32[]{:S(2)}, u32[]{:S(2)}) collective-permute-start(bf16[512,512]{1,0:T(8,128)(2,1)S(1)} %collective-permute-done.refs_6_), channel_id=1, source_target_pairs={{0,8},{8,0},{16,24},{24,16},{32,40},{40,32},{48,56},{56,48},{1,9},... | collective-permute-start | bytes 1572872 | tf_op jit(solution)/shard_map/ppermute | solution.py:16
  54.7 21.3 %collective-permute-start.10 = (bf16[256,1024]{1,0:T(8,128)(2,1)}, bf16[256,1024]{1,0:T(8,128)(2,1)}, u32[]{:S(2)}, u32[]{:S(2)}) collective-permute-start(bf16[256,1024]{1,0:T(8,128)(2,1)} %get-tuple-element.82), channel_id=1, source_target_pairs={{0,2},{1,3},{2,4},{3,5},{4,6},{5,7},{6,0},{7,1},{8,10},{9,11},{10,... | collective-permute-start | bytes 1572872 | tf_op jit(solution)/shard_map/ppermute | solution.py:16
  71.8 13.9 %collective-permute-start.9 = (bf16[256,1024]{1,0:T(8,128)(2,1)}, bf16[256,1024]{1,0:T(8,128)(2,1)}, u32[]{:S(2)}, u32[]{:S(2)}) collective-permute-start(bf16[256,1024]{1,0:T(8,128)(2,1)} %get-tuple-element.83), channel_id=1, source_target_pairs={{0,6},{1,7},{2,0},{3,1},{4,2},{5,3},{6,4},{7,5},{8,14},{9,15},{10,... | collective-permute-start | bytes 1572872 | tf_op jit(solution)/shard_map/ppermute | solution.py:16
  72.4 16.6 %copy-start.16 = (f32[2,256,1024]{2,1,0:T(8,128)S(1)}, f32[2,256,1024]{2,1,0:T(8,128)}, u32[]{:S(2)}) copy-start(f32[2,256,1024]{2,1,0:T(8,128)} %get-tuple-element.51) | copy-start | bytes 6291460
  76.0 17.1 %copy-start.11 = (bf16[256,4096]{1,0:T(8,128)(2,1)S(1)}, bf16[256,4096]{1,0:T(8,128)(2,1)}, u32[]{:S(2)}) copy-start(bf16[256,4096]{1,0:T(8,128)(2,1)} %get-tuple-element.49) | copy-start | bytes 6291460
  85.8 19.7 %collective-permute-start.12 = (bf16[512,512]{1,0:T(8,128)(2,1)S(1)}, bf16[512,512]{1,0:T(8,128)(2,1)S(1)}, u32[]{:S(2)}, u32[]{:S(2)}) collective-permute-start(bf16[512,512]{1,0:T(8,128)(2,1)S(1)} %collective-permute-done.refs_6_), channel_id=1, source_target_pairs={{0,16},{8,24},{16,32},{24,40},{32,48},{40,56},{48,0},{56,8},{1,17}... | collective-permute-start | bytes 1572872 | tf_op jit(solution)/shard_map/ppermute | solution.py:16
  85.8 19.7 %collective-permute-start.13 = (bf16[512,512]{1,0:T(8,128)(2,1)S(1)}, bf16[512,512]{1,0:T(8,128)(2,1)S(1)}, u32[]{:S(2)}, u32[]{:S(2)}) collective-permute-start(bf16[512,512]{1,0:T(8,128)(2,1)S(1)} %collective-permute-done.refs_6_), channel_id=1, source_target_pairs={{0,48},{8,56},{16,0},{24,8},{32,16},{40,24},{48,32},{56,40},{1,49}... | collective-permute-start | bytes 1572872 | tf_op jit(solution)/shard_map/ppermute | solution.py:16
  93.1 4.2 %copy-start.24 = (bf16[512,512]{1,0:T(8,128)(2,1)S(1)}, bf16[512,512]{1,0:T(8,128)(2,1)}, u32[]{:S(2)}) copy-start(bf16[512,512]{1,0:T(8,128)(2,1)} %copy-done.23) | copy-start | bytes 1572868
  93.2 4.5 %copy-start.25 = (bf16[512,512]{1,0:T(8,128)(2,1)S(1)}, bf16[512,512]{1,0:T(8,128)(2,1)}, u32[]{:S(2)}) copy-start(bf16[512,512]{1,0:T(8,128)(2,1)} %param.8) | copy-start | bytes 1572868
  93.2 12.3 %collective-permute-start.11 = (bf16[512,512]{1,0:T(8,128)(2,1)S(1)}, bf16[512,512]{1,0:T(8,128)(2,1)S(1)}, u32[]{:S(2)}, u32[]{:S(2)}) collective-permute-start(bf16[512,512]{1,0:T(8,128)(2,1)S(1)} %pad_maximum_fusion.9), channel_id=1, source_target_pairs={{0,8},{8,0},{16,24},{24,16},{32,40},{40,32},{48,56},{56,48},{1,9},... | collective-permute-start | bytes 1572872 | tf_op jit(solution)/shard_map/ppermute | solution.py:16
  93.3 23.8 %collective-permute-start.15 = (bf16[2,256,1024]{2,1,0:T(8,128)(2,1)}, bf16[2,256,1024]{2,1,0:T(8,128)(2,1)}, u32[]{:S(2)}, u32[]{:S(2)}) collective-permute-start(bf16[2,256,1024]{2,1,0:T(8,128)(2,1)} %pad_maximum_fusion.3), channel_id=1, source_target_pairs={{0,6},{1,7},{2,0},{3,1},{4,2},{5,3},{6,4},{7,5},{8,14},{9,15},{10,... | collective-permute-start | bytes 3145736 | tf_op jit(solution)/shard_map/ppermute | solution.py:16
  95.4 24.1 %collective-permute-start.16 = (bf16[2,256,1024]{2,1,0:T(8,128)(2,1)}, bf16[2,256,1024]{2,1,0:T(8,128)(2,1)}, u32[]{:S(2)}, u32[]{:S(2)}) collective-permute-start(bf16[2,256,1024]{2,1,0:T(8,128)(2,1)} %pad_maximum_fusion.4), channel_id=1, source_target_pairs={{0,2},{1,3},{2,4},{3,5},{4,6},{5,7},{6,0},{7,1},{8,10},{9,11},{10,... | collective-permute-start | bytes 3145736 | tf_op jit(solution)/shard_map/ppermute | solution.py:16
  97.2 10.2 %copy-start.8 = (bf16[512,4096]{1,0:T(8,128)(2,1)}, bf16[512,4096]{1,0:T(8,128)(2,1)S(1)}, u32[]{:S(2)}) copy-start(bf16[512,4096]{1,0:T(8,128)(2,1)S(1)} %constant_dynamic-update-slice_fusion) | copy-start | bytes 12582916
  98.1 5.8 %copy-start.20 = (bf16[512,512]{1,0:T(8,128)(2,1)S(1)}, bf16[512,512]{1,0:T(8,128)(2,1)}, u32[]{:S(2)}) copy-start(bf16[512,512]{1,0:T(8,128)(2,1)} %copy-done.19) | copy-start | bytes 1572868
  107.0 25.5 %collective-permute-start.20 = (bf16[2048,512]{1,0:T(8,128)(2,1)}, bf16[2048,512]{1,0:T(8,128)(2,1)}, u32[]{:S(2)}, u32[]{:S(2)}) collective-permute-start(bf16[2048,512]{1,0:T(8,128)(2,1)} %pad_maximum_fusion.1), channel_id=1, source_target_pairs={{0,64},{64,0},{1,65},{65,1},{2,66},{66,2},{3,67},{67,3},{4,68},{68... | collective-permute-start | bytes 6291464 | tf_op jit(solution)/shard_map/ppermute | solution.py:20
  109.0 3.1 %collective-permute-start.14 = (f32[256,512]{1,0:T(8,128)}, f32[256,512]{1,0:T(8,128)S(1)}, u32[]{:S(2)}, u32[]{:S(2)}) collective-permute-start(f32[256,512]{1,0:T(8,128)} %slice.127), channel_id=1, source_target_pairs={{0,64},{64,0},{1,65},{65,1},{2,66},{66,2},{3,67},{67,3},{4,68},{68... | collective-permute-start | bytes 1572872 | tf_op jit(solution)/shard_map/ppermute | solution.py:20
  109.5 13.5 %copy-start.10 = (f32[2,256,1024]{2,1,0:T(8,128)S(1)}, f32[2,256,1024]{2,1,0:T(8,128)}, u32[]{:S(2)}) copy-start(f32[2,256,1024]{2,1,0:T(8,128)} %get-tuple-element.68) | copy-start | bytes 6291460
  109.7 20.7 %collective-permute-start.18 = (bf16[768,512]{1,0:T(8,128)(2,1)S(1)}, bf16[768,512]{1,0:T(8,128)(2,1)S(1)}, u32[]{:S(2)}, u32[]{:S(2)}) collective-permute-start(bf16[768,512]{1,0:T(8,128)(2,1)S(1)} %get-tuple-element.85), channel_id=1, source_target_pairs={{0,16},{8,24},{16,32},{24,40},{32,48},{40,56},{48,0},{56,8},{1,17}... | collective-permute-start | bytes 2359304 | tf_op jit(solution)/shard_map/ppermute | solution.py:16
  112.9 19.6 %collective-permute-start.19 = (bf16[768,512]{1,0:T(8,128)(2,1)S(1)}, bf16[768,512]{1,0:T(8,128)(2,1)S(1)}, u32[]{:S(2)}, u32[]{:S(2)}) collective-permute-start(bf16[768,512]{1,0:T(8,128)(2,1)S(1)} %get-tuple-element.84), channel_id=1, source_target_pairs={{0,48},{8,56},{16,0},{24,8},{32,16},{40,24},{48,32},{56,40},{1,49}... | collective-permute-start | bytes 2359304 | tf_op jit(solution)/shard_map/ppermute | solution.py:16
  119.5 13.0 %collective-permute-start.17 = (bf16[256,512]{1,0:T(8,128)(2,1)S(1)}, bf16[256,512]{1,0:T(8,128)(2,1)S(1)}, u32[]{:S(2)}, u32[]{:S(2)}) collective-permute-start(bf16[256,512]{1,0:T(8,128)(2,1)S(1)} %multiply_convert_fusion), channel_id=1, source_target_pairs={{0,1},{1,0},{2,3},{3,2},{4,5},{5,4},{6,7},{7,6},{8,9},{9,8},{10,11... | collective-permute-start | bytes 786440 | tf_op jit(solution)/shard_map/ppermute | solution.py:16
  125.2 23.8 %copy-start.14 = (f32[2,256,1024]{2,1,0:T(8,128)}, f32[2,256,1024]{2,1,0:T(8,128)S(1)}, u32[]{:S(2)}) copy-start(f32[2,256,1024]{2,1,0:T(8,128)S(1)} %convert_add_fusion) | copy-start | bytes 6291460
  125.3 16.0 %collective-permute-start.24 = (bf16[256,1024]{1,0:T(8,128)(2,1)S(1)}, bf16[256,1024]{1,0:T(8,128)(2,1)S(1)}, u32[]{:S(2)}, u32[]{:S(2)}) collective-permute-start(bf16[256,1024]{1,0:T(8,128)(2,1)S(1)} %fusion.8), channel_id=1, source_target_pairs={{0,1},{1,0},{2,3},{3,2},{4,5},{5,4},{6,7},{7,6},{8,9},{9,8},{10,11... | collective-permute-start | bytes 1572872 | tf_op jit(solution)/shard_map/ppermute | solution.py:16
  132.5 16.6 %copy-start.5 = (bf16[256,512]{1,0:T(8,128)(2,1)}, bf16[256,512]{1,0:T(8,128)(2,1)S(1)}, u32[]{:S(2)}) copy-start(bf16[256,512]{1,0:T(8,128)(2,1)S(1)} %collective-permute-done.17) | copy-start | bytes 786436
  132.6 16.5 %collective-permute-start.23 = (bf16[512,512]{1,0:T(8,128)(2,1)S(1)}, bf16[512,512]{1,0:T(8,128)(2,1)S(1)}, u32[]{:S(2)}, u32[]{:S(2)}) collective-permute-start(bf16[512,512]{1,0:T(8,128)(2,1)S(1)} %pad_maximum_fusion.10), channel_id=1, source_target_pairs={{0,8},{8,0},{16,24},{24,16},{32,40},{40,32},{48,56},{56,48},{1,9},... | collective-permute-start | bytes 1572872 | tf_op jit(solution)/shard_map/ppermute | solution.py:16
  133.5 15.6 %collective-permute-start.21 = (bf16[512,512]{1,0:T(8,128)(2,1)S(1)}, bf16[512,512]{1,0:T(8,128)(2,1)}, u32[]{:S(2)}, u32[]{:S(2)}) collective-permute-start(bf16[512,512]{1,0:T(8,128)(2,1)S(1)} %constant_dynamic-update-slice_fusion.2), channel_id=1, source_target_pairs={{0,2},{1,3},{2,4},{3,5},{4,6},{5,7},{6,0},{7,1},{8,10},{9,11},{10,... | collective-permute-start | bytes 1572872 | tf_op jit(solution)/shard_map/ppermute | solution.py:16
  133.6 15.5 %collective-permute-start.22 = (bf16[512,512]{1,0:T(8,128)(2,1)S(1)}, bf16[512,512]{1,0:T(8,128)(2,1)}, u32[]{:S(2)}, u32[]{:S(2)}) collective-permute-start(bf16[512,512]{1,0:T(8,128)(2,1)S(1)} %constant_dynamic-update-slice_fusion.2), channel_id=1, source_target_pairs={{0,6},{1,7},{2,0},{3,1},{4,2},{5,3},{6,4},{7,5},{8,14},{9,15},{10,... | collective-permute-start | bytes 1572872 | tf_op jit(solution)/shard_map/ppermute | solution.py:16
  141.3 7.7 %copy-start.26 = (bf16[256,1024]{1,0:T(8,128)(2,1)}, bf16[256,1024]{1,0:T(8,128)(2,1)S(1)}, u32[]{:S(2)}) copy-start(bf16[256,1024]{1,0:T(8,128)(2,1)S(1)} %collective-permute-done.24) | copy-start | bytes 1572868
  151.4 11.4 %collective-permute-start.27 = (bf16[2048,512]{1,0:T(8,128)(2,1)}, bf16[2048,512]{1,0:T(8,128)(2,1)}, u32[]{:S(2)}, u32[]{:S(2)}) collective-permute-start(bf16[2048,512]{1,0:T(8,128)(2,1)} %pad_maximum_fusion.2), channel_id=1, source_target_pairs={{0,64},{64,0},{1,65},{65,1},{2,66},{66,2},{3,67},{67,3},{4,68},{68... | collective-permute-start | bytes 6291464 | tf_op jit(solution)/shard_map/ppermute | solution.py:20
  152.5 10.0 %collective-permute-start.25 = (bf16[256,512]{1,0:T(8,128)(2,1)S(1)}, bf16[256,512]{1,0:T(8,128)(2,1)S(1)}, u32[]{:S(2)}, u32[]{:S(2)}) collective-permute-start(bf16[256,512]{1,0:T(8,128)(2,1)S(1)} %slice.111), channel_id=1, source_target_pairs={{0,2},{1,3},{2,4},{3,5},{4,6},{5,7},{6,0},{7,1},{8,10},{9,11},{10,... | collective-permute-start | bytes 786440 | tf_op jit(solution)/shard_map/ppermute | solution.py:16
  153.6 9.2 %collective-permute-start.26 = (bf16[256,512]{1,0:T(8,128)(2,1)S(1)}, bf16[256,512]{1,0:T(8,128)(2,1)S(1)}, u32[]{:S(2)}, u32[]{:S(2)}) collective-permute-start(bf16[256,512]{1,0:T(8,128)(2,1)S(1)} %slice.112), channel_id=1, source_target_pairs={{0,6},{1,7},{2,0},{3,1},{4,2},{5,3},{6,4},{7,5},{8,14},{9,15},{10,... | collective-permute-start | bytes 786440 | tf_op jit(solution)/shard_map/ppermute | solution.py:16
  178.4 37.3 %copy-start.13 = (f32[512,512]{1,0:T(8,128)S(1)}, f32[512,512]{1,0:T(8,128)}, u32[]{:S(2)}) copy-start(f32[512,512]{1,0:T(8,128)} %copy-done.12) | copy-start | bytes 3145732
  178.4 36.9 %all-to-all-start = ((bf16[8,272,512]{2,1,0:T(8,128)(2,1)}), bf16[8,272,512]{2,1,0:T(8,128)(2,1)S(1)}, u32[]{:S(2)}, u32[]{:S(2)}) async-start(bf16[8,272,512]{2,1,0:T(8,128)(2,1)} %shard_map.69), calls=%async_computation | async-start | bytes 4456448 | tf_op jit(solution)/shard_map/all_to_all | solution.py:287
  215.3 3.8 %copy-start.9 = (bf16[512,4096]{1,0:T(8,128)(2,1)S(1)}, bf16[512,4096]{1,0:T(8,128)(2,1)}, u32[]{:S(2)}) copy-start(bf16[512,4096]{1,0:T(8,128)(2,1)} %copy-done.8) | copy-start | bytes 12582916
  217.3 1.9 collective-permute-start.28
  (11 other events, 17.9 us)

commit v8 on v7

--- a/solution.py
+++ b/solution.py
@@ -213,8 +213,13 @@
             swap.append((d * 8 + t, to * 8 + d))
     projector = lax.ppermute(projector, ("dp", "tensor"), swap)
 
+    mine = lax.dynamic_slice_in_dim(student_in, role * wide, wide, axis=1)
+    theirs = lax.dynamic_slice_in_dim(student_in, (1 - role) * wide, wide, axis=1)
+    mine, theirs = lax.optimization_barrier((mine, theirs))
+    theirs = flip(theirs)
+
     own, away = teach(jnp.full((1,), role, jnp.int32), teacher_in, teacher_weight, n_tensor, cols)
-    away, projector, *w_first = lax.optimization_barrier((away, projector, *w_first))
+    away, projector, theirs, *w_first = lax.optimization_barrier((away, projector, theirs, *w_first))
     away = flip(away)
 
     up, down = ring_operands(student_weight, w_first)
@@ -230,13 +235,10 @@
     teacher = dict(zip(teacher, lax.optimization_barrier(tuple(teacher.values()))))
     over = [shift(teacher[2][0], "tensor", -1, 0), shift(teacher[2][1], "tensor", 1, 0)]
 
-    student_in = after(student_in, teacher[2])
-    mine = lax.dynamic_slice_in_dim(student_in, role * wide, wide, axis=1)
-    theirs = flip(lax.dynamic_slice_in_dim(student_in, (1 - role) * wide, wide, axis=1))
-
-    projector, p_other, theirs, *over = lax.optimization_barrier((projector, p_other, theirs, *over, *w_middle))[:5]
-    teacher[1] = jnp.stack([teacher[1][0] + over[0].astype(F32), teacher[1][1]]).astype(BF16)
-    teacher[-1] = jnp.stack([teacher[-1][0], teacher[-1][1] + over[1].astype(F32)]).astype(BF16)
+    projector, p_other, *moved = lax.optimization_barrier((projector, p_other, *over, *w_middle))
+    over, w_middle = moved[:2], moved[2:]
+    teacher[1] = (teacher[1] + jnp.pad(over[0][None].astype(F32), ((0, 1), (0, 0), (0, 0)))).astype(BF16)
+    teacher[-1] = (teacher[-1] + jnp.pad(over[1][None].astype(F32), ((1, 0), (0, 0), (0, 0)))).astype(BF16)
     teacher[1], teacher[-1], student_weight = lax.optimization_barrier((teacher[1], teacher[-1], student_weight))
     for k in (1, -1):
         teacher[k] = shift(teacher[k], "tensor", -k, 0)

time: 281 us -> 266 us (0.947)
  waiting for transfers between devices: 96.8 us -> 82.8 us
  starting transfers between devices: 44.5 us -> 50.1 us
  matrix products: 10.7 us -> 6.17 us
    ppermute x6, waiting for transfers between devices: 11.3 us -> 3.25 us  [flip(): return lax.ppermute(value, 'role', [(0, 1), (1, 0)])]
    ppermute x22, starting transfers between devices: 34.4 us -> 41.8 us  [shift(): return lax.ppermute(value, axis, perm)]
    ppermute x22, waiting for transfers between devices: 56 us -> 50.1 us  [shift(): return lax.ppermute(value, axis, perm)]
    dot_general x10, matrix products: 10.7 us -> 6.17 us  [dot(): return lax.dot_general(a, b, (dims, ((), ())), preferred_element_type=F32)]
    another operation x3 -> x0, other arithmetic: 4.05 us -> none  [the longest x2 2.98 us: shards(): jnp.stack([teacher[1][0] + over[0].astype(F32), teacher[1][1]]).astype(BF16)]
    convert_element_type x0 -> x1, other arithmetic: none -> 3.85 us  [shards(): (teacher[-1] + jnp.pad(over[1][None].astype(F32), ((1, 0), (0, 0), (0, 0)...]
    unnamed x56 -> x66, local copies, waits for them, and re-layouts: 8.06 us -> 9.62 us
  transfers between devices with their start and end apart: 30 -> 30, of which waited for: 15 -> 17; matrix products, arithmetic and copies ran while one was open for 11% -> 10% of each run, Pallas kernels for 5% -> 5%
where the time goes in v8:
time: 266 us; the launch traced here: 265 us
  waiting for transfers between devices  82.8 us (31%)
  blocking collectives  54 us (20%)
  starting transfers between devices  50.1 us (19%)
  Pallas kernels  25.6 us (10%)
  other arithmetic  24.8 us (9%)
  local copies, waits for them, and re-layouts  18.9 us (7%)
  matrix products  6.17 us (2%)
  between operations  2.99 us (1%)
    all_to_all x1, blocking collectives, shards(): grad = lax.all_to_all(grad, 'dp', 0, 0, tiled=True)  54 us
    ppermute x22, waiting for transfers between devices, shift(): return lax.ppermute(value, axis, perm)  50.1 us
    ppermute x22, starting transfers between devices, shift(): return lax.ppermute(value, axis, perm)  41.8 us
    all_to_all x1, waiting for transfers between devices, shards(): back = lax.all_to_all(back, 'tensor', 0, 0, tiled=True)  29.4 us
    pallas_call x1, Pallas kernels, teach(): pl.pallas_call(teach_kernel, grid_spec=pltpu.PrefetchScalarGridSpec(num_s...  13.2 us
    pallas_call x1, Pallas kernels, project(): pl.pallas_call(project_kernel, in_specs=[pl.BlockSpec(memory_space=pltpu....  12.4 us
    unnamed x66, local copies, waits for them, and re-layouts  9.62 us
    convert_element_type x1, other arithmetic, shards(): teacher[k] = pair.astype(BF16) if k == 2 else pair  7.32 us
  transfers between devices with their start and end apart: 30, of which 17 were waited for; matrix products, arithmetic and copies ran while one was open for 10% of the time, Pallas kernels for 5%

profile of v8, /device:TPU:0, one launch (start us, length us, event | category | flops | bytes accessed | tf_op | source)
XLA Modules:
  0.0 265.2 jit_solution(7053090998514167790)
XLA Ops:
  0.7 4.2 %constant_dynamic-slice_fusion = (bf16[256,4096]{1,0:T(8,128)(2,1)S(1)}, bf16[256,4096]{1,0:T(8,128)(2,1)}) fusion(bf16[256,8192]{1,0:T(8,128)(2,1)} %param.7, s32[]{:T(128)S(6)} %select_n.86, s32[]{:T(128)S(6)} %select_n.85), kind=kLoop, calls=%fused_computation.76 | loop fusion | bytes 8388616 | tf_op jit(solution)/shard_map/dynamic_slice | solution.py:217
  4.8 1.6 collective-permute-start.2
  6.4 1.6 collective-permute-start.3
  8.0 1.7 collective-permute-start.4
  10.4 13.2 %shard_map.68 = (bf16[8,256,1024]{2,1,0:T(8,128)(2,1)S(1)}, bf16[8,256,1024]{2,1,0:T(8,128)(2,1)}) custom-call(s32[1]{0:T(128)} %bitcast.role, bf16[512,1024]{1,0:T(8,128)(2,1)S(1)} %bitcast.46, bf16[1024,8192]{1,0:T(8,128)(2,1)} %weight.1), custom_call_target="tpu_custom_call" | custom-call | flops 8589934592 | bytes 16777216 | tf_op jit(solution)/shard_map/pallas_call | solution.py:173
  23.6 2.0 copy-done
  25.6 1.3 copy-done.20
  27.0 1.3 pad_maximum_fusion.3
  28.3 13.8 %collective-permute-start.10 = (bf16[768,512]{1,0:T(8,128)(2,1)}, bf16[768,512]{1,0:T(8,128)(2,1)S(1)}, u32[]{:S(2)}, u32[]{:S(2)}) collective-permute-start(bf16[768,512]{1,0:T(8,128)(2,1)} %get-tuple-element.92), channel_id=1, source_target_pairs={{0,48},{8,56},{16,0},{24,8},{32,16},{40,24},{48,32},{56,40},{1,49}... | collective-permute-start | bytes 2359304 | tf_op jit(solution)/shard_map/ppermute | solution.py:16
  42.3 7.3 %add_convert_fusion.2 = (bf16[2,256,1024]{2,1,0:T(8,128)(2,1)S(1)}, f32[2,256,1024]{2,1,0:T(8,128)}, f32[2,256,1024]{2,1,0:T(8,128)}, f32[2,256,1024]{2,1,0:T(8,128)}) fusion(bf16[8,256,1024]{2,1,0:T(8,128)(2,1)} %collective-permute-done.6, s32[]{:T(128)S(6)} %select_n.90, bf16[8,256,1024]{2,1,0:T(8,128)(2,1)} %copy-done, s32[]{:T(128)S(6)} %select_n.89, ...), kind=kLoop, calls=%fused_computation.9 | loop fusion | flops 6815744 | bytes 15728656 | tf_op jit(solution)/shard_map/convert_element_type | solution.py:234
  49.6 1.1 slice_bitcast_fusion
  50.7 3.6 %collective-permute-start.7 = (bf16[256,1024]{1,0:T(8,128)(2,1)}, bf16[256,1024]{1,0:T(8,128)(2,1)}, u32[]{:S(2)}, u32[]{:S(2)}) collective-permute-start(bf16[256,1024]{1,0:T(8,128)(2,1)} %get-tuple-element.89), channel_id=1, source_target_pairs={{0,6},{1,7},{2,0},{3,1},{4,2},{5,3},{6,4},{7,5},{8,14},{9,15},{10,... | collective-permute-start | bytes 1572872 | tf_op jit(solution)/shard_map/ppermute | solution.py:16
  54.3 2.0 collective-permute-done.5.refs_7_
  56.3 3.6 %collective-permute-done.10 = bf16[768,512]{1,0:T(8,128)(2,1)S(1)} collective-permute-done((bf16[768,512]{1,0:T(8,128)(2,1)}, bf16[768,512]{1,0:T(8,128)(2,1)S(1)}, u32[]{:S(2)}, u32[]{:S(2)}) %collective-permute-start.10) | collective-permute-done | bytes 786464 | tf_op jit(solution)/shard_map/ppermute | solution.py:16
  59.9 3.3 %collective-permute-done.9 = bf16[768,512]{1,0:T(8,128)(2,1)S(1)} collective-permute-done((bf16[768,512]{1,0:T(8,128)(2,1)}, bf16[768,512]{1,0:T(8,128)(2,1)S(1)}, u32[]{:S(2)}, u32[]{:S(2)}) %collective-permute-start.9) | collective-permute-done | bytes 786464 | tf_op jit(solution)/shard_map/ppermute | solution.py:16
  63.2 2.9 %collective-permute-done.7 = bf16[256,1024]{1,0:T(8,128)(2,1)} collective-permute-done((bf16[256,1024]{1,0:T(8,128)(2,1)}, bf16[256,1024]{1,0:T(8,128)(2,1)}, u32[]{:S(2)}, u32[]{:S(2)}) %collective-permute-start.7) | collective-permute-done | bytes 524320 | tf_op jit(solution)/shard_map/ppermute | solution.py:16
  66.1 3.4 %collective-permute-done.8 = bf16[256,1024]{1,0:T(8,128)(2,1)} collective-permute-done((bf16[256,1024]{1,0:T(8,128)(2,1)}, bf16[256,1024]{1,0:T(8,128)(2,1)}, u32[]{:S(2)}, u32[]{:S(2)}) %collective-permute-start.8) | collective-permute-done | bytes 524320 | tf_op jit(solution)/shard_map/ppermute | solution.py:16
  70.5 2.3 collective-permute-start.13
  74.3 3.9 %add_convert_fusion = (bf16[2,256,1024]{2,1,0:T(8,128)(2,1)}, bf16[2,256,1024]{2,1,0:T(8,128)(2,1)}) fusion(f32[2,256,1024]{2,1,0:T(8,128)S(1)} %copy-done.13, bf16[1,256,1024]{2,1,0:T(8,128)(2,1)} %bitcast.21, f32[2,256,1024]{2,1,0:T(8,128)} %get-tuple-element.57, bf16[1,256,1024]{2,1,0:T(8,128)(2,1)} %bitcast.20), kind=kLoop, calls=%fused_computation.7 | loop fusion | flops 3145728 | bytes 7340032 | tf_op jit(solution)/shard_map/convert_element_type | solution.py:241
  78.4 1.4 copy-done.21
  79.9 1.0 copy-done.23
  82.0 1.7 collective-permute-start.16
  86.2 1.5 pad_maximum_fusion.1
  90.8 1.7 collective-permute-done.14
  93.3 1.7 collective-permute-start.19
  95.1 1.2 multiply_convert_fusion
  96.3 9.0 %collective-permute-done.15 = bf16[2,256,1024]{2,1,0:T(8,128)(2,1)} collective-permute-done((bf16[2,256,1024]{2,1,0:T(8,128)(2,1)}, bf16[2,256,1024]{2,1,0:T(8,128)(2,1)}, u32[]{:S(2)}, u32[]{:S(2)}) %collective-permute-start.15) | collective-permute-done | bytes 1048608 | tf_op jit(solution)/shard_map/ppermute | solution.py:16
  105.3 1.6 collective-permute-done.16
  106.9 3.6 %collective-permute-start.17 = (bf16[256,512]{1,0:T(8,128)(2,1)S(1)}, bf16[256,512]{1,0:T(8,128)(2,1)S(1)}, u32[]{:S(2)}, u32[]{:S(2)}) collective-permute-start(bf16[256,512]{1,0:T(8,128)(2,1)S(1)} %multiply_convert_fusion), channel_id=1, source_target_pairs={{0,1},{1,0},{2,3},{3,2},{4,5},{5,4},{6,7},{7,6},{8,9},{9,8},{10,11... | collective-permute-start | bytes 786440 | tf_op jit(solution)/shard_map/ppermute | solution.py:16
  110.4 2.2 convert_add_fusion
  112.9 4.3 %collective-permute-done.17 = bf16[256,512]{1,0:T(8,128)(2,1)S(1)} collective-permute-done((bf16[256,512]{1,0:T(8,128)(2,1)S(1)}, bf16[256,512]{1,0:T(8,128)(2,1)S(1)}, u32[]{:S(2)}, u32[]{:S(2)}) %collective-permute-start.17) | collective-permute-done | bytes 262176 | tf_op jit(solution)/shard_map/ppermute | solution.py:16
  117.3 1.4 collective-permute-start.23
  119.3 2.8 %collective-permute-start.22 = (bf16[512,512]{1,0:T(8,128)(2,1)S(1)}, bf16[512,512]{1,0:T(8,128)(2,1)}, u32[]{:S(2)}, u32[]{:S(2)}) collective-permute-start(bf16[512,512]{1,0:T(8,128)(2,1)S(1)} %constant_dynamic-update-slice_fusion.2), channel_id=1, source_target_pairs={{0,6},{1,7},{2,0},{3,1},{4,2},{5,3},{6,4},{7,5},{8,14},{9,15},{10,... | collective-permute-start | bytes 1572872 | tf_op jit(solution)/shard_map/ppermute | solution.py:16
  122.1 7.1 %collective-permute-done.24 = bf16[256,1024]{1,0:T(8,128)(2,1)S(1)} collective-permute-done((bf16[256,1024]{1,0:T(8,128)(2,1)S(1)}, bf16[256,1024]{1,0:T(8,128)(2,1)S(1)}, u32[]{:S(2)}, u32[]{:S(2)}) %collective-permute-start.24) | collective-permute-done | bytes 524320 | tf_op jit(solution)/shard_map/ppermute | solution.py:16
  129.2 8.0 %collective-permute-done.23.refs_12_ = bf16[512,512]{1,0:T(8,128)(2,1)S(1)} collective-permute-done((bf16[512,512]{1,0:T(8,128)(2,1)S(1)}, bf16[512,512]{1,0:T(8,128)(2,1)S(1)}, u32[]{:S(2)}, u32[]{:S(2)}) %collective-permute-start.23) | collective-permute-done | bytes 524320 | tf_op jit(solution)/shard_map/ppermute | solution.py:16
  138.0 1.6 pad_maximum_fusion.2
  140.5 1.1 slice.93
  142.7 3.3 %collective-permute-start.26 = (bf16[256,512]{1,0:T(8,128)(2,1)S(1)}, bf16[256,512]{1,0:T(8,128)(2,1)S(1)}, u32[]{:S(2)}, u32[]{:S(2)}) collective-permute-start(bf16[256,512]{1,0:T(8,128)(2,1)S(1)} %slice.94), channel_id=1, source_target_pairs={{0,6},{1,7},{2,0},{3,1},{4,2},{5,3},{6,4},{7,5},{8,14},{9,15},{10,... | collective-permute-start | bytes 786440 | tf_op jit(solution)/shard_map/ppermute | solution.py:16
  145.9 1.6 bitcast_add_fusion.refs_15_
  147.5 4.1 %collective-permute-done.25 = bf16[256,512]{1,0:T(8,128)(2,1)S(1)} collective-permute-done((bf16[256,512]{1,0:T(8,128)(2,1)S(1)}, bf16[256,512]{1,0:T(8,128)(2,1)S(1)}, u32[]{:S(2)}, u32[]{:S(2)}) %collective-permute-start.25) | collective-permute-done | bytes 262176 | tf_op jit(solution)/shard_map/ppermute | solution.py:16
  151.9 12.4 %shard_map.69 = bf16[8,272,512]{2,1,0:T(8,128)(2,1)} custom-call(s32[17]{0:T(128)S(1)} %stack.68.order, bf16[1,256,512]{2,1,0:T(8,128)(2,1)S(1)} %bitcast.43, bf16[1,256,512]{2,1,0:T(8,128)(2,1)S(1)} %bitcast.44, bf16[2,256,512]{2,1,0:T(8,128)(2,1)} %bitcast.25.refs_2_, bf16[1,256,512]{2,1,0:T(8,128)(2,1)S(1)} %bitcast.47, ...), custom_call_target="tpu_custom_call" | custom-call | flops 4294967296 | bytes 8388608 | tf_op jit(solution)/shard_map/pallas_call | solution.py:137
  164.3 6.6 %all-to-all-start = ((bf16[8,272,512]{2,1,0:T(8,128)(2,1)}), bf16[8,272,512]{2,1,0:T(8,128)(2,1)S(1)}, u32[]{:S(2)}, u32[]{:S(2)}) async-start(bf16[8,272,512]{2,1,0:T(8,128)(2,1)} %shard_map.69), calls=%async_computation | async-start | bytes 4456448 | tf_op jit(solution)/shard_map/all_to_all | solution.py:289
  171.0 29.4 %all-to-all-done = bf16[8,272,512]{2,1,0:T(8,128)(2,1)S(1)} async-done(((bf16[8,272,512]{2,1,0:T(8,128)(2,1)}), bf16[8,272,512]{2,1,0:T(8,128)(2,1)S(1)}, u32[]{:S(2)}, u32[]{:S(2)}) %all-to-all-start) | async-done | bytes 2228256 | tf_op jit(solution)/shard_map/all_to_all | solution.py:289
  200.8 1.5 fusion.5
  202.7 1.5 collective-permute-done.28
  204.3 2.5 convolution_convert_fusion
  207.2 54.0 %all_to_all.10 = bf16[8,528,512]{2,1,0:T(8,128)(2,1)S(1)} all-to-all(bf16[8,528,512]{2,1,0:T(8,128)(2,1)S(1)} %pad_maximum_fusion), channel_id=1, replica_groups=mesh['role'=2,'dp'=8,'tensor'=8] {'dp'}, dimensions={0} | all-to-all | bytes 8650752 | tf_op jit(solution)/shard_map/all_to_all | solution.py:302
  261.9 1.1 slice_multiply_fusion
  (137 shorter events, 17.5 us)
Async XLA Ops:
  0.6 4.2 %copy-start.28 = (bf16[512,512]{1,0:T(8,128)(2,1)S(1)}, bf16[512,512]{1,0:T(8,128)(2,1)}, u32[]{:S(2)}) copy-start(bf16[512,512]{1,0:T(8,128)(2,1)} %param.8) | copy-start | bytes 1572868
  0.6 9.0 %copy-start.31 = (bf16[512,512]{1,0:T(8,128)(2,1)S(1)}, bf16[512,512]{1,0:T(8,128)(2,1)}, u32[]{:S(2)}) copy-start(bf16[512,512]{1,0:T(8,128)(2,1)} %param.9) | copy-start | bytes 1572868
  0.7 9.7 %copy-start.9 = (bf16[2,256,1024]{2,1,0:T(8,128)(2,1)S(1)}, bf16[2,256,1024]{2,1,0:T(8,128)(2,1)}, u32[]{:S(2)}) copy-start(bf16[2,256,1024]{2,1,0:T(8,128)(2,1)} %param.5) | copy-start | bytes 3145732
  4.8 20.8 %collective-permute-start.1 = (bf16[256,4096]{1,0:T(8,128)(2,1)S(1)}, bf16[256,4096]{1,0:T(8,128)(2,1)S(1)}, u32[]{:S(2)}, u32[]{:S(2)}) collective-permute-start(bf16[256,4096]{1,0:T(8,128)(2,1)S(1)} %get-tuple-element.43), channel_id=1, source_target_pairs={{0,64},{64,0},{1,65},{65,1},{2,66},{66,2},{3,67},{67,3},{4,68},{68... | collective-permute-start | bytes 6291464 | tf_op jit(solution)/shard_map/ppermute | solution.py:20
  4.8 20.7 %collective-permute-start.2 = (bf16[512,512]{1,0:T(8,128)(2,1)S(1)}, bf16[512,512]{1,0:T(8,128)(2,1)S(1)}, u32[]{:S(2)}, u32[]{:S(2)}) collective-permute-start(bf16[512,512]{1,0:T(8,128)(2,1)S(1)} %copy-done.28), channel_id=1, source_target_pairs={{0,8},{8,0},{16,24},{24,16},{32,40},{40,32},{48,56},{56,48},{1,9},... | collective-permute-start | bytes 1572872 | tf_op jit(solution)/shard_map/ppermute | solution.py:16
  6.4 19.1 %collective-permute-start.3 = (bf16[512,512]{1,0:T(8,128)(2,1)S(1)}, bf16[512,512]{1,0:T(8,128)(2,1)S(1)}, u32[]{:S(2)}, u32[]{:S(2)}) collective-permute-start(bf16[512,512]{1,0:T(8,128)(2,1)S(1)} %copy-done.28), channel_id=1, source_target_pairs={{0,16},{8,24},{16,32},{24,40},{32,48},{40,56},{48,0},{56,8},{1,17}... | collective-permute-start | bytes 1572872 | tf_op jit(solution)/shard_map/ppermute | solution.py:16
  8.0 17.6 %collective-permute-start.4 = (bf16[512,512]{1,0:T(8,128)(2,1)S(1)}, bf16[512,512]{1,0:T(8,128)(2,1)S(1)}, u32[]{:S(2)}, u32[]{:S(2)}) collective-permute-start(bf16[512,512]{1,0:T(8,128)(2,1)S(1)} %copy-done.28), channel_id=1, source_target_pairs={{0,48},{8,56},{16,0},{24,8},{32,16},{40,24},{48,32},{56,40},{1,49}... | collective-permute-start | bytes 1572872 | tf_op jit(solution)/shard_map/ppermute | solution.py:16
  9.7 15.9 %collective-permute-start = (bf16[512,512]{1,0:T(8,128)(2,1)S(1)}, bf16[512,512]{1,0:T(8,128)(2,1)S(1)}, u32[]{:S(2)}, u32[]{:S(2)}) collective-permute-start(bf16[512,512]{1,0:T(8,128)(2,1)S(1)} %copy-done.31), channel_id=1, source_target_pairs={{0,0},{1,8},{2,16},{3,24},{4,32},{5,40},{6,48},{7,56},{8,9},{9,1},... | collective-permute-start | bytes 1572872 | tf_op jit(solution)/shard_map/ppermute | solution.py:214
  25.6 60.6 %copy-start.1 = (bf16[512,512]{1,0:T(8,128)(2,1)}, bf16[512,512]{1,0:T(8,128)(2,1)S(1)}, u32[]{:S(2)}) copy-start(bf16[512,512]{1,0:T(8,128)(2,1)S(1)} %collective-permute-done.refs_6_) | copy-start | bytes 1572868
  25.6 16.6 %copy-start.24 = (bf16[512,512]{1,0:T(8,128)(2,1)}, bf16[512,512]{1,0:T(8,128)(2,1)S(1)}, u32[]{:S(2)}) copy-start(bf16[512,512]{1,0:T(8,128)(2,1)S(1)} %collective-permute-done.3) | copy-start | bytes 1572868
  25.6 16.6 %copy-start.26 = (bf16[512,512]{1,0:T(8,128)(2,1)}, bf16[512,512]{1,0:T(8,128)(2,1)S(1)}, u32[]{:S(2)}) copy-start(bf16[512,512]{1,0:T(8,128)(2,1)S(1)} %collective-permute-done.4) | copy-start | bytes 1572868
  27.0 15.3 %collective-permute-start.6 = (bf16[8,256,1024]{2,1,0:T(8,128)(2,1)}, bf16[8,256,1024]{2,1,0:T(8,128)(2,1)}, u32[]{:S(2)}, u32[]{:S(2)}) collective-permute-start(bf16[8,256,1024]{2,1,0:T(8,128)(2,1)} %get-tuple-element.46), channel_id=1, source_target_pairs={{0,64},{64,0},{1,65},{65,1},{2,66},{66,2},{3,67},{67,3},{4,68},{68... | collective-permute-start | bytes 12582920 | tf_op jit(solution)/shard_map/ppermute | solution.py:20
  28.3 31.6 %collective-permute-start.10 = (bf16[768,512]{1,0:T(8,128)(2,1)}, bf16[768,512]{1,0:T(8,128)(2,1)S(1)}, u32[]{:S(2)}, u32[]{:S(2)}) collective-permute-start(bf16[768,512]{1,0:T(8,128)(2,1)} %get-tuple-element.92), channel_id=1, source_target_pairs={{0,48},{8,56},{16,0},{24,8},{32,16},{40,24},{48,32},{56,40},{1,49}... | collective-permute-start | bytes 2359304 | tf_op jit(solution)/shard_map/ppermute | solution.py:16
  42.2 21.1 %collective-permute-start.9 = (bf16[768,512]{1,0:T(8,128)(2,1)}, bf16[768,512]{1,0:T(8,128)(2,1)S(1)}, u32[]{:S(2)}, u32[]{:S(2)}) collective-permute-start(bf16[768,512]{1,0:T(8,128)(2,1)} %get-tuple-element.93), channel_id=1, source_target_pairs={{0,16},{8,24},{16,32},{24,40},{32,48},{40,56},{48,0},{56,8},{1,17}... | collective-permute-start | bytes 2359304 | tf_op jit(solution)/shard_map/ppermute | solution.py:16
  42.2 14.1 %collective-permute-start.5 = (bf16[512,512]{1,0:T(8,128)(2,1)S(1)}, bf16[512,512]{1,0:T(8,128)(2,1)S(1)}, u32[]{:S(2)}, u32[]{:S(2)}) collective-permute-start(bf16[512,512]{1,0:T(8,128)(2,1)S(1)} %collective-permute-done.refs_6_), channel_id=1, source_target_pairs={{0,8},{8,0},{16,24},{24,16},{32,40},{40,32},{48,56},{56,48},{1,9},... | collective-permute-start | bytes 1572872 | tf_op jit(solution)/shard_map/ppermute | solution.py:16
  50.7 15.4 %collective-permute-start.7 = (bf16[256,1024]{1,0:T(8,128)(2,1)}, bf16[256,1024]{1,0:T(8,128)(2,1)}, u32[]{:S(2)}, u32[]{:S(2)}) collective-permute-start(bf16[256,1024]{1,0:T(8,128)(2,1)} %get-tuple-element.89), channel_id=1, source_target_pairs={{0,6},{1,7},{2,0},{3,1},{4,2},{5,3},{6,4},{7,5},{8,14},{9,15},{10,... | collective-permute-start | bytes 1572872 | tf_op jit(solution)/shard_map/ppermute | solution.py:16
  54.3 15.2 %collective-permute-start.8 = (bf16[256,1024]{1,0:T(8,128)(2,1)}, bf16[256,1024]{1,0:T(8,128)(2,1)}, u32[]{:S(2)}, u32[]{:S(2)}) collective-permute-start(bf16[256,1024]{1,0:T(8,128)(2,1)} %get-tuple-element.88), channel_id=1, source_target_pairs={{0,2},{1,3},{2,4},{3,5},{4,6},{5,7},{6,0},{7,1},{8,10},{9,11},{10,... | collective-permute-start | bytes 1572872 | tf_op jit(solution)/shard_map/ppermute | solution.py:16
  54.3 20.0 %copy-start.13 = (f32[2,256,1024]{2,1,0:T(8,128)S(1)}, f32[2,256,1024]{2,1,0:T(8,128)}, u32[]{:S(2)}) copy-start(f32[2,256,1024]{2,1,0:T(8,128)} %get-tuple-element.59) | copy-start | bytes 6291460
  69.5 16.7 %collective-permute-start.12 = (bf16[512,512]{1,0:T(8,128)(2,1)S(1)}, bf16[512,512]{1,0:T(8,128)(2,1)S(1)}, u32[]{:S(2)}, u32[]{:S(2)}) collective-permute-start(bf16[512,512]{1,0:T(8,128)(2,1)S(1)} %collective-permute-done.refs_6_), channel_id=1, source_target_pairs={{0,16},{8,24},{16,32},{24,40},{32,48},{40,56},{48,0},{56,8},{1,17}... | collective-permute-start | bytes 1572872 | tf_op jit(solution)/shard_map/ppermute | solution.py:16
  70.5 15.7 %collective-permute-start.13 = (bf16[512,512]{1,0:T(8,128)(2,1)S(1)}, bf16[512,512]{1,0:T(8,128)(2,1)S(1)}, u32[]{:S(2)}, u32[]{:S(2)}) collective-permute-start(bf16[512,512]{1,0:T(8,128)(2,1)S(1)} %collective-permute-done.refs_6_), channel_id=1, source_target_pairs={{0,48},{8,56},{16,0},{24,8},{32,16},{40,24},{48,32},{56,40},{1,49}... | collective-permute-start | bytes 1572872 | tf_op jit(solution)/shard_map/ppermute | solution.py:16
  73.8 12.4 %collective-permute-start.11 = (bf16[512,512]{1,0:T(8,128)(2,1)S(1)}, bf16[512,512]{1,0:T(8,128)(2,1)S(1)}, u32[]{:S(2)}, u32[]{:S(2)}) collective-permute-start(bf16[512,512]{1,0:T(8,128)(2,1)S(1)} %pad_maximum_fusion.7), channel_id=1, source_target_pairs={{0,8},{8,0},{16,24},{24,16},{32,40},{40,32},{48,56},{56,48},{1,9},... | collective-permute-start | bytes 1572872 | tf_op jit(solution)/shard_map/ppermute | solution.py:16
  80.9 7.6 %copy-start.10 = (bf16[512,4096]{1,0:T(8,128)(2,1)}, bf16[512,4096]{1,0:T(8,128)(2,1)S(1)}, u32[]{:S(2)}) copy-start(bf16[512,4096]{1,0:T(8,128)(2,1)S(1)} %constant_dynamic-update-slice_fusion) | copy-start | bytes 12582916
  81.7 23.6 %collective-permute-start.15 = (bf16[2,256,1024]{2,1,0:T(8,128)(2,1)}, bf16[2,256,1024]{2,1,0:T(8,128)(2,1)}, u32[]{:S(2)}, u32[]{:S(2)}) collective-permute-start(bf16[2,256,1024]{2,1,0:T(8,128)(2,1)} %get-tuple-element.65), channel_id=1, source_target_pairs={{0,6},{1,7},{2,0},{3,1},{4,2},{5,3},{6,4},{7,5},{8,14},{9,15},{10,... | collective-permute-start | bytes 3145736 | tf_op jit(solution)/shard_map/ppermute | solution.py:16
  82.0 24.8 %collective-permute-start.16 = (bf16[2,256,1024]{2,1,0:T(8,128)(2,1)}, bf16[2,256,1024]{2,1,0:T(8,128)(2,1)}, u32[]{:S(2)}, u32[]{:S(2)}) collective-permute-start(bf16[2,256,1024]{2,1,0:T(8,128)(2,1)} %get-tuple-element.66), channel_id=1, source_target_pairs={{0,2},{1,3},{2,4},{3,5},{4,6},{5,7},{6,0},{7,1},{8,10},{9,11},{10,... | collective-permute-start | bytes 3145736 | tf_op jit(solution)/shard_map/ppermute | solution.py:16
  87.6 29.6 %collective-permute-start.20 = (bf16[2048,512]{1,0:T(8,128)(2,1)}, bf16[2048,512]{1,0:T(8,128)(2,1)}, u32[]{:S(2)}, u32[]{:S(2)}) collective-permute-start(bf16[2048,512]{1,0:T(8,128)(2,1)} %pad_maximum_fusion.1), channel_id=1, source_target_pairs={{0,64},{64,0},{1,65},{65,1},{2,66},{66,2},{3,67},{67,3},{4,68},{68... | collective-permute-start | bytes 6291464 | tf_op jit(solution)/shard_map/ppermute | solution.py:20
  90.0 2.6 collective-permute-start.14
  90.6 4.5 %copy-start.16 = (f32[512,512]{1,0:T(8,128)S(1)}, f32[512,512]{1,0:T(8,128)}, u32[]{:S(2)}) copy-start(f32[512,512]{1,0:T(8,128)} %copy-done.15) | copy-start | bytes 3145732
  90.6 19.8 %copy-start.12 = (f32[2,256,1024]{2,1,0:T(8,128)S(1)}, f32[2,256,1024]{2,1,0:T(8,128)}, u32[]{:S(2)}) copy-start(f32[2,256,1024]{2,1,0:T(8,128)} %get-tuple-element.74) | copy-start | bytes 6291460
  90.8 22.1 %collective-permute-start.18 = (bf16[768,512]{1,0:T(8,128)(2,1)S(1)}, bf16[768,512]{1,0:T(8,128)(2,1)S(1)}, u32[]{:S(2)}, u32[]{:S(2)}) collective-permute-start(bf16[768,512]{1,0:T(8,128)(2,1)S(1)} %get-tuple-element.91), channel_id=1, source_target_pairs={{0,16},{8,24},{16,32},{24,40},{32,48},{40,56},{48,0},{56,8},{1,17}... | collective-permute-start | bytes 2359304 | tf_op jit(solution)/shard_map/ppermute | solution.py:16
  93.3 19.6 %collective-permute-start.19 = (bf16[768,512]{1,0:T(8,128)(2,1)S(1)}, bf16[768,512]{1,0:T(8,128)(2,1)S(1)}, u32[]{:S(2)}, u32[]{:S(2)}) collective-permute-start(bf16[768,512]{1,0:T(8,128)(2,1)S(1)} %get-tuple-element.90), channel_id=1, source_target_pairs={{0,48},{8,56},{16,0},{24,8},{32,16},{40,24},{48,32},{56,40},{1,49}... | collective-permute-start | bytes 2359304 | tf_op jit(solution)/shard_map/ppermute | solution.py:16
  106.9 10.3 %collective-permute-start.17 = (bf16[256,512]{1,0:T(8,128)(2,1)S(1)}, bf16[256,512]{1,0:T(8,128)(2,1)S(1)}, u32[]{:S(2)}, u32[]{:S(2)}) collective-permute-start(bf16[256,512]{1,0:T(8,128)(2,1)S(1)} %multiply_convert_fusion), channel_id=1, source_target_pairs={{0,1},{1,0},{2,3},{3,2},{4,5},{5,4},{6,7},{7,6},{8,9},{9,8},{10,11... | collective-permute-start | bytes 786440 | tf_op jit(solution)/shard_map/ppermute | solution.py:16
  112.6 24.6 %copy-start.17 = (f32[2,256,1024]{2,1,0:T(8,128)}, f32[2,256,1024]{2,1,0:T(8,128)S(1)}, u32[]{:S(2)}) copy-start(f32[2,256,1024]{2,1,0:T(8,128)S(1)} %convert_add_fusion) | copy-start | bytes 6291460
  112.7 16.4 %collective-permute-start.24 = (bf16[256,1024]{1,0:T(8,128)(2,1)S(1)}, bf16[256,1024]{1,0:T(8,128)(2,1)S(1)}, u32[]{:S(2)}, u32[]{:S(2)}) collective-permute-start(bf16[256,1024]{1,0:T(8,128)(2,1)S(1)} %fusion.3), channel_id=1, source_target_pairs={{0,1},{1,0},{2,3},{3,2},{4,5},{5,4},{6,7},{7,6},{8,9},{9,8},{10,11... | collective-permute-start | bytes 1572872 | tf_op jit(solution)/shard_map/ppermute | solution.py:16
  117.2 20.0 %copy-start.5 = (bf16[256,512]{1,0:T(8,128)(2,1)}, bf16[256,512]{1,0:T(8,128)(2,1)S(1)}, u32[]{:S(2)}) copy-start(bf16[256,512]{1,0:T(8,128)(2,1)S(1)} %collective-permute-done.17) | copy-start | bytes 786436
  117.3 19.9 %collective-permute-start.23 = (bf16[512,512]{1,0:T(8,128)(2,1)S(1)}, bf16[512,512]{1,0:T(8,128)(2,1)S(1)}, u32[]{:S(2)}, u32[]{:S(2)}) collective-permute-start(bf16[512,512]{1,0:T(8,128)(2,1)S(1)} %pad_maximum_fusion.8), channel_id=1, source_target_pairs={{0,8},{8,0},{16,24},{24,16},{32,40},{40,32},{48,56},{56,48},{1,9},... | collective-permute-start | bytes 1572872 | tf_op jit(solution)/shard_map/ppermute | solution.py:16
  118.8 18.4 %collective-permute-start.21 = (bf16[512,512]{1,0:T(8,128)(2,1)S(1)}, bf16[512,512]{1,0:T(8,128)(2,1)S(1)}, u32[]{:S(2)}, u32[]{:S(2)}) collective-permute-start(bf16[512,512]{1,0:T(8,128)(2,1)S(1)} %constant_dynamic-update-slice_fusion.2), channel_id=1, source_target_pairs={{0,2},{1,3},{2,4},{3,5},{4,6},{5,7},{6,0},{7,1},{8,10},{9,11},{10,... | collective-permute-start | bytes 1572872 | tf_op jit(solution)/shard_map/ppermute | solution.py:16
  119.3 18.7 %collective-permute-start.22 = (bf16[512,512]{1,0:T(8,128)(2,1)S(1)}, bf16[512,512]{1,0:T(8,128)(2,1)}, u32[]{:S(2)}, u32[]{:S(2)}) collective-permute-start(bf16[512,512]{1,0:T(8,128)(2,1)S(1)} %constant_dynamic-update-slice_fusion.2), channel_id=1, source_target_pairs={{0,6},{1,7},{2,0},{3,1},{4,2},{5,3},{6,4},{7,5},{8,14},{9,15},{10,... | collective-permute-start | bytes 1572872 | tf_op jit(solution)/shard_map/ppermute | solution.py:16
  129.2 8.1 %copy-start.30 = (bf16[256,1024]{1,0:T(8,128)(2,1)}, bf16[256,1024]{1,0:T(8,128)(2,1)S(1)}, u32[]{:S(2)}) copy-start(bf16[256,1024]{1,0:T(8,128)(2,1)S(1)} %collective-permute-done.24) | copy-start | bytes 1572868
  140.4 11.5 %collective-permute-start.27 = (bf16[2048,512]{1,0:T(8,128)(2,1)}, bf16[2048,512]{1,0:T(8,128)(2,1)}, u32[]{:S(2)}, u32[]{:S(2)}) collective-permute-start(bf16[2048,512]{1,0:T(8,128)(2,1)} %pad_maximum_fusion.2), channel_id=1, source_target_pairs={{0,64},{64,0},{1,65},{65,1},{2,66},{66,2},{3,67},{67,3},{4,68},{68... | collective-permute-start | bytes 6291464 | tf_op jit(solution)/shard_map/ppermute | solution.py:20
  140.5 11.4 %copy-start.2 = (bf16[512,512]{1,0:T(8,128)(2,1)S(1)}, bf16[512,512]{1,0:T(8,128)(2,1)}, u32[]{:S(2)}) copy-start(bf16[512,512]{1,0:T(8,128)(2,1)} %copy-done.1) | copy-start | bytes 1572868
  140.5 11.4 %copy-start.4 = (bf16[512,512]{1,0:T(8,128)(2,1)S(1)}, bf16[512,512]{1,0:T(8,128)(2,1)}, u32[]{:S(2)}) copy-start(bf16[512,512]{1,0:T(8,128)(2,1)} %copy-done.3) | copy-start | bytes 1572868
  140.5 11.4 %copy-start.6 = (bf16[256,512]{1,0:T(8,128)(2,1)S(1)}, bf16[256,512]{1,0:T(8,128)(2,1)}, u32[]{:S(2)}) copy-start(bf16[256,512]{1,0:T(8,128)(2,1)} %copy-done.5) | copy-start | bytes 786436
  140.5 11.4 %copy-start.8 = (bf16[512,512]{1,0:T(8,128)(2,1)S(1)}, bf16[512,512]{1,0:T(8,128)(2,1)}, u32[]{:S(2)}) copy-start(bf16[512,512]{1,0:T(8,128)(2,1)} %copy-done.7) | copy-start | bytes 1572868
  141.6 10.0 %collective-permute-start.25 = (bf16[256,512]{1,0:T(8,128)(2,1)S(1)}, bf16[256,512]{1,0:T(8,128)(2,1)S(1)}, u32[]{:S(2)}, u32[]{:S(2)}) collective-permute-start(bf16[256,512]{1,0:T(8,128)(2,1)S(1)} %slice.93), channel_id=1, source_target_pairs={{0,2},{1,3},{2,4},{3,5},{4,6},{5,7},{6,0},{7,1},{8,10},{9,11},{10,... | collective-permute-start | bytes 786440 | tf_op jit(solution)/shard_map/ppermute | solution.py:16
  142.7 9.2 %collective-permute-start.26 = (bf16[256,512]{1,0:T(8,128)(2,1)S(1)}, bf16[256,512]{1,0:T(8,128)(2,1)S(1)}, u32[]{:S(2)}, u32[]{:S(2)}) collective-permute-start(bf16[256,512]{1,0:T(8,128)(2,1)S(1)} %slice.94), channel_id=1, source_target_pairs={{0,6},{1,7},{2,0},{3,1},{4,2},{5,3},{6,4},{7,5},{8,14},{9,15},{10,... | collective-permute-start | bytes 786440 | tf_op jit(solution)/shard_map/ppermute | solution.py:16
  164.3 36.1 %all-to-all-start = ((bf16[8,272,512]{2,1,0:T(8,128)(2,1)}), bf16[8,272,512]{2,1,0:T(8,128)(2,1)S(1)}, u32[]{:S(2)}, u32[]{:S(2)}) async-start(bf16[8,272,512]{2,1,0:T(8,128)(2,1)} %shard_map.69), calls=%async_computation | async-start | bytes 4456448 | tf_op jit(solution)/shard_map/all_to_all | solution.py:289
  171.0 29.9 %copy-start.19 = (f32[256,512]{1,0:T(8,128)S(1)}, f32[256,512]{1,0:T(8,128)}, u32[]{:S(2)}) copy-start(f32[256,512]{1,0:T(8,128)} %copy-done.18) | copy-start | bytes 1572868
  202.4 1.9 collective-permute-start.28
  (14 other events, 25.3 us)

commit v9 on v8

--- a/solution.py
+++ b/solution.py
@@ -63,13 +63,13 @@
 
 
 def project_kernel(order, *refs):
-    h_refs, own_refs, other_refs = refs[:6], refs[6:13], refs[13:15]
-    teacher, out, h_kept, p_kept, total, residual, h_sem, p_sem = refs[15:]
+    h_refs, own_refs, other_refs = refs[:6], refs[6:14], refs[14:16]
+    teacher, out, h_kept, p_kept, total, residual, h_sem, p_sem = refs[16:]
     n, width = out.shape[1] - NOTE, out.shape[2]
     size = p_kept.shape[2]
     half = size // 2
-    lengths = [size] * 4 + [size + half] * 2 + [size]
-    starts = [0, size, 2 * size, 3 * size, 0, size + half, 2 * (size + half)]
+    lengths = [size] * 4 + [size + half] * 2 + [half] * 2
+    starts = [0, size, 2 * size, 3 * size, 0, size + half, 2 * (size + half), 3 * size + half]
     other_refs = [
         other_refs[i // 4].at[pl.ds(at, length)] for i, (at, length) in enumerate(zip(starts, lengths))
     ]
@@ -81,12 +81,13 @@
     low, high = pl.ds(0, half), pl.ds(half, half)
 
     def pieces(parts):
-        block, other, before, nxt, up, down, far = parts
+        block, other, before, nxt, up, down, *far = parts
         for whole in (block, other, before, nxt):
             yield whole.at[low], whole.at[high]
         yield up.at[pl.ds(size, half)], down.at[pl.ds(size, half)]
-        for whole in (up, down, far):
+        for whole in (up, down):
             yield whole.at[low], whole.at[high]
+        yield far[0].at[low], far[1].at[low]
 
     for j, sources_ in enumerate(zip(pieces(own_refs), pieces(other_refs))):
         for side, halves in enumerate(sources_):
@@ -136,7 +137,7 @@
     inside = pl.BlockSpec(memory_space=pltpu.VMEM)
     return pl.pallas_call(
         project_kernel,
-        in_specs=[pl.BlockSpec(memory_space=pltpu.SMEM)] + [anywhere] * 15 + [inside],
+        in_specs=[pl.BlockSpec(memory_space=pltpu.SMEM)] + [anywhere] * 16 + [inside],
         out_specs=inside,
         scratch_shapes=[
             pltpu.VMEM((8, rows, size), BF16),
@@ -264,21 +265,22 @@
     hidden = (pre * sigma).astype(BF16)
 
     p_middle = gather_middle(projector, p_first, "dp")
-    hidden, teacher[1], teacher[-1] = lax.optimization_barrier((hidden, teacher[1], teacher[-1]))
     h_other = shift(hidden, "tensor", 0, 1)
+    h_other, up, down, teacher[1], teacher[-1] = lax.optimization_barrier(
+        (h_other, *p_middle, teacher[1], teacher[-1])
+    )
+    p_flip = flip(jnp.concatenate([after(projector, h_other), *p_first], axis=0))
     near = teacher[0] + teacher[1].astype(F32) + teacher[-1].astype(F32)
     cross = lax.dynamic_index_in_dim(near, 1 - xh, 0, False).astype(BF16)
     cross = shift(cross, "tensor", 0, 1)
-    p_flip = flip(jnp.concatenate([projector, *p_first], axis=0))
-    h_other, up, down, p_flip = lax.optimization_barrier((h_other, *p_middle, p_flip))
     h_pair = jnp.concatenate([hidden, h_other], axis=0)
     h_before, h_after = shift(h_pair, "tensor", 1, 0), shift(h_pair, "tensor", -1, 0)
-    p_far = shift(jnp.concatenate([up[feat:], down[feat:]], axis=0), "dp", 0, 1)
-    h_before, h_after, p_far, cross = lax.optimization_barrier((h_before, h_after, p_far, cross))
+    p_far = [shift(up[:part], "dp", 1, 0), shift(down[part:feat], "dp", -1, 0)]
+    h_before, h_after, cross, *p_far = lax.optimization_barrier((h_before, h_after, cross, *p_far))
     far_0 = shift(h_before[:own_rows], "tensor", 1, 0)
     far_1 = shift(h_after[own_rows:], "tensor", -1, 0)
-    p_own = [projector, *p_first, up, down, p_far]
-    p_flip = [p_flip, flip(jnp.concatenate([up, down, p_far], axis=0))]
+    p_own = [projector, *p_first, up, down, *p_far]
+    p_flip = [p_flip, flip(jnp.concatenate([up, down, *p_far], axis=0))]
     teacher = lax.dynamic_index_in_dim(near, xh, 0, False) + cross.astype(F32)
     hidden = [x.reshape(-1, own_rows, hid) for x in (hidden, h_other, h_after, far_0, far_1, h_before)]
 

time: 266 us -> 259 us (0.974)
  waiting for transfers between devices: 82.8 us -> 70.6 us
  starting transfers between devices: 50.1 us -> 55.2 us
    ppermute x22 -> x23, waiting for transfers between devices: 50.1 us -> 39.6 us  [shift(): return lax.ppermute(value, axis, perm)]
    ppermute x22 -> x23, starting transfers between devices: 41.8 us -> 48.9 us  [shift(): return lax.ppermute(value, axis, perm)]
    unnamed x66 -> x59, local copies, waits for them, and re-layouts: 9.62 us -> 7.24 us
  transfers between devices with their start and end apart: 30 -> 31, of which waited for: 17 -> 14; matrix products, arithmetic and copies ran while one was open for 10% -> 11% of each run, Pallas kernels for 5% -> 5%
where the time goes in v9:
time: 259 us
  waiting for transfers between devices  70.6 us (27%)
  starting transfers between devices  55.2 us (21%)
  blocking collectives  55 us (21%)
  other arithmetic  26.3 us (10%)
  Pallas kernels  25.8 us (10%)
  local copies, waits for them, and re-layouts  16.5 us (6%)
  matrix products  6.17 us (2%)
  between operations  3.01 us (1%)
    all_to_all x1, blocking collectives, shards(): grad = lax.all_to_all(grad, 'dp', 0, 0, tiled=True)  55 us
    ppermute x23, starting transfers between devices, shift(): return lax.ppermute(value, axis, perm)  48.9 us
    ppermute x23, waiting for transfers between devices, shift(): return lax.ppermute(value, axis, perm)  39.6 us
    all_to_all x1, waiting for transfers between devices, shards(): back = lax.all_to_all(back, 'tensor', 0, 0, tiled=True)  29.4 us
    pallas_call x1, Pallas kernels, teach(): pl.pallas_call(teach_kernel, grid_spec=pltpu.PrefetchScalarGridSpec(num_s...  13.2 us
    pallas_call x1, Pallas kernels, project(): pl.pallas_call(project_kernel, in_specs=[pl.BlockSpec(memory_space=pltpu....  12.6 us
    convert_element_type x1, other arithmetic, shards(): teacher[k] = pair.astype(BF16) if k == 2 else pair  7.33 us
    unnamed x59, local copies, waits for them, and re-layouts  7.24 us
  transfers between devices with their start and end apart: 31, of which 14 were waited for; matrix products, arithmetic and copies ran while one was open for 11% of the time, Pallas kernels for 5%

profile of v9, /device:TPU:0, one launch (start us, length us, event | category | flops | bytes accessed | tf_op | source)
XLA Modules:
  0.0 258.6 jit_solution(1813632737145369275)
XLA Ops:
  0.7 4.2 %constant_dynamic-slice_fusion = (bf16[256,4096]{1,0:T(8,128)(2,1)S(1)}, bf16[256,4096]{1,0:T(8,128)(2,1)}) fusion(bf16[256,8192]{1,0:T(8,128)(2,1)} %param.7, s32[]{:T(128)S(6)} %select_n.86, s32[]{:T(128)S(6)} %select_n.85), kind=kLoop, calls=%fused_computation.74 | loop fusion | bytes 8388616 | tf_op jit(solution)/shard_map/dynamic_slice | solution.py:218
  4.8 1.6 collective-permute-start.2
  6.4 1.6 collective-permute-start.3
  8.0 1.7 collective-permute-start.4
  10.4 13.2 %shard_map.68 = (bf16[8,256,1024]{2,1,0:T(8,128)(2,1)S(1)}, bf16[8,256,1024]{2,1,0:T(8,128)(2,1)}) custom-call(s32[1]{0:T(128)} %bitcast.role, bf16[512,1024]{1,0:T(8,128)(2,1)S(1)} %bitcast.44, bf16[1024,8192]{1,0:T(8,128)(2,1)} %weight.1), custom_call_target="tpu_custom_call" | custom-call | flops 8589934592 | bytes 16777216 | tf_op jit(solution)/shard_map/pallas_call | solution.py:174
  23.6 2.0 copy-done
  25.6 1.4 copy-done.17
  27.0 1.3 pad_maximum_fusion.3
  28.3 13.8 %collective-permute-start.10 = (bf16[768,512]{1,0:T(8,128)(2,1)}, bf16[768,512]{1,0:T(8,128)(2,1)S(1)}, u32[]{:S(2)}, u32[]{:S(2)}) collective-permute-start(bf16[768,512]{1,0:T(8,128)(2,1)} %get-tuple-element.92), channel_id=1, source_target_pairs={{0,48},{8,56},{16,0},{24,8},{32,16},{40,24},{48,32},{56,40},{1,49}... | collective-permute-start | bytes 2359304 | tf_op jit(solution)/shard_map/ppermute | solution.py:16
  42.3 7.3 %add_convert_fusion.2 = (bf16[2,256,1024]{2,1,0:T(8,128)(2,1)S(1)}, f32[2,256,1024]{2,1,0:T(8,128)}, f32[2,256,1024]{2,1,0:T(8,128)}, f32[2,256,1024]{2,1,0:T(8,128)}) fusion(bf16[8,256,1024]{2,1,0:T(8,128)(2,1)} %collective-permute-done.6, s32[]{:T(128)S(6)} %select_n.90, bf16[8,256,1024]{2,1,0:T(8,128)(2,1)} %copy-done, s32[]{:T(128)S(6)} %select_n.89, ...), kind=kLoop, calls=%fused_computation.9 | loop fusion | flops 6815744 | bytes 15728656 | tf_op jit(solution)/shard_map/convert_element_type | solution.py:235
  49.6 1.0 slice_bitcast_fusion
  50.6 3.6 %collective-permute-start.7 = (bf16[256,1024]{1,0:T(8,128)(2,1)}, bf16[256,1024]{1,0:T(8,128)(2,1)}, u32[]{:S(2)}, u32[]{:S(2)}) collective-permute-start(bf16[256,1024]{1,0:T(8,128)(2,1)} %get-tuple-element.89), channel_id=1, source_target_pairs={{0,6},{1,7},{2,0},{3,1},{4,2},{5,3},{6,4},{7,5},{8,14},{9,15},{10,... | collective-permute-start | bytes 1572872 | tf_op jit(solution)/shard_map/ppermute | solution.py:16
  54.3 2.0 collective-permute-done.5.refs_7_
  56.3 3.6 %collective-permute-done.10 = bf16[768,512]{1,0:T(8,128)(2,1)S(1)} collective-permute-done((bf16[768,512]{1,0:T(8,128)(2,1)}, bf16[768,512]{1,0:T(8,128)(2,1)S(1)}, u32[]{:S(2)}, u32[]{:S(2)}) %collective-permute-start.10) | collective-permute-done | bytes 786464 | tf_op jit(solution)/shard_map/ppermute | solution.py:16
  59.9 3.3 %collective-permute-done.9 = bf16[768,512]{1,0:T(8,128)(2,1)S(1)} collective-permute-done((bf16[768,512]{1,0:T(8,128)(2,1)}, bf16[768,512]{1,0:T(8,128)(2,1)S(1)}, u32[]{:S(2)}, u32[]{:S(2)}) %collective-permute-start.9) | collective-permute-done | bytes 786464 | tf_op jit(solution)/shard_map/ppermute | solution.py:16
  63.2 2.8 %collective-permute-done.7 = bf16[256,1024]{1,0:T(8,128)(2,1)} collective-permute-done((bf16[256,1024]{1,0:T(8,128)(2,1)}, bf16[256,1024]{1,0:T(8,128)(2,1)}, u32[]{:S(2)}, u32[]{:S(2)}) %collective-permute-start.7) | collective-permute-done | bytes 524320 | tf_op jit(solution)/shard_map/ppermute | solution.py:16
  66.1 3.4 %collective-permute-done.8 = bf16[256,1024]{1,0:T(8,128)(2,1)} collective-permute-done((bf16[256,1024]{1,0:T(8,128)(2,1)}, bf16[256,1024]{1,0:T(8,128)(2,1)}, u32[]{:S(2)}, u32[]{:S(2)}) %collective-permute-start.8) | collective-permute-done | bytes 524320 | tf_op jit(solution)/shard_map/ppermute | solution.py:16
  70.4 2.3 collective-permute-start.13
  74.3 3.8 %add_convert_fusion = (bf16[2,256,1024]{2,1,0:T(8,128)(2,1)}, bf16[2,256,1024]{2,1,0:T(8,128)(2,1)}) fusion(f32[2,256,1024]{2,1,0:T(8,128)S(1)} %copy-done.11, bf16[1,256,1024]{2,1,0:T(8,128)(2,1)} %bitcast.21, f32[2,256,1024]{2,1,0:T(8,128)} %get-tuple-element.57, bf16[1,256,1024]{2,1,0:T(8,128)(2,1)} %bitcast.20), kind=kLoop, calls=%fused_computation.7 | loop fusion | flops 3145728 | bytes 7340032 | tf_op jit(solution)/shard_map/convert_element_type | solution.py:242
  78.3 1.4 copy-done.18
  82.3 1.7 collective-permute-start.19
  87.0 1.3 pad_maximum_fusion.5
  88.7 2.9 %collective-permute-start.17 = (bf16[768,512]{1,0:T(8,128)(2,1)}, bf16[768,512]{1,0:T(8,128)(2,1)S(1)}, u32[]{:S(2)}, u32[]{:S(2)}) collective-permute-start(bf16[768,512]{1,0:T(8,128)(2,1)} %get-tuple-element.90), channel_id=1, source_target_pairs={{0,48},{8,56},{16,0},{24,8},{32,16},{40,24},{48,32},{56,40},{1,49}... | collective-permute-start | bytes 2359304 | tf_op jit(solution)/shard_map/ppermute | solution.py:16
  92.3 3.6 %collective-permute-start.15 = (bf16[256,512]{1,0:T(8,128)(2,1)S(1)}, bf16[256,512]{1,0:T(8,128)(2,1)}, u32[]{:S(2)}, u32[]{:S(2)}) collective-permute-start(bf16[256,512]{1,0:T(8,128)(2,1)S(1)} %multiply_convert_fusion), channel_id=1, source_target_pairs={{0,1},{1,0},{2,3},{3,2},{4,5},{5,4},{6,7},{7,6},{8,9},{9,8},{10,11... | collective-permute-start | bytes 786440 | tf_op jit(solution)/shard_map/ppermute | solution.py:16
  95.9 9.6 %collective-permute-done.18 = bf16[2,256,1024]{2,1,0:T(8,128)(2,1)} collective-permute-done((bf16[2,256,1024]{2,1,0:T(8,128)(2,1)}, bf16[2,256,1024]{2,1,0:T(8,128)(2,1)}, u32[]{:S(2)}, u32[]{:S(2)}) %collective-permute-start.18) | collective-permute-done | bytes 1048608 | tf_op jit(solution)/shard_map/ppermute | solution.py:16
  105.5 1.6 collective-permute-done.19
  107.1 2.5 collective-permute-done.16.refs_10_
  109.6 2.6 %convert_add_fusion = f32[2,256,1024]{2,1,0:T(8,128)S(1)} fusion(bf16[2,256,1024]{2,1,0:T(8,128)(2,1)} %collective-permute-done.19, f32[2,256,1024]{2,1,0:T(8,128)} %get-tuple-element.71, bf16[2,256,1024]{2,1,0:T(8,128)(2,1)} %collective-permute-done.18), kind=kLoop, calls=%fused_computation.6 | loop fusion | flops 2097152 | bytes 6291456 | tf_op jit(solution)/shard_map/add | solution.py:273
  112.4 3.7 %collective-permute-start.22 = (bf16[256,1024]{1,0:T(8,128)(2,1)S(1)}, bf16[256,1024]{1,0:T(8,128)(2,1)S(1)}, u32[]{:S(2)}, u32[]{:S(2)}) collective-permute-start(bf16[256,1024]{1,0:T(8,128)(2,1)S(1)} %fusion.3), channel_id=1, source_target_pairs={{0,1},{1,0},{2,3},{3,2},{4,5},{5,4},{6,7},{7,6},{8,9},{9,8},{10,11... | collective-permute-start | bytes 1572872 | tf_op jit(solution)/shard_map/ppermute | solution.py:16
  116.1 1.0 pad_maximum_fusion.8
  117.2 3.2 %collective-permute-start.21 = (bf16[512,512]{1,0:T(8,128)(2,1)S(1)}, bf16[512,512]{1,0:T(8,128)(2,1)}, u32[]{:S(2)}, u32[]{:S(2)}) collective-permute-start(bf16[512,512]{1,0:T(8,128)(2,1)S(1)} %pad_maximum_fusion.8), channel_id=1, source_target_pairs={{0,6},{1,7},{2,0},{3,1},{4,2},{5,3},{6,4},{7,5},{8,14},{9,15},{10,... | collective-permute-start | bytes 1572872 | tf_op jit(solution)/shard_map/ppermute | solution.py:16
  120.5 3.3 %collective-permute-start.24 = (bf16[256,512]{1,0:T(8,128)(2,1)S(1)}, bf16[256,512]{1,0:T(8,128)(2,1)S(1)}, u32[]{:S(2)}, u32[]{:S(2)}) collective-permute-start(bf16[256,512]{1,0:T(8,128)(2,1)S(1)} %slice.92), channel_id=1, source_target_pairs={{0,48},{8,56},{16,0},{24,8},{32,16},{40,24},{48,32},{56,40},{1,49}... | collective-permute-start | bytes 786440 | tf_op jit(solution)/shard_map/ppermute | solution.py:16
  123.8 1.6 pad_maximum_fusion.1
  125.4 3.4 %collective-permute-done.23.refs_12_ = bf16[256,512]{1,0:T(8,128)(2,1)S(1)} collective-permute-done((bf16[256,512]{1,0:T(8,128)(2,1)S(1)}, bf16[256,512]{1,0:T(8,128)(2,1)S(1)}, u32[]{:S(2)}, u32[]{:S(2)}) %collective-permute-start.23) | collective-permute-done | bytes 262176 | tf_op jit(solution)/shard_map/ppermute | solution.py:16
  128.8 2.9 %collective-permute-done.20 = bf16[512,512]{1,0:T(8,128)(2,1)} collective-permute-done((bf16[512,512]{1,0:T(8,128)(2,1)S(1)}, bf16[512,512]{1,0:T(8,128)(2,1)}, u32[]{:S(2)}, u32[]{:S(2)}) %collective-permute-start.20) | collective-permute-done | bytes 524320 | tf_op jit(solution)/shard_map/ppermute | solution.py:16
  131.7 1.4 pad_maximum_fusion.2
  134.0 1.1 slice.93
  136.1 3.3 %collective-permute-start.26 = (bf16[256,512]{1,0:T(8,128)(2,1)S(1)}, bf16[256,512]{1,0:T(8,128)(2,1)S(1)}, u32[]{:S(2)}, u32[]{:S(2)}) collective-permute-start(bf16[256,512]{1,0:T(8,128)(2,1)S(1)} %slice.94), channel_id=1, source_target_pairs={{0,6},{1,7},{2,0},{3,1},{4,2},{5,3},{6,4},{7,5},{8,14},{9,15},{10,... | collective-permute-start | bytes 786440 | tf_op jit(solution)/shard_map/ppermute | solution.py:16
  139.4 1.6 bitcast_add_fusion.refs_16_
  141.0 4.1 %collective-permute-done.25 = bf16[256,512]{1,0:T(8,128)(2,1)S(1)} collective-permute-done((bf16[256,512]{1,0:T(8,128)(2,1)S(1)}, bf16[256,512]{1,0:T(8,128)(2,1)S(1)}, u32[]{:S(2)}, u32[]{:S(2)}) %collective-permute-start.25) | collective-permute-done | bytes 262176 | tf_op jit(solution)/shard_map/ppermute | solution.py:16
  145.4 12.6 %shard_map.69 = bf16[8,272,512]{2,1,0:T(8,128)(2,1)} custom-call(s32[17]{0:T(128)S(1)} %stack.68.order, bf16[1,256,512]{2,1,0:T(8,128)(2,1)S(1)} %bitcast.43, bf16[1,256,512]{2,1,0:T(8,128)(2,1)} %bitcast.23.refs_1_, bf16[2,256,512]{2,1,0:T(8,128)(2,1)} %bitcast.25.refs_2_, bf16[1,256,512]{2,1,0:T(8,128)(2,1)S(1)} %bitcast.45, ...), custom_call_target="tpu_custom_call" | custom-call | flops 4294967296 | bytes 8388608 | tf_op jit(solution)/shard_map/pallas_call | solution.py:138
  158.0 5.2 %all-to-all-start = ((bf16[8,272,512]{2,1,0:T(8,128)(2,1)}), bf16[8,272,512]{2,1,0:T(8,128)(2,1)S(1)}, u32[]{:S(2)}, u32[]{:S(2)}) async-start(bf16[8,272,512]{2,1,0:T(8,128)(2,1)} %shard_map.69), calls=%async_computation | async-start | bytes 4456448 | tf_op jit(solution)/shard_map/all_to_all | solution.py:291
  163.3 29.4 %all-to-all-done = bf16[8,272,512]{2,1,0:T(8,128)(2,1)S(1)} async-done(((bf16[8,272,512]{2,1,0:T(8,128)(2,1)}), bf16[8,272,512]{2,1,0:T(8,128)(2,1)S(1)}, u32[]{:S(2)}, u32[]{:S(2)}) %all-to-all-start) | async-done | bytes 2228256 | tf_op jit(solution)/shard_map/all_to_all | solution.py:291
  193.2 1.5 fusion.5
  195.0 1.5 collective-permute-done.29
  196.6 2.5 convolution_convert_fusion
  199.6 55.0 %all_to_all.10 = bf16[8,528,512]{2,1,0:T(8,128)(2,1)S(1)} all-to-all(bf16[8,528,512]{2,1,0:T(8,128)(2,1)S(1)} %pad_maximum_fusion), channel_id=1, replica_groups=mesh['role'=2,'dp'=8,'tensor'=8] {'dp'}, dimensions={0} | all-to-all | bytes 8650752 | tf_op jit(solution)/shard_map/all_to_all | solution.py:304
  255.2 1.1 slice_multiply_fusion
  (131 shorter events, 15.0 us)
Async XLA Ops:
  0.6 4.2 %copy-start.25 = (bf16[512,512]{1,0:T(8,128)(2,1)S(1)}, bf16[512,512]{1,0:T(8,128)(2,1)}, u32[]{:S(2)}) copy-start(bf16[512,512]{1,0:T(8,128)(2,1)} %param.8) | copy-start | bytes 1572868
  0.6 9.0 %copy-start.28 = (bf16[512,512]{1,0:T(8,128)(2,1)S(1)}, bf16[512,512]{1,0:T(8,128)(2,1)}, u32[]{:S(2)}) copy-start(bf16[512,512]{1,0:T(8,128)(2,1)} %param.9) | copy-start | bytes 1572868
  0.7 9.7 %copy-start.8 = (bf16[2,256,1024]{2,1,0:T(8,128)(2,1)S(1)}, bf16[2,256,1024]{2,1,0:T(8,128)(2,1)}, u32[]{:S(2)}) copy-start(bf16[2,256,1024]{2,1,0:T(8,128)(2,1)} %param.5) | copy-start | bytes 3145732
  4.8 20.8 %collective-permute-start.1 = (bf16[256,4096]{1,0:T(8,128)(2,1)S(1)}, bf16[256,4096]{1,0:T(8,128)(2,1)S(1)}, u32[]{:S(2)}, u32[]{:S(2)}) collective-permute-start(bf16[256,4096]{1,0:T(8,128)(2,1)S(1)} %get-tuple-element.43), channel_id=1, source_target_pairs={{0,64},{64,0},{1,65},{65,1},{2,66},{66,2},{3,67},{67,3},{4,68},{68... | collective-permute-start | bytes 6291464 | tf_op jit(solution)/shard_map/ppermute | solution.py:20
  4.8 20.7 %collective-permute-start.2 = (bf16[512,512]{1,0:T(8,128)(2,1)S(1)}, bf16[512,512]{1,0:T(8,128)(2,1)S(1)}, u32[]{:S(2)}, u32[]{:S(2)}) collective-permute-start(bf16[512,512]{1,0:T(8,128)(2,1)S(1)} %copy-done.25), channel_id=1, source_target_pairs={{0,8},{8,0},{16,24},{24,16},{32,40},{40,32},{48,56},{56,48},{1,9},... | collective-permute-start | bytes 1572872 | tf_op jit(solution)/shard_map/ppermute | solution.py:16
  6.4 19.1 %collective-permute-start.3 = (bf16[512,512]{1,0:T(8,128)(2,1)S(1)}, bf16[512,512]{1,0:T(8,128)(2,1)S(1)}, u32[]{:S(2)}, u32[]{:S(2)}) collective-permute-start(bf16[512,512]{1,0:T(8,128)(2,1)S(1)} %copy-done.25), channel_id=1, source_target_pairs={{0,16},{8,24},{16,32},{24,40},{32,48},{40,56},{48,0},{56,8},{1,17}... | collective-permute-start | bytes 1572872 | tf_op jit(solution)/shard_map/ppermute | solution.py:16
  8.0 17.6 %collective-permute-start.4 = (bf16[512,512]{1,0:T(8,128)(2,1)S(1)}, bf16[512,512]{1,0:T(8,128)(2,1)S(1)}, u32[]{:S(2)}, u32[]{:S(2)}) collective-permute-start(bf16[512,512]{1,0:T(8,128)(2,1)S(1)} %copy-done.25), channel_id=1, source_target_pairs={{0,48},{8,56},{16,0},{24,8},{32,16},{40,24},{48,32},{56,40},{1,49}... | collective-permute-start | bytes 1572872 | tf_op jit(solution)/shard_map/ppermute | solution.py:16
  9.7 15.9 %collective-permute-start = (bf16[512,512]{1,0:T(8,128)(2,1)S(1)}, bf16[512,512]{1,0:T(8,128)(2,1)S(1)}, u32[]{:S(2)}, u32[]{:S(2)}) collective-permute-start(bf16[512,512]{1,0:T(8,128)(2,1)S(1)} %copy-done.28), channel_id=1, source_target_pairs={{0,0},{1,8},{2,16},{3,24},{4,32},{5,40},{6,48},{7,56},{8,9},{9,1},... | collective-permute-start | bytes 1572872 | tf_op jit(solution)/shard_map/ppermute | solution.py:215
  25.5 44.9 %copy-start.1 = (bf16[512,512]{1,0:T(8,128)(2,1)}, bf16[512,512]{1,0:T(8,128)(2,1)S(1)}, u32[]{:S(2)}) copy-start(bf16[512,512]{1,0:T(8,128)(2,1)S(1)} %collective-permute-done.refs_6_) | copy-start | bytes 1572868
  25.6 16.6 %copy-start.21 = (bf16[512,512]{1,0:T(8,128)(2,1)}, bf16[512,512]{1,0:T(8,128)(2,1)S(1)}, u32[]{:S(2)}) copy-start(bf16[512,512]{1,0:T(8,128)(2,1)S(1)} %collective-permute-done.3) | copy-start | bytes 1572868
  25.6 16.6 %copy-start.23 = (bf16[512,512]{1,0:T(8,128)(2,1)}, bf16[512,512]{1,0:T(8,128)(2,1)S(1)}, u32[]{:S(2)}) copy-start(bf16[512,512]{1,0:T(8,128)(2,1)S(1)} %collective-permute-done.4) | copy-start | bytes 1572868
  27.0 15.3 %collective-permute-start.6 = (bf16[8,256,1024]{2,1,0:T(8,128)(2,1)}, bf16[8,256,1024]{2,1,0:T(8,128)(2,1)}, u32[]{:S(2)}, u32[]{:S(2)}) collective-permute-start(bf16[8,256,1024]{2,1,0:T(8,128)(2,1)} %get-tuple-element.46), channel_id=1, source_target_pairs={{0,64},{64,0},{1,65},{65,1},{2,66},{66,2},{3,67},{67,3},{4,68},{68... | collective-permute-start | bytes 12582920 | tf_op jit(solution)/shard_map/ppermute | solution.py:20
  28.3 31.6 %collective-permute-start.10 = (bf16[768,512]{1,0:T(8,128)(2,1)}, bf16[768,512]{1,0:T(8,128)(2,1)S(1)}, u32[]{:S(2)}, u32[]{:S(2)}) collective-permute-start(bf16[768,512]{1,0:T(8,128)(2,1)} %get-tuple-element.92), channel_id=1, source_target_pairs={{0,48},{8,56},{16,0},{24,8},{32,16},{40,24},{48,32},{56,40},{1,49}... | collective-permute-start | bytes 2359304 | tf_op jit(solution)/shard_map/ppermute | solution.py:16
  42.2 21.1 %collective-permute-start.9 = (bf16[768,512]{1,0:T(8,128)(2,1)}, bf16[768,512]{1,0:T(8,128)(2,1)S(1)}, u32[]{:S(2)}, u32[]{:S(2)}) collective-permute-start(bf16[768,512]{1,0:T(8,128)(2,1)} %get-tuple-element.93), channel_id=1, source_target_pairs={{0,16},{8,24},{16,32},{24,40},{32,48},{40,56},{48,0},{56,8},{1,17}... | collective-permute-start | bytes 2359304 | tf_op jit(solution)/shard_map/ppermute | solution.py:16
  42.2 14.1 %collective-permute-start.5 = (bf16[512,512]{1,0:T(8,128)(2,1)S(1)}, bf16[512,512]{1,0:T(8,128)(2,1)S(1)}, u32[]{:S(2)}, u32[]{:S(2)}) collective-permute-start(bf16[512,512]{1,0:T(8,128)(2,1)S(1)} %collective-permute-done.refs_6_), channel_id=1, source_target_pairs={{0,8},{8,0},{16,24},{24,16},{32,40},{40,32},{48,56},{56,48},{1,9},... | collective-permute-start | bytes 1572872 | tf_op jit(solution)/shard_map/ppermute | solution.py:16
  50.6 15.4 %collective-permute-start.7 = (bf16[256,1024]{1,0:T(8,128)(2,1)}, bf16[256,1024]{1,0:T(8,128)(2,1)}, u32[]{:S(2)}, u32[]{:S(2)}) collective-permute-start(bf16[256,1024]{1,0:T(8,128)(2,1)} %get-tuple-element.89), channel_id=1, source_target_pairs={{0,6},{1,7},{2,0},{3,1},{4,2},{5,3},{6,4},{7,5},{8,14},{9,15},{10,... | collective-permute-start | bytes 1572872 | tf_op jit(solution)/shard_map/ppermute | solution.py:16
  54.3 15.2 %collective-permute-start.8 = (bf16[256,1024]{1,0:T(8,128)(2,1)}, bf16[256,1024]{1,0:T(8,128)(2,1)}, u32[]{:S(2)}, u32[]{:S(2)}) collective-permute-start(bf16[256,1024]{1,0:T(8,128)(2,1)} %get-tuple-element.88), channel_id=1, source_target_pairs={{0,2},{1,3},{2,4},{3,5},{4,6},{5,7},{6,0},{7,1},{8,10},{9,11},{10,... | collective-permute-start | bytes 1572872 | tf_op jit(solution)/shard_map/ppermute | solution.py:16
  54.3 20.0 %copy-start.11 = (f32[2,256,1024]{2,1,0:T(8,128)S(1)}, f32[2,256,1024]{2,1,0:T(8,128)}, u32[]{:S(2)}) copy-start(f32[2,256,1024]{2,1,0:T(8,128)} %get-tuple-element.59) | copy-start | bytes 6291460
  69.5 16.9 %collective-permute-start.12 = (bf16[512,512]{1,0:T(8,128)(2,1)S(1)}, bf16[512,512]{1,0:T(8,128)(2,1)S(1)}, u32[]{:S(2)}, u32[]{:S(2)}) collective-permute-start(bf16[512,512]{1,0:T(8,128)(2,1)S(1)} %collective-permute-done.refs_6_), channel_id=1, source_target_pairs={{0,16},{8,24},{16,32},{24,40},{32,48},{40,56},{48,0},{56,8},{1,17}... | collective-permute-start | bytes 1572872 | tf_op jit(solution)/shard_map/ppermute | solution.py:16
  70.4 15.9 %collective-permute-start.13 = (bf16[512,512]{1,0:T(8,128)(2,1)S(1)}, bf16[512,512]{1,0:T(8,128)(2,1)S(1)}, u32[]{:S(2)}, u32[]{:S(2)}) collective-permute-start(bf16[512,512]{1,0:T(8,128)(2,1)S(1)} %collective-permute-done.refs_6_), channel_id=1, source_target_pairs={{0,48},{8,56},{16,0},{24,8},{32,16},{40,24},{48,32},{56,40},{1,49}... | collective-permute-start | bytes 1572872 | tf_op jit(solution)/shard_map/ppermute | solution.py:16
  73.8 12.6 %collective-permute-start.11 = (bf16[512,512]{1,0:T(8,128)(2,1)S(1)}, bf16[512,512]{1,0:T(8,128)(2,1)S(1)}, u32[]{:S(2)}, u32[]{:S(2)}) collective-permute-start(bf16[512,512]{1,0:T(8,128)(2,1)S(1)} %pad_maximum_fusion.7), channel_id=1, source_target_pairs={{0,8},{8,0},{16,24},{24,16},{32,40},{40,32},{48,56},{56,48},{1,9},... | collective-permute-start | bytes 1572872 | tf_op jit(solution)/shard_map/ppermute | solution.py:16
  80.9 5.5 %copy-start.9 = (bf16[512,4096]{1,0:T(8,128)(2,1)}, bf16[512,4096]{1,0:T(8,128)(2,1)S(1)}, u32[]{:S(2)}) copy-start(bf16[512,4096]{1,0:T(8,128)(2,1)S(1)} %constant_dynamic-update-slice_fusion) | copy-start | bytes 12582916
  81.9 23.6 %collective-permute-start.18 = (bf16[2,256,1024]{2,1,0:T(8,128)(2,1)}, bf16[2,256,1024]{2,1,0:T(8,128)(2,1)}, u32[]{:S(2)}, u32[]{:S(2)}) collective-permute-start(bf16[2,256,1024]{2,1,0:T(8,128)(2,1)} %get-tuple-element.68), channel_id=1, source_target_pairs={{0,6},{1,7},{2,0},{3,1},{4,2},{5,3},{6,4},{7,5},{8,14},{9,15},{10,... | collective-permute-start | bytes 3145736 | tf_op jit(solution)/shard_map/ppermute | solution.py:16
  82.3 24.8 %collective-permute-start.19 = (bf16[2,256,1024]{2,1,0:T(8,128)(2,1)}, bf16[2,256,1024]{2,1,0:T(8,128)(2,1)}, u32[]{:S(2)}, u32[]{:S(2)}) collective-permute-start(bf16[2,256,1024]{2,1,0:T(8,128)(2,1)} %get-tuple-element.69), channel_id=1, source_target_pairs={{0,2},{1,3},{2,4},{3,5},{4,6},{5,7},{6,0},{7,1},{8,10},{9,11},{10,... | collective-permute-start | bytes 3145736 | tf_op jit(solution)/shard_map/ppermute | solution.py:16
  86.8 4.7 %copy-start.13 = (f32[512,512]{1,0:T(8,128)}, f32[512,512]{1,0:T(8,128)S(1)}, u32[]{:S(2)}) copy-start(f32[512,512]{1,0:T(8,128)S(1)} %convolution_add_fusion) | copy-start | bytes 3145732
  86.9 4.7 %collective-permute-start.14 = (f32[256,512]{1,0:T(8,128)S(1)}, f32[256,512]{1,0:T(8,128)S(1)}, u32[]{:S(2)}, u32[]{:S(2)}) collective-permute-start(f32[256,512]{1,0:T(8,128)S(1)} %slice.103), channel_id=1, source_target_pairs={{0,64},{64,0},{1,65},{65,1},{2,66},{66,2},{3,67},{67,3},{4,68},{68... | collective-permute-start | bytes 1572872 | tf_op jit(solution)/shard_map/ppermute | solution.py:20
  88.3 21.3 %collective-permute-start.16 = (bf16[768,512]{1,0:T(8,128)(2,1)}, bf16[768,512]{1,0:T(8,128)(2,1)S(1)}, u32[]{:S(2)}, u32[]{:S(2)}) collective-permute-start(bf16[768,512]{1,0:T(8,128)(2,1)} %get-tuple-element.91), channel_id=1, source_target_pairs={{0,16},{8,24},{16,32},{24,40},{32,48},{40,56},{48,0},{56,8},{1,17}... | collective-permute-start | bytes 2359304 | tf_op jit(solution)/shard_map/ppermute | solution.py:16
  88.7 21.0 %collective-permute-start.17 = (bf16[768,512]{1,0:T(8,128)(2,1)}, bf16[768,512]{1,0:T(8,128)(2,1)S(1)}, u32[]{:S(2)}, u32[]{:S(2)}) collective-permute-start(bf16[768,512]{1,0:T(8,128)(2,1)} %get-tuple-element.90), channel_id=1, source_target_pairs={{0,48},{8,56},{16,0},{24,8},{32,16},{40,24},{48,32},{56,40},{1,49}... | collective-permute-start | bytes 2359304 | tf_op jit(solution)/shard_map/ppermute | solution.py:16
  92.3 17.3 %collective-permute-start.15 = (bf16[256,512]{1,0:T(8,128)(2,1)S(1)}, bf16[256,512]{1,0:T(8,128)(2,1)}, u32[]{:S(2)}, u32[]{:S(2)}) collective-permute-start(bf16[256,512]{1,0:T(8,128)(2,1)S(1)} %multiply_convert_fusion), channel_id=1, source_target_pairs={{0,1},{1,0},{2,3},{3,2},{4,5},{5,4},{6,7},{7,6},{8,9},{9,8},{10,11... | collective-permute-start | bytes 786440 | tf_op jit(solution)/shard_map/ppermute | solution.py:16
  112.3 8.2 %copy-start.14 = (f32[2,256,1024]{2,1,0:T(8,128)}, f32[2,256,1024]{2,1,0:T(8,128)S(1)}, u32[]{:S(2)}) copy-start(f32[2,256,1024]{2,1,0:T(8,128)S(1)} %convert_add_fusion) | copy-start | bytes 6291460
  112.3 11.5 %copy-start.2 = (bf16[512,512]{1,0:T(8,128)(2,1)S(1)}, bf16[512,512]{1,0:T(8,128)(2,1)}, u32[]{:S(2)}) copy-start(bf16[512,512]{1,0:T(8,128)(2,1)} %copy-done.1) | copy-start | bytes 1572868
  112.4 16.4 %collective-permute-start.22 = (bf16[256,1024]{1,0:T(8,128)(2,1)S(1)}, bf16[256,1024]{1,0:T(8,128)(2,1)S(1)}, u32[]{:S(2)}, u32[]{:S(2)}) collective-permute-start(bf16[256,1024]{1,0:T(8,128)(2,1)S(1)} %fusion.3), channel_id=1, source_target_pairs={{0,1},{1,0},{2,3},{3,2},{4,5},{5,4},{6,7},{7,6},{8,9},{9,8},{10,11... | collective-permute-start | bytes 1572872 | tf_op jit(solution)/shard_map/ppermute | solution.py:16
  117.1 14.6 %collective-permute-start.20 = (bf16[512,512]{1,0:T(8,128)(2,1)S(1)}, bf16[512,512]{1,0:T(8,128)(2,1)}, u32[]{:S(2)}, u32[]{:S(2)}) collective-permute-start(bf16[512,512]{1,0:T(8,128)(2,1)S(1)} %pad_maximum_fusion.8), channel_id=1, source_target_pairs={{0,2},{1,3},{2,4},{3,5},{4,6},{5,7},{6,0},{7,1},{8,10},{9,11},{10,... | collective-permute-start | bytes 1572872 | tf_op jit(solution)/shard_map/ppermute | solution.py:16
  117.2 14.5 %collective-permute-start.21 = (bf16[512,512]{1,0:T(8,128)(2,1)S(1)}, bf16[512,512]{1,0:T(8,128)(2,1)}, u32[]{:S(2)}, u32[]{:S(2)}) collective-permute-start(bf16[512,512]{1,0:T(8,128)(2,1)S(1)} %pad_maximum_fusion.8), channel_id=1, source_target_pairs={{0,6},{1,7},{2,0},{3,1},{4,2},{5,3},{6,4},{7,5},{8,14},{9,15},{10,... | collective-permute-start | bytes 1572872 | tf_op jit(solution)/shard_map/ppermute | solution.py:16
  120.4 8.3 %collective-permute-start.23 = (bf16[256,512]{1,0:T(8,128)(2,1)S(1)}, bf16[256,512]{1,0:T(8,128)(2,1)S(1)}, u32[]{:S(2)}, u32[]{:S(2)}) collective-permute-start(bf16[256,512]{1,0:T(8,128)(2,1)S(1)} %slice.91), channel_id=1, source_target_pairs={{0,16},{8,24},{16,32},{24,40},{32,48},{40,56},{48,0},{56,8},{1,17}... | collective-permute-start | bytes 786440 | tf_op jit(solution)/shard_map/ppermute | solution.py:16
  120.5 8.2 %collective-permute-start.24 = (bf16[256,512]{1,0:T(8,128)(2,1)S(1)}, bf16[256,512]{1,0:T(8,128)(2,1)S(1)}, u32[]{:S(2)}, u32[]{:S(2)}) collective-permute-start(bf16[256,512]{1,0:T(8,128)(2,1)S(1)} %slice.92), channel_id=1, source_target_pairs={{0,48},{8,56},{16,0},{24,8},{32,16},{40,24},{48,32},{56,40},{1,49}... | collective-permute-start | bytes 786440 | tf_op jit(solution)/shard_map/ppermute | solution.py:16
  128.7 16.6 %collective-permute-start.27 = (bf16[2048,512]{1,0:T(8,128)(2,1)}, bf16[2048,512]{1,0:T(8,128)(2,1)}, u32[]{:S(2)}, u32[]{:S(2)}) collective-permute-start(bf16[2048,512]{1,0:T(8,128)(2,1)} %pad_maximum_fusion.1), channel_id=1, source_target_pairs={{0,64},{64,0},{1,65},{65,1},{2,66},{66,2},{3,67},{67,3},{4,68},{68... | collective-permute-start | bytes 6291464 | tf_op jit(solution)/shard_map/ppermute | solution.py:20
  128.7 4.4 %copy-start.6 = (bf16[256,512]{1,0:T(8,128)(2,1)}, bf16[256,512]{1,0:T(8,128)(2,1)S(1)}, u32[]{:S(2)}) copy-start(bf16[256,512]{1,0:T(8,128)(2,1)S(1)} %collective-permute-done.24.refs_13_) | copy-start | bytes 786436
  133.9 11.5 %collective-permute-start.28 = (bf16[2048,512]{1,0:T(8,128)(2,1)}, bf16[2048,512]{1,0:T(8,128)(2,1)}, u32[]{:S(2)}, u32[]{:S(2)}) collective-permute-start(bf16[2048,512]{1,0:T(8,128)(2,1)} %pad_maximum_fusion.2), channel_id=1, source_target_pairs={{0,64},{64,0},{1,65},{65,1},{2,66},{66,2},{3,67},{67,3},{4,68},{68... | collective-permute-start | bytes 6291464 | tf_op jit(solution)/shard_map/ppermute | solution.py:20
  134.0 11.4 %copy-start.3 = (bf16[512,512]{1,0:T(8,128)(2,1)S(1)}, bf16[512,512]{1,0:T(8,128)(2,1)}, u32[]{:S(2)}) copy-start(bf16[512,512]{1,0:T(8,128)(2,1)} %copy-done.1) | copy-start | bytes 1572868
  134.0 11.4 %copy-start.5 = (bf16[256,512]{1,0:T(8,128)(2,1)S(1)}, bf16[256,512]{1,0:T(8,128)(2,1)}, u32[]{:S(2)}) copy-start(bf16[256,512]{1,0:T(8,128)(2,1)} %copy-done.4) | copy-start | bytes 786436
  134.0 11.4 %copy-start.7 = (bf16[256,512]{1,0:T(8,128)(2,1)S(1)}, bf16[256,512]{1,0:T(8,128)(2,1)}, u32[]{:S(2)}) copy-start(bf16[256,512]{1,0:T(8,128)(2,1)} %copy-done.6) | copy-start | bytes 786436
  135.1 10.0 %collective-permute-start.25 = (bf16[256,512]{1,0:T(8,128)(2,1)S(1)}, bf16[256,512]{1,0:T(8,128)(2,1)S(1)}, u32[]{:S(2)}, u32[]{:S(2)}) collective-permute-start(bf16[256,512]{1,0:T(8,128)(2,1)S(1)} %slice.93), channel_id=1, source_target_pairs={{0,2},{1,3},{2,4},{3,5},{4,6},{5,7},{6,0},{7,1},{8,10},{9,11},{10,... | collective-permute-start | bytes 786440 | tf_op jit(solution)/shard_map/ppermute | solution.py:16
  136.1 9.3 %collective-permute-start.26 = (bf16[256,512]{1,0:T(8,128)(2,1)S(1)}, bf16[256,512]{1,0:T(8,128)(2,1)S(1)}, u32[]{:S(2)}, u32[]{:S(2)}) collective-permute-start(bf16[256,512]{1,0:T(8,128)(2,1)S(1)} %slice.94), channel_id=1, source_target_pairs={{0,6},{1,7},{2,0},{3,1},{4,2},{5,3},{6,4},{7,5},{8,14},{9,15},{10,... | collective-permute-start | bytes 786440 | tf_op jit(solution)/shard_map/ppermute | solution.py:16
  158.0 34.7 %all-to-all-start = ((bf16[8,272,512]{2,1,0:T(8,128)(2,1)}), bf16[8,272,512]{2,1,0:T(8,128)(2,1)S(1)}, u32[]{:S(2)}, u32[]{:S(2)}) async-start(bf16[8,272,512]{2,1,0:T(8,128)(2,1)} %shard_map.69), calls=%async_computation | async-start | bytes 4456448 | tf_op jit(solution)/shard_map/all_to_all | solution.py:291
  163.3 29.9 %copy-start.16 = (f32[256,512]{1,0:T(8,128)S(1)}, f32[256,512]{1,0:T(8,128)}, u32[]{:S(2)}) copy-start(f32[256,512]{1,0:T(8,128)} %copy-done.15) | copy-start | bytes 1572868
  192.7 3.8 %copy-start.10 = (bf16[512,4096]{1,0:T(8,128)(2,1)S(1)}, bf16[512,4096]{1,0:T(8,128)(2,1)}, u32[]{:S(2)}) copy-start(bf16[512,4096]{1,0:T(8,128)(2,1)} %copy-done.9) | copy-start | bytes 12582916
  194.7 1.9 collective-permute-start.29
  (12 other events, 24.5 us)

commit v10 on v9

--- a/solution.py
+++ b/solution.py
@@ -228,38 +228,44 @@
     p_other = shift(projector, "dp", 0, 1)
 
     zt = lax.axis_index("tensor") >> 1
-    teacher = {}
-    for k in (0, 1, -1, 2):
-        at = ((zt - k) & 3) * 2
-        pair = lax.dynamic_slice_in_dim(own, at, 2, axis=0).astype(F32) + lax.dynamic_slice_in_dim(away, at, 2, axis=0).astype(F32)
-        teacher[k] = pair.astype(BF16) if k == 2 else pair
-    teacher = dict(zip(teacher, lax.optimization_barrier(tuple(teacher.values()))))
-    over = [shift(teacher[2][0], "tensor", -1, 0), shift(teacher[2][1], "tensor", 1, 0)]
-
-    projector, p_other, *moved = lax.optimization_barrier((projector, p_other, *over, *w_middle))
+
+    def teacher_part(k, first, count):
+        at = ((zt - k) & 3) * 2 + first
+        parts = (lax.dynamic_slice_in_dim(x, at, count, axis=0).astype(F32) for x in (own, away))
+        return sum(parts)
+
+    over = [teacher_part(2, e, 1).astype(BF16) for e in (0, 1)]
+    *over, own, away = lax.optimization_barrier((*over, own, away))
+    over = [shift(over[0], "tensor", -1, 0), shift(over[1], "tensor", 1, 0)]
+    teacher = {k: teacher_part(k, 0, 2) for k in (0, 1, -1)}
+
+    part = feat // 2
+    at = sources("dp")
+    student = jnp.concatenate([mine, theirs], axis=0)
+    pre = sum(
+        dot(lax.dynamic_slice_in_dim(student, at[j] * feat, feat, axis=1), block)
+        for j, block in enumerate((student_weight, *w_first))
+    )
+    projector, p_other, pre, *moved = lax.optimization_barrier((projector, p_other, pre, *over, *w_middle))
     over, w_middle = moved[:2], moved[2:]
-    teacher[1] = (teacher[1] + jnp.pad(over[0][None].astype(F32), ((0, 1), (0, 0), (0, 0)))).astype(BF16)
-    teacher[-1] = (teacher[-1] + jnp.pad(over[1][None].astype(F32), ((1, 0), (0, 0), (0, 0)))).astype(BF16)
+    teacher[1] = (teacher[1] + jnp.pad(over[0].astype(F32), ((0, 1), (0, 0), (0, 0)))).astype(BF16)
+    teacher[-1] = (teacher[-1] + jnp.pad(over[1].astype(F32), ((1, 0), (0, 0), (0, 0)))).astype(BF16)
     teacher[1], teacher[-1], student_weight = lax.optimization_barrier((teacher[1], teacher[-1], student_weight))
     for k in (1, -1):
         teacher[k] = shift(teacher[k], "tensor", -k, 0)
     up, down = w_middle
-    w_far, mine, theirs = lax.optimization_barrier((jnp.concatenate([up[feat:], down[feat:]], axis=0), mine, theirs))
-    w_far = shift(w_far, "dp", 0, 1)
-    student = jnp.concatenate([mine, theirs], axis=0)
+    w_far = shift(jnp.concatenate([up[feat:], down[feat:]], axis=0), "dp", 0, 1)
     p_first = [shift(projector, "dp", 1, 0), shift(projector, "dp", -1, 0)]
     w_far, *p_first = lax.optimization_barrier((w_far, *p_first))
     p_first = [p_other, *p_first]
 
-    part = feat // 2
-    at = sources("dp")
-    pre = 0.0
-    for j, block in enumerate((student_weight, *w_first, None, up[:feat], down[:feat], w_far)):
-        columns = lax.dynamic_slice_in_dim(student, at[j] * feat, feat, axis=1)
-        if block is None:
-            pre = pre + dot(columns[:, :part], up[feat:]) + dot(columns[:, part:], down[feat:])
-        else:
-            pre = pre + dot(columns, block)
+    def block_product(j, block):
+        return dot(lax.dynamic_slice_in_dim(student, at[j] * feat, feat, axis=1), block)
+
+    columns = lax.dynamic_slice_in_dim(student, at[4] * feat, feat, axis=1)
+    pre = pre + block_product(5, up[:feat]) + block_product(6, down[:feat])
+    pre = pre + dot(columns[:, :part], up[feat:]) + dot(columns[:, part:], down[feat:])
+    pre = pre + block_product(7, w_far)
     pre = pre[:own_rows] + flip(pre[own_rows:])
     sigma = jax.nn.sigmoid(pre)
     hidden = (pre * sigma).astype(BF16)

time: 259 us -> 255 us (0.985)
  waiting for transfers between devices: 70.6 us -> 81.7 us
  starting transfers between devices: 55.2 us -> 47.4 us
  other arithmetic: 26.3 us -> 20 us
    ppermute x23, waiting for transfers between devices: 39.6 us -> 50.8 us  [shift(): return lax.ppermute(value, axis, perm)]
    ppermute x23, starting transfers between devices: 48.9 us -> 39.2 us  [shift(): return lax.ppermute(value, axis, perm)]
    convert_element_type x2, other arithmetic: 11.1 us -> 5.69 us  [the longest x1 4.1 us: shards(): (teacher[-1] + jnp.pad(over[1].astype(F32), ((1, 0), (0, 0), (0, 0)))).as...]
    unnamed x59 -> x55, local copies, waits for them, and re-layouts: 7.24 us -> 10.8 us
  transfers between devices with their start and end apart: 31 -> 31, of which waited for: 14 -> 15; matrix products, arithmetic and copies ran while one was open for 11% -> 8% of each run, Pallas kernels for 5% -> 5%
where the time goes in v10:
time: 255 us
  waiting for transfers between devices  81.7 us (32%)
  blocking collectives  54 us (21%)
  starting transfers between devices  47.4 us (19%)
  Pallas kernels  25.8 us (10%)
  other arithmetic  20 us (8%)
  local copies, waits for them, and re-layouts  16.5 us (6%)
  matrix products  6.17 us (2%)
  between operations  3.07 us (1%)
    all_to_all x1, blocking collectives, shards(): grad = lax.all_to_all(grad, 'dp', 0, 0, tiled=True)  54 us
    ppermute x23, waiting for transfers between devices, shift(): return lax.ppermute(value, axis, perm)  50.8 us
    ppermute x23, starting transfers between devices, shift(): return lax.ppermute(value, axis, perm)  39.2 us
    all_to_all x1, waiting for transfers between devices, shards(): back = lax.all_to_all(back, 'tensor', 0, 0, tiled=True)  29.4 us
    pallas_call x1, Pallas kernels, teach(): pl.pallas_call(teach_kernel, grid_spec=pltpu.PrefetchScalarGridSpec(num_s...  13.1 us
    pallas_call x1, Pallas kernels, project(): pl.pallas_call(project_kernel, in_specs=[pl.BlockSpec(memory_space=pltpu....  12.6 us
    unnamed x55, local copies, waits for them, and re-layouts  10.8 us
    all_to_all x1, starting transfers between devices, shards(): back = lax.all_to_all(back, 'tensor', 0, 0, tiled=True)  7.05 us
  transfers between devices with their start and end apart: 31, of which 15 were waited for; matrix products, arithmetic and copies ran while one was open for 8% of the time, Pallas kernels for 5%

profile of v10, /device:TPU:0, one launch (start us, length us, event | category | flops | bytes accessed | tf_op | source)
XLA Modules:
  0.0 254.7 jit_solution(656496327973430736)
XLA Ops:
  0.7 2.7 %constant_dynamic-slice_fusion = (bf16[256,4096]{1,0:T(8,128)(2,1)S(1)}, bf16[256,4096]{1,0:T(8,128)(2,1)S(1)}) fusion(bf16[256,8192]{1,0:T(8,128)(2,1)} %param.7, s32[]{:T(128)S(6)} %select_n.90, s32[]{:T(128)S(6)} %select_n.89), kind=kLoop, calls=%fused_computation.68 | loop fusion | bytes 8388616 | tf_op jit(solution)/shard_map/dynamic_slice | solution.py:218
  3.5 3.2 %collective-permute-start.4 = (bf16[512,512]{1,0:T(8,128)(2,1)S(1)}, bf16[512,512]{1,0:T(8,128)(2,1)S(1)}, u32[]{:S(2)}, u32[]{:S(2)}) collective-permute-start(bf16[512,512]{1,0:T(8,128)(2,1)S(1)} %copy-done.24), channel_id=1, source_target_pairs={{0,48},{8,56},{16,0},{24,8},{32,16},{40,24},{48,32},{56,40},{1,49}... | collective-permute-start | bytes 1572872 | tf_op jit(solution)/shard_map/ppermute | solution.py:16
  6.7 1.5 collective-permute-start.2
  8.9 13.1 %shard_map.68 = (bf16[8,256,1024]{2,1,0:T(8,128)(2,1)S(1)}, bf16[8,256,1024]{2,1,0:T(8,128)(2,1)}) custom-call(s32[1]{0:T(128)} %bitcast.role, bf16[512,1024]{1,0:T(8,128)(2,1)S(1)} %bitcast.38, bf16[1024,8192]{1,0:T(8,128)(2,1)} %weight.1), custom_call_target="tpu_custom_call" | custom-call | flops 8589934592 | bytes 16777216 | tf_op jit(solution)/shard_map/pallas_call | solution.py:174
  22.0 2.0 copy-done
  24.1 5.7 %collective-permute-done.4 = bf16[512,512]{1,0:T(8,128)(2,1)S(1)} collective-permute-done((bf16[512,512]{1,0:T(8,128)(2,1)S(1)}, bf16[512,512]{1,0:T(8,128)(2,1)S(1)}, u32[]{:S(2)}, u32[]{:S(2)}) %collective-permute-start.4) | collective-permute-done | bytes 524320 | tf_op jit(solution)/shard_map/ppermute | solution.py:16
  29.8 1.7 copy-done.16
  31.8 1.9 collective-permute-start.5
  33.8 6.2 %collective-permute-start.10 = (bf16[768,512]{1,0:T(8,128)(2,1)S(1)}, bf16[768,512]{1,0:T(8,128)(2,1)S(1)}, u32[]{:S(2)}, u32[]{:S(2)}) collective-permute-start(bf16[768,512]{1,0:T(8,128)(2,1)S(1)} %get-tuple-element.84), channel_id=1, source_target_pairs={{0,48},{8,56},{16,0},{24,8},{32,16},{40,24},{48,32},{56,40},{1,49}... | collective-permute-start | bytes 2359304 | tf_op jit(solution)/shard_map/ppermute | solution.py:16
  41.1 2.6 %copy-done.1 = bf16[8,256,1024]{2,1,0:T(8,128)(2,1)S(1)} copy-done((bf16[8,256,1024]{2,1,0:T(8,128)(2,1)S(1)}, bf16[8,256,1024]{2,1,0:T(8,128)(2,1)}, u32[]{:S(2)}) %copy-start.1) | copy-done | bytes 4194328
  43.7 1.6 add_convert_fusion.2
  45.3 2.8 %collective-permute-start.7 = (bf16[1,256,1024]{2,1,0:T(8,128)(2,1)S(1)}, bf16[1,256,1024]{2,1,0:T(8,128)(2,1)S(1)}, u32[]{:S(2)}, u32[]{:S(2)}) collective-permute-start(bf16[1,256,1024]{2,1,0:T(8,128)(2,1)S(1)} %get-tuple-element.49), channel_id=1, source_target_pairs={{0,6},{1,7},{2,0},{3,1},{4,2},{5,3},{6,4},{7,5},{8,14},{9,15},{10,... | collective-permute-start | bytes 1572872 | tf_op jit(solution)/shard_map/ppermute | solution.py:16
  49.0 8.4 %collective-permute-done.10 = bf16[768,512]{1,0:T(8,128)(2,1)S(1)} collective-permute-done((bf16[768,512]{1,0:T(8,128)(2,1)S(1)}, bf16[768,512]{1,0:T(8,128)(2,1)S(1)}, u32[]{:S(2)}, u32[]{:S(2)}) %collective-permute-start.10) | collective-permute-done | bytes 786464 | tf_op jit(solution)/shard_map/ppermute | solution.py:16
  57.4 3.4 %collective-permute-done.9 = bf16[768,512]{1,0:T(8,128)(2,1)S(1)} collective-permute-done((bf16[768,512]{1,0:T(8,128)(2,1)S(1)}, bf16[768,512]{1,0:T(8,128)(2,1)S(1)}, u32[]{:S(2)}, u32[]{:S(2)}) %collective-permute-start.9) | collective-permute-done | bytes 786464 | tf_op jit(solution)/shard_map/ppermute | solution.py:16
  60.8 2.1 collective-permute-done.8
  63.1 1.9 collective-permute-start.12
  65.1 1.5 collective-permute-start.11
  67.5 4.1 %add_convert_fusion = (bf16[2,256,1024]{2,1,0:T(8,128)(2,1)}, bf16[2,256,1024]{2,1,0:T(8,128)(2,1)}) fusion(bf16[1,256,1024]{2,1,0:T(8,128)(2,1)S(1)} %collective-permute-done.8, bf16[8,256,1024]{2,1,0:T(8,128)(2,1)} %collective-permute-done.6, s32[]{:T(128)S(6)} %select_n.102, bf16[8,256,1024]{2,1,0:T(8,128)(2,1)S(1)} %copy-done.1, ...), kind=kLoop, calls=%fused_computation.7 | loop fusion | flops 6291456 | bytes 7340040 | tf_op jit(solution)/shard_map/convert_element_type | solution.py:252
  71.9 1.7 collective-permute-start.19
  74.3 3.2 %collective-permute-done.11 = bf16[512,512]{1,0:T(8,128)(2,1)S(1)} collective-permute-done((bf16[512,512]{1,0:T(8,128)(2,1)S(1)}, bf16[512,512]{1,0:T(8,128)(2,1)S(1)}, u32[]{:S(2)}, u32[]{:S(2)}) %collective-permute-start.11) | collective-permute-done | bytes 524320 | tf_op jit(solution)/shard_map/ppermute | solution.py:16
  78.1 1.3 pad_maximum_fusion.5
  79.4 1.5 collective-permute-start.17
  82.2 4.2 %collective-permute-start.15 = (bf16[256,512]{1,0:T(8,128)(2,1)S(1)}, bf16[256,512]{1,0:T(8,128)(2,1)}, u32[]{:S(2)}, u32[]{:S(2)}) collective-permute-start(bf16[256,512]{1,0:T(8,128)(2,1)S(1)} %multiply_convert_fusion), channel_id=1, source_target_pairs={{0,1},{1,0},{2,3},{3,2},{4,5},{5,4},{6,7},{7,6},{8,9},{9,8},{10,11... | collective-permute-start | bytes 786440 | tf_op jit(solution)/shard_map/ppermute | solution.py:16
  86.4 8.7 %collective-permute-done.18 = bf16[2,256,1024]{2,1,0:T(8,128)(2,1)} collective-permute-done((bf16[2,256,1024]{2,1,0:T(8,128)(2,1)}, bf16[2,256,1024]{2,1,0:T(8,128)(2,1)}, u32[]{:S(2)}, u32[]{:S(2)}) %collective-permute-start.18) | collective-permute-done | bytes 1048608 | tf_op jit(solution)/shard_map/ppermute | solution.py:16
  95.1 1.5 collective-permute-done.19
  96.7 2.9 %collective-permute-done.17.refs_11_ = bf16[768,512]{1,0:T(8,128)(2,1)S(1)} collective-permute-done((bf16[768,512]{1,0:T(8,128)(2,1)}, bf16[768,512]{1,0:T(8,128)(2,1)S(1)}, u32[]{:S(2)}, u32[]{:S(2)}) %collective-permute-start.17) | collective-permute-done | bytes 786464 | tf_op jit(solution)/shard_map/ppermute | solution.py:16
  99.5 2.4 collective-permute-done.16.refs_10_
  103.7 1.3 collective-permute-start.20
  105.1 3.0 %convert_add_fusion = f32[2,256,1024]{2,1,0:T(8,128)S(1)} fusion(bf16[2,256,1024]{2,1,0:T(8,128)(2,1)} %collective-permute-done.19, bf16[2,256,1024]{2,1,0:T(8,128)(2,1)} %collective-permute-done.18, bf16[8,256,1024]{2,1,0:T(8,128)(2,1)} %collective-permute-done.6, s32[]{:T(128)S(6)} %select_n.103, bf16[8,256,1024]{2,1,0:T(8,128)(2,1)} %copy-done), kind=kLoop, calls=%fused_computation.6 | loop fusion | flops 3670016 | bytes 6291460 | tf_op jit(solution)/shard_map/add | solution.py:279
  108.2 4.4 %collective-permute-start.22 = (bf16[256,1024]{1,0:T(8,128)(2,1)S(1)}, bf16[256,1024]{1,0:T(8,128)(2,1)}, u32[]{:S(2)}, u32[]{:S(2)}) collective-permute-start(bf16[256,1024]{1,0:T(8,128)(2,1)S(1)} %fusion.1), channel_id=1, source_target_pairs={{0,1},{1,0},{2,3},{3,2},{4,5},{5,4},{6,7},{7,6},{8,9},{9,8},{10,11... | collective-permute-start | bytes 1572872 | tf_op jit(solution)/shard_map/ppermute | solution.py:16
  113.0 1.7 collective-permute-start.23
  114.7 1.5 pad_maximum_fusion.1
  116.3 3.2 %collective-permute-done.24.refs_13_ = bf16[256,512]{1,0:T(8,128)(2,1)S(1)} collective-permute-done((bf16[256,512]{1,0:T(8,128)(2,1)S(1)}, bf16[256,512]{1,0:T(8,128)(2,1)S(1)}, u32[]{:S(2)}, u32[]{:S(2)}) %collective-permute-start.24) | collective-permute-done | bytes 262176 | tf_op jit(solution)/shard_map/ppermute | solution.py:16
  119.5 1.5 collective-permute-done.23.refs_12_
  121.0 2.6 %collective-permute-done.22 = bf16[256,1024]{1,0:T(8,128)(2,1)} collective-permute-done((bf16[256,1024]{1,0:T(8,128)(2,1)S(1)}, bf16[256,1024]{1,0:T(8,128)(2,1)}, u32[]{:S(2)}, u32[]{:S(2)}) %collective-permute-start.22) | collective-permute-done | bytes 524320 | tf_op jit(solution)/shard_map/ppermute | solution.py:16
  123.6 1.4 pad_maximum_fusion.2
  128.1 3.0 %collective-permute-start.26 = (bf16[256,512]{1,0:T(8,128)(2,1)S(1)}, bf16[256,512]{1,0:T(8,128)(2,1)S(1)}, u32[]{:S(2)}, u32[]{:S(2)}) collective-permute-start(bf16[256,512]{1,0:T(8,128)(2,1)S(1)} %slice.86), channel_id=1, source_target_pairs={{0,6},{1,7},{2,0},{3,1},{4,2},{5,3},{6,4},{7,5},{8,14},{9,15},{10,... | collective-permute-start | bytes 786440 | tf_op jit(solution)/shard_map/ppermute | solution.py:16
  131.1 1.6 bitcast_add_fusion.refs_16_
  132.7 5.1 %collective-permute-done.25 = bf16[256,512]{1,0:T(8,128)(2,1)S(1)} collective-permute-done((bf16[256,512]{1,0:T(8,128)(2,1)S(1)}, bf16[256,512]{1,0:T(8,128)(2,1)S(1)}, u32[]{:S(2)}, u32[]{:S(2)}) %collective-permute-start.25) | collective-permute-done | bytes 262176 | tf_op jit(solution)/shard_map/ppermute | solution.py:16
  137.8 1.0 copy-done.4
  140.7 12.6 %shard_map.69 = bf16[8,272,512]{2,1,0:T(8,128)(2,1)} custom-call(s32[17]{0:T(128)S(1)} %stack.68.order, bf16[1,256,512]{2,1,0:T(8,128)(2,1)S(1)} %bitcast.37, bf16[1,256,512]{2,1,0:T(8,128)(2,1)} %bitcast.19.refs_1_, bf16[2,256,512]{2,1,0:T(8,128)(2,1)} %bitcast.21.refs_2_, bf16[1,256,512]{2,1,0:T(8,128)(2,1)S(1)} %bitcast.39, ...), custom_call_target="tpu_custom_call" | custom-call | flops 4294967296 | bytes 8388608 | tf_op jit(solution)/shard_map/pallas_call | solution.py:138
  153.4 7.1 %all-to-all-start = ((bf16[8,272,512]{2,1,0:T(8,128)(2,1)}), bf16[8,272,512]{2,1,0:T(8,128)(2,1)S(1)}, u32[]{:S(2)}, u32[]{:S(2)}) async-start(bf16[8,272,512]{2,1,0:T(8,128)(2,1)} %shard_map.69), calls=%async_computation | async-start | bytes 4456448 | tf_op jit(solution)/shard_map/all_to_all | solution.py:297
  160.4 29.4 %all-to-all-done = bf16[8,272,512]{2,1,0:T(8,128)(2,1)S(1)} async-done(((bf16[8,272,512]{2,1,0:T(8,128)(2,1)}), bf16[8,272,512]{2,1,0:T(8,128)(2,1)S(1)}, u32[]{:S(2)}, u32[]{:S(2)}) %all-to-all-start) | async-done | bytes 2228256 | tf_op jit(solution)/shard_map/all_to_all | solution.py:297
  190.3 1.5 fusion.3
  192.1 1.5 collective-permute-done.29
  193.7 2.5 convolution_convert_fusion
  196.7 54.0 %all_to_all.10 = bf16[8,528,512]{2,1,0:T(8,128)(2,1)S(1)} all-to-all(bf16[8,528,512]{2,1,0:T(8,128)(2,1)S(1)} %pad_maximum_fusion), channel_id=1, replica_groups=mesh['role'=2,'dp'=8,'tensor'=8] {'dp'}, dimensions={0} | all-to-all | bytes 8650752 | tf_op jit(solution)/shard_map/all_to_all | solution.py:310
  251.3 1.1 slice_multiply_fusion
  (127 shorter events, 16.7 us)
Async XLA Ops:
  0.6 2.9 %copy-start.24 = (bf16[512,512]{1,0:T(8,128)(2,1)S(1)}, bf16[512,512]{1,0:T(8,128)(2,1)}, u32[]{:S(2)}) copy-start(bf16[512,512]{1,0:T(8,128)(2,1)} %param.8) | copy-start | bytes 1572868
  0.6 7.5 %copy-start.26 = (bf16[512,512]{1,0:T(8,128)(2,1)S(1)}, bf16[512,512]{1,0:T(8,128)(2,1)}, u32[]{:S(2)}) copy-start(bf16[512,512]{1,0:T(8,128)(2,1)} %param.9) | copy-start | bytes 1572868
  0.7 8.2 %copy-start.9 = (bf16[2,256,1024]{2,1,0:T(8,128)(2,1)S(1)}, bf16[2,256,1024]{2,1,0:T(8,128)(2,1)}, u32[]{:S(2)}) copy-start(bf16[2,256,1024]{2,1,0:T(8,128)(2,1)} %param.5) | copy-start | bytes 3145732
  3.4 26.3 %collective-permute-start.1 = (bf16[256,4096]{1,0:T(8,128)(2,1)S(1)}, bf16[256,4096]{1,0:T(8,128)(2,1)S(1)}, u32[]{:S(2)}, u32[]{:S(2)}) collective-permute-start(bf16[256,4096]{1,0:T(8,128)(2,1)S(1)} %get-tuple-element.41), channel_id=1, source_target_pairs={{0,64},{64,0},{1,65},{65,1},{2,66},{66,2},{3,67},{67,3},{4,68},{68... | collective-permute-start | bytes 6291464 | tf_op jit(solution)/shard_map/ppermute | solution.py:20
  3.5 26.2 %collective-permute-start.4 = (bf16[512,512]{1,0:T(8,128)(2,1)S(1)}, bf16[512,512]{1,0:T(8,128)(2,1)S(1)}, u32[]{:S(2)}, u32[]{:S(2)}) collective-permute-start(bf16[512,512]{1,0:T(8,128)(2,1)S(1)} %copy-done.24), channel_id=1, source_target_pairs={{0,48},{8,56},{16,0},{24,8},{32,16},{40,24},{48,32},{56,40},{1,49}... | collective-permute-start | bytes 1572872 | tf_op jit(solution)/shard_map/ppermute | solution.py:16
  6.7 23.0 %collective-permute-start.3 = (bf16[512,512]{1,0:T(8,128)(2,1)S(1)}, bf16[512,512]{1,0:T(8,128)(2,1)S(1)}, u32[]{:S(2)}, u32[]{:S(2)}) collective-permute-start(bf16[512,512]{1,0:T(8,128)(2,1)S(1)} %copy-done.24), channel_id=1, source_target_pairs={{0,16},{8,24},{16,32},{24,40},{32,48},{40,56},{48,0},{56,8},{1,17}... | collective-permute-start | bytes 1572872 | tf_op jit(solution)/shard_map/ppermute | solution.py:16
  6.7 23.0 %collective-permute-start.2 = (bf16[512,512]{1,0:T(8,128)(2,1)S(1)}, bf16[512,512]{1,0:T(8,128)(2,1)S(1)}, u32[]{:S(2)}, u32[]{:S(2)}) collective-permute-start(bf16[512,512]{1,0:T(8,128)(2,1)S(1)} %copy-done.24), channel_id=1, source_target_pairs={{0,8},{8,0},{16,24},{24,16},{32,40},{40,32},{48,56},{56,48},{1,9},... | collective-permute-start | bytes 1572872 | tf_op jit(solution)/shard_map/ppermute | solution.py:16
  8.2 15.9 %collective-permute-start = (bf16[512,512]{1,0:T(8,128)(2,1)S(1)}, bf16[512,512]{1,0:T(8,128)(2,1)S(1)}, u32[]{:S(2)}, u32[]{:S(2)}) collective-permute-start(bf16[512,512]{1,0:T(8,128)(2,1)S(1)} %copy-done.26), channel_id=1, source_target_pairs={{0,0},{1,8},{2,16},{3,24},{4,32},{5,40},{6,48},{7,56},{8,9},{9,1},... | collective-permute-start | bytes 1572872 | tf_op jit(solution)/shard_map/ppermute | solution.py:215
  24.0 39.0 %copy-start.2 = (bf16[512,512]{1,0:T(8,128)(2,1)}, bf16[512,512]{1,0:T(8,128)(2,1)S(1)}, u32[]{:S(2)}) copy-start(bf16[512,512]{1,0:T(8,128)(2,1)S(1)} %collective-permute-done.refs_6_) | copy-start | bytes 1572868
  31.4 9.6 %collective-permute-start.6 = (bf16[8,256,1024]{2,1,0:T(8,128)(2,1)}, bf16[8,256,1024]{2,1,0:T(8,128)(2,1)}, u32[]{:S(2)}, u32[]{:S(2)}) collective-permute-start(bf16[8,256,1024]{2,1,0:T(8,128)(2,1)} %get-tuple-element.48), channel_id=1, source_target_pairs={{0,64},{64,0},{1,65},{65,1},{2,66},{66,2},{3,67},{67,3},{4,68},{68... | collective-permute-start | bytes 12582920 | tf_op jit(solution)/shard_map/ppermute | solution.py:20
  31.5 2.3 slice-start
  31.6 8.4 %copy-start.17 = (bf16[256,4096]{1,0:T(8,128)(2,1)S(1)}, bf16[256,4096]{1,0:T(8,128)(2,1)}, u32[]{:S(2)}) copy-start(bf16[256,4096]{1,0:T(8,128)(2,1)} %copy-done.16) | copy-start | bytes 6291460
  31.8 8.3 %copy-start.25 = (bf16[512,512]{1,0:T(8,128)(2,1)S(1)}, bf16[512,512]{1,0:T(8,128)(2,1)}, u32[]{:S(2)}) copy-start(bf16[512,512]{1,0:T(8,128)(2,1)} %param.8) | copy-start | bytes 1572868
  31.8 17.2 %collective-permute-start.5 = (bf16[512,512]{1,0:T(8,128)(2,1)S(1)}, bf16[512,512]{1,0:T(8,128)(2,1)S(1)}, u32[]{:S(2)}, u32[]{:S(2)}) collective-permute-start(bf16[512,512]{1,0:T(8,128)(2,1)S(1)} %collective-permute-done.refs_6_), channel_id=1, source_target_pairs={{0,8},{8,0},{16,24},{24,16},{32,40},{40,32},{48,56},{56,48},{1,9},... | collective-permute-start | bytes 1572872 | tf_op jit(solution)/shard_map/ppermute | solution.py:16
  33.8 23.6 %collective-permute-start.10 = (bf16[768,512]{1,0:T(8,128)(2,1)S(1)}, bf16[768,512]{1,0:T(8,128)(2,1)S(1)}, u32[]{:S(2)}, u32[]{:S(2)}) collective-permute-start(bf16[768,512]{1,0:T(8,128)(2,1)S(1)} %get-tuple-element.84), channel_id=1, source_target_pairs={{0,48},{8,56},{16,0},{24,8},{32,16},{40,24},{48,32},{56,40},{1,49}... | collective-permute-start | bytes 2359304 | tf_op jit(solution)/shard_map/ppermute | solution.py:16
  40.0 3.7 %copy-start.1 = (bf16[8,256,1024]{2,1,0:T(8,128)(2,1)S(1)}, bf16[8,256,1024]{2,1,0:T(8,128)(2,1)}, u32[]{:S(2)}) copy-start(bf16[8,256,1024]{2,1,0:T(8,128)(2,1)} %copy-done) | copy-start | bytes 12582916
  40.0 20.8 %collective-permute-start.9 = (bf16[768,512]{1,0:T(8,128)(2,1)S(1)}, bf16[768,512]{1,0:T(8,128)(2,1)S(1)}, u32[]{:S(2)}, u32[]{:S(2)}) collective-permute-start(bf16[768,512]{1,0:T(8,128)(2,1)S(1)} %get-tuple-element.85), channel_id=1, source_target_pairs={{0,16},{8,24},{16,32},{24,40},{32,48},{40,56},{48,0},{56,8},{1,17}... | collective-permute-start | bytes 2359304 | tf_op jit(solution)/shard_map/ppermute | solution.py:16
  40.1 37.3 %copy-start.10 = (bf16[512,4096]{1,0:T(8,128)(2,1)}, bf16[512,4096]{1,0:T(8,128)(2,1)S(1)}, u32[]{:S(2)}) copy-start(bf16[512,4096]{1,0:T(8,128)(2,1)S(1)} %constant_dynamic-update-slice_fusion) | copy-start | bytes 12582916
  40.2 7.9 %copy-start.21 = (bf16[512,512]{1,0:T(8,128)(2,1)S(1)}, bf16[512,512]{1,0:T(8,128)(2,1)}, u32[]{:S(2)}) copy-start(bf16[512,512]{1,0:T(8,128)(2,1)} %copy-done.20) | copy-start | bytes 1572868
  40.6 7.9 %copy-start.23 = (bf16[512,512]{1,0:T(8,128)(2,1)S(1)}, bf16[512,512]{1,0:T(8,128)(2,1)}, u32[]{:S(2)}) copy-start(bf16[512,512]{1,0:T(8,128)(2,1)} %copy-done.22) | copy-start | bytes 1572868
  45.3 15.5 %collective-permute-start.7 = (bf16[1,256,1024]{2,1,0:T(8,128)(2,1)S(1)}, bf16[1,256,1024]{2,1,0:T(8,128)(2,1)S(1)}, u32[]{:S(2)}, u32[]{:S(2)}) collective-permute-start(bf16[1,256,1024]{2,1,0:T(8,128)(2,1)S(1)} %get-tuple-element.49), channel_id=1, source_target_pairs={{0,6},{1,7},{2,0},{3,1},{4,2},{5,3},{6,4},{7,5},{8,14},{9,15},{10,... | collective-permute-start | bytes 1572872 | tf_op jit(solution)/shard_map/ppermute | solution.py:16
  48.1 14.9 %collective-permute-start.8 = (bf16[1,256,1024]{2,1,0:T(8,128)(2,1)S(1)}, bf16[1,256,1024]{2,1,0:T(8,128)(2,1)S(1)}, u32[]{:S(2)}, u32[]{:S(2)}) collective-permute-start(bf16[1,256,1024]{2,1,0:T(8,128)(2,1)S(1)} %get-tuple-element.50), channel_id=1, source_target_pairs={{0,2},{1,3},{2,4},{3,5},{4,6},{5,7},{6,0},{7,1},{8,10},{9,11},{10,... | collective-permute-start | bytes 1572872 | tf_op jit(solution)/shard_map/ppermute | solution.py:16
  63.0 14.5 %collective-permute-start.13 = (bf16[512,512]{1,0:T(8,128)(2,1)S(1)}, bf16[512,512]{1,0:T(8,128)(2,1)S(1)}, u32[]{:S(2)}, u32[]{:S(2)}) collective-permute-start(bf16[512,512]{1,0:T(8,128)(2,1)S(1)} %collective-permute-done.refs_6_), channel_id=1, source_target_pairs={{0,48},{8,56},{16,0},{24,8},{32,16},{40,24},{48,32},{56,40},{1,49}... | collective-permute-start | bytes 1572872 | tf_op jit(solution)/shard_map/ppermute | solution.py:16
  63.1 14.4 %collective-permute-start.12 = (bf16[512,512]{1,0:T(8,128)(2,1)S(1)}, bf16[512,512]{1,0:T(8,128)(2,1)S(1)}, u32[]{:S(2)}, u32[]{:S(2)}) collective-permute-start(bf16[512,512]{1,0:T(8,128)(2,1)S(1)} %collective-permute-done.refs_6_), channel_id=1, source_target_pairs={{0,16},{8,24},{16,32},{24,40},{32,48},{40,56},{48,0},{56,8},{1,17}... | collective-permute-start | bytes 1572872 | tf_op jit(solution)/shard_map/ppermute | solution.py:16
  65.1 12.3 %collective-permute-start.11 = (bf16[512,512]{1,0:T(8,128)(2,1)S(1)}, bf16[512,512]{1,0:T(8,128)(2,1)S(1)}, u32[]{:S(2)}, u32[]{:S(2)}) collective-permute-start(bf16[512,512]{1,0:T(8,128)(2,1)S(1)} %pad_maximum_fusion.7), channel_id=1, source_target_pairs={{0,8},{8,0},{16,24},{24,16},{32,40},{40,32},{48,56},{56,48},{1,9},... | collective-permute-start | bytes 1572872 | tf_op jit(solution)/shard_map/ppermute | solution.py:16
  71.6 23.5 %collective-permute-start.18 = (bf16[2,256,1024]{2,1,0:T(8,128)(2,1)}, bf16[2,256,1024]{2,1,0:T(8,128)(2,1)}, u32[]{:S(2)}, u32[]{:S(2)}) collective-permute-start(bf16[2,256,1024]{2,1,0:T(8,128)(2,1)} %get-tuple-element.63), channel_id=1, source_target_pairs={{0,6},{1,7},{2,0},{3,1},{4,2},{5,3},{6,4},{7,5},{8,14},{9,15},{10,... | collective-permute-start | bytes 3145736 | tf_op jit(solution)/shard_map/ppermute | solution.py:16
  71.9 24.8 %collective-permute-start.19 = (bf16[2,256,1024]{2,1,0:T(8,128)(2,1)}, bf16[2,256,1024]{2,1,0:T(8,128)(2,1)}, u32[]{:S(2)}, u32[]{:S(2)}) collective-permute-start(bf16[2,256,1024]{2,1,0:T(8,128)(2,1)} %get-tuple-element.64), channel_id=1, source_target_pairs={{0,2},{1,3},{2,4},{3,5},{4,6},{5,7},{6,0},{7,1},{8,10},{9,11},{10,... | collective-permute-start | bytes 3145736 | tf_op jit(solution)/shard_map/ppermute | solution.py:16
  77.9 3.6 %copy-start.12 = (f32[512,512]{1,0:T(8,128)}, f32[512,512]{1,0:T(8,128)S(1)}, u32[]{:S(2)}) copy-start(f32[512,512]{1,0:T(8,128)S(1)} %convolution_add_fusion) | copy-start | bytes 3145732
  77.9 3.5 %collective-permute-start.14 = (f32[256,512]{1,0:T(8,128)S(1)}, f32[256,512]{1,0:T(8,128)S(1)}, u32[]{:S(2)}, u32[]{:S(2)}) collective-permute-start(f32[256,512]{1,0:T(8,128)S(1)} %slice.95), channel_id=1, source_target_pairs={{0,64},{64,0},{1,65},{65,1},{2,66},{66,2},{3,67},{67,3},{4,68},{68... | collective-permute-start | bytes 1572872 | tf_op jit(solution)/shard_map/ppermute | solution.py:20
  79.4 20.1 %collective-permute-start.17 = (bf16[768,512]{1,0:T(8,128)(2,1)}, bf16[768,512]{1,0:T(8,128)(2,1)S(1)}, u32[]{:S(2)}, u32[]{:S(2)}) collective-permute-start(bf16[768,512]{1,0:T(8,128)(2,1)} %get-tuple-element.82), channel_id=1, source_target_pairs={{0,48},{8,56},{16,0},{24,8},{32,16},{40,24},{48,32},{56,40},{1,49}... | collective-permute-start | bytes 2359304 | tf_op jit(solution)/shard_map/ppermute | solution.py:16
  80.9 21.1 %collective-permute-start.16 = (bf16[768,512]{1,0:T(8,128)(2,1)}, bf16[768,512]{1,0:T(8,128)(2,1)S(1)}, u32[]{:S(2)}, u32[]{:S(2)}) collective-permute-start(bf16[768,512]{1,0:T(8,128)(2,1)} %get-tuple-element.83), channel_id=1, source_target_pairs={{0,16},{8,24},{16,32},{24,40},{32,48},{40,56},{48,0},{56,8},{1,17}... | collective-permute-start | bytes 2359304 | tf_op jit(solution)/shard_map/ppermute | solution.py:16
  82.2 14.4 %collective-permute-start.15 = (bf16[256,512]{1,0:T(8,128)(2,1)S(1)}, bf16[256,512]{1,0:T(8,128)(2,1)}, u32[]{:S(2)}, u32[]{:S(2)}) collective-permute-start(bf16[256,512]{1,0:T(8,128)(2,1)S(1)} %multiply_convert_fusion), channel_id=1, source_target_pairs={{0,1},{1,0},{2,3},{3,2},{4,5},{5,4},{6,7},{7,6},{8,9},{9,8},{10,11... | collective-permute-start | bytes 786440 | tf_op jit(solution)/shard_map/ppermute | solution.py:16
  102.9 11.8 %copy-start.3 = (bf16[512,512]{1,0:T(8,128)(2,1)S(1)}, bf16[512,512]{1,0:T(8,128)(2,1)}, u32[]{:S(2)}) copy-start(bf16[512,512]{1,0:T(8,128)(2,1)} %copy-done.2) | copy-start | bytes 1572868
  103.0 18.0 %collective-permute-start.21 = (bf16[512,512]{1,0:T(8,128)(2,1)S(1)}, bf16[512,512]{1,0:T(8,128)(2,1)}, u32[]{:S(2)}, u32[]{:S(2)}) collective-permute-start(bf16[512,512]{1,0:T(8,128)(2,1)S(1)} %pad_maximum_fusion.8), channel_id=1, source_target_pairs={{0,6},{1,7},{2,0},{3,1},{4,2},{5,3},{6,4},{7,5},{8,14},{9,15},{10,... | collective-permute-start | bytes 1572872 | tf_op jit(solution)/shard_map/ppermute | solution.py:16
  103.7 17.3 %collective-permute-start.20 = (bf16[512,512]{1,0:T(8,128)(2,1)S(1)}, bf16[512,512]{1,0:T(8,128)(2,1)}, u32[]{:S(2)}, u32[]{:S(2)}) collective-permute-start(bf16[512,512]{1,0:T(8,128)(2,1)S(1)} %pad_maximum_fusion.8), channel_id=1, source_target_pairs={{0,2},{1,3},{2,4},{3,5},{4,6},{5,7},{6,0},{7,1},{8,10},{9,11},{10,... | collective-permute-start | bytes 1572872 | tf_op jit(solution)/shard_map/ppermute | solution.py:16
  108.1 4.6 %copy-start.14 = (f32[2,256,1024]{2,1,0:T(8,128)}, f32[2,256,1024]{2,1,0:T(8,128)S(1)}, u32[]{:S(2)}) copy-start(f32[2,256,1024]{2,1,0:T(8,128)S(1)} %convert_add_fusion) | copy-start | bytes 6291460
  108.2 15.4 %collective-permute-start.22 = (bf16[256,1024]{1,0:T(8,128)(2,1)S(1)}, bf16[256,1024]{1,0:T(8,128)(2,1)}, u32[]{:S(2)}, u32[]{:S(2)}) collective-permute-start(bf16[256,1024]{1,0:T(8,128)(2,1)S(1)} %fusion.1), channel_id=1, source_target_pairs={{0,1},{1,0},{2,3},{3,2},{4,5},{5,4},{6,7},{7,6},{8,9},{9,8},{10,11... | collective-permute-start | bytes 1572872 | tf_op jit(solution)/shard_map/ppermute | solution.py:16
  112.6 6.8 %collective-permute-start.24 = (bf16[256,512]{1,0:T(8,128)(2,1)S(1)}, bf16[256,512]{1,0:T(8,128)(2,1)S(1)}, u32[]{:S(2)}, u32[]{:S(2)}) collective-permute-start(bf16[256,512]{1,0:T(8,128)(2,1)S(1)} %slice.84), channel_id=1, source_target_pairs={{0,48},{8,56},{16,0},{24,8},{32,16},{40,24},{48,32},{56,40},{1,49}... | collective-permute-start | bytes 786440 | tf_op jit(solution)/shard_map/ppermute | solution.py:16
  113.0 8.0 %collective-permute-start.23 = (bf16[256,512]{1,0:T(8,128)(2,1)S(1)}, bf16[256,512]{1,0:T(8,128)(2,1)S(1)}, u32[]{:S(2)}, u32[]{:S(2)}) collective-permute-start(bf16[256,512]{1,0:T(8,128)(2,1)S(1)} %slice.83), channel_id=1, source_target_pairs={{0,16},{8,24},{16,32},{24,40},{32,48},{40,56},{48,0},{56,8},{1,17}... | collective-permute-start | bytes 786440 | tf_op jit(solution)/shard_map/ppermute | solution.py:16
  119.5 18.3 %collective-permute-start.27 = (bf16[2048,512]{1,0:T(8,128)(2,1)}, bf16[2048,512]{1,0:T(8,128)(2,1)}, u32[]{:S(2)}, u32[]{:S(2)}) collective-permute-start(bf16[2048,512]{1,0:T(8,128)(2,1)} %pad_maximum_fusion.1), channel_id=1, source_target_pairs={{0,64},{64,0},{1,65},{65,1},{2,66},{66,2},{3,67},{67,3},{4,68},{68... | collective-permute-start | bytes 6291464 | tf_op jit(solution)/shard_map/ppermute | solution.py:20
  121.0 4.0 %copy-start.7 = (bf16[256,512]{1,0:T(8,128)(2,1)}, bf16[256,512]{1,0:T(8,128)(2,1)S(1)}, u32[]{:S(2)}) copy-start(bf16[256,512]{1,0:T(8,128)(2,1)S(1)} %collective-permute-done.23.refs_12_) | copy-start | bytes 786436
  125.7 12.1 %collective-permute-start.28 = (bf16[2048,512]{1,0:T(8,128)(2,1)}, bf16[2048,512]{1,0:T(8,128)(2,1)}, u32[]{:S(2)}, u32[]{:S(2)}) collective-permute-start(bf16[2048,512]{1,0:T(8,128)(2,1)} %pad_maximum_fusion.2), channel_id=1, source_target_pairs={{0,64},{64,0},{1,65},{65,1},{2,66},{66,2},{3,67},{67,3},{4,68},{68... | collective-permute-start | bytes 6291464 | tf_op jit(solution)/shard_map/ppermute | solution.py:20
  127.8 10.0 %collective-permute-start.25 = (bf16[256,512]{1,0:T(8,128)(2,1)S(1)}, bf16[256,512]{1,0:T(8,128)(2,1)S(1)}, u32[]{:S(2)}, u32[]{:S(2)}) collective-permute-start(bf16[256,512]{1,0:T(8,128)(2,1)S(1)} %slice.85), channel_id=1, source_target_pairs={{0,2},{1,3},{2,4},{3,5},{4,6},{5,7},{6,0},{7,1},{8,10},{9,11},{10,... | collective-permute-start | bytes 786440 | tf_op jit(solution)/shard_map/ppermute | solution.py:16
  128.1 9.6 %collective-permute-start.26 = (bf16[256,512]{1,0:T(8,128)(2,1)S(1)}, bf16[256,512]{1,0:T(8,128)(2,1)S(1)}, u32[]{:S(2)}, u32[]{:S(2)}) collective-permute-start(bf16[256,512]{1,0:T(8,128)(2,1)S(1)} %slice.86), channel_id=1, source_target_pairs={{0,6},{1,7},{2,0},{3,1},{4,2},{5,3},{6,4},{7,5},{8,14},{9,15},{10,... | collective-permute-start | bytes 786440 | tf_op jit(solution)/shard_map/ppermute | solution.py:16
  153.4 36.9 %copy-start.13 = (f32[512,512]{1,0:T(8,128)S(1)}, f32[512,512]{1,0:T(8,128)}, u32[]{:S(2)}) copy-start(f32[512,512]{1,0:T(8,128)} %copy-done.12) | copy-start | bytes 3145732
  153.4 36.5 %all-to-all-start = ((bf16[8,272,512]{2,1,0:T(8,128)(2,1)}), bf16[8,272,512]{2,1,0:T(8,128)(2,1)S(1)}, u32[]{:S(2)}, u32[]{:S(2)}) async-start(bf16[8,272,512]{2,1,0:T(8,128)(2,1)} %shard_map.69), calls=%async_computation | async-start | bytes 4456448 | tf_op jit(solution)/shard_map/all_to_all | solution.py:297
  189.9 3.8 %copy-start.11 = (bf16[512,4096]{1,0:T(8,128)(2,1)S(1)}, bf16[512,4096]{1,0:T(8,128)(2,1)}, u32[]{:S(2)}) copy-start(bf16[512,4096]{1,0:T(8,128)(2,1)} %copy-done.10) | copy-start | bytes 12582916
  191.8 1.9 collective-permute-start.29
  (11 other events, 15.8 us)

commit v11 on v10

--- a/solution.py
+++ b/solution.py
@@ -102,14 +102,16 @@
     for copy in h_copies:
         copy.wait()
 
-    @pl.loop(0, 8)
-    def _(j):
-        h = h_kept[order[j]]
+    @pl.loop(0, 4)
+    def _(i):
+        h = jnp.concatenate([h_kept[order[2 * i]], h_kept[order[2 * i + 1]]], axis=1)
         for side in range(2):
-            for part in range(2):
-                target = p_kept.at[side, j, pl.ds(part * half, half)]
-                pltpu.make_async_copy(target, target, p_sem.at[side, j, part]).wait()
-            total[side] += jnp.dot(h, p_kept[side, j], preferred_element_type=F32)
+            for j in (2 * i, 2 * i + 1):
+                for part in range(2):
+                    target = p_kept.at[side, j, pl.ds(part * half, half)]
+                    pltpu.make_async_copy(target, target, p_sem.at[side, j, part]).wait()
+            block = p_kept[side, pl.ds(2 * i, 2)].reshape(2 * size, width)
+            total[side] += jnp.dot(h, block, preferred_element_type=F32)
 
     squares = total[0] * total[0] + total[1] * total[1]
     value = jnp.broadcast_to(jnp.sum(squares, keepdims=True), (1, width))

time: 255 us -> 254 us (level)
  no operation moved by 1% of the time
where the time goes in v11:
time: 254 us; the launch traced here: 253 us
  waiting for transfers between devices  81.7 us (32%)
  blocking collectives  54 us (21%)
  starting transfers between devices  47.4 us (19%)
  Pallas kernels  24.4 us (10%)
  other arithmetic  20 us (8%)
  local copies, waits for them, and re-layouts  16.5 us (6%)
  matrix products  6.17 us (2%)
  between operations  3.07 us (1%)
    all_to_all x1, blocking collectives, shards(): grad = lax.all_to_all(grad, 'dp', 0, 0, tiled=True)  54 us
    ppermute x23, waiting for transfers between devices, shift(): return lax.ppermute(value, axis, perm)  50.8 us
    ppermute x23, starting transfers between devices, shift(): return lax.ppermute(value, axis, perm)  39.2 us
    all_to_all x1, waiting for transfers between devices, shards(): back = lax.all_to_all(back, 'tensor', 0, 0, tiled=True)  29.4 us
    pallas_call x1, Pallas kernels, teach(): pl.pallas_call(teach_kernel, grid_spec=pltpu.PrefetchScalarGridSpec(num_s...  13.1 us
    pallas_call x1, Pallas kernels, project(): pl.pallas_call(project_kernel, in_specs=[pl.BlockSpec(memory_space=pltpu....  11.3 us
    unnamed x55, local copies, waits for them, and re-layouts  10.8 us
    all_to_all x1, starting transfers between devices, shards(): back = lax.all_to_all(back, 'tensor', 0, 0, tiled=True)  7.05 us
  transfers between devices with their start and end apart: 31, of which 15 were waited for; matrix products, arithmetic and copies ran while one was open for 8% of the time, Pallas kernels for 5%

profile of v11, /device:TPU:0, one launch (start us, length us, event | category | flops | bytes accessed | tf_op | source)
XLA Modules:
  0.0 253.4 jit_solution(43830404243727592)
XLA Ops:
  0.7 2.7 %constant_dynamic-slice_fusion = (bf16[256,4096]{1,0:T(8,128)(2,1)S(1)}, bf16[256,4096]{1,0:T(8,128)(2,1)S(1)}) fusion(bf16[256,8192]{1,0:T(8,128)(2,1)} %param.7, s32[]{:T(128)S(6)} %select_n.90, s32[]{:T(128)S(6)} %select_n.89), kind=kLoop, calls=%fused_computation.68 | loop fusion | bytes 8388616 | tf_op jit(solution)/shard_map/dynamic_slice | solution.py:220
  3.5 3.2 %collective-permute-start.4 = (bf16[512,512]{1,0:T(8,128)(2,1)S(1)}, bf16[512,512]{1,0:T(8,128)(2,1)S(1)}, u32[]{:S(2)}, u32[]{:S(2)}) collective-permute-start(bf16[512,512]{1,0:T(8,128)(2,1)S(1)} %copy-done.24), channel_id=1, source_target_pairs={{0,48},{8,56},{16,0},{24,8},{32,16},{40,24},{48,32},{56,40},{1,49}... | collective-permute-start | bytes 1572872 | tf_op jit(solution)/shard_map/ppermute | solution.py:16
  6.7 1.5 collective-permute-start.2
  8.9 13.1 %shard_map.68 = (bf16[8,256,1024]{2,1,0:T(8,128)(2,1)S(1)}, bf16[8,256,1024]{2,1,0:T(8,128)(2,1)}) custom-call(s32[1]{0:T(128)} %bitcast.role, bf16[512,1024]{1,0:T(8,128)(2,1)S(1)} %bitcast.38, bf16[1024,8192]{1,0:T(8,128)(2,1)} %weight.1), custom_call_target="tpu_custom_call" | custom-call | flops 8589934592 | bytes 16777216 | tf_op jit(solution)/shard_map/pallas_call | solution.py:176
  22.0 2.0 copy-done
  24.1 5.7 %collective-permute-done.4 = bf16[512,512]{1,0:T(8,128)(2,1)S(1)} collective-permute-done((bf16[512,512]{1,0:T(8,128)(2,1)S(1)}, bf16[512,512]{1,0:T(8,128)(2,1)S(1)}, u32[]{:S(2)}, u32[]{:S(2)}) %collective-permute-start.4) | collective-permute-done | bytes 524320 | tf_op jit(solution)/shard_map/ppermute | solution.py:16
  29.8 1.7 copy-done.16
  31.8 1.9 collective-permute-start.5
  33.8 6.2 %collective-permute-start.10 = (bf16[768,512]{1,0:T(8,128)(2,1)S(1)}, bf16[768,512]{1,0:T(8,128)(2,1)S(1)}, u32[]{:S(2)}, u32[]{:S(2)}) collective-permute-start(bf16[768,512]{1,0:T(8,128)(2,1)S(1)} %get-tuple-element.84), channel_id=1, source_target_pairs={{0,48},{8,56},{16,0},{24,8},{32,16},{40,24},{48,32},{56,40},{1,49}... | collective-permute-start | bytes 2359304 | tf_op jit(solution)/shard_map/ppermute | solution.py:16
  41.1 2.6 %copy-done.1 = bf16[8,256,1024]{2,1,0:T(8,128)(2,1)S(1)} copy-done((bf16[8,256,1024]{2,1,0:T(8,128)(2,1)S(1)}, bf16[8,256,1024]{2,1,0:T(8,128)(2,1)}, u32[]{:S(2)}) %copy-start.1) | copy-done | bytes 4194328
  43.7 1.6 add_convert_fusion.2
  45.3 2.8 %collective-permute-start.7 = (bf16[1,256,1024]{2,1,0:T(8,128)(2,1)S(1)}, bf16[1,256,1024]{2,1,0:T(8,128)(2,1)S(1)}, u32[]{:S(2)}, u32[]{:S(2)}) collective-permute-start(bf16[1,256,1024]{2,1,0:T(8,128)(2,1)S(1)} %get-tuple-element.49), channel_id=1, source_target_pairs={{0,6},{1,7},{2,0},{3,1},{4,2},{5,3},{6,4},{7,5},{8,14},{9,15},{10,... | collective-permute-start | bytes 1572872 | tf_op jit(solution)/shard_map/ppermute | solution.py:16
  49.0 8.4 %collective-permute-done.10 = bf16[768,512]{1,0:T(8,128)(2,1)S(1)} collective-permute-done((bf16[768,512]{1,0:T(8,128)(2,1)S(1)}, bf16[768,512]{1,0:T(8,128)(2,1)S(1)}, u32[]{:S(2)}, u32[]{:S(2)}) %collective-permute-start.10) | collective-permute-done | bytes 786464 | tf_op jit(solution)/shard_map/ppermute | solution.py:16
  57.4 3.4 %collective-permute-done.9 = bf16[768,512]{1,0:T(8,128)(2,1)S(1)} collective-permute-done((bf16[768,512]{1,0:T(8,128)(2,1)S(1)}, bf16[768,512]{1,0:T(8,128)(2,1)S(1)}, u32[]{:S(2)}, u32[]{:S(2)}) %collective-permute-start.9) | collective-permute-done | bytes 786464 | tf_op jit(solution)/shard_map/ppermute | solution.py:16
  60.8 2.1 collective-permute-done.8
  63.1 1.9 collective-permute-start.12
  65.1 1.5 collective-permute-start.11
  67.5 4.1 %add_convert_fusion = (bf16[2,256,1024]{2,1,0:T(8,128)(2,1)}, bf16[2,256,1024]{2,1,0:T(8,128)(2,1)}) fusion(bf16[1,256,1024]{2,1,0:T(8,128)(2,1)S(1)} %collective-permute-done.8, bf16[8,256,1024]{2,1,0:T(8,128)(2,1)} %collective-permute-done.6, s32[]{:T(128)S(6)} %select_n.102, bf16[8,256,1024]{2,1,0:T(8,128)(2,1)S(1)} %copy-done.1, ...), kind=kLoop, calls=%fused_computation.7 | loop fusion | flops 6291456 | bytes 7340040 | tf_op jit(solution)/shard_map/convert_element_type | solution.py:254
  71.9 1.7 collective-permute-start.19
  74.3 3.2 %collective-permute-done.11 = bf16[512,512]{1,0:T(8,128)(2,1)S(1)} collective-permute-done((bf16[512,512]{1,0:T(8,128)(2,1)S(1)}, bf16[512,512]{1,0:T(8,128)(2,1)S(1)}, u32[]{:S(2)}, u32[]{:S(2)}) %collective-permute-start.11) | collective-permute-done | bytes 524320 | tf_op jit(solution)/shard_map/ppermute | solution.py:16
  78.1 1.3 pad_maximum_fusion.5
  79.4 1.5 collective-permute-start.17
  82.2 4.2 %collective-permute-start.15 = (bf16[256,512]{1,0:T(8,128)(2,1)S(1)}, bf16[256,512]{1,0:T(8,128)(2,1)}, u32[]{:S(2)}, u32[]{:S(2)}) collective-permute-start(bf16[256,512]{1,0:T(8,128)(2,1)S(1)} %multiply_convert_fusion), channel_id=1, source_target_pairs={{0,1},{1,0},{2,3},{3,2},{4,5},{5,4},{6,7},{7,6},{8,9},{9,8},{10,11... | collective-permute-start | bytes 786440 | tf_op jit(solution)/shard_map/ppermute | solution.py:16
  86.4 8.7 %collective-permute-done.18 = bf16[2,256,1024]{2,1,0:T(8,128)(2,1)} collective-permute-done((bf16[2,256,1024]{2,1,0:T(8,128)(2,1)}, bf16[2,256,1024]{2,1,0:T(8,128)(2,1)}, u32[]{:S(2)}, u32[]{:S(2)}) %collective-permute-start.18) | collective-permute-done | bytes 1048608 | tf_op jit(solution)/shard_map/ppermute | solution.py:16
  95.1 1.5 collective-permute-done.19
  96.7 2.9 %collective-permute-done.17.refs_11_ = bf16[768,512]{1,0:T(8,128)(2,1)S(1)} collective-permute-done((bf16[768,512]{1,0:T(8,128)(2,1)}, bf16[768,512]{1,0:T(8,128)(2,1)S(1)}, u32[]{:S(2)}, u32[]{:S(2)}) %collective-permute-start.17) | collective-permute-done | bytes 786464 | tf_op jit(solution)/shard_map/ppermute | solution.py:16
  99.5 2.4 collective-permute-done.16.refs_10_
  103.7 1.3 collective-permute-start.20
  105.1 3.0 %convert_add_fusion = f32[2,256,1024]{2,1,0:T(8,128)S(1)} fusion(bf16[2,256,1024]{2,1,0:T(8,128)(2,1)} %collective-permute-done.19, bf16[2,256,1024]{2,1,0:T(8,128)(2,1)} %collective-permute-done.18, bf16[8,256,1024]{2,1,0:T(8,128)(2,1)} %collective-permute-done.6, s32[]{:T(128)S(6)} %select_n.103, bf16[8,256,1024]{2,1,0:T(8,128)(2,1)} %copy-done), kind=kLoop, calls=%fused_computation.6 | loop fusion | flops 3670016 | bytes 6291460 | tf_op jit(solution)/shard_map/add | solution.py:281
  108.2 4.4 %collective-permute-start.22 = (bf16[256,1024]{1,0:T(8,128)(2,1)S(1)}, bf16[256,1024]{1,0:T(8,128)(2,1)}, u32[]{:S(2)}, u32[]{:S(2)}) collective-permute-start(bf16[256,1024]{1,0:T(8,128)(2,1)S(1)} %fusion.1), channel_id=1, source_target_pairs={{0,1},{1,0},{2,3},{3,2},{4,5},{5,4},{6,7},{7,6},{8,9},{9,8},{10,11... | collective-permute-start | bytes 1572872 | tf_op jit(solution)/shard_map/ppermute | solution.py:16
  113.0 1.7 collective-permute-start.23
  114.7 1.5 pad_maximum_fusion.1
  116.3 3.2 %collective-permute-done.24.refs_13_ = bf16[256,512]{1,0:T(8,128)(2,1)S(1)} collective-permute-done((bf16[256,512]{1,0:T(8,128)(2,1)S(1)}, bf16[256,512]{1,0:T(8,128)(2,1)S(1)}, u32[]{:S(2)}, u32[]{:S(2)}) %collective-permute-start.24) | collective-permute-done | bytes 262176 | tf_op jit(solution)/shard_map/ppermute | solution.py:16
  119.5 1.5 collective-permute-done.23.refs_12_
  121.0 2.6 %collective-permute-done.22 = bf16[256,1024]{1,0:T(8,128)(2,1)} collective-permute-done((bf16[256,1024]{1,0:T(8,128)(2,1)S(1)}, bf16[256,1024]{1,0:T(8,128)(2,1)}, u32[]{:S(2)}, u32[]{:S(2)}) %collective-permute-start.22) | collective-permute-done | bytes 524320 | tf_op jit(solution)/shard_map/ppermute | solution.py:16
  123.6 1.4 pad_maximum_fusion.2
  128.1 3.0 %collective-permute-start.26 = (bf16[256,512]{1,0:T(8,128)(2,1)S(1)}, bf16[256,512]{1,0:T(8,128)(2,1)S(1)}, u32[]{:S(2)}, u32[]{:S(2)}) collective-permute-start(bf16[256,512]{1,0:T(8,128)(2,1)S(1)} %slice.86), channel_id=1, source_target_pairs={{0,6},{1,7},{2,0},{3,1},{4,2},{5,3},{6,4},{7,5},{8,14},{9,15},{10,... | collective-permute-start | bytes 786440 | tf_op jit(solution)/shard_map/ppermute | solution.py:16
  131.1 1.6 bitcast_add_fusion.refs_16_
  132.7 5.1 %collective-permute-done.25 = bf16[256,512]{1,0:T(8,128)(2,1)S(1)} collective-permute-done((bf16[256,512]{1,0:T(8,128)(2,1)S(1)}, bf16[256,512]{1,0:T(8,128)(2,1)S(1)}, u32[]{:S(2)}, u32[]{:S(2)}) %collective-permute-start.25) | collective-permute-done | bytes 262176 | tf_op jit(solution)/shard_map/ppermute | solution.py:16
  137.8 1.0 copy-done.4
  140.7 11.3 %shard_map.69 = bf16[8,272,512]{2,1,0:T(8,128)(2,1)} custom-call(s32[17]{0:T(128)S(1)} %stack.68.order, bf16[1,256,512]{2,1,0:T(8,128)(2,1)S(1)} %bitcast.37, bf16[1,256,512]{2,1,0:T(8,128)(2,1)} %bitcast.19.refs_1_, bf16[2,256,512]{2,1,0:T(8,128)(2,1)} %bitcast.21.refs_2_, bf16[1,256,512]{2,1,0:T(8,128)(2,1)S(1)} %bitcast.39, ...), custom_call_target="tpu_custom_call" | custom-call | flops 4294967296 | bytes 8388608 | tf_op jit(solution)/shard_map/pallas_call | solution.py:140
  152.0 7.1 %all-to-all-start = ((bf16[8,272,512]{2,1,0:T(8,128)(2,1)}), bf16[8,272,512]{2,1,0:T(8,128)(2,1)S(1)}, u32[]{:S(2)}, u32[]{:S(2)}) async-start(bf16[8,272,512]{2,1,0:T(8,128)(2,1)} %shard_map.69), calls=%async_computation | async-start | bytes 4456448 | tf_op jit(solution)/shard_map/all_to_all | solution.py:299
  159.1 29.4 %all-to-all-done = bf16[8,272,512]{2,1,0:T(8,128)(2,1)S(1)} async-done(((bf16[8,272,512]{2,1,0:T(8,128)(2,1)}), bf16[8,272,512]{2,1,0:T(8,128)(2,1)S(1)}, u32[]{:S(2)}, u32[]{:S(2)}) %all-to-all-start) | async-done | bytes 2228256 | tf_op jit(solution)/shard_map/all_to_all | solution.py:299
  189.0 1.5 fusion.3
  190.8 1.5 collective-permute-done.29
  192.4 2.5 convolution_convert_fusion
  195.4 54.0 %all_to_all.10 = bf16[8,528,512]{2,1,0:T(8,128)(2,1)S(1)} all-to-all(bf16[8,528,512]{2,1,0:T(8,128)(2,1)S(1)} %pad_maximum_fusion), channel_id=1, replica_groups=mesh['role'=2,'dp'=8,'tensor'=8] {'dp'}, dimensions={0} | all-to-all | bytes 8650752 | tf_op jit(solution)/shard_map/all_to_all | solution.py:312
  250.0 1.1 slice_multiply_fusion
  (127 shorter events, 16.7 us)
Async XLA Ops:
  0.6 2.9 %copy-start.24 = (bf16[512,512]{1,0:T(8,128)(2,1)S(1)}, bf16[512,512]{1,0:T(8,128)(2,1)}, u32[]{:S(2)}) copy-start(bf16[512,512]{1,0:T(8,128)(2,1)} %param.8) | copy-start | bytes 1572868
  0.6 7.5 %copy-start.26 = (bf16[512,512]{1,0:T(8,128)(2,1)S(1)}, bf16[512,512]{1,0:T(8,128)(2,1)}, u32[]{:S(2)}) copy-start(bf16[512,512]{1,0:T(8,128)(2,1)} %param.9) | copy-start | bytes 1572868
  0.7 8.2 %copy-start.9 = (bf16[2,256,1024]{2,1,0:T(8,128)(2,1)S(1)}, bf16[2,256,1024]{2,1,0:T(8,128)(2,1)}, u32[]{:S(2)}) copy-start(bf16[2,256,1024]{2,1,0:T(8,128)(2,1)} %param.5) | copy-start | bytes 3145732
  3.4 26.3 %collective-permute-start.1 = (bf16[256,4096]{1,0:T(8,128)(2,1)S(1)}, bf16[256,4096]{1,0:T(8,128)(2,1)S(1)}, u32[]{:S(2)}, u32[]{:S(2)}) collective-permute-start(bf16[256,4096]{1,0:T(8,128)(2,1)S(1)} %get-tuple-element.41), channel_id=1, source_target_pairs={{0,64},{64,0},{1,65},{65,1},{2,66},{66,2},{3,67},{67,3},{4,68},{68... | collective-permute-start | bytes 6291464 | tf_op jit(solution)/shard_map/ppermute | solution.py:20
  3.5 26.2 %collective-permute-start.4 = (bf16[512,512]{1,0:T(8,128)(2,1)S(1)}, bf16[512,512]{1,0:T(8,128)(2,1)S(1)}, u32[]{:S(2)}, u32[]{:S(2)}) collective-permute-start(bf16[512,512]{1,0:T(8,128)(2,1)S(1)} %copy-done.24), channel_id=1, source_target_pairs={{0,48},{8,56},{16,0},{24,8},{32,16},{40,24},{48,32},{56,40},{1,49}... | collective-permute-start | bytes 1572872 | tf_op jit(solution)/shard_map/ppermute | solution.py:16
  6.7 23.0 %collective-permute-start.3 = (bf16[512,512]{1,0:T(8,128)(2,1)S(1)}, bf16[512,512]{1,0:T(8,128)(2,1)S(1)}, u32[]{:S(2)}, u32[]{:S(2)}) collective-permute-start(bf16[512,512]{1,0:T(8,128)(2,1)S(1)} %copy-done.24), channel_id=1, source_target_pairs={{0,16},{8,24},{16,32},{24,40},{32,48},{40,56},{48,0},{56,8},{1,17}... | collective-permute-start | bytes 1572872 | tf_op jit(solution)/shard_map/ppermute | solution.py:16
  6.7 23.0 %collective-permute-start.2 = (bf16[512,512]{1,0:T(8,128)(2,1)S(1)}, bf16[512,512]{1,0:T(8,128)(2,1)S(1)}, u32[]{:S(2)}, u32[]{:S(2)}) collective-permute-start(bf16[512,512]{1,0:T(8,128)(2,1)S(1)} %copy-done.24), channel_id=1, source_target_pairs={{0,8},{8,0},{16,24},{24,16},{32,40},{40,32},{48,56},{56,48},{1,9},... | collective-permute-start | bytes 1572872 | tf_op jit(solution)/shard_map/ppermute | solution.py:16
  8.2 15.9 %collective-permute-start = (bf16[512,512]{1,0:T(8,128)(2,1)S(1)}, bf16[512,512]{1,0:T(8,128)(2,1)S(1)}, u32[]{:S(2)}, u32[]{:S(2)}) collective-permute-start(bf16[512,512]{1,0:T(8,128)(2,1)S(1)} %copy-done.26), channel_id=1, source_target_pairs={{0,0},{1,8},{2,16},{3,24},{4,32},{5,40},{6,48},{7,56},{8,9},{9,1},... | collective-permute-start | bytes 1572872 | tf_op jit(solution)/shard_map/ppermute | solution.py:217
  24.0 39.0 %copy-start.2 = (bf16[512,512]{1,0:T(8,128)(2,1)}, bf16[512,512]{1,0:T(8,128)(2,1)S(1)}, u32[]{:S(2)}) copy-start(bf16[512,512]{1,0:T(8,128)(2,1)S(1)} %collective-permute-done.refs_6_) | copy-start | bytes 1572868
  31.4 9.6 %collective-permute-start.6 = (bf16[8,256,1024]{2,1,0:T(8,128)(2,1)}, bf16[8,256,1024]{2,1,0:T(8,128)(2,1)}, u32[]{:S(2)}, u32[]{:S(2)}) collective-permute-start(bf16[8,256,1024]{2,1,0:T(8,128)(2,1)} %get-tuple-element.48), channel_id=1, source_target_pairs={{0,64},{64,0},{1,65},{65,1},{2,66},{66,2},{3,67},{67,3},{4,68},{68... | collective-permute-start | bytes 12582920 | tf_op jit(solution)/shard_map/ppermute | solution.py:20
  31.5 2.3 slice-start
  31.6 8.4 %copy-start.17 = (bf16[256,4096]{1,0:T(8,128)(2,1)S(1)}, bf16[256,4096]{1,0:T(8,128)(2,1)}, u32[]{:S(2)}) copy-start(bf16[256,4096]{1,0:T(8,128)(2,1)} %copy-done.16) | copy-start | bytes 6291460
  31.8 8.3 %copy-start.25 = (bf16[512,512]{1,0:T(8,128)(2,1)S(1)}, bf16[512,512]{1,0:T(8,128)(2,1)}, u32[]{:S(2)}) copy-start(bf16[512,512]{1,0:T(8,128)(2,1)} %param.8) | copy-start | bytes 1572868
  31.8 17.2 %collective-permute-start.5 = (bf16[512,512]{1,0:T(8,128)(2,1)S(1)}, bf16[512,512]{1,0:T(8,128)(2,1)S(1)}, u32[]{:S(2)}, u32[]{:S(2)}) collective-permute-start(bf16[512,512]{1,0:T(8,128)(2,1)S(1)} %collective-permute-done.refs_6_), channel_id=1, source_target_pairs={{0,8},{8,0},{16,24},{24,16},{32,40},{40,32},{48,56},{56,48},{1,9},... | collective-permute-start | bytes 1572872 | tf_op jit(solution)/shard_map/ppermute | solution.py:16
  33.8 23.6 %collective-permute-start.10 = (bf16[768,512]{1,0:T(8,128)(2,1)S(1)}, bf16[768,512]{1,0:T(8,128)(2,1)S(1)}, u32[]{:S(2)}, u32[]{:S(2)}) collective-permute-start(bf16[768,512]{1,0:T(8,128)(2,1)S(1)} %get-tuple-element.84), channel_id=1, source_target_pairs={{0,48},{8,56},{16,0},{24,8},{32,16},{40,24},{48,32},{56,40},{1,49}... | collective-permute-start | bytes 2359304 | tf_op jit(solution)/shard_map/ppermute | solution.py:16
  40.0 3.7 %copy-start.1 = (bf16[8,256,1024]{2,1,0:T(8,128)(2,1)S(1)}, bf16[8,256,1024]{2,1,0:T(8,128)(2,1)}, u32[]{:S(2)}) copy-start(bf16[8,256,1024]{2,1,0:T(8,128)(2,1)} %copy-done) | copy-start | bytes 12582916
  40.0 20.8 %collective-permute-start.9 = (bf16[768,512]{1,0:T(8,128)(2,1)S(1)}, bf16[768,512]{1,0:T(8,128)(2,1)S(1)}, u32[]{:S(2)}, u32[]{:S(2)}) collective-permute-start(bf16[768,512]{1,0:T(8,128)(2,1)S(1)} %get-tuple-element.85), channel_id=1, source_target_pairs={{0,16},{8,24},{16,32},{24,40},{32,48},{40,56},{48,0},{56,8},{1,17}... | collective-permute-start | bytes 2359304 | tf_op jit(solution)/shard_map/ppermute | solution.py:16
  40.1 37.3 %copy-start.10 = (bf16[512,4096]{1,0:T(8,128)(2,1)}, bf16[512,4096]{1,0:T(8,128)(2,1)S(1)}, u32[]{:S(2)}) copy-start(bf16[512,4096]{1,0:T(8,128)(2,1)S(1)} %constant_dynamic-update-slice_fusion) | copy-start | bytes 12582916
  40.2 7.9 %copy-start.21 = (bf16[512,512]{1,0:T(8,128)(2,1)S(1)}, bf16[512,512]{1,0:T(8,128)(2,1)}, u32[]{:S(2)}) copy-start(bf16[512,512]{1,0:T(8,128)(2,1)} %copy-done.20) | copy-start | bytes 1572868
  40.6 7.9 %copy-start.23 = (bf16[512,512]{1,0:T(8,128)(2,1)S(1)}, bf16[512,512]{1,0:T(8,128)(2,1)}, u32[]{:S(2)}) copy-start(bf16[512,512]{1,0:T(8,128)(2,1)} %copy-done.22) | copy-start | bytes 1572868
  45.3 15.5 %collective-permute-start.7 = (bf16[1,256,1024]{2,1,0:T(8,128)(2,1)S(1)}, bf16[1,256,1024]{2,1,0:T(8,128)(2,1)S(1)}, u32[]{:S(2)}, u32[]{:S(2)}) collective-permute-start(bf16[1,256,1024]{2,1,0:T(8,128)(2,1)S(1)} %get-tuple-element.49), channel_id=1, source_target_pairs={{0,6},{1,7},{2,0},{3,1},{4,2},{5,3},{6,4},{7,5},{8,14},{9,15},{10,... | collective-permute-start | bytes 1572872 | tf_op jit(solution)/shard_map/ppermute | solution.py:16
  48.1 14.9 %collective-permute-start.8 = (bf16[1,256,1024]{2,1,0:T(8,128)(2,1)S(1)}, bf16[1,256,1024]{2,1,0:T(8,128)(2,1)S(1)}, u32[]{:S(2)}, u32[]{:S(2)}) collective-permute-start(bf16[1,256,1024]{2,1,0:T(8,128)(2,1)S(1)} %get-tuple-element.50), channel_id=1, source_target_pairs={{0,2},{1,3},{2,4},{3,5},{4,6},{5,7},{6,0},{7,1},{8,10},{9,11},{10,... | collective-permute-start | bytes 1572872 | tf_op jit(solution)/shard_map/ppermute | solution.py:16
  63.0 14.5 %collective-permute-start.13 = (bf16[512,512]{1,0:T(8,128)(2,1)S(1)}, bf16[512,512]{1,0:T(8,128)(2,1)S(1)}, u32[]{:S(2)}, u32[]{:S(2)}) collective-permute-start(bf16[512,512]{1,0:T(8,128)(2,1)S(1)} %collective-permute-done.refs_6_), channel_id=1, source_target_pairs={{0,48},{8,56},{16,0},{24,8},{32,16},{40,24},{48,32},{56,40},{1,49}... | collective-permute-start | bytes 1572872 | tf_op jit(solution)/shard_map/ppermute | solution.py:16
  63.1 14.4 %collective-permute-start.12 = (bf16[512,512]{1,0:T(8,128)(2,1)S(1)}, bf16[512,512]{1,0:T(8,128)(2,1)S(1)}, u32[]{:S(2)}, u32[]{:S(2)}) collective-permute-start(bf16[512,512]{1,0:T(8,128)(2,1)S(1)} %collective-permute-done.refs_6_), channel_id=1, source_target_pairs={{0,16},{8,24},{16,32},{24,40},{32,48},{40,56},{48,0},{56,8},{1,17}... | collective-permute-start | bytes 1572872 | tf_op jit(solution)/shard_map/ppermute | solution.py:16
  65.1 12.3 %collective-permute-start.11 = (bf16[512,512]{1,0:T(8,128)(2,1)S(1)}, bf16[512,512]{1,0:T(8,128)(2,1)S(1)}, u32[]{:S(2)}, u32[]{:S(2)}) collective-permute-start(bf16[512,512]{1,0:T(8,128)(2,1)S(1)} %pad_maximum_fusion.7), channel_id=1, source_target_pairs={{0,8},{8,0},{16,24},{24,16},{32,40},{40,32},{48,56},{56,48},{1,9},... | collective-permute-start | bytes 1572872 | tf_op jit(solution)/shard_map/ppermute | solution.py:16
  71.6 23.5 %collective-permute-start.18 = (bf16[2,256,1024]{2,1,0:T(8,128)(2,1)}, bf16[2,256,1024]{2,1,0:T(8,128)(2,1)}, u32[]{:S(2)}, u32[]{:S(2)}) collective-permute-start(bf16[2,256,1024]{2,1,0:T(8,128)(2,1)} %get-tuple-element.63), channel_id=1, source_target_pairs={{0,6},{1,7},{2,0},{3,1},{4,2},{5,3},{6,4},{7,5},{8,14},{9,15},{10,... | collective-permute-start | bytes 3145736 | tf_op jit(solution)/shard_map/ppermute | solution.py:16
  71.9 24.8 %collective-permute-start.19 = (bf16[2,256,1024]{2,1,0:T(8,128)(2,1)}, bf16[2,256,1024]{2,1,0:T(8,128)(2,1)}, u32[]{:S(2)}, u32[]{:S(2)}) collective-permute-start(bf16[2,256,1024]{2,1,0:T(8,128)(2,1)} %get-tuple-element.64), channel_id=1, source_target_pairs={{0,2},{1,3},{2,4},{3,5},{4,6},{5,7},{6,0},{7,1},{8,10},{9,11},{10,... | collective-permute-start | bytes 3145736 | tf_op jit(solution)/shard_map/ppermute | solution.py:16
  77.9 3.6 %copy-start.12 = (f32[512,512]{1,0:T(8,128)}, f32[512,512]{1,0:T(8,128)S(1)}, u32[]{:S(2)}) copy-start(f32[512,512]{1,0:T(8,128)S(1)} %convolution_add_fusion) | copy-start | bytes 3145732
  77.9 3.5 %collective-permute-start.14 = (f32[256,512]{1,0:T(8,128)S(1)}, f32[256,512]{1,0:T(8,128)S(1)}, u32[]{:S(2)}, u32[]{:S(2)}) collective-permute-start(f32[256,512]{1,0:T(8,128)S(1)} %slice.95), channel_id=1, source_target_pairs={{0,64},{64,0},{1,65},{65,1},{2,66},{66,2},{3,67},{67,3},{4,68},{68... | collective-permute-start | bytes 1572872 | tf_op jit(solution)/shard_map/ppermute | solution.py:20
  79.4 20.1 %collective-permute-start.17 = (bf16[768,512]{1,0:T(8,128)(2,1)}, bf16[768,512]{1,0:T(8,128)(2,1)S(1)}, u32[]{:S(2)}, u32[]{:S(2)}) collective-permute-start(bf16[768,512]{1,0:T(8,128)(2,1)} %get-tuple-element.82), channel_id=1, source_target_pairs={{0,48},{8,56},{16,0},{24,8},{32,16},{40,24},{48,32},{56,40},{1,49}... | collective-permute-start | bytes 2359304 | tf_op jit(solution)/shard_map/ppermute | solution.py:16
  80.9 21.1 %collective-permute-start.16 = (bf16[768,512]{1,0:T(8,128)(2,1)}, bf16[768,512]{1,0:T(8,128)(2,1)S(1)}, u32[]{:S(2)}, u32[]{:S(2)}) collective-permute-start(bf16[768,512]{1,0:T(8,128)(2,1)} %get-tuple-element.83), channel_id=1, source_target_pairs={{0,16},{8,24},{16,32},{24,40},{32,48},{40,56},{48,0},{56,8},{1,17}... | collective-permute-start | bytes 2359304 | tf_op jit(solution)/shard_map/ppermute | solution.py:16
  82.2 14.4 %collective-permute-start.15 = (bf16[256,512]{1,0:T(8,128)(2,1)S(1)}, bf16[256,512]{1,0:T(8,128)(2,1)}, u32[]{:S(2)}, u32[]{:S(2)}) collective-permute-start(bf16[256,512]{1,0:T(8,128)(2,1)S(1)} %multiply_convert_fusion), channel_id=1, source_target_pairs={{0,1},{1,0},{2,3},{3,2},{4,5},{5,4},{6,7},{7,6},{8,9},{9,8},{10,11... | collective-permute-start | bytes 786440 | tf_op jit(solution)/shard_map/ppermute | solution.py:16
  102.9 11.8 %copy-start.3 = (bf16[512,512]{1,0:T(8,128)(2,1)S(1)}, bf16[512,512]{1,0:T(8,128)(2,1)}, u32[]{:S(2)}) copy-start(bf16[512,512]{1,0:T(8,128)(2,1)} %copy-done.2) | copy-start | bytes 1572868
  103.0 18.0 %collective-permute-start.21 = (bf16[512,512]{1,0:T(8,128)(2,1)S(1)}, bf16[512,512]{1,0:T(8,128)(2,1)}, u32[]{:S(2)}, u32[]{:S(2)}) collective-permute-start(bf16[512,512]{1,0:T(8,128)(2,1)S(1)} %pad_maximum_fusion.8), channel_id=1, source_target_pairs={{0,6},{1,7},{2,0},{3,1},{4,2},{5,3},{6,4},{7,5},{8,14},{9,15},{10,... | collective-permute-start | bytes 1572872 | tf_op jit(solution)/shard_map/ppermute | solution.py:16
  103.7 17.3 %collective-permute-start.20 = (bf16[512,512]{1,0:T(8,128)(2,1)S(1)}, bf16[512,512]{1,0:T(8,128)(2,1)}, u32[]{:S(2)}, u32[]{:S(2)}) collective-permute-start(bf16[512,512]{1,0:T(8,128)(2,1)S(1)} %pad_maximum_fusion.8), channel_id=1, source_target_pairs={{0,2},{1,3},{2,4},{3,5},{4,6},{5,7},{6,0},{7,1},{8,10},{9,11},{10,... | collective-permute-start | bytes 1572872 | tf_op jit(solution)/shard_map/ppermute | solution.py:16
  108.1 4.6 %copy-start.14 = (f32[2,256,1024]{2,1,0:T(8,128)}, f32[2,256,1024]{2,1,0:T(8,128)S(1)}, u32[]{:S(2)}) copy-start(f32[2,256,1024]{2,1,0:T(8,128)S(1)} %convert_add_fusion) | copy-start | bytes 6291460
  108.2 15.4 %collective-permute-start.22 = (bf16[256,1024]{1,0:T(8,128)(2,1)S(1)}, bf16[256,1024]{1,0:T(8,128)(2,1)}, u32[]{:S(2)}, u32[]{:S(2)}) collective-permute-start(bf16[256,1024]{1,0:T(8,128)(2,1)S(1)} %fusion.1), channel_id=1, source_target_pairs={{0,1},{1,0},{2,3},{3,2},{4,5},{5,4},{6,7},{7,6},{8,9},{9,8},{10,11... | collective-permute-start | bytes 1572872 | tf_op jit(solution)/shard_map/ppermute | solution.py:16
  112.6 6.8 %collective-permute-start.24 = (bf16[256,512]{1,0:T(8,128)(2,1)S(1)}, bf16[256,512]{1,0:T(8,128)(2,1)S(1)}, u32[]{:S(2)}, u32[]{:S(2)}) collective-permute-start(bf16[256,512]{1,0:T(8,128)(2,1)S(1)} %slice.84), channel_id=1, source_target_pairs={{0,48},{8,56},{16,0},{24,8},{32,16},{40,24},{48,32},{56,40},{1,49}... | collective-permute-start | bytes 786440 | tf_op jit(solution)/shard_map/ppermute | solution.py:16
  113.0 8.0 %collective-permute-start.23 = (bf16[256,512]{1,0:T(8,128)(2,1)S(1)}, bf16[256,512]{1,0:T(8,128)(2,1)S(1)}, u32[]{:S(2)}, u32[]{:S(2)}) collective-permute-start(bf16[256,512]{1,0:T(8,128)(2,1)S(1)} %slice.83), channel_id=1, source_target_pairs={{0,16},{8,24},{16,32},{24,40},{32,48},{40,56},{48,0},{56,8},{1,17}... | collective-permute-start | bytes 786440 | tf_op jit(solution)/shard_map/ppermute | solution.py:16
  119.5 18.3 %collective-permute-start.27 = (bf16[2048,512]{1,0:T(8,128)(2,1)}, bf16[2048,512]{1,0:T(8,128)(2,1)}, u32[]{:S(2)}, u32[]{:S(2)}) collective-permute-start(bf16[2048,512]{1,0:T(8,128)(2,1)} %pad_maximum_fusion.1), channel_id=1, source_target_pairs={{0,64},{64,0},{1,65},{65,1},{2,66},{66,2},{3,67},{67,3},{4,68},{68... | collective-permute-start | bytes 6291464 | tf_op jit(solution)/shard_map/ppermute | solution.py:20
  121.0 4.0 %copy-start.7 = (bf16[256,512]{1,0:T(8,128)(2,1)}, bf16[256,512]{1,0:T(8,128)(2,1)S(1)}, u32[]{:S(2)}) copy-start(bf16[256,512]{1,0:T(8,128)(2,1)S(1)} %collective-permute-done.23.refs_12_) | copy-start | bytes 786436
  125.7 12.1 %collective-permute-start.28 = (bf16[2048,512]{1,0:T(8,128)(2,1)}, bf16[2048,512]{1,0:T(8,128)(2,1)}, u32[]{:S(2)}, u32[]{:S(2)}) collective-permute-start(bf16[2048,512]{1,0:T(8,128)(2,1)} %pad_maximum_fusion.2), channel_id=1, source_target_pairs={{0,64},{64,0},{1,65},{65,1},{2,66},{66,2},{3,67},{67,3},{4,68},{68... | collective-permute-start | bytes 6291464 | tf_op jit(solution)/shard_map/ppermute | solution.py:20
  127.8 10.0 %collective-permute-start.25 = (bf16[256,512]{1,0:T(8,128)(2,1)S(1)}, bf16[256,512]{1,0:T(8,128)(2,1)S(1)}, u32[]{:S(2)}, u32[]{:S(2)}) collective-permute-start(bf16[256,512]{1,0:T(8,128)(2,1)S(1)} %slice.85), channel_id=1, source_target_pairs={{0,2},{1,3},{2,4},{3,5},{4,6},{5,7},{6,0},{7,1},{8,10},{9,11},{10,... | collective-permute-start | bytes 786440 | tf_op jit(solution)/shard_map/ppermute | solution.py:16
  128.1 9.6 %collective-permute-start.26 = (bf16[256,512]{1,0:T(8,128)(2,1)S(1)}, bf16[256,512]{1,0:T(8,128)(2,1)S(1)}, u32[]{:S(2)}, u32[]{:S(2)}) collective-permute-start(bf16[256,512]{1,0:T(8,128)(2,1)S(1)} %slice.86), channel_id=1, source_target_pairs={{0,6},{1,7},{2,0},{3,1},{4,2},{5,3},{6,4},{7,5},{8,14},{9,15},{10,... | collective-permute-start | bytes 786440 | tf_op jit(solution)/shard_map/ppermute | solution.py:16
  152.0 36.9 %copy-start.13 = (f32[512,512]{1,0:T(8,128)S(1)}, f32[512,512]{1,0:T(8,128)}, u32[]{:S(2)}) copy-start(f32[512,512]{1,0:T(8,128)} %copy-done.12) | copy-start | bytes 3145732
  152.0 36.5 %all-to-all-start = ((bf16[8,272,512]{2,1,0:T(8,128)(2,1)}), bf16[8,272,512]{2,1,0:T(8,128)(2,1)S(1)}, u32[]{:S(2)}, u32[]{:S(2)}) async-start(bf16[8,272,512]{2,1,0:T(8,128)(2,1)} %shard_map.69), calls=%async_computation | async-start | bytes 4456448 | tf_op jit(solution)/shard_map/all_to_all | solution.py:299
  188.6 3.8 %copy-start.11 = (bf16[512,4096]{1,0:T(8,128)(2,1)S(1)}, bf16[512,4096]{1,0:T(8,128)(2,1)}, u32[]{:S(2)}) copy-start(bf16[512,4096]{1,0:T(8,128)(2,1)} %copy-done.10) | copy-start | bytes 12582916
  190.5 1.9 collective-permute-start.29
  (11 other events, 15.8 us)
